TPU v7x, 32 devices: a whole 2x2x4 slice. The times are simulated.
32 devices in a mesh: ctx: 8 (over y, x, core), ch: 4 (over z).
Axes of the slice: x: 2, y: 2, z: 4, core: 2. Of those that a mesh axis runs over, the one named last changes fastest.
Arguments:
- pre_gate: bfloat16 [128, 65536], P('ch', 'ctx'), may hold values from -6 to 6
- value: bfloat16 [128, 65536], P('ch', 'ctx'), may hold values from -6 to 6
- post_gate: bfloat16 [128, 65536], P('ch', 'ctx'), may hold values from -6 to 6
- filter_taps: float32 [8, 65536], P('ch', 'ctx'), may hold values from -0.015625 to 0.015625, as said below
- skip: float32 [128], P('ch'), may hold values from -6 to 6
Outputs:
- mixed: bfloat16 [128, 65536], P(None, ('ctx', 'ch'))
Inputs may be any that keep to these rules, and one draw needn't show every extreme that they name: `filter_taps`: one row of taps for each filter group.
All inputs are finite; a program needn't handle non-finite values.
Results may differ from a plain program's by a relative error of at most 0.013.
Values may be sent and summed in bfloat16 or wider, within the bound.
No kernel may reach another device: no remote copies, remote signals or barrier semaphores. Data moves between devices by JAX's collectives and lax.ppermute only.
A program may use at most 128 MiB of HBM per device.

v0:
```python
import functools

import jax
import jax.numpy as jnp
from jax import lax
from jax.experimental import pallas as pl
from jax.experimental.pallas import tpu as pltpu
from jax.sharding import PartitionSpec as P

W = 256
HALF = 128
SEGMENT = 4


def whole_vmem():
    return pl.BlockSpec(memory_space=pltpu.VMEM)


def pack_kernel(parts, own, blocks, group, pre_ref, val_ref, post_ref, taps_ref, send_ref, gate_ref, sig_s, gate_s):
    rows = own * blocks
    for j in range(blocks):
        cols = pl.ds(W * j, W)
        product = pre_ref[:, cols].astype(jnp.float32) * val_ref[:, cols].astype(jnp.float32)
        gate = post_ref[:, cols].astype(jnp.float32)
        for i in range(parts):
            sig_s[i, pl.ds(own * j, own), :] = product[own * i : own * i + own, :]
            gate_s[i, pl.ds(own * j, own), :] = gate[own * i : own * i + own, :]
        row = taps_ref[:, cols]
        for i in range(parts):
            which = own * i // group
            sig_s[i, pl.ds(rows + j, 1), :] = row[which : which + 1, :]
    send_ref[...] = sig_s[...].astype(jnp.bfloat16)
    gate_ref[...] = gate_s[...].astype(jnp.bfloat16)


def pack(pre_gate, value, post_gate, taps, parts):
    channels, block = value.shape
    own = channels // parts
    group = channels // taps.shape[0]
    blocks = block // W
    rows = own * blocks
    return pl.pallas_call(
        functools.partial(pack_kernel, parts, own, blocks, group),
        out_shape=(
            jax.ShapeDtypeStruct((parts, rows + blocks, W), jnp.bfloat16),
            jax.ShapeDtypeStruct((parts, rows, W), jnp.bfloat16),
        ),
        in_specs=[whole_vmem()] * 4,
        out_specs=(whole_vmem(), whole_vmem()),
        scratch_shapes=[
            pltpu.VMEM((parts, rows + blocks, W), jnp.float32),
            pltpu.VMEM((parts, rows, W), jnp.float32),
        ],
        compiler_params=pltpu.CompilerParams(vmem_limit_bytes=32 * 2**20),
        name="pack",
    )(pre_gate, value, post_gate, taps)


def conv_kernel(own, step_rows, got_ref, skip_ref, out_ref, x_wide, x_tall, taps_s, t_a, t_b, total):
    parts, local, _ = got_ref.shape
    blocks = local // (own + 1)
    local_rows = own * blocks
    rows = parts * local_rows
    shifts = step_rows // own
    steps = rows // step_rows

    x_tall[0:step_rows, :] = jnp.zeros((step_rows, W), jnp.float32)
    taps_s[0:8, :] = jnp.zeros((8, W), jnp.float32)
    for p in range(parts):
        x_tall[step_rows + p * local_rows : step_rows + (p + 1) * local_rows, :] = got_ref[
            p, 0:local_rows, :
        ].astype(jnp.float32)
        taps_s[8 + p * blocks : 8 + (p + 1) * blocks, :] = got_ref[p, local_rows:local, :].astype(jnp.float32)
    taps_s[8 + parts * blocks :, :] = jnp.zeros((taps_s.shape[0] - 8 - parts * blocks, W), jnp.float32)
    for s in range(shifts):
        first = step_rows - own * s
        x_wide[:, W * s : W * (s + 1)] = x_tall[first : first + rows, :].astype(jnp.bfloat16)
    total[...] = jnp.zeros(total.shape, jnp.float32)

    lane = lax.broadcasted_iota(jnp.int32, (HALF, HALF), 1)
    sub = lax.broadcasted_iota(jnp.int32, (HALF, HALF), 0)
    upper = lane >= sub

    def rolled(near, block, half):
        row = near[8 + block : 9 + block, HALF * half : HALF * (half + 1)]
        wide = jnp.broadcast_to(row, (HALF, HALF))
        return pltpu.roll(wide, 0, 1, stride=1, stride_axis=0)

    def build(t_ref, step):
        near = taps_s[pl.ds(pl.multiple_of(step * shifts, 8), 8 + shifts), :]
        last = rolled(near, -1, 1)
        odd = jnp.where(upper, last, rolled(near, -1, 0)).astype(jnp.bfloat16)
        for s in range(shifts):
            first = rolled(near, s, 0)
            even = jnp.where(upper, first, last).astype(jnp.bfloat16)
            last = rolled(near, s, 1)
            t_ref[W * s + HALF : W * (s + 1), 0:HALF] = odd
            odd = jnp.where(upper, last, first).astype(jnp.bfloat16)
            t_ref[W * s : W * s + HALF, 0:HALF] = even
            t_ref[W * s + HALF : W * (s + 1), HALF:W] = even
            t_ref[W * s : W * s + HALF, HALF:W] = odd

    def accumulate(t_ref, step, count):
        at = pl.ds(pl.multiple_of(step * step_rows, step_rows), count)
        total[at, :] += jnp.dot(x_wide[0:count, :], t_ref[...], preferred_element_type=jnp.float32)

    build(t_a, 0)
    for segment in range(steps // SEGMENT):
        count = rows - segment * SEGMENT * step_rows

        def two(it, carry, segment=segment, count=count):
            step = segment * SEGMENT + 2 * it
            build(t_b, step + 1)
            accumulate(t_a, step, count)
            build(t_a, step + 2)
            accumulate(t_b, step + 1, count)
            return carry

        lax.fori_loop(0, SEGMENT // 2, two, 0)

    me = lax.axis_index("ctx")
    channel = lax.broadcasted_iota(jnp.int32, (step_rows, W), 0) % own
    weight = jnp.zeros((step_rows, W), jnp.float32)
    for c in range(own):
        weight = jnp.where(channel == c, skip_ref[own * me + c], weight)
    for at in range(0, rows, step_rows):
        out_ref[at : at + step_rows, :] = (
            total[at : at + step_rows, :] + weight * x_tall[step_rows + at : 2 * step_rows + at, :]
        )


def convolve(got, skip, own):
    parts, local, _ = got.shape
    blocks = local // (own + 1)
    rows = parts * blocks * own
    step_rows = 32 if own >= 4 else 16
    shifts = step_rows // own
    steps = rows // step_rows
    return pl.pallas_call(
        functools.partial(conv_kernel, own, step_rows),
        out_shape=jax.ShapeDtypeStruct((rows, W), jnp.float32),
        in_specs=[whole_vmem(), pl.BlockSpec(memory_space=pltpu.SMEM)],
        out_specs=whole_vmem(),
        scratch_shapes=[
            pltpu.VMEM((rows, W * shifts), jnp.bfloat16),
            pltpu.VMEM((rows + step_rows, W), jnp.float32),
            pltpu.VMEM((8 + (steps + 2) * shifts, W), jnp.float32),
            pltpu.VMEM((W * shifts, W), jnp.bfloat16),
            pltpu.VMEM((W * shifts, W), jnp.bfloat16),
            pltpu.VMEM((rows + SEGMENT * step_rows, W), jnp.float32),
        ],
        compiler_params=pltpu.CompilerParams(vmem_limit_bytes=48 * 2**20),
        cost_estimate=pl.CostEstimate(
            flops=rows * rows * W * W // own, bytes_accessed=4 * rows * W, transcendentals=0
        ),
        name="toeplitz",
    )(got, skip)


def gate_kernel(ctx_count, ch_count, z_ref, gate_ref, out_ref):
    rows = out_ref.shape[1]
    for k in range(ctx_count):
        for m in range(ch_count):
            at = (k * ch_count + m) * rows
            part = z_ref[at : at + rows, :] * gate_ref[at : at + rows, :].astype(jnp.float32)
            out_ref[m * ctx_count + k, :, :] = part.astype(jnp.bfloat16)


def gate_rows(z, gate, ctx_count, ch_count):
    count = z.shape[0] // (ctx_count * ch_count)
    if count % 16:
        mixed = (z * gate.astype(jnp.float32)).astype(jnp.bfloat16)
        return mixed.reshape(ctx_count, ch_count, count, W).swapaxes(0, 1).reshape(-1, count, W)
    return pl.pallas_call(
        functools.partial(gate_kernel, ctx_count, ch_count),
        out_shape=jax.ShapeDtypeStruct((ctx_count * ch_count, count, W), jnp.bfloat16),
        in_specs=[whole_vmem()] * 2,
        out_specs=whole_vmem(),
        compiler_params=pltpu.CompilerParams(vmem_limit_bytes=16 * 2**20),
        name="gate",
    )(z, gate)


def unpack_kernel(own, got_ref, out_ref, tall):
    sources, rows, _ = got_ref.shape
    for p in range(sources):
        part = got_ref[p].astype(jnp.float32)
        for j in range(rows // own):
            tall[pl.ds(own * p, own), W * j : W * (j + 1)] = part[own * j : own * (j + 1), :]
    out_ref[...] = tall[...].astype(jnp.bfloat16)


def unpack(got, own):
    sources, rows, _ = got.shape
    shape = (sources * own, rows // own * W)
    if rows % 16:
        return got.reshape(sources, rows // own, own, W).swapaxes(1, 2).reshape(shape)
    return pl.pallas_call(
        functools.partial(unpack_kernel, own),
        out_shape=jax.ShapeDtypeStruct(shape, jnp.bfloat16),
        in_specs=[whole_vmem()],
        out_specs=whole_vmem(),
        scratch_shapes=[pltpu.VMEM(shape, jnp.float32)],
        compiler_params=pltpu.CompilerParams(vmem_limit_bytes=16 * 2**20),
        name="unpack",
    )(got)


def body(pre_gate, value, post_gate, filter_taps, skip):
    ctx_count = lax.axis_size("ctx")
    ch_count = lax.axis_size("ch")
    own = value.shape[0] // ctx_count
    send, gate = pack(pre_gate, value, post_gate, filter_taps, ctx_count)
    got = lax.all_to_all(send, "ctx", split_axis=0, concat_axis=0, tiled=True)
    gate = lax.all_to_all(gate, "ctx", split_axis=0, concat_axis=0, tiled=True)
    z = convolve(got, skip, own)
    mixed = gate_rows(z, gate.reshape(z.shape), ctx_count, ch_count)
    mixed = lax.all_to_all(mixed, ("ch", "ctx"), split_axis=0, concat_axis=0, tiled=True)
    return unpack(mixed, own)


def solution(mesh):
    placed = (P("ch", "ctx"), P("ch", "ctx"), P("ch", "ctx"), P("ch", "ctx"), P("ch"))
    return jax.shard_map(
        body, mesh=mesh, in_specs=placed, out_specs=P(None, ("ctx", "ch")), check_vma=False
    )
```

profile of v0, /device:TPU:1, one launch (start us, length us, event | category | flops | bytes accessed | tf_op | source)
XLA Modules:
  0.0 73.3 jit_solution(12031623054706091254)
XLA Ops:
  0.0 0.0 copy-start
  0.0 1.0 %copy-done = bf16[32,8192]{1,0:T(8,128)(2,1)S(1)} copy-done((bf16[32,8192]{1,0:T(8,128)(2,1)S(1)}, bf16[32,8192]{1,0:T(8,128)(2,1)}, u32[]{:S(2)}) %copy-start) | copy-done | bytes 524312
  1.0 0.0 copy-start.1
  1.0 1.0 %copy-done.1 = bf16[32,8192]{1,0:T(8,128)(2,1)S(1)} copy-done((bf16[32,8192]{1,0:T(8,128)(2,1)S(1)}, bf16[32,8192]{1,0:T(8,128)(2,1)}, u32[]{:S(2)}) %copy-start.1) | copy-done | bytes 524312
  2.1 0.0 copy-start.2
  2.1 1.0 %copy-done.2 = bf16[32,8192]{1,0:T(8,128)(2,1)S(1)} copy-done((bf16[32,8192]{1,0:T(8,128)(2,1)S(1)}, bf16[32,8192]{1,0:T(8,128)(2,1)}, u32[]{:S(2)}) %copy-start.2) | copy-done | bytes 524312
  3.1 0.0 copy-start.3
  3.1 0.8 %copy-done.3 = f32[2,8192]{1,0:T(2,128)S(1)} copy-done((f32[2,8192]{1,0:T(2,128)S(1)}, f32[2,8192]{1,0:T(2,128)}, u32[]{:S(2)}) %copy-start.3) | copy-done | bytes 65560
  4.0 1.3 %pack.1 = (bf16[8,160,256]{2,1,0:T(8,128)(2,1)S(1)}, bf16[8,128,256]{2,1,0:T(8,128)(2,1)}) custom-call(bf16[32,8192]{1,0:T(8,128)(2,1)S(1)} %copy-done, bf16[32,8192]{1,0:T(8,128)(2,1)S(1)} %copy-done.1, bf16[32,8192]{1,0:T(8,128)(2,1)S(1)} %copy-done.2, f32[2,8192]{1,0:T(2,128)S(1)} %copy-done.3), custom_call_target="tpu_custom_call" | custom-call | tf_op jit(solution)/shard_map/pack/pallas_call | solution.py:42
  5.2 15.3 %all_to_all.15.got_ref = bf16[8,160,256]{2,1,0:T(8,128)(2,1)S(1)} all-to-all(bf16[8,160,256]{2,1,0:T(8,128)(2,1)S(1)} %get-tuple-element.7), channel_id=1, replica_groups=mesh['ctx'=8,'ch'=4] {'ctx'}, dimensions={0} | all-to-all | bytes 1310720 | tf_op jit(solution)/shard_map/all_to_all | solution.py:214
  20.5 0.0 copy-start.4
  20.5 4.4 %all-to-all-start.1 = ((bf16[8,128,256]{2,1,0:T(8,128)(2,1)}), bf16[8,128,256]{2,1,0:T(8,128)(2,1)S(1)}, u32[]{:S(2)}, u32[]{:S(2)}) async-start(bf16[8,128,256]{2,1,0:T(8,128)(2,1)} %get-tuple-element.8), calls=%async_computation.1 | async-start | bytes 1048576 | tf_op jit(solution)/shard_map/all_to_all | solution.py:215
  24.9 0.0 copy-done.4
  24.9 26.2 %toeplitz.1.z_ref = f32[1024,256]{1,0:T(8,128)S(1)} custom-call(bf16[8,160,256]{2,1,0:T(8,128)(2,1)S(1)} %all_to_all.15.got_ref, f32[32]{0:T(128)S(1)} %copy-done.4), custom_call_target="tpu_custom_call" | custom-call | flops 17179869184 | bytes 1048576 | tf_op jit(solution)/shard_map/toeplitz/pallas_call | solution.py:139
  51.1 0.0 all-to-all-done.1
  51.1 0.1 gate.1
  51.2 21.1 %all_to_all.16.got_ref = bf16[32,32,256]{2,1,0:T(8,128)(2,1)S(1)} all-to-all(bf16[32,32,256]{2,1,0:T(8,128)(2,1)S(1)} %gate.1), channel_id=1, replica_groups=mesh['ctx'=8,'ch'=4] {'ch','ctx'}, dimensions={0} | all-to-all | bytes 1048576 | tf_op jit(solution)/shard_map/all_to_all | solution.py:218
  72.3 1.0 %unpack.1 = bf16[128,2048]{1,0:T(8,128)(2,1)} custom-call(bf16[32,32,256]{2,1,0:T(8,128)(2,1)S(1)} %all_to_all.16.got_ref), custom_call_target="tpu_custom_call" | custom-call | tf_op jit(solution)/shard_map/unpack/pallas_call | solution.py:198
Async XLA Ops:
  0.0 1.0 %copy-start = (bf16[32,8192]{1,0:T(8,128)(2,1)S(1)}, bf16[32,8192]{1,0:T(8,128)(2,1)}, u32[]{:S(2)}) copy-start(bf16[32,8192]{1,0:T(8,128)(2,1)} %pre_ref.1) | copy-start | bytes 1572868
  1.0 1.0 %copy-start.1 = (bf16[32,8192]{1,0:T(8,128)(2,1)S(1)}, bf16[32,8192]{1,0:T(8,128)(2,1)}, u32[]{:S(2)}) copy-start(bf16[32,8192]{1,0:T(8,128)(2,1)} %val_ref.1) | copy-start | bytes 1572868
  2.1 1.0 %copy-start.2 = (bf16[32,8192]{1,0:T(8,128)(2,1)S(1)}, bf16[32,8192]{1,0:T(8,128)(2,1)}, u32[]{:S(2)}) copy-start(bf16[32,8192]{1,0:T(8,128)(2,1)} %post_ref.1) | copy-start | bytes 1572868
  3.1 0.8 %copy-start.3 = (f32[2,8192]{1,0:T(2,128)S(1)}, f32[2,8192]{1,0:T(2,128)}, u32[]{:S(2)}) copy-start(f32[2,8192]{1,0:T(2,128)} %taps_ref.1) | copy-start | bytes 196612
  20.5 4.4 %copy-start.4 = (f32[32]{0:T(128)S(1)}, f32[32]{0:T(128)}, u32[]{:S(2)}) copy-start(f32[32]{0:T(128)} %skip_ref.1) | copy-start | bytes 388
  20.5 30.6 %all-to-all-start.1 = ((bf16[8,128,256]{2,1,0:T(8,128)(2,1)}), bf16[8,128,256]{2,1,0:T(8,128)(2,1)S(1)}, u32[]{:S(2)}, u32[]{:S(2)}) async-start(bf16[8,128,256]{2,1,0:T(8,128)(2,1)} %get-tuple-element.8), calls=%async_computation.1 | async-start | bytes 1048576 | tf_op jit(solution)/shard_map/all_to_all | solution.py:215
where the time goes:
time: 74.3 us; the launch traced here: 73.3 us
  blocking collectives  36.4 us (49%)
  Pallas kernels  28.5 us (38%)
  starting transfers between devices  4.4 us (6%)
  local copies, waits for them, and re-layouts  3.97 us (5%)
    pallas_call x1, Pallas kernels, convolve(): pl.pallas_call(functools.partial(conv_kernel, own, step_rows), out_shape=...  26.2 us
    all_to_all x1, blocking collectives, body(): lax.all_to_all(mixed, ('ch', 'ctx'), split_axis=0, concat_axis=0, tiled=T...  21.1 us
    all_to_all x1, blocking collectives, body(): got = lax.all_to_all(send, 'ctx', split_axis=0, concat_axis=0, tiled=True)  15.3 us
    all_to_all x1, starting transfers between devices, body(): gate = lax.all_to_all(gate, 'ctx', split_axis=0, concat_axis=0, tiled=True)  4.4 us
    unnamed x10, local copies, waits for them, and re-layouts  3.97 us
  transfers between devices with their start and end apart: 1, of which 0 were waited for; matrix products, arithmetic and copies ran while one was open for 0% of the time, Pallas kernels for 36%

commit v1 on v0

v1 whole, which is shorter than its diff:
```python
import functools

import jax
import jax.numpy as jnp
from jax import lax
from jax.experimental import pallas as pl
from jax.experimental.pallas import tpu as pltpu
from jax.sharding import PartitionSpec as P

W = 256
HALF = 128
TILE = 16
CUTS = 4


def whole_vmem():
    return pl.BlockSpec(memory_space=pltpu.VMEM)


def in_hbm():
    return pl.BlockSpec(memory_space=pltpu.HBM)


def pack_signal_kernel(parts, own, blocks, group, pre_ref, val_ref, taps_ref, *rest):
    out_refs = rest[:parts]
    pre_s, val_s, taps_s, tall, sems = rest[parts:]
    rows = own * blocks
    width = blocks * W // CUTS
    copies = []
    for q in range(CUTS):
        cols = pl.ds(q * width, width)
        copies.append(
            [
                pltpu.make_async_copy(pre_ref.at[:, cols], pre_s.at[:, cols], sems.at[q, 0]),
                pltpu.make_async_copy(val_ref.at[:, cols], val_s.at[:, cols], sems.at[q, 1]),
            ]
        )
    taps_copy = pltpu.make_async_copy(taps_ref, taps_s, sems.at[CUTS, 0])
    taps_copy.start()
    for pair in copies:
        for copy in pair:
            copy.start()
    taps_copy.wait()
    for j in range(blocks):
        row = taps_s[:, W * j : W * (j + 1)]
        for i in range(parts):
            which = own * i // group
            tall[i, rows + j : rows + j + 1, :] = row[which : which + 1, :]
    for j in range(blocks):
        if j % (blocks // CUTS) == 0:
            for copy in copies[j // (blocks // CUTS)]:
                copy.wait()
        cols = slice(W * j, W * (j + 1))
        product = pre_s[:, cols].astype(jnp.float32) * val_s[:, cols].astype(jnp.float32)
        for i in range(parts):
            tall[i, own * j : own * (j + 1), :] = product[own * i : own * (i + 1), :]
    me = lax.axis_index("ctx")
    for d in range(parts):
        out_refs[d][...] = tall[jnp.bitwise_xor(me, d)].astype(jnp.bfloat16)


def pack_signal(pre_gate, value, taps, parts):
    channels, block = value.shape
    own = channels // parts
    group = channels // taps.shape[0]
    blocks = block // W
    rows = own * blocks + blocks
    return pl.pallas_call(
        functools.partial(pack_signal_kernel, parts, own, blocks, group),
        out_shape=[jax.ShapeDtypeStruct((rows, W), jnp.bfloat16)] * parts,
        in_specs=[in_hbm()] * 3,
        out_specs=[whole_vmem()] * parts,
        scratch_shapes=[
            pltpu.VMEM(pre_gate.shape, jnp.bfloat16),
            pltpu.VMEM(value.shape, jnp.bfloat16),
            pltpu.VMEM(taps.shape, jnp.float32),
            pltpu.VMEM((parts, rows, W), jnp.float32),
            pltpu.SemaphoreType.DMA((CUTS + 1, 2)),
        ],
        compiler_params=pltpu.CompilerParams(vmem_limit_bytes=24 * 2**20),
        name="pack_signal",
    )(pre_gate, value, taps)


def pack_gate_kernel(parts, own, blocks, post_ref, *rest):
    out_refs = rest[:parts]
    post_s, tall, sems = rest[parts:]
    width = blocks * W // CUTS
    copies = []
    for q in range(CUTS):
        cols = pl.ds(q * width, width)
        copies.append(pltpu.make_async_copy(post_ref.at[:, cols], post_s.at[:, cols], sems.at[q]))
    for copy in copies:
        copy.start()
    for j in range(blocks):
        if j % (blocks // CUTS) == 0:
            copies[j // (blocks // CUTS)].wait()
        gate = post_s[:, W * j : W * (j + 1)].astype(jnp.float32)
        for i in range(parts):
            tall[i, own * j : own * (j + 1), :] = gate[own * i : own * (i + 1), :]
    me = lax.axis_index("ctx")
    for d in range(parts):
        out_refs[d][...] = tall[jnp.bitwise_xor(me, d)].astype(jnp.bfloat16)


def pack_gate(post_gate, parts):
    channels, block = post_gate.shape
    own = channels // parts
    blocks = block // W
    rows = own * blocks
    return pl.pallas_call(
        functools.partial(pack_gate_kernel, parts, own, blocks),
        out_shape=[jax.ShapeDtypeStruct((rows, W), jnp.bfloat16)] * parts,
        in_specs=[in_hbm()],
        out_specs=[whole_vmem()] * parts,
        scratch_shapes=[
            pltpu.VMEM(post_gate.shape, jnp.bfloat16),
            pltpu.VMEM((parts, rows, W), jnp.float32),
            pltpu.SemaphoreType.DMA((CUTS,)),
        ],
        compiler_params=pltpu.CompilerParams(vmem_limit_bytes=24 * 2**20),
        name="pack_gate",
    )(post_gate)


def swap_all(pieces):
    parts = len(pieces)
    got = [pieces[0]]
    for d in range(1, parts):
        got.append(lax.ppermute(pieces[d], "ctx", [(i, i ^ d) for i in range(parts)]))
    return got


def conv_kernel(own, step_rows, parts, skip_ref, *rest):
    got_refs = rest[:parts]
    out_ref, x_wide, x_tall, taps_s, t_a, t_b, total = rest[parts:]
    local = got_refs[0].shape[0]
    blocks = local // (own + 1)
    local_rows = own * blocks
    rows = parts * local_rows
    shifts = step_rows // own
    steps = rows // step_rows
    fine = TILE // own
    tiles = shifts // fine
    head = TILE * (tiles - 1)
    me = lax.axis_index("ctx")

    x_tall[0:TILE, :] = jnp.zeros((TILE, W), jnp.float32)
    taps_s[0:8, :] = jnp.zeros((8, W), jnp.float32)
    for d in range(parts):
        p = jnp.bitwise_xor(me, d)
        x_tall[pl.ds(pl.multiple_of(TILE + p * local_rows, 8), local_rows), :] = got_refs[d][
            0:local_rows, :
        ].astype(jnp.float32)
        taps_s[pl.ds(pl.multiple_of(8 + p * blocks, 8), blocks), :] = got_refs[d][local_rows:local, :].astype(
            jnp.float32
        )
    if head:
        x_wide[0:head, :] = jnp.zeros((head, W * fine), jnp.bfloat16)
    for s in range(fine):
        first = TILE - own * s
        x_wide[head : head + rows, W * s : W * (s + 1)] = x_tall[first : first + rows, :].astype(jnp.bfloat16)

    lane = lax.broadcasted_iota(jnp.int32, (HALF, HALF), 1)
    sub = lax.broadcasted_iota(jnp.int32, (HALF, HALF), 0)
    upper = lane >= sub

    def rolled(near, block, half):
        row = near[8 + block : 9 + block, HALF * half : HALF * (half + 1)]
        wide = jnp.broadcast_to(row, (HALF, HALF))
        return pltpu.roll(wide, 0, 1, stride=1, stride_axis=0)

    def build(t_ref, pair):
        near = taps_s[2 * pair * shifts : 2 * (pair + 1) * shifts + 8, :]
        last = rolled(near, -1, 1)
        odd = jnp.where(upper, last, rolled(near, -1, 0)).astype(jnp.bfloat16)
        for s in range(2 * shifts):
            first = rolled(near, s, 0)
            even = jnp.where(upper, first, last).astype(jnp.bfloat16)
            last = rolled(near, s, 1)
            row = W * (s % shifts)
            col = W * (s // shifts)
            t_ref[row + HALF : row + W, col : col + HALF] = odd
            odd = jnp.where(upper, last, first).astype(jnp.bfloat16)
            t_ref[row : row + HALF, col : col + HALF] = even
            t_ref[row + HALF : row + W, col + HALF : col + W] = even
            t_ref[row : row + HALF, col + HALF : col + W] = odd

    def accumulate(t_ref, pair):
        at = 2 * pair * step_rows
        count = rows - at
        depth = W * fine
        product = jnp.dot(
            x_wide[head : head + count, :], t_ref[0:depth, :], preferred_element_type=jnp.float32
        )
        for u in range(1, tiles):
            first = head - TILE * u
            product += jnp.dot(
                x_wide[first : first + count, :],
                t_ref[depth * u : depth * (u + 1), :],
                preferred_element_type=jnp.float32,
            )
        if pair == 0:
            total[...] = product[:, 0:W]
        else:
            total[at:rows, :] += product[:, 0:W]
        total[at + step_rows : rows, :] += product[0 : count - step_rows, W : 2 * W]

    build(t_a, 0)
    for pair in range(steps // 2):
        now, later = (t_a, t_b) if pair % 2 == 0 else (t_b, t_a)
        if pair + 1 < steps // 2:
            build(later, pair + 1)
        accumulate(now, pair)

    channel = lax.broadcasted_iota(jnp.int32, (step_rows, W), 0) % own
    weight = jnp.zeros((step_rows, W), jnp.float32)
    for c in range(own):
        weight = jnp.where(channel == c, skip_ref[own * me + c], weight)
    for at in range(0, rows, step_rows):
        out_ref[at : at + step_rows, :] = (
            total[at : at + step_rows, :] + weight * x_tall[TILE + at : TILE + at + step_rows, :]
        )


def convolve(got, skip, own):
    parts = len(got)
    local, _ = got[0].shape
    blocks = local // (own + 1)
    rows = parts * blocks * own
    step_rows = 32 if own >= 4 else TILE
    shifts = step_rows // own
    steps = rows // step_rows
    head = step_rows - TILE
    return pl.pallas_call(
        functools.partial(conv_kernel, own, step_rows, parts),
        out_shape=jax.ShapeDtypeStruct((rows, W), jnp.float32),
        in_specs=[pl.BlockSpec(memory_space=pltpu.SMEM)] + [whole_vmem()] * parts,
        out_specs=whole_vmem(),
        scratch_shapes=[
            pltpu.VMEM((head + rows, W * (TILE // own)), jnp.bfloat16),
            pltpu.VMEM((rows + TILE, W), jnp.float32),
            pltpu.VMEM((8 + steps * shifts, W), jnp.float32),
            pltpu.VMEM((W * shifts, 2 * W), jnp.bfloat16),
            pltpu.VMEM((W * shifts, 2 * W), jnp.bfloat16),
            pltpu.VMEM((rows, W), jnp.float32),
        ],
        compiler_params=pltpu.CompilerParams(vmem_limit_bytes=48 * 2**20),
        cost_estimate=pl.CostEstimate(
            flops=rows * rows * W * W // own, bytes_accessed=4 * rows * W, transcendentals=0
        ),
        name="toeplitz",
    )(skip, *got)


def gate_kernel(ctx_count, ch_count, z_ref, *rest):
    gate_refs = rest[:ctx_count]
    out_ref = rest[ctx_count]
    rows = out_ref.shape[1]
    me = lax.axis_index("ctx")
    for d in range(ctx_count):
        k = jnp.bitwise_xor(me, d)
        for m in range(ch_count):
            at = pl.multiple_of((k * ch_count + m) * rows, rows)
            part = z_ref[pl.ds(at, rows), :] * gate_refs[d][m * rows : (m + 1) * rows, :].astype(jnp.float32)
            out_ref[m * ctx_count + k] = part.astype(jnp.bfloat16)


def gate_rows(z, gates, ctx_count, ch_count):
    count = z.shape[0] // (ctx_count * ch_count)
    if count % TILE:
        me = lax.axis_index("ctx")
        order = jnp.bitwise_xor(me, jnp.arange(ctx_count))
        gate = jnp.stack(gates)[order].reshape(z.shape)
        mixed = (z * gate.astype(jnp.float32)).astype(jnp.bfloat16)
        return mixed.reshape(ctx_count, ch_count, count, W).swapaxes(0, 1).reshape(-1, count, W)
    return pl.pallas_call(
        functools.partial(gate_kernel, ctx_count, ch_count),
        out_shape=jax.ShapeDtypeStruct((ctx_count * ch_count, count, W), jnp.bfloat16),
        in_specs=[whole_vmem()] * (1 + ctx_count),
        out_specs=whole_vmem(),
        compiler_params=pltpu.CompilerParams(vmem_limit_bytes=16 * 2**20),
        name="gate",
    )(z, *gates)


def unpack_kernel(own, got_ref, out_ref, tall):
    sources, rows, _ = got_ref.shape
    for p in range(sources):
        part = got_ref[p].astype(jnp.float32)
        for j in range(rows // own):
            tall[own * p : own * (p + 1), W * j : W * (j + 1)] = part[own * j : own * (j + 1), :]
    out_ref[...] = tall[...].astype(jnp.bfloat16)


def unpack(got, own):
    sources, rows, _ = got.shape
    shape = (sources * own, rows // own * W)
    if rows % TILE:
        return got.reshape(sources, rows // own, own, W).swapaxes(1, 2).reshape(shape)
    return pl.pallas_call(
        functools.partial(unpack_kernel, own),
        out_shape=jax.ShapeDtypeStruct(shape, jnp.bfloat16),
        in_specs=[whole_vmem()],
        out_specs=whole_vmem(),
        scratch_shapes=[pltpu.VMEM(shape, jnp.float32)],
        compiler_params=pltpu.CompilerParams(vmem_limit_bytes=16 * 2**20),
        name="unpack",
    )(got)


def body(pre_gate, value, post_gate, filter_taps, skip):
    ctx_count = lax.axis_size("ctx")
    ch_count = lax.axis_size("ch")
    own = value.shape[0] // ctx_count
    got = swap_all(pack_signal(pre_gate, value, filter_taps, ctx_count))
    gates = swap_all(pack_gate(post_gate, ctx_count))
    z = convolve(got, skip, own)
    mixed = gate_rows(z, gates, ctx_count, ch_count)
    mixed = lax.all_to_all(mixed, ("ch", "ctx"), split_axis=0, concat_axis=0, tiled=True)
    return unpack(mixed, own)


def solution(mesh):
    placed = (P("ch", "ctx"), P("ch", "ctx"), P("ch", "ctx"), P("ch", "ctx"), P("ch"))
    return jax.shard_map(
        body, mesh=mesh, in_specs=placed, out_specs=P(None, ("ctx", "ch")), check_vma=False
    )
```

time: 74.3 us -> 69.3 us (0.933)
  blocking collectives: 36.4 us -> 19.2 us
  starting transfers between devices: 4.4 us -> 14.2 us
  waiting for transfers between devices: 0.01 us -> 7.91 us
  Pallas kernels: 28.5 us -> 24.1 us
  local copies, waits for them, and re-layouts: 3.97 us -> 2.93 us
    all_to_all x1 -> x0, blocking collectives: 15.3 us -> none  [body(): got = lax.all_to_all(send, 'ctx', split_axis=0, concat_axis=0, tiled=True)]
    ppermute x0 -> x14, starting transfers between devices: none -> 14.2 us  [swap_all(): lax.ppermute(pieces[d], 'ctx', [(i, i ^ d) for i in range(parts)])]
    ppermute x0 -> x14, waiting for transfers between devices: none -> 7.91 us  [swap_all(): lax.ppermute(pieces[d], 'ctx', [(i, i ^ d) for i in range(parts)])]
    pallas_call x2 -> x3, Pallas kernels: 27.4 us -> 23 us  [the longest x1 21.8 us: convolve(): pl.pallas_call(functools.partial(conv_kernel, own, step_rows, parts), out...]
    all_to_all x1 -> x0, starting transfers between devices: 4.4 us -> none  [body(): gate = lax.all_to_all(gate, 'ctx', split_axis=0, concat_axis=0, tiled=True)]
    all_to_all x1, blocking collectives: 21.1 us -> 19.2 us  [body(): lax.all_to_all(mixed, ('ch', 'ctx'), split_axis=0, concat_axis=0, tiled=T...]
    unnamed x10, local copies, waits for them, and re-layouts: 3.97 us -> 2.93 us
  transfers between devices with their start and end apart: 1 -> 14, of which waited for: 0 -> 3; matrix products, arithmetic and copies ran while one was open for 0% -> 0% of each run, Pallas kernels for 36% -> 32%
where the time goes in v1:
time: 69.3 us; the launch traced here: 68.4 us
  Pallas kernels  24.1 us (35%)
  blocking collectives  19.2 us (28%)
  starting transfers between devices  14.2 us (20%)
  waiting for transfers between devices  7.91 us (11%)
  local copies, waits for them, and re-layouts  2.93 us (4%)
    pallas_call x1, Pallas kernels, convolve(): pl.pallas_call(functools.partial(conv_kernel, own, step_rows, parts), out...  21.8 us
    all_to_all x1, blocking collectives, body(): lax.all_to_all(mixed, ('ch', 'ctx'), split_axis=0, concat_axis=0, tiled=T...  19.2 us
    ppermute x14, starting transfers between devices, swap_all(): lax.ppermute(pieces[d], 'ctx', [(i, i ^ d) for i in range(parts)])  14.2 us
    ppermute x14, waiting for transfers between devices, swap_all(): lax.ppermute(pieces[d], 'ctx', [(i, i ^ d) for i in range(parts)])  7.91 us
    unnamed x10, local copies, waits for them, and re-layouts  2.93 us
  transfers between devices with their start and end apart: 14, of which 3 were waited for; matrix products, arithmetic and copies ran while one was open for 0% of the time, Pallas kernels for 32%

profile of v1, /device:TPU:1, one launch (start us, length us, event | category | flops | bytes accessed | tf_op | source)
XLA Modules:
  0.0 68.4 jit_solution(3122279194404192872)
XLA Ops:
  0.0 1.0 %copy-done = bf16[32,8192]{1,0:T(8,128)(2,1)S(1)} copy-done((bf16[32,8192]{1,0:T(8,128)(2,1)S(1)}, bf16[32,8192]{1,0:T(8,128)(2,1)}, u32[]{:S(2)}) %copy-start) | copy-done | bytes 524312
  1.0 1.0 %copy-done.1 = bf16[32,8192]{1,0:T(8,128)(2,1)S(1)} copy-done((bf16[32,8192]{1,0:T(8,128)(2,1)S(1)}, bf16[32,8192]{1,0:T(8,128)(2,1)}, u32[]{:S(2)}) %copy-start.1) | copy-done | bytes 524312
  2.1 0.8 %copy-done.3 = f32[2,8192]{1,0:T(2,128)S(1)} copy-done((f32[2,8192]{1,0:T(2,128)S(1)}, f32[2,8192]{1,0:T(2,128)}, u32[]{:S(2)}) %copy-start.3) | copy-done | bytes 65560
  2.9 0.8 %pack_signal.1 = (bf16[160,256]{1,0:T(8,128)(2,1)S(1)}, bf16[160,256]{1,0:T(8,128)(2,1)S(1)}, bf16[160,256]{1,0:T(8,128)(2,1)S(1)}, bf16[160,256]{1,0:T(8,128)(2...) custom-call(bf16[32,8192]{1,0:T(8,128)(2,1)S(1)} %copy-done, ...), custom_call_target="tpu_custom_call" | custom-call | tf_op jit(solution)/shard_map/pack_signal/pallas_call | solution.py:68
  3.9 2.7 %collective-permute-start.1 = (bf16[160,256]{1,0:T(8,128)(2,1)S(1)}, bf16[160,256]{1,0:T(8,128)(2,1)S(1)}, u32[]{:S(2)}, u32[]{:S(2)}) collective-permute-start(bf16[160,256]{1,0:T(8,128)(2,1)S(1)} %get-tuple-element.23), channel_id=1, source_target_pairs={{0,8},{4,12},{8,0},{12,4},{16,24},{20,28},{24,16},{28,20},{1,9},{5... | collective-permute-start | bytes 245768 | tf_op jit(solution)/shard_map/ppermute | solution.py:130
  6.5 0.4 pack_gate.1
  6.9 1.3 %collective-permute-start.10 = (bf16[128,256]{1,0:T(8,128)(2,1)S(1)}, bf16[128,256]{1,0:T(8,128)(2,1)S(1)}, u32[]{:S(2)}, u32[]{:S(2)}) collective-permute-start(bf16[128,256]{1,0:T(8,128)(2,1)S(1)} %get-tuple-element.33), channel_id=1, source_target_pairs={{0,16},{4,20},{8,24},{12,28},{16,0},{20,4},{24,8},{28,12},{1,17},{... | collective-permute-start | bytes 196616 | tf_op jit(solution)/shard_map/ppermute | solution.py:130
  8.2 0.7 %collective-permute-start.11 = (bf16[128,256]{1,0:T(8,128)(2,1)S(1)}, bf16[128,256]{1,0:T(8,128)(2,1)S(1)}, u32[]{:S(2)}, u32[]{:S(2)}) collective-permute-start(bf16[128,256]{1,0:T(8,128)(2,1)S(1)} %get-tuple-element.34), channel_id=1, source_target_pairs={{0,20},{4,16},{8,28},{12,24},{16,4},{20,0},{24,12},{28,8},{1,21},{... | collective-permute-start | bytes 196616 | tf_op jit(solution)/shard_map/ppermute | solution.py:130
  9.0 1.1 %collective-permute-done.10.rest_4_ = bf16[128,256]{1,0:T(8,128)(2,1)S(1)} collective-permute-done((bf16[128,256]{1,0:T(8,128)(2,1)S(1)}, bf16[128,256]{1,0:T(8,128)(2,1)S(1)}, u32[]{:S(2)}, u32[]{:S(2)}) %collective-permute-start.10) | collective-permute-done | bytes 65568 | tf_op jit(solution)/shard_map/ppermute | solution.py:130
  10.1 1.2 %collective-permute-start.3 = (bf16[160,256]{1,0:T(8,128)(2,1)S(1)}, bf16[160,256]{1,0:T(8,128)(2,1)S(1)}, u32[]{:S(2)}, u32[]{:S(2)}) collective-permute-start(bf16[160,256]{1,0:T(8,128)(2,1)S(1)} %get-tuple-element.25), channel_id=1, source_target_pairs={{0,16},{4,20},{8,24},{12,28},{16,0},{20,4},{24,8},{28,12},{1,17},{... | collective-permute-start | bytes 245768 | tf_op jit(solution)/shard_map/ppermute | solution.py:130
  11.4 1.5 %collective-permute-done.11.rest_5_ = bf16[128,256]{1,0:T(8,128)(2,1)S(1)} collective-permute-done((bf16[128,256]{1,0:T(8,128)(2,1)S(1)}, bf16[128,256]{1,0:T(8,128)(2,1)S(1)}, u32[]{:S(2)}, u32[]{:S(2)}) %collective-permute-start.11) | collective-permute-done | bytes 65568 | tf_op jit(solution)/shard_map/ppermute | solution.py:130
  12.9 0.5 collective-permute-start.4
  13.4 1.7 %collective-permute-start.5 = (bf16[160,256]{1,0:T(8,128)(2,1)S(1)}, bf16[160,256]{1,0:T(8,128)(2,1)S(1)}, u32[]{:S(2)}, u32[]{:S(2)}) collective-permute-start(bf16[160,256]{1,0:T(8,128)(2,1)S(1)} %get-tuple-element.27), channel_id=1, source_target_pairs={{0,24},{4,28},{8,16},{12,20},{16,8},{20,12},{24,0},{28,4},{1,25},{... | collective-permute-start | bytes 245768 | tf_op jit(solution)/shard_map/ppermute | solution.py:130
  15.1 1.5 %collective-permute-start.6 = (bf16[160,256]{1,0:T(8,128)(2,1)S(1)}, bf16[160,256]{1,0:T(8,128)(2,1)S(1)}, u32[]{:S(2)}, u32[]{:S(2)}) collective-permute-start(bf16[160,256]{1,0:T(8,128)(2,1)S(1)} %get-tuple-element.28), channel_id=1, source_target_pairs={{0,28},{4,24},{8,20},{12,16},{16,12},{20,8},{24,4},{28,0},{1,29},{... | collective-permute-start | bytes 245768 | tf_op jit(solution)/shard_map/ppermute | solution.py:130
  16.6 0.7 collective-permute-start.12
  17.2 1.5 %collective-permute-start.13 = (bf16[128,256]{1,0:T(8,128)(2,1)S(1)}, bf16[128,256]{1,0:T(8,128)(2,1)S(1)}, u32[]{:S(2)}, u32[]{:S(2)}) collective-permute-start(bf16[128,256]{1,0:T(8,128)(2,1)S(1)} %get-tuple-element.36), channel_id=1, source_target_pairs={{0,28},{4,24},{8,20},{12,16},{16,12},{20,8},{24,4},{28,0},{1,29},{... | collective-permute-start | bytes 196616 | tf_op jit(solution)/shard_map/ppermute | solution.py:130
  18.7 5.3 %collective-permute-done.4.rest_5_ = bf16[160,256]{1,0:T(8,128)(2,1)S(1)} collective-permute-done((bf16[160,256]{1,0:T(8,128)(2,1)S(1)}, bf16[160,256]{1,0:T(8,128)(2,1)S(1)}, u32[]{:S(2)}, u32[]{:S(2)}) %collective-permute-start.4) | collective-permute-done | bytes 81952 | tf_op jit(solution)/shard_map/ppermute | solution.py:130
  24.0 0.6 collective-permute-start.7
  24.6 0.3 collective-permute-start.8
  24.9 1.4 %collective-permute-start.9 = (bf16[128,256]{1,0:T(8,128)(2,1)S(1)}, bf16[128,256]{1,0:T(8,128)(2,1)S(1)}, u32[]{:S(2)}, u32[]{:S(2)}) collective-permute-start(bf16[128,256]{1,0:T(8,128)(2,1)S(1)} %get-tuple-element.32), channel_id=1, source_target_pairs={{0,12},{4,8},{8,4},{12,0},{16,28},{20,24},{24,20},{28,16},{1,13},{... | collective-permute-start | bytes 196616 | tf_op jit(solution)/shard_map/ppermute | solution.py:130
  26.3 21.8 %toeplitz.1.z_ref = f32[1024,256]{1,0:T(8,128)S(1)} custom-call(f32[32]{0:T(128)S(1)} %copy-done.4, bf16[160,256]{1,0:T(8,128)(2,1)S(1)} %get-tuple-element.21.rest_0_, bf16[160,256]{1,0:T(8,128)(2,1)S(1)} %collective-permute-done.rest_1_, bf16[160,256]{1,0:T(8,128)(2,1)S(1)} %collective-permute-done.1.rest_2_, ...), custom_call_target="tpu_custom_call" | custom-call | flops 17179869184 | bytes 1048576 | tf_op jit(solution)/shard_map/toeplitz/pallas_call | solution.py:235
  48.1 0.1 gate.1
  48.3 19.2 %all_to_all.5.got_ref = bf16[32,32,256]{2,1,0:T(8,128)(2,1)S(1)} all-to-all(bf16[32,32,256]{2,1,0:T(8,128)(2,1)S(1)} %gate.1), channel_id=1, replica_groups=mesh['ctx'=8,'ch'=4] {'ch','ctx'}, dimensions={0} | all-to-all | bytes 1048576 | tf_op jit(solution)/shard_map/all_to_all | solution.py:320
  67.5 1.0 %unpack.1 = bf16[128,2048]{1,0:T(8,128)(2,1)} custom-call(bf16[32,32,256]{2,1,0:T(8,128)(2,1)S(1)} %all_to_all.5.got_ref), custom_call_target="tpu_custom_call" | custom-call | tf_op jit(solution)/shard_map/unpack/pallas_call | solution.py:301
  (20 shorter events, 0.2 us)
Async XLA Ops:
  0.0 1.0 %copy-start = (bf16[32,8192]{1,0:T(8,128)(2,1)S(1)}, bf16[32,8192]{1,0:T(8,128)(2,1)}, u32[]{:S(2)}) copy-start(bf16[32,8192]{1,0:T(8,128)(2,1)} %pre_ref.1) | copy-start | bytes 1572868
  1.0 1.0 %copy-start.1 = (bf16[32,8192]{1,0:T(8,128)(2,1)S(1)}, bf16[32,8192]{1,0:T(8,128)(2,1)}, u32[]{:S(2)}) copy-start(bf16[32,8192]{1,0:T(8,128)(2,1)} %val_ref.1) | copy-start | bytes 1572868
  2.1 0.8 %copy-start.3 = (f32[2,8192]{1,0:T(2,128)S(1)}, f32[2,8192]{1,0:T(2,128)}, u32[]{:S(2)}) copy-start(f32[2,8192]{1,0:T(2,128)} %taps_ref.1) | copy-start | bytes 196612
  2.9 3.6 %copy-start.2 = (bf16[32,8192]{1,0:T(8,128)(2,1)S(1)}, bf16[32,8192]{1,0:T(8,128)(2,1)}, u32[]{:S(2)}) copy-start(bf16[32,8192]{1,0:T(8,128)(2,1)} %post_ref.1) | copy-start | bytes 1572868
  3.7 9.7 %collective-permute-start = (bf16[160,256]{1,0:T(8,128)(2,1)S(1)}, bf16[160,256]{1,0:T(8,128)(2,1)S(1)}, u32[]{:S(2)}, u32[]{:S(2)}) collective-permute-start(bf16[160,256]{1,0:T(8,128)(2,1)S(1)} %get-tuple-element.22), channel_id=1, source_target_pairs={{0,4},{4,0},{8,12},{12,8},{16,20},{20,16},{24,28},{28,24},{1,5},{5... | collective-permute-start | bytes 245768 | tf_op jit(solution)/shard_map/ppermute | solution.py:130
  3.9 11.2 %collective-permute-start.1 = (bf16[160,256]{1,0:T(8,128)(2,1)S(1)}, bf16[160,256]{1,0:T(8,128)(2,1)S(1)}, u32[]{:S(2)}, u32[]{:S(2)}) collective-permute-start(bf16[160,256]{1,0:T(8,128)(2,1)S(1)} %get-tuple-element.23), channel_id=1, source_target_pairs={{0,8},{4,12},{8,0},{12,4},{16,24},{20,28},{24,16},{28,20},{1,9},{5... | collective-permute-start | bytes 245768 | tf_op jit(solution)/shard_map/ppermute | solution.py:130
  6.9 3.2 %collective-permute-start.10 = (bf16[128,256]{1,0:T(8,128)(2,1)S(1)}, bf16[128,256]{1,0:T(8,128)(2,1)S(1)}, u32[]{:S(2)}, u32[]{:S(2)}) collective-permute-start(bf16[128,256]{1,0:T(8,128)(2,1)S(1)} %get-tuple-element.33), channel_id=1, source_target_pairs={{0,16},{4,20},{8,24},{12,28},{16,0},{20,4},{24,8},{28,12},{1,17},{... | collective-permute-start | bytes 196616 | tf_op jit(solution)/shard_map/ppermute | solution.py:130
  8.2 4.6 %collective-permute-start.11 = (bf16[128,256]{1,0:T(8,128)(2,1)S(1)}, bf16[128,256]{1,0:T(8,128)(2,1)S(1)}, u32[]{:S(2)}, u32[]{:S(2)}) collective-permute-start(bf16[128,256]{1,0:T(8,128)(2,1)S(1)} %get-tuple-element.34), channel_id=1, source_target_pairs={{0,20},{4,16},{8,28},{12,24},{16,4},{20,0},{24,12},{28,8},{1,21},{... | collective-permute-start | bytes 196616 | tf_op jit(solution)/shard_map/ppermute | solution.py:130
  9.0 7.6 %collective-permute-start.2 = (bf16[160,256]{1,0:T(8,128)(2,1)S(1)}, bf16[160,256]{1,0:T(8,128)(2,1)S(1)}, u32[]{:S(2)}, u32[]{:S(2)}) collective-permute-start(bf16[160,256]{1,0:T(8,128)(2,1)S(1)} %get-tuple-element.24), channel_id=1, source_target_pairs={{0,12},{4,8},{8,4},{12,0},{16,28},{20,24},{24,20},{28,16},{1,13},{... | collective-permute-start | bytes 245768 | tf_op jit(solution)/shard_map/ppermute | solution.py:130
  10.1 7.1 %collective-permute-start.3 = (bf16[160,256]{1,0:T(8,128)(2,1)S(1)}, bf16[160,256]{1,0:T(8,128)(2,1)S(1)}, u32[]{:S(2)}, u32[]{:S(2)}) collective-permute-start(bf16[160,256]{1,0:T(8,128)(2,1)S(1)} %get-tuple-element.25), channel_id=1, source_target_pairs={{0,16},{4,20},{8,24},{12,28},{16,0},{20,4},{24,8},{28,12},{1,17},{... | collective-permute-start | bytes 245768 | tf_op jit(solution)/shard_map/ppermute | solution.py:130
  12.9 11.1 %collective-permute-start.4 = (bf16[160,256]{1,0:T(8,128)(2,1)S(1)}, bf16[160,256]{1,0:T(8,128)(2,1)S(1)}, u32[]{:S(2)}, u32[]{:S(2)}) collective-permute-start(bf16[160,256]{1,0:T(8,128)(2,1)S(1)} %get-tuple-element.26), channel_id=1, source_target_pairs={{0,20},{4,16},{8,28},{12,24},{16,4},{20,0},{24,12},{28,8},{1,21},{... | collective-permute-start | bytes 245768 | tf_op jit(solution)/shard_map/ppermute | solution.py:130
  13.4 11.2 %collective-permute-start.5 = (bf16[160,256]{1,0:T(8,128)(2,1)S(1)}, bf16[160,256]{1,0:T(8,128)(2,1)S(1)}, u32[]{:S(2)}, u32[]{:S(2)}) collective-permute-start(bf16[160,256]{1,0:T(8,128)(2,1)S(1)} %get-tuple-element.27), channel_id=1, source_target_pairs={{0,24},{4,28},{8,16},{12,20},{16,8},{20,12},{24,0},{28,4},{1,25},{... | collective-permute-start | bytes 245768 | tf_op jit(solution)/shard_map/ppermute | solution.py:130
  15.1 9.8 %collective-permute-start.6 = (bf16[160,256]{1,0:T(8,128)(2,1)S(1)}, bf16[160,256]{1,0:T(8,128)(2,1)S(1)}, u32[]{:S(2)}, u32[]{:S(2)}) collective-permute-start(bf16[160,256]{1,0:T(8,128)(2,1)S(1)} %get-tuple-element.28), channel_id=1, source_target_pairs={{0,28},{4,24},{8,20},{12,16},{16,12},{20,8},{24,4},{28,0},{1,29},{... | collective-permute-start | bytes 245768 | tf_op jit(solution)/shard_map/ppermute | solution.py:130
  16.6 31.5 %collective-permute-start.12 = (bf16[128,256]{1,0:T(8,128)(2,1)S(1)}, bf16[128,256]{1,0:T(8,128)(2,1)S(1)}, u32[]{:S(2)}, u32[]{:S(2)}) collective-permute-start(bf16[128,256]{1,0:T(8,128)(2,1)S(1)} %get-tuple-element.35), channel_id=1, source_target_pairs={{0,24},{4,28},{8,16},{12,20},{16,8},{20,12},{24,0},{28,4},{1,25},{... | collective-permute-start | bytes 196616 | tf_op jit(solution)/shard_map/ppermute | solution.py:130
  17.2 30.9 %collective-permute-start.13 = (bf16[128,256]{1,0:T(8,128)(2,1)S(1)}, bf16[128,256]{1,0:T(8,128)(2,1)S(1)}, u32[]{:S(2)}, u32[]{:S(2)}) collective-permute-start(bf16[128,256]{1,0:T(8,128)(2,1)S(1)} %get-tuple-element.36), channel_id=1, source_target_pairs={{0,28},{4,24},{8,20},{12,16},{16,12},{20,8},{24,4},{28,0},{1,29},{... | collective-permute-start | bytes 196616 | tf_op jit(solution)/shard_map/ppermute | solution.py:130
  24.0 24.1 %collective-permute-start.7 = (bf16[128,256]{1,0:T(8,128)(2,1)S(1)}, bf16[128,256]{1,0:T(8,128)(2,1)S(1)}, u32[]{:S(2)}, u32[]{:S(2)}) collective-permute-start(bf16[128,256]{1,0:T(8,128)(2,1)S(1)} %get-tuple-element.30), channel_id=1, source_target_pairs={{0,4},{4,0},{8,12},{12,8},{16,20},{20,16},{24,28},{28,24},{1,5},{5... | collective-permute-start | bytes 196616 | tf_op jit(solution)/shard_map/ppermute | solution.py:130
  24.6 23.5 %collective-permute-start.8 = (bf16[128,256]{1,0:T(8,128)(2,1)S(1)}, bf16[128,256]{1,0:T(8,128)(2,1)S(1)}, u32[]{:S(2)}, u32[]{:S(2)}) collective-permute-start(bf16[128,256]{1,0:T(8,128)(2,1)S(1)} %get-tuple-element.31), channel_id=1, source_target_pairs={{0,8},{4,12},{8,0},{12,4},{16,24},{20,28},{24,16},{28,20},{1,9},{5... | collective-permute-start | bytes 196616 | tf_op jit(solution)/shard_map/ppermute | solution.py:130
  24.9 1.4 %copy-start.4 = (f32[32]{0:T(128)S(1)}, f32[32]{0:T(128)}, u32[]{:S(2)}) copy-start(f32[32]{0:T(128)} %skip_ref.1) | copy-start | bytes 388
  24.9 23.2 %collective-permute-start.9 = (bf16[128,256]{1,0:T(8,128)(2,1)S(1)}, bf16[128,256]{1,0:T(8,128)(2,1)S(1)}, u32[]{:S(2)}, u32[]{:S(2)}) collective-permute-start(bf16[128,256]{1,0:T(8,128)(2,1)S(1)} %get-tuple-element.32), channel_id=1, source_target_pairs={{0,12},{4,8},{8,4},{12,0},{16,28},{20,24},{24,20},{28,16},{1,13},{... | collective-permute-start | bytes 196616 | tf_op jit(solution)/shard_map/ppermute | solution.py:130

commit v2 on v0

v2 whole, which is shorter than its diff:
```python
import functools

import jax
import jax.numpy as jnp
import numpy as np
from jax import lax
from jax.experimental import pallas as pl
from jax.experimental.pallas import tpu as pltpu
from jax.sharding import PartitionSpec as P

W = 256
LANES = 128
TILE = 16
CHUNK = 64


def whole_vmem():
    return pl.BlockSpec(memory_space=pltpu.VMEM)


def dft_tables(blocks):
    length = blocks * W
    k = np.arange(blocks)[:, None]
    angle = 2 * np.pi * ((4 * k + 1) * np.arange(blocks)[None, :] % (4 * blocks)) / (4 * blocks)
    outer = np.concatenate([np.cos(angle), -np.sin(angle)], 0)
    turn = 2 * np.pi * ((4 * k + 1) * np.arange(W)[None, :]) / (4 * length)
    near = 2 * np.pi * (np.arange(W)[:, None] * np.arange(W)[None, :] % W) / W
    inner = np.concatenate([np.cos(near), np.sin(near)], 0)
    turns = np.concatenate([np.cos(turn), np.sin(turn)], 1)
    return [jnp.asarray(table, jnp.float32) for table in (outer, outer.T, inner, turns)]


def spread(flat, first, count, stride, value):
    for h in range(W // LANES):
        flat[h, pl.ds(first, count, stride=stride), :] = value[:, LANES * h : LANES * (h + 1)]


def joined(flat, first, count):
    return jnp.concatenate([flat[h, first : first + count, :] for h in range(W // LANES)], 1)


def pack_signal_kernel(own, blocks, group, signal_ref, taps_ref, out_ref, flat, taps_flat):
    parts = out_ref.shape[0]
    rows = own * blocks
    for j in range(blocks):
        spread(taps_flat, j, taps_ref.shape[0], blocks, taps_ref[:, W * j : W * (j + 1)])
        spread(flat, j, own * parts, blocks, signal_ref[:, W * j : W * (j + 1)].astype(jnp.float32))
    for i in range(parts):
        out_ref[i, 0:rows, :] = joined(flat, i * rows, rows).astype(jnp.bfloat16)
        which = own * i // group
        out_ref[i, rows : rows + blocks, :] = joined(taps_flat, which * blocks, blocks).astype(jnp.bfloat16)


def pack_signal(signal, taps, parts):
    channels, block = signal.shape
    own = channels // parts
    group = channels // taps.shape[0]
    blocks = block // W
    return pl.pallas_call(
        functools.partial(pack_signal_kernel, own, blocks, group),
        out_shape=jax.ShapeDtypeStruct((parts, (own + 1) * blocks, W), jnp.bfloat16),
        in_specs=[whole_vmem()] * 2,
        out_specs=whole_vmem(),
        scratch_shapes=[
            pltpu.VMEM((W // LANES, channels * blocks, LANES), jnp.float32),
            pltpu.VMEM((W // LANES, taps.shape[0] * blocks, LANES), jnp.float32),
        ],
        compiler_params=pltpu.CompilerParams(vmem_limit_bytes=24 * 2**20),
        name="pack_signal",
    )(signal, taps)


def pack_gate_kernel(blocks, gate_ref, out_ref, flat):
    parts, rows, _ = out_ref.shape
    for j in range(blocks):
        spread(flat, j, parts * rows // blocks, blocks, gate_ref[:, W * j : W * (j + 1)].astype(jnp.float32))
    for i in range(parts):
        out_ref[i] = joined(flat, i * rows, rows).astype(jnp.bfloat16)


def pack_gate(post_gate, parts):
    channels, block = post_gate.shape
    blocks = block // W
    return pl.pallas_call(
        functools.partial(pack_gate_kernel, blocks),
        out_shape=jax.ShapeDtypeStruct((parts, channels // parts * blocks, W), jnp.bfloat16),
        in_specs=[whole_vmem()],
        out_specs=whole_vmem(),
        scratch_shapes=[pltpu.VMEM((W // LANES, channels * blocks, LANES), jnp.float32)],
        compiler_params=pltpu.CompilerParams(vmem_limit_bytes=24 * 2**20),
        name="pack_gate",
    )(post_gate)


def conv_kernel(own, skip_ref, got_ref, outer_ref, back_ref, inner_ref, turns_ref, out_ref, x_all, r_all, ahead, rear):
    parts, local, _ = got_ref.shape
    near = local // (own + 1)
    blocks = parts * near
    length = blocks * W
    for p in range(parts):
        for c in range(own + 1):
            x_all[p * near : (p + 1) * near, W * c : W * (c + 1)] = got_ref[p, c * near : (c + 1) * near, :]

    near_cos, near_sin = inner_ref[0:W, :].astype(jnp.bfloat16), inner_ref[W:, :].astype(jnp.bfloat16)
    for table, sign in ((ahead, -1), (rear, 1)):
        table[0:W, 0:W] = near_cos
        table[0:W, W:] = near_sin * sign
        table[W:, 0:W] = near_sin * -sign
        table[W:, W:] = near_cos

    def dot(left, right):
        return jnp.dot(left, right, preferred_element_type=jnp.float32)

    for first in range(0, blocks, CHUNK):
        here = slice(first, first + CHUNK)
        there = slice(blocks + first, blocks + first + CHUNK)
        real = dot(outer_ref[here, :].astype(jnp.bfloat16), x_all[...])
        imag = dot(outer_ref[there, :].astype(jnp.bfloat16), x_all[...])
        turn_cos, turn_sin = turns_ref[here, 0:W], turns_ref[here, W:]
        rows = []
        for c in range(own + 1):
            re, im = real[:, W * c : W * (c + 1)], imag[:, W * c : W * (c + 1)]
            pair = [re * turn_cos + im * turn_sin, im * turn_cos - re * turn_sin]
            rows.append(jnp.concatenate(pair, 1).astype(jnp.bfloat16))
        spectrum = dot(jnp.concatenate(rows, 0), ahead[...])
        filt_re = spectrum[CHUNK * own :, 0:W] * (1.0 / length)
        filt_im = spectrum[CHUNK * own :, W:] * (1.0 / length)
        rows = []
        for c in range(own):
            part = spectrum[CHUNK * c : CHUNK * (c + 1), :]
            re, im = part[:, 0:W], part[:, W:]
            pair = [re * filt_re - im * filt_im, re * filt_im + im * filt_re]
            rows.append(jnp.concatenate(pair, 1).astype(jnp.bfloat16))
        middle = dot(jnp.concatenate(rows, 0), rear[...])
        for c in range(own):
            part = middle[CHUNK * c : CHUNK * (c + 1), :]
            re, im = part[:, 0:W], part[:, W:]
            cols = slice(W * c, W * (c + 1))
            r_all[here, cols] = (re * turn_cos - im * turn_sin).astype(jnp.bfloat16)
            r_all[there, cols] = (re * turn_sin + im * turn_cos).astype(jnp.bfloat16)

    me = lax.axis_index("ctx")
    for c in range(own):
        cols = slice(W * c, W * (c + 1))
        conv = dot(back_ref[...].astype(jnp.bfloat16), r_all[:, cols])
        out_ref[c] = conv + skip_ref[own * me + c] * x_all[:, cols].astype(jnp.float32)


def convolve(got, skip, own):
    parts, local, _ = got.shape
    blocks = parts * (local // (own + 1))
    tables = dft_tables(blocks)
    steps = 8 * blocks * W * W * (3 * own + 2)
    return pl.pallas_call(
        functools.partial(conv_kernel, own),
        out_shape=jax.ShapeDtypeStruct((own, blocks, W), jnp.float32),
        in_specs=[pl.BlockSpec(memory_space=pltpu.SMEM)] + [whole_vmem()] * (1 + len(tables)),
        out_specs=whole_vmem(),
        scratch_shapes=[
            pltpu.VMEM((blocks, W * (own + 1)), jnp.bfloat16),
            pltpu.VMEM((2 * blocks, W * own), jnp.bfloat16),
            pltpu.VMEM((2 * W, 2 * W), jnp.bfloat16),
            pltpu.VMEM((2 * W, 2 * W), jnp.bfloat16),
        ],
        compiler_params=pltpu.CompilerParams(vmem_limit_bytes=32 * 2**20),
        cost_estimate=pl.CostEstimate(flops=steps, bytes_accessed=4 * own * blocks * W, transcendentals=0),
        name="convolve",
    )(skip, got, *tables)


def gate_kernel(ch_count, z_ref, gate_ref, out_ref):
    own = z_ref.shape[0]
    ctx_count, local, _ = gate_ref.shape
    near = local // own
    some = near // ch_count
    for k in range(ctx_count):
        parts = []
        for c in range(own):
            gate = gate_ref[k, c * near : (c + 1) * near, :].astype(jnp.float32)
            parts.append(gate * z_ref[c, k * near : (k + 1) * near, :])
        for m in range(ch_count):
            rows = [part[m * some : (m + 1) * some, :] for part in parts]
            out_ref[m * ctx_count + k] = jnp.concatenate(rows, 0).astype(jnp.bfloat16)


def gate_rows(z, gate, ch_count):
    own = z.shape[0]
    ctx_count, local, _ = gate.shape
    near = local // own
    some = near // ch_count
    if some % 8 or own * some % TILE:
        gate = gate.reshape(ctx_count, own, near, W).swapaxes(0, 1).reshape(z.shape)
        mixed = (z * gate.astype(jnp.float32)).astype(jnp.bfloat16)
        mixed = mixed.reshape(own, ctx_count, ch_count, some, W)
        return mixed.transpose(2, 1, 0, 3, 4).reshape(-1, own * some, W)
    return pl.pallas_call(
        functools.partial(gate_kernel, ch_count),
        out_shape=jax.ShapeDtypeStruct((ctx_count * ch_count, own * some, W), jnp.bfloat16),
        in_specs=[whole_vmem()] * 2,
        out_specs=whole_vmem(),
        compiler_params=pltpu.CompilerParams(vmem_limit_bytes=16 * 2**20),
        name="gate",
    )(z, gate)


def unpack_kernel(own, got_ref, out_ref, flat):
    sources, rows, _ = got_ref.shape
    some = rows // own
    for p in range(sources):
        part = got_ref[p].astype(jnp.float32)
        for h in range(W // LANES):
            flat[h, p * rows : (p + 1) * rows, :] = part[:, LANES * h : LANES * (h + 1)]
    for j in range(some):
        for h in range(W // LANES):
            part = flat[h, pl.ds(j, sources * own, stride=some), :]
            first = W * j + LANES * h
            out_ref[:, first : first + LANES] = part.astype(jnp.bfloat16)


def unpack(got, own):
    sources, rows, _ = got.shape
    shape = (sources * own, rows // own * W)
    if rows % TILE:
        return got.reshape(shape)
    return pl.pallas_call(
        functools.partial(unpack_kernel, own),
        out_shape=jax.ShapeDtypeStruct(shape, jnp.bfloat16),
        in_specs=[whole_vmem()],
        out_specs=whole_vmem(),
        scratch_shapes=[pltpu.VMEM((W // LANES, sources * rows, LANES), jnp.float32)],
        compiler_params=pltpu.CompilerParams(vmem_limit_bytes=16 * 2**20),
        name="unpack",
    )(got)


def body(pre_gate, value, post_gate, filter_taps, skip):
    ctx_count = lax.axis_size("ctx")
    ch_count = lax.axis_size("ch")
    own = value.shape[0] // ctx_count
    signal = (pre_gate.astype(jnp.float32) * value.astype(jnp.float32)).astype(jnp.bfloat16)
    send = pack_signal(signal, filter_taps, ctx_count)
    got = lax.all_to_all(send, "ctx", split_axis=0, concat_axis=0, tiled=True)
    post_gate, _ = lax.optimization_barrier((post_gate, send))
    gate = pack_gate(post_gate, ctx_count)
    gate = lax.all_to_all(gate, "ctx", split_axis=0, concat_axis=0, tiled=True)
    z = convolve(got, skip, own)
    mixed = gate_rows(z, gate, ch_count)
    mixed = lax.all_to_all(mixed, ("ch", "ctx"), split_axis=0, concat_axis=0, tiled=True)
    return unpack(mixed, own)


def solution(mesh):
    placed = (P("ch", "ctx"), P("ch", "ctx"), P("ch", "ctx"), P("ch", "ctx"), P("ch"))
    return jax.shard_map(
        body, mesh=mesh, in_specs=placed, out_specs=P(None, ("ctx", "ch")), check_vma=False
    )
```

time: 74.3 us -> 53.9 us (0.73)
  Pallas kernels: 28.5 us -> 9.12 us
  blocking collectives: 36.4 us -> 21.7 us
  starting transfers between devices: 4.4 us -> 12.2 us
  waiting for transfers between devices: 0.01 us -> 6.37 us
  local copies, waits for them, and re-layouts: 3.97 us -> 2.1 us
  other arithmetic: 0 us -> 1.35 us
    pallas_call x3 -> x4, Pallas kernels: 27.5 us -> 8.05 us  [the longest x1 4.08 us: convolve(): pl.pallas_call(functools.partial(conv_kernel, own), out_shape=jax.ShapeDt...]
    all_to_all x1 -> x0, blocking collectives: 15.3 us -> none  [body(): got = lax.all_to_all(send, 'ctx', split_axis=0, concat_axis=0, tiled=True)]
    all_to_all x0 -> x1, waiting for transfers between devices: none -> 5.81 us  [body(): got = lax.all_to_all(send, 'ctx', split_axis=0, concat_axis=0, tiled=True)]
    all_to_all x0 -> x1, starting transfers between devices: none -> 5.35 us  [body(): got = lax.all_to_all(send, 'ctx', split_axis=0, concat_axis=0, tiled=True)]
    all_to_all x1, starting transfers between devices: 4.4 us -> 6.85 us  [body(): gate = lax.all_to_all(gate, 'ctx', split_axis=0, concat_axis=0, tiled=True)]
    unnamed x10 -> x14, local copies, waits for them, and re-layouts: 3.97 us -> 2.1 us
    convert_element_type x0 -> x1, other arithmetic: none -> 1.35 us  [body(): (pre_gate.astype(jnp.float32) * value.astype(jnp.float32)).astype(jnp.bfl...]
  transfers between devices with their start and end apart: 1 -> 2, of which waited for: 0 -> 2; matrix products, arithmetic and copies ran while one was open for 0% -> 0% of each run, Pallas kernels for 36% -> 11%
where the time goes in v2:
time: 53.9 us; the launch traced here: 52.9 us
  blocking collectives  21.7 us (40%)
  starting transfers between devices  12.2 us (23%)
  Pallas kernels  9.12 us (17%)
  waiting for transfers between devices  6.37 us (12%)
  local copies, waits for them, and re-layouts  2.1 us (4%)
  other arithmetic  1.35 us (3%)
    all_to_all x1, blocking collectives, body(): lax.all_to_all(mixed, ('ch', 'ctx'), split_axis=0, concat_axis=0, tiled=T...  21.7 us
    all_to_all x1, starting transfers between devices, body(): gate = lax.all_to_all(gate, 'ctx', split_axis=0, concat_axis=0, tiled=True)  6.85 us
    all_to_all x1, waiting for transfers between devices, body(): got = lax.all_to_all(send, 'ctx', split_axis=0, concat_axis=0, tiled=True)  5.81 us
    all_to_all x1, starting transfers between devices, body(): got = lax.all_to_all(send, 'ctx', split_axis=0, concat_axis=0, tiled=True)  5.35 us
    pallas_call x1, Pallas kernels, convolve(): pl.pallas_call(functools.partial(conv_kernel, own), out_shape=jax.ShapeDt...  4.08 us
    unnamed x14, local copies, waits for them, and re-layouts  2.1 us
    pallas_call x1, Pallas kernels, pack_signal(): pl.pallas_call(functools.partial(pack_signal_kernel, own, blocks, group),...  1.99 us
    pallas_call x1, Pallas kernels, pack_gate(): pl.pallas_call(functools.partial(pack_gate_kernel, blocks), out_shape=jax...  1.88 us
  transfers between devices with their start and end apart: 2, of which 2 were waited for; matrix products, arithmetic and copies ran while one was open for 0% of the time, Pallas kernels for 11%

profile of v2, /device:TPU:1, one launch (start us, length us, event | category | flops | bytes accessed | tf_op | source)
XLA Modules:
  0.0 52.9 jit_solution(7063095069567148572)
XLA Ops:
  0.0 0.0 copy-start.1
  0.0 1.4 %multiply_convert_fusion.signal_ref = bf16[32,8192]{1,0:T(8,128)(2,1)S(1)} fusion(bf16[32,8192]{1,0:T(8,128)(2,1)} %param.10, bf16[32,8192]{1,0:T(8,128)(2,1)} %param.9), kind=kLoop, calls=%fused_computation | loop fusion | flops 1048576 | bytes 1572864 | tf_op jit(solution)/shard_map/convert_element_type | solution.py:240
  1.4 0.0 copy-done.1
  1.4 2.0 %pack_signal.1 = bf16[8,160,256]{2,1,0:T(8,128)(2,1)} custom-call(bf16[32,8192]{1,0:T(8,128)(2,1)S(1)} %multiply_convert_fusion.signal_ref, f32[2,8192]{1,0:T(2,128)S(1)} %copy-done.1), custom_call_target="tpu_custom_call" | custom-call | tf_op jit(solution)/shard_map/pack_signal/pallas_call | solution.py:59
  3.4 0.0 copy-start
  3.4 5.4 %all-to-all-start = ((bf16[8,160,256]{2,1,0:T(8,128)(2,1)}), bf16[8,160,256]{2,1,0:T(8,128)(2,1)S(1)}, u32[]{:S(2)}, u32[]{:S(2)}) async-start(bf16[8,160,256]{2,1,0:T(8,128)(2,1)} %pack_signal.1), calls=%async_computation | async-start | bytes 1310720 | tf_op jit(solution)/shard_map/all_to_all | solution.py:242
  8.7 0.0 copy-done
  8.7 0.0 copy-start.4
  8.7 1.9 %pack_gate.1 = bf16[8,128,256]{2,1,0:T(8,128)(2,1)} custom-call(bf16[32,8192]{1,0:T(8,128)(2,1)S(1)} %copy-done), custom_call_target="tpu_custom_call" | custom-call | tf_op jit(solution)/shard_map/pack_gate/pallas_call | solution.py:84
  10.6 0.0 copy-start.2
  10.6 0.0 copy-start.3
  10.6 5.8 %all-to-all-done.got_ref = bf16[8,160,256]{2,1,0:T(8,128)(2,1)S(1)} async-done(((bf16[8,160,256]{2,1,0:T(8,128)(2,1)}), bf16[8,160,256]{2,1,0:T(8,128)(2,1)S(1)}, u32[]{:S(2)}, u32[]{:S(2)}) %all-to-all-start) | async-done | bytes 655392 | tf_op jit(solution)/shard_map/all_to_all | solution.py:242
  16.4 6.8 %all-to-all-start.1 = ((bf16[8,128,256]{2,1,0:T(8,128)(2,1)}), bf16[8,128,256]{2,1,0:T(8,128)(2,1)S(1)}, u32[]{:S(2)}, u32[]{:S(2)}) async-start(bf16[8,128,256]{2,1,0:T(8,128)(2,1)} %pack_gate.1), calls=%async_computation.1 | async-start | bytes 1048576 | tf_op jit(solution)/shard_map/all_to_all | solution.py:245
  23.3 0.0 copy-done.4
  23.3 0.0 copy-done.2
  23.3 0.0 copy-done.3
  23.3 0.0 copy-start.5
  23.3 1.0 %copy-done.5 = f32[256,512]{1,0:T(8,128)S(1)} copy-done((f32[256,512]{1,0:T(8,128)S(1)}, f32[256,512]{1,0:T(8,128)}, u32[]{:S(2)}) %copy-start.5) | copy-done | bytes 524312
  24.3 1.0 %copy-done.6 = f32[512,256]{1,0:T(8,128)S(1)} copy-done((f32[512,256]{1,0:T(8,128)S(1)}, f32[512,256]{1,0:T(8,128)}, u32[]{:S(2)}) %copy-start.6) | copy-done | bytes 524312
  25.4 4.1 %convolve.1.z_ref = f32[4,256,256]{2,1,0:T(8,128)S(1)} custom-call(f32[32]{0:T(128)S(1)} %copy-done.2, bf16[8,160,256]{2,1,0:T(8,128)(2,1)S(1)} %all-to-all-done.got_ref, f32[512,256]{1,0:T(8,128)S(1)} %copy-done.6, f32[256,512]{1,0:T(8,128)S(1)} %copy-done.5, f32[512,256]{1,0:T(8,128)S(1)} %copy-done.4, f32[256,512]{1,0:T(8,128)S(1)} %copy-done.3), custom_call_target="tpu_custom_call" | custom-call | flops 1879048192 | bytes 1048576 | tf_op jit(solution)/shard_map/convolve/pallas_call | solution.py:154
  29.5 0.6 %all-to-all-done.1.gate_ref = bf16[8,128,256]{2,1,0:T(8,128)(2,1)S(1)} async-done(((bf16[8,128,256]{2,1,0:T(8,128)(2,1)}), bf16[8,128,256]{2,1,0:T(8,128)(2,1)S(1)}, u32[]{:S(2)}, u32[]{:S(2)}) %all-to-all-start.1) | async-done | bytes 524320 | tf_op jit(solution)/shard_map/all_to_all | solution.py:245
  30.0 0.1 gate.1
  30.1 21.7 %all_to_all.15.got_ref = bf16[32,32,256]{2,1,0:T(8,128)(2,1)S(1)} all-to-all(bf16[32,32,256]{2,1,0:T(8,128)(2,1)S(1)} %gate.1), channel_id=1, replica_groups=mesh['ctx'=8,'ch'=4] {'ch','ctx'}, dimensions={0} | all-to-all | bytes 1048576 | tf_op jit(solution)/shard_map/all_to_all | solution.py:248
  51.9 1.1 %unpack.1 = bf16[128,2048]{1,0:T(8,128)(2,1)} custom-call(bf16[32,32,256]{2,1,0:T(8,128)(2,1)S(1)} %all_to_all.15.got_ref), custom_call_target="tpu_custom_call" | custom-call | tf_op jit(solution)/shard_map/unpack/pallas_call | solution.py:225
  (1 shorter events, 0.0 us)
Async XLA Ops:
  0.0 1.4 %copy-start.1 = (f32[2,8192]{1,0:T(2,128)S(1)}, f32[2,8192]{1,0:T(2,128)}, u32[]{:S(2)}) copy-start(f32[2,8192]{1,0:T(2,128)} %taps_ref.1) | copy-start | bytes 196612
  3.4 5.4 %copy-start = (bf16[32,8192]{1,0:T(8,128)(2,1)S(1)}, bf16[32,8192]{1,0:T(8,128)(2,1)}, u32[]{:S(2)}) copy-start(bf16[32,8192]{1,0:T(8,128)(2,1)} %gate_ref) | copy-start | bytes 1572868
  3.4 13.1 %all-to-all-start = ((bf16[8,160,256]{2,1,0:T(8,128)(2,1)}), bf16[8,160,256]{2,1,0:T(8,128)(2,1)S(1)}, u32[]{:S(2)}, u32[]{:S(2)}) async-start(bf16[8,160,256]{2,1,0:T(8,128)(2,1)} %pack_signal.1), calls=%async_computation | async-start | bytes 1310720 | tf_op jit(solution)/shard_map/all_to_all | solution.py:242
  8.7 14.6 %copy-start.4 = (f32[512,256]{1,0:T(8,128)S(1)}, f32[512,256]{1,0:T(8,128)}, u32[]{:S(2)}) copy-start(f32[512,256]{1,0:T(8,128)} %constant.10.clone.inner_ref) | copy-start | bytes 1572868
  10.6 12.7 %copy-start.2 = (f32[32]{0:T(128)S(1)}, f32[32]{0:T(128)}, u32[]{:S(2)}) copy-start(f32[32]{0:T(128)} %skip_ref.1) | copy-start | bytes 388
  10.6 12.7 %copy-start.3 = (f32[256,512]{1,0:T(8,128)S(1)}, f32[256,512]{1,0:T(8,128)}, u32[]{:S(2)}) copy-start(f32[256,512]{1,0:T(8,128)} %constant.11.clone.turns_ref) | copy-start | bytes 1572868
  16.4 13.6 %all-to-all-start.1 = ((bf16[8,128,256]{2,1,0:T(8,128)(2,1)}), bf16[8,128,256]{2,1,0:T(8,128)(2,1)S(1)}, u32[]{:S(2)}, u32[]{:S(2)}) async-start(bf16[8,128,256]{2,1,0:T(8,128)(2,1)} %pack_gate.1), calls=%async_computation.1 | async-start | bytes 1048576 | tf_op jit(solution)/shard_map/all_to_all | solution.py:245
  23.3 1.0 %copy-start.5 = (f32[256,512]{1,0:T(8,128)S(1)}, f32[256,512]{1,0:T(8,128)}, u32[]{:S(2)}) copy-start(f32[256,512]{1,0:T(8,128)} %constant.9.clone.back_ref) | copy-start | bytes 1572868
  24.3 1.0 %copy-start.6 = (f32[512,256]{1,0:T(8,128)S(1)}, f32[512,256]{1,0:T(8,128)}, u32[]{:S(2)}) copy-start(f32[512,256]{1,0:T(8,128)} %constant.8.clone.outer_ref) | copy-start | bytes 1572868

commit v3 on v2

v3 whole, which is shorter than its diff:
```python
import functools

import jax
import jax.numpy as jnp
import numpy as np
from jax import lax
from jax.experimental import pallas as pl
from jax.experimental.pallas import tpu as pltpu
from jax.sharding import PartitionSpec as P

W = 256
LANES = 128
TILE = 16
CHUNK = 64


def whole_vmem():
    return pl.BlockSpec(memory_space=pltpu.VMEM)


def dft_tables(blocks):
    length = blocks * W
    k = np.arange(blocks)[:, None]
    angle = 2 * np.pi * ((4 * k + 1) * np.arange(blocks)[None, :] % (4 * blocks)) / (4 * blocks)
    outer = np.concatenate([np.cos(angle), -np.sin(angle)], 0)
    turn = 2 * np.pi * ((4 * k + 1) * np.arange(W)[None, :]) / (4 * length)
    near = 2 * np.pi * (np.arange(W)[:, None] * np.arange(W)[None, :] % W) / W
    inner = np.concatenate([np.cos(near), np.sin(near)], 0)
    turns = np.concatenate([np.cos(turn), np.sin(turn)], 1)
    return [jnp.asarray(table, jnp.float32) for table in (outer, outer.T, inner, turns)]


def spread(flat, first, count, stride, value):
    for h in range(W // LANES):
        flat[h, pl.ds(first, count, stride=stride), :] = value[:, LANES * h : LANES * (h + 1)]


def joined(flat, first, count):
    return jnp.concatenate([flat[h, pl.ds(first, count), :] for h in range(W // LANES)], 1)


def pack_signal_kernel(own, blocks, group, pre_ref, val_ref, taps_ref, out_ref, flat, taps_flat):
    step = pl.program_id(0)
    rows = own * blocks
    channels = pre_ref.shape[0]

    @pl.when(step == 0)
    def _():
        for j in range(blocks):
            spread(taps_flat, j, taps_ref.shape[0], blocks, taps_ref[:, W * j : W * (j + 1)])

    for j in range(blocks):
        cols = slice(W * j, W * (j + 1))
        product = pre_ref[:, cols].astype(jnp.float32) * val_ref[:, cols].astype(jnp.float32)
        spread(flat, j, channels, blocks, product)
    for i in range(channels // own):
        out_ref[i, 0:rows, :] = joined(flat, i * rows, rows).astype(jnp.bfloat16)
        which = (step * channels + own * i) // group
        taps = joined(taps_flat, pl.multiple_of(which * blocks, 8), blocks)
        out_ref[i, rows : rows + blocks, :] = taps.astype(jnp.bfloat16)


def pack_signal(pre_gate, value, taps, parts):
    channels, block = value.shape
    own = channels // parts
    group = channels // taps.shape[0]
    blocks = block // W
    some = min(TILE, channels)
    return pl.pallas_call(
        functools.partial(pack_signal_kernel, own, blocks, group),
        grid=(channels // some,),
        out_shape=jax.ShapeDtypeStruct((parts, (own + 1) * blocks, W), jnp.bfloat16),
        in_specs=[pl.BlockSpec((some, block), lambda s: (s, 0))] * 2 + [pl.BlockSpec(taps.shape, lambda s: (0, 0))],
        out_specs=pl.BlockSpec((some // own, (own + 1) * blocks, W), lambda s: (s, 0, 0)),
        scratch_shapes=[
            pltpu.VMEM((W // LANES, some * blocks, LANES), jnp.float32),
            pltpu.VMEM((W // LANES, taps.shape[0] * blocks, LANES), jnp.float32),
        ],
        compiler_params=pltpu.CompilerParams(vmem_limit_bytes=60 * 2**20),
        name="pack_signal",
    )(pre_gate, value, taps)


def split_gate_kernel(gate_ref, *out_refs):
    me = lax.axis_index("ch")
    width = out_refs[0].shape[1]
    for d, out_ref in enumerate(out_refs):
        first = pl.multiple_of(jnp.bitwise_xor(me, d) * width, LANES)
        out_ref[...] = gate_ref[:, pl.ds(first, width)]


def split_gate(post_gate, parts):
    channels, block = post_gate.shape
    return pl.pallas_call(
        split_gate_kernel,
        out_shape=[jax.ShapeDtypeStruct((channels, block // parts), jnp.bfloat16)] * parts,
        in_specs=[whole_vmem()],
        out_specs=[whole_vmem()] * parts,
        compiler_params=pltpu.CompilerParams(vmem_limit_bytes=24 * 2**20),
        name="split_gate",
    )(post_gate)


def tables_kernel(outer_ref, back_ref, inner_ref, outer_out, back_out, ahead, rear):
    outer_out[...] = outer_ref[...].astype(jnp.bfloat16)
    back_out[...] = back_ref[...].astype(jnp.bfloat16)
    near_cos, near_sin = inner_ref[0:W, :].astype(jnp.bfloat16), inner_ref[W:, :].astype(jnp.bfloat16)
    for table, sign in ((ahead, -1), (rear, 1)):
        table[0:W, 0:W] = near_cos
        table[0:W, W:] = near_sin * sign
        table[W:, 0:W] = near_sin * -sign
        table[W:, W:] = near_cos


def make_tables(outer, back, inner):
    shapes = (outer.shape, back.shape, (2 * W, 2 * W), (2 * W, 2 * W))
    return pl.pallas_call(
        tables_kernel,
        out_shape=[jax.ShapeDtypeStruct(shape, jnp.bfloat16) for shape in shapes],
        in_specs=[whole_vmem()] * 3,
        out_specs=[whole_vmem()] * 4,
        compiler_params=pltpu.CompilerParams(vmem_limit_bytes=24 * 2**20),
        name="make_tables",
    )(outer, back, inner)


def conv_kernel(own, skip_ref, got_ref, outer_ref, back_ref, ahead, rear, turns_ref, out_ref, x_all, r_all, z_all):
    parts, local, _ = got_ref.shape
    near = local // (own + 1)
    blocks = parts * near
    length = blocks * W
    for p in range(parts):
        for c in range(own + 1):
            x_all[p * near : (p + 1) * near, W * c : W * (c + 1)] = got_ref[p, c * near : (c + 1) * near, :]

    def dot(left, right):
        return jnp.dot(left, right, preferred_element_type=jnp.float32)

    for first in range(0, blocks, CHUNK):
        here = slice(first, first + CHUNK)
        there = slice(blocks + first, blocks + first + CHUNK)
        real = dot(outer_ref[here, :], x_all[...])
        imag = dot(outer_ref[there, :], x_all[...])
        turn_cos, turn_sin = turns_ref[here, 0:W], turns_ref[here, W:]
        rows = []
        for c in range(own + 1):
            re, im = real[:, W * c : W * (c + 1)], imag[:, W * c : W * (c + 1)]
            pair = [re * turn_cos + im * turn_sin, im * turn_cos - re * turn_sin]
            rows.append(jnp.concatenate(pair, 1).astype(jnp.bfloat16))
        spectrum = dot(jnp.concatenate(rows, 0), ahead[...])
        filt_re = spectrum[CHUNK * own :, 0:W] * (1.0 / length)
        filt_im = spectrum[CHUNK * own :, W:] * (1.0 / length)
        rows = []
        for c in range(own):
            part = spectrum[CHUNK * c : CHUNK * (c + 1), :]
            re, im = part[:, 0:W], part[:, W:]
            pair = [re * filt_re - im * filt_im, re * filt_im + im * filt_re]
            rows.append(jnp.concatenate(pair, 1).astype(jnp.bfloat16))
        middle = dot(jnp.concatenate(rows, 0), rear[...])
        for c in range(own):
            part = middle[CHUNK * c : CHUNK * (c + 1), :]
            re, im = part[:, 0:W], part[:, W:]
            cols = slice(W * c, W * (c + 1))
            r_all[here, cols] = (re * turn_cos - im * turn_sin).astype(jnp.bfloat16)
            r_all[there, cols] = (re * turn_sin + im * turn_cos).astype(jnp.bfloat16)

    me = lax.axis_index("ctx")
    for c in range(own):
        cols = slice(W * c, W * (c + 1))
        conv = dot(back_ref[...], r_all[:, cols])
        z_all[c] = conv + skip_ref[own * me + c] * x_all[:, cols].astype(jnp.float32)
    some = out_ref.shape[1] // own
    ch_count = near // some
    for k in range(parts):
        for m in range(ch_count):
            first = k * near + m * some
            rows = [z_all[c, first : first + some, :] for c in range(own)]
            out_ref[m * parts + k] = jnp.concatenate(rows, 0).astype(jnp.bfloat16)


def convolve(got, skip, tables, own, ch_count):
    parts, local, _ = got.shape
    blocks = parts * (local // (own + 1))
    steps = 8 * blocks * W * W * (3 * own + 2)
    owners = parts * ch_count
    return pl.pallas_call(
        functools.partial(conv_kernel, own),
        out_shape=jax.ShapeDtypeStruct((owners, own * blocks // owners, W), jnp.bfloat16),
        in_specs=[pl.BlockSpec(memory_space=pltpu.SMEM)] + [whole_vmem()] * (1 + len(tables)),
        out_specs=whole_vmem(),
        scratch_shapes=[
            pltpu.VMEM((blocks, W * (own + 1)), jnp.bfloat16),
            pltpu.VMEM((2 * blocks, W * own), jnp.bfloat16),
            pltpu.VMEM((own, blocks, W), jnp.float32),
        ],
        compiler_params=pltpu.CompilerParams(vmem_limit_bytes=32 * 2**20),
        cost_estimate=pl.CostEstimate(flops=steps, bytes_accessed=4 * own * blocks * W, transcendentals=0),
        name="convolve",
    )(skip, got, *tables)


def unpack_kernel(own, got_ref, *rest):
    gate_refs, (out_ref, flat, gate_s) = rest[:-3], rest[-3:]
    sources, rows, _ = got_ref.shape
    some = rows // own
    me = lax.axis_index("ch")
    channels = gate_refs[0].shape[0]
    for d, gate_ref in enumerate(gate_refs):
        first = pl.multiple_of(jnp.bitwise_xor(me, d) * channels, TILE)
        gate_s[pl.ds(first, channels), :] = gate_ref[...]
    for p in range(sources):
        part = got_ref[p].astype(jnp.float32)
        for h in range(W // LANES):
            flat[h, p * rows : (p + 1) * rows, :] = part[:, LANES * h : LANES * (h + 1)]
    for j in range(some):
        for h in range(W // LANES):
            part = flat[h, pl.ds(j, sources * own, stride=some), :]
            first = W * j + LANES * h
            cols = slice(first, first + LANES)
            out_ref[:, cols] = (part * gate_s[:, cols].astype(jnp.float32)).astype(jnp.bfloat16)


def unpack(got, gates, own):
    sources, rows, _ = got.shape
    shape = (sources * own, rows // own * W)
    if rows % TILE:
        order = jnp.bitwise_xor(lax.axis_index("ch"), jnp.arange(len(gates)))
        gate = jnp.stack(gates)[order].reshape(shape)
        return (got.reshape(shape).astype(jnp.float32) * gate.astype(jnp.float32)).astype(jnp.bfloat16)
    return pl.pallas_call(
        functools.partial(unpack_kernel, own),
        out_shape=jax.ShapeDtypeStruct(shape, jnp.bfloat16),
        in_specs=[whole_vmem()] * (1 + len(gates)),
        out_specs=whole_vmem(),
        scratch_shapes=[
            pltpu.VMEM((W // LANES, sources * rows, LANES), jnp.float32),
            pltpu.VMEM(shape, jnp.bfloat16),
        ],
        compiler_params=pltpu.CompilerParams(vmem_limit_bytes=24 * 2**20),
        name="unpack",
    )(got, *gates)


def body(pre_gate, value, post_gate, filter_taps, skip):
    ctx_count = lax.axis_size("ctx")
    ch_count = lax.axis_size("ch")
    own = value.shape[0] // ctx_count
    blocks = value.shape[1] // W * ctx_count
    send = pack_signal(pre_gate, value, filter_taps, ctx_count)
    got = lax.all_to_all(send, "ctx", split_axis=0, concat_axis=0, tiled=True)
    tables = dft_tables(blocks)
    post_gate, tables, _ = lax.optimization_barrier((post_gate, tables, send))
    gates = list(split_gate(post_gate, ch_count))
    for d in range(1, ch_count):
        gates[d] = lax.ppermute(gates[d], "ch", [(i, i ^ d) for i in range(ch_count)])
    tables = list(make_tables(*tables[:3])) + [tables[3]]
    mixed = convolve(got, skip, tables, own, ch_count)
    mixed = lax.all_to_all(mixed, ("ch", "ctx"), split_axis=0, concat_axis=0, tiled=True)
    return unpack(mixed, gates, own)


def solution(mesh):
    placed = (P("ch", "ctx"), P("ch", "ctx"), P("ch", "ctx"), P("ch", "ctx"), P("ch"))
    return jax.shard_map(
        body, mesh=mesh, in_specs=placed, out_specs=P(None, ("ctx", "ch")), check_vma=False
    )
```

time: 53.9 us -> 56.4 us (1.046)
  the two profiles are of different devices: /device:TPU:1 before, /device:TPU:0 now
where the time goes in v3:
time: 56.4 us; the launch traced here: 56 us
  waiting for transfers between devices  29.7 us (53%)
  starting transfers between devices  13.7 us (24%)
  Pallas kernels  9.18 us (16%)
  local copies, waits for them, and re-layouts  3.36 us (6%)
    ppermute x3, waiting for transfers between devices, body(): lax.ppermute(gates[d], 'ch', [(i, i ^ d) for i in range(ch_count)])  19.4 us
    all_to_all x1, waiting for transfers between devices, body(): got = lax.all_to_all(send, 'ctx', split_axis=0, concat_axis=0, tiled=True)  10.3 us
    all_to_all x1, starting transfers between devices, body(): got = lax.all_to_all(send, 'ctx', split_axis=0, concat_axis=0, tiled=True)  5.31 us
    pallas_call x1, Pallas kernels, convolve(): pl.pallas_call(functools.partial(conv_kernel, own), out_shape=jax.ShapeDt...  4.87 us
    ppermute x3, starting transfers between devices, body(): lax.ppermute(gates[d], 'ch', [(i, i ^ d) for i in range(ch_count)])  4.45 us
    all_to_all x1, starting transfers between devices, body(): lax.all_to_all(mixed, ('ch', 'ctx'), split_axis=0, concat_axis=0, tiled=T...  3.96 us
    unnamed x16, local copies, waits for them, and re-layouts  3.36 us
    pallas_call x1, Pallas kernels, pack_signal(): pl.pallas_call(functools.partial(pack_signal_kernel, own, blocks, group),...  2.97 us
  transfers between devices with their start and end apart: 5, of which 3 were waited for; matrix products, arithmetic and copies ran while one was open for 0% of the time, Pallas kernels for 0%

profile of v3, /device:TPU:0, one launch (start us, length us, event | category | flops | bytes accessed | tf_op | source)
XLA Modules:
  0.0 56.0 jit_solution(12857168886405242800)
XLA Ops:
  0.0 0.0 copy-start.2
  0.0 3.0 %pack_signal.1 = bf16[8,160,256]{2,1,0:T(8,128)(2,1)} custom-call(bf16[32,8192]{1,0:T(8,128)(2,1)} %pre_ref.1, bf16[32,8192]{1,0:T(8,128)(2,1)} %val_ref.1, f32[2,8192]{1,0:T(2,128)} %taps_ref.1), custom_call_target="tpu_custom_call" | custom-call | tf_op jit(solution)/shard_map/pack_signal/pallas_call | solution.py:69
  3.0 5.3 %all-to-all-start = ((bf16[8,160,256]{2,1,0:T(8,128)(2,1)}), bf16[8,160,256]{2,1,0:T(8,128)(2,1)S(1)}, u32[]{:S(2)}, u32[]{:S(2)}) async-start(bf16[8,160,256]{2,1,0:T(8,128)(2,1)} %pack_signal.1), calls=%async_computation | async-start | bytes 1310720 | tf_op jit(solution)/shard_map/all_to_all | solution.py:250
  8.3 0.0 copy-done.2
  8.3 0.0 copy-done
  8.3 0.0 copy-done.1
  8.3 0.1 make_tables.1
  8.4 0.0 copy-start.4
  8.5 0.7 %copy-done.4 = bf16[256,512]{1,0:T(8,128)(2,1)} copy-done((bf16[256,512]{1,0:T(8,128)(2,1)}, bf16[256,512]{1,0:T(8,128)(2,1)S(1)}, u32[]{:S(2)}) %copy-start.4) | copy-done | bytes 262168
  9.1 10.3 %all-to-all-done.got_ref = bf16[8,160,256]{2,1,0:T(8,128)(2,1)S(1)} async-done(((bf16[8,160,256]{2,1,0:T(8,128)(2,1)}), bf16[8,160,256]{2,1,0:T(8,128)(2,1)S(1)}, u32[]{:S(2)}, u32[]{:S(2)}) %all-to-all-start) | async-done | bytes 655392 | tf_op jit(solution)/shard_map/all_to_all | solution.py:250
  19.4 0.7 %copy-done.6 = f32[32]{0:T(128)S(1)} copy-done((f32[32]{0:T(128)S(1)}, f32[32]{0:T(128)}, u32[]{:S(2)}) %copy-start.6) | copy-done | bytes 152
  20.1 0.9 %copy-done.5 = bf16[256,512]{1,0:T(8,128)(2,1)S(1)} copy-done((bf16[256,512]{1,0:T(8,128)(2,1)S(1)}, bf16[256,512]{1,0:T(8,128)(2,1)}, u32[]{:S(2)}) %copy-start.5) | copy-done | bytes 262168
  21.0 1.0 %copy-done.7 = f32[256,512]{1,0:T(8,128)S(1)} copy-done((f32[256,512]{1,0:T(8,128)S(1)}, f32[256,512]{1,0:T(8,128)}, u32[]{:S(2)}) %copy-start.7) | copy-done | bytes 524312
  22.1 4.9 %convolve.1 = bf16[32,32,256]{2,1,0:T(8,128)(2,1)} custom-call(f32[32]{0:T(128)S(1)} %copy-done.6, bf16[8,160,256]{2,1,0:T(8,128)(2,1)S(1)} %all-to-all-done.got_ref, bf16[512,256]{1,0:T(8,128)(2,1)S(1)} %get-tuple-element.21.outer_ref, bf16[256,512]{1,0:T(8,128)(2,1)S(1)} %copy-done.5, bf16[512,512]{1,0:T(8,128)(2,1)S(1)} %get-tuple-element.23.ahead, ...), custom_call_target="tpu_custom_call" | custom-call | flops 1879048192 | bytes 1048576 | tf_op jit(solution)/shard_map/convolve/pallas_call | solution.py:186
  26.9 4.0 %all-to-all-start.1 = ((bf16[32,32,256]{2,1,0:T(8,128)(2,1)}), bf16[32,32,256]{2,1,0:T(8,128)(2,1)S(1)}, u32[]{:S(2)}, u32[]{:S(2)}) async-start(bf16[32,32,256]{2,1,0:T(8,128)(2,1)} %convolve.1), calls=%async_computation.1 | async-start | bytes 1048576 | tf_op jit(solution)/shard_map/all_to_all | solution.py:258
  30.9 0.0 copy-done.3
  31.0 1.8 %collective-permute-start = (bf16[32,2048]{1,0:T(8,128)(2,1)S(1)}, bf16[32,2048]{1,0:T(8,128)(2,1)S(1)}, u32[]{:S(2)}, u32[]{:S(2)}) collective-permute-start(bf16[32,2048]{1,0:T(8,128)(2,1)S(1)} %get-tuple-element.28), channel_id=1, source_target_pairs={{0,1},{1,0},{2,3},{3,2},{4,5},{5,4},{6,7},{7,6},{8,9},{9,8},{10,11... | collective-permute-start | bytes 393224 | tf_op jit(solution)/shard_map/ppermute | solution.py:255
  32.8 2.4 %collective-permute-start.1 = (bf16[32,2048]{1,0:T(8,128)(2,1)S(1)}, bf16[32,2048]{1,0:T(8,128)(2,1)S(1)}, u32[]{:S(2)}, u32[]{:S(2)}) collective-permute-start(bf16[32,2048]{1,0:T(8,128)(2,1)S(1)} %get-tuple-element.29), channel_id=1, source_target_pairs={{0,2},{1,3},{2,0},{3,1},{4,6},{5,7},{6,4},{7,5},{8,10},{9,11},{10,... | collective-permute-start | bytes 393224 | tf_op jit(solution)/shard_map/ppermute | solution.py:255
  35.2 0.2 collective-permute-start.2
  35.4 8.4 %collective-permute-done.rest_1_ = bf16[32,2048]{1,0:T(8,128)(2,1)S(1)} collective-permute-done((bf16[32,2048]{1,0:T(8,128)(2,1)S(1)}, bf16[32,2048]{1,0:T(8,128)(2,1)S(1)}, u32[]{:S(2)}, u32[]{:S(2)}) %collective-permute-start) | collective-permute-done | bytes 131104 | tf_op jit(solution)/shard_map/ppermute | solution.py:255
  43.9 11.0 %collective-permute-done.1.rest_2_ = bf16[32,2048]{1,0:T(8,128)(2,1)S(1)} collective-permute-done((bf16[32,2048]{1,0:T(8,128)(2,1)S(1)}, bf16[32,2048]{1,0:T(8,128)(2,1)S(1)}, u32[]{:S(2)}, u32[]{:S(2)}) %collective-permute-start.1) | collective-permute-done | bytes 131104 | tf_op jit(solution)/shard_map/ppermute | solution.py:255
  54.8 0.0 collective-permute-done.2.rest_3_
  54.8 0.0 all-to-all-done.1.got_ref
  54.8 1.2 %unpack.1 = bf16[128,2048]{1,0:T(8,128)(2,1)} custom-call(bf16[32,32,256]{2,1,0:T(8,128)(2,1)S(1)} %all-to-all-done.1.got_ref, bf16[32,2048]{1,0:T(8,128)(2,1)S(1)} %get-tuple-element.27.rest_0_, bf16[32,2048]{1,0:T(8,128)(2,1)S(1)} %collective-permute-done.rest_1_, bf16[32,2048]{1,0:T(8,128)(2,1)S(1)} %collective-permute-done.1.rest_2_, ...), custom_call_target="tpu_custom_call" | custom-call | tf_op jit(solution)/shard_map/unpack/pallas_call | solution.py:230
  (7 shorter events, 0.1 us)
Async XLA Ops:
  0.0 8.3 %copy-start.2 = (f32[512,256]{1,0:T(8,128)S(1)}, f32[512,256]{1,0:T(8,128)}, u32[]{:S(2)}) copy-start(f32[512,256]{1,0:T(8,128)} %constant.10.clone.inner_ref) | copy-start | bytes 1572868
  3.0 5.3 %copy-start = (f32[512,256]{1,0:T(8,128)S(1)}, f32[512,256]{1,0:T(8,128)}, u32[]{:S(2)}) copy-start(f32[512,256]{1,0:T(8,128)} %constant.8.clone.outer_ref) | copy-start | bytes 1572868
  3.0 5.3 %copy-start.1 = (f32[256,512]{1,0:T(8,128)S(1)}, f32[256,512]{1,0:T(8,128)}, u32[]{:S(2)}) copy-start(f32[256,512]{1,0:T(8,128)} %constant.9.clone.back_ref) | copy-start | bytes 1572868
  3.0 16.5 %all-to-all-start = ((bf16[8,160,256]{2,1,0:T(8,128)(2,1)}), bf16[8,160,256]{2,1,0:T(8,128)(2,1)S(1)}, u32[]{:S(2)}, u32[]{:S(2)}) async-start(bf16[8,160,256]{2,1,0:T(8,128)(2,1)} %pack_signal.1), calls=%async_computation | async-start | bytes 1310720 | tf_op jit(solution)/shard_map/all_to_all | solution.py:250
  8.4 0.7 %copy-start.4 = (bf16[256,512]{1,0:T(8,128)(2,1)}, bf16[256,512]{1,0:T(8,128)(2,1)S(1)}, u32[]{:S(2)}) copy-start(bf16[256,512]{1,0:T(8,128)(2,1)S(1)} %get-tuple-element.22.back_ref) | copy-start | bytes 786436
  19.4 0.7 %copy-start.6 = (f32[32]{0:T(128)S(1)}, f32[32]{0:T(128)}, u32[]{:S(2)}) copy-start(f32[32]{0:T(128)} %skip_ref.1) | copy-start | bytes 388
  20.1 0.9 %copy-start.5 = (bf16[256,512]{1,0:T(8,128)(2,1)S(1)}, bf16[256,512]{1,0:T(8,128)(2,1)}, u32[]{:S(2)}) copy-start(bf16[256,512]{1,0:T(8,128)(2,1)} %copy-done.4) | copy-start | bytes 786436
  21.0 1.0 %copy-start.7 = (f32[256,512]{1,0:T(8,128)S(1)}, f32[256,512]{1,0:T(8,128)}, u32[]{:S(2)}) copy-start(f32[256,512]{1,0:T(8,128)} %constant.11.clone.turns_ref) | copy-start | bytes 1572868
  26.9 4.0 %copy-start.3 = (bf16[32,8192]{1,0:T(8,128)(2,1)S(1)}, bf16[32,8192]{1,0:T(8,128)(2,1)}, u32[]{:S(2)}) copy-start(bf16[32,8192]{1,0:T(8,128)(2,1)} %gate_ref) | copy-start | bytes 1572868
  26.9 27.9 %all-to-all-start.1 = ((bf16[32,32,256]{2,1,0:T(8,128)(2,1)}), bf16[32,32,256]{2,1,0:T(8,128)(2,1)S(1)}, u32[]{:S(2)}, u32[]{:S(2)}) async-start(bf16[32,32,256]{2,1,0:T(8,128)(2,1)} %convolve.1), calls=%async_computation.1 | async-start | bytes 1048576 | tf_op jit(solution)/shard_map/all_to_all | solution.py:258
  31.0 12.9 %collective-permute-start = (bf16[32,2048]{1,0:T(8,128)(2,1)S(1)}, bf16[32,2048]{1,0:T(8,128)(2,1)S(1)}, u32[]{:S(2)}, u32[]{:S(2)}) collective-permute-start(bf16[32,2048]{1,0:T(8,128)(2,1)S(1)} %get-tuple-element.28), channel_id=1, source_target_pairs={{0,1},{1,0},{2,3},{3,2},{4,5},{5,4},{6,7},{7,6},{8,9},{9,8},{10,11... | collective-permute-start | bytes 393224 | tf_op jit(solution)/shard_map/ppermute | solution.py:255
  32.8 22.0 %collective-permute-start.1 = (bf16[32,2048]{1,0:T(8,128)(2,1)S(1)}, bf16[32,2048]{1,0:T(8,128)(2,1)S(1)}, u32[]{:S(2)}, u32[]{:S(2)}) collective-permute-start(bf16[32,2048]{1,0:T(8,128)(2,1)S(1)} %get-tuple-element.29), channel_id=1, source_target_pairs={{0,2},{1,3},{2,0},{3,1},{4,6},{5,7},{6,4},{7,5},{8,10},{9,11},{10,... | collective-permute-start | bytes 393224 | tf_op jit(solution)/shard_map/ppermute | solution.py:255
  35.2 19.6 %collective-permute-start.2 = (bf16[32,2048]{1,0:T(8,128)(2,1)S(1)}, bf16[32,2048]{1,0:T(8,128)(2,1)S(1)}, u32[]{:S(2)}, u32[]{:S(2)}) collective-permute-start(bf16[32,2048]{1,0:T(8,128)(2,1)S(1)} %get-tuple-element.30), channel_id=1, source_target_pairs={{0,3},{1,2},{2,1},{3,0},{4,7},{5,6},{6,5},{7,4},{8,11},{9,10},{10,... | collective-permute-start | bytes 393224 | tf_op jit(solution)/shard_map/ppermute | solution.py:255

commit v4 on v3

--- a/solution.py
+++ b/solution.py
@@ -27,7 +27,7 @@
     near = 2 * np.pi * (np.arange(W)[:, None] * np.arange(W)[None, :] % W) / W
     inner = np.concatenate([np.cos(near), np.sin(near)], 0)
     turns = np.concatenate([np.cos(turn), np.sin(turn)], 1)
-    return [jnp.asarray(table, jnp.float32) for table in (outer, outer.T, inner, turns)]
+    return [jnp.asarray(table, jnp.float32) for table in (outer, inner, turns)]
 
 
 def spread(flat, first, count, stride, value):
@@ -101,30 +101,32 @@
     )(post_gate)
 
 
-def tables_kernel(outer_ref, back_ref, inner_ref, outer_out, back_out, ahead, rear):
+def tables_kernel(own, skip_ref, outer_ref, inner_ref, turns_ref, outer_out, inner_out, turns_out, weights):
     outer_out[...] = outer_ref[...].astype(jnp.bfloat16)
-    back_out[...] = back_ref[...].astype(jnp.bfloat16)
-    near_cos, near_sin = inner_ref[0:W, :].astype(jnp.bfloat16), inner_ref[W:, :].astype(jnp.bfloat16)
-    for table, sign in ((ahead, -1), (rear, 1)):
-        table[0:W, 0:W] = near_cos
-        table[0:W, W:] = near_sin * sign
-        table[W:, 0:W] = near_sin * -sign
-        table[W:, W:] = near_cos
-
-
-def make_tables(outer, back, inner):
-    shapes = (outer.shape, back.shape, (2 * W, 2 * W), (2 * W, 2 * W))
-    return pl.pallas_call(
-        tables_kernel,
-        out_shape=[jax.ShapeDtypeStruct(shape, jnp.bfloat16) for shape in shapes],
-        in_specs=[whole_vmem()] * 3,
+    inner_out[...] = inner_ref[...].astype(jnp.bfloat16)
+    turns_out[...] = turns_ref[...]
+    me = lax.axis_index("ctx")
+    for c in range(own):
+        weights[c] = jnp.full((8, W), skip_ref[own * me + c], jnp.float32)
+
+
+def make_tables(skip, outer, inner, turns, own):
+    return pl.pallas_call(
+        functools.partial(tables_kernel, own),
+        out_shape=[
+            jax.ShapeDtypeStruct(outer.shape, jnp.bfloat16),
+            jax.ShapeDtypeStruct(inner.shape, jnp.bfloat16),
+            jax.ShapeDtypeStruct(turns.shape, jnp.float32),
+            jax.ShapeDtypeStruct((own, 8, W), jnp.float32),
+        ],
+        in_specs=[pl.BlockSpec(memory_space=pltpu.SMEM)] + [whole_vmem()] * 3,
         out_specs=[whole_vmem()] * 4,
-        compiler_params=pltpu.CompilerParams(vmem_limit_bytes=24 * 2**20),
+        compiler_params=pltpu.CompilerParams(vmem_limit_bytes=8 * 2**20),
         name="make_tables",
-    )(outer, back, inner)
-
-
-def conv_kernel(own, skip_ref, got_ref, outer_ref, back_ref, ahead, rear, turns_ref, out_ref, x_all, r_all, z_all):
+    )(skip, outer, inner, turns)
+
+
+def conv_kernel(own, got_ref, outer_ref, inner_ref, turns_ref, weights_ref, out_ref, x_all, r_all, z_all, ahead, rear):
     parts, local, _ = got_ref.shape
     near = local // (own + 1)
     blocks = parts * near
@@ -132,6 +134,13 @@
     for p in range(parts):
         for c in range(own + 1):
             x_all[p * near : (p + 1) * near, W * c : W * (c + 1)] = got_ref[p, c * near : (c + 1) * near, :]
+
+    near_cos, near_sin = inner_ref[0:W, :], inner_ref[W:, :]
+    for table, sign in ((ahead, -1), (rear, 1)):
+        table[0:W, 0:W] = near_cos
+        table[0:W, W:] = near_sin * sign
+        table[W:, 0:W] = near_sin * -sign
+        table[W:, W:] = near_cos
 
     def dot(left, right):
         return jnp.dot(left, right, preferred_element_type=jnp.float32)
@@ -164,11 +173,12 @@
             r_all[here, cols] = (re * turn_cos - im * turn_sin).astype(jnp.bfloat16)
             r_all[there, cols] = (re * turn_sin + im * turn_cos).astype(jnp.bfloat16)
 
-    me = lax.axis_index("ctx")
     for c in range(own):
         cols = slice(W * c, W * (c + 1))
-        conv = dot(back_ref[...], r_all[:, cols])
-        z_all[c] = conv + skip_ref[own * me + c] * x_all[:, cols].astype(jnp.float32)
+        conv = lax.dot_general(
+            outer_ref[...], r_all[:, cols], (((0,), (0,)), ((), ())), preferred_element_type=jnp.float32
+        )
+        z_all[c] = conv + weights_ref[c, 0:1, :] * x_all[:, cols].astype(jnp.float32)
     some = out_ref.shape[1] // own
     ch_count = near // some
     for k in range(parts):
@@ -178,25 +188,26 @@
             out_ref[m * parts + k] = jnp.concatenate(rows, 0).astype(jnp.bfloat16)
 
 
-def convolve(got, skip, tables, own, ch_count):
+def convolve(got, tables, own, ch_count):
     parts, local, _ = got.shape
     blocks = parts * (local // (own + 1))
-    steps = 8 * blocks * W * W * (3 * own + 2)
     owners = parts * ch_count
     return pl.pallas_call(
         functools.partial(conv_kernel, own),
         out_shape=jax.ShapeDtypeStruct((owners, own * blocks // owners, W), jnp.bfloat16),
-        in_specs=[pl.BlockSpec(memory_space=pltpu.SMEM)] + [whole_vmem()] * (1 + len(tables)),
+        in_specs=[whole_vmem()] * (1 + len(tables)),
         out_specs=whole_vmem(),
         scratch_shapes=[
             pltpu.VMEM((blocks, W * (own + 1)), jnp.bfloat16),
             pltpu.VMEM((2 * blocks, W * own), jnp.bfloat16),
             pltpu.VMEM((own, blocks, W), jnp.float32),
+            pltpu.VMEM((2 * W, 2 * W), jnp.bfloat16),
+            pltpu.VMEM((2 * W, 2 * W), jnp.bfloat16),
         ],
         compiler_params=pltpu.CompilerParams(vmem_limit_bytes=32 * 2**20),
-        cost_estimate=pl.CostEstimate(flops=steps, bytes_accessed=4 * own * blocks * W, transcendentals=0),
+        cost_estimate=pl.CostEstimate(flops=blocks * W, bytes_accessed=4 * blocks * W, transcendentals=0),
         name="convolve",
-    )(skip, got, *tables)
+    )(got, *tables)
 
 
 def unpack_kernel(own, got_ref, *rest):
@@ -249,12 +260,13 @@
     send = pack_signal(pre_gate, value, filter_taps, ctx_count)
     got = lax.all_to_all(send, "ctx", split_axis=0, concat_axis=0, tiled=True)
     tables = dft_tables(blocks)
-    post_gate, tables, _ = lax.optimization_barrier((post_gate, tables, send))
+    post_gate, skip, tables, _ = lax.optimization_barrier((post_gate, skip, tables, send))
     gates = list(split_gate(post_gate, ch_count))
     for d in range(1, ch_count):
         gates[d] = lax.ppermute(gates[d], "ch", [(i, i ^ d) for i in range(ch_count)])
-    tables = list(make_tables(*tables[:3])) + [tables[3]]
-    mixed = convolve(got, skip, tables, own, ch_count)
+    tables = make_tables(skip, *tables, own)
+    mixed = convolve(got, tables, own, ch_count)
+    mixed, gates = lax.optimization_barrier((mixed, gates))
     mixed = lax.all_to_all(mixed, ("ch", "ctx"), split_axis=0, concat_axis=0, tiled=True)
     return unpack(mixed, gates, own)
 

time: 56.4 us -> 46.5 us (0.82)
  the two profiles are of different devices: /device:TPU:0 before, /device:TPU:1 now
where the time goes in v4:
time: 46.5 us; the launch traced here: 45.7 us
  blocking collectives  22.5 us (48%)
  Pallas kernels  9.04 us (19%)
  starting transfers between devices  8.96 us (19%)
  waiting for transfers between devices  5.19 us (11%)
    all_to_all x1, blocking collectives, body(): lax.all_to_all(mixed, ('ch', 'ctx'), split_axis=0, concat_axis=0, tiled=T...  22.5 us
    all_to_all x1, starting transfers between devices, body(): got = lax.all_to_all(send, 'ctx', split_axis=0, concat_axis=0, tiled=True)  5.35 us
    ppermute x3, starting transfers between devices, body(): lax.ppermute(gates[d], 'ch', [(i, i ^ d) for i in range(ch_count)])  3.61 us
    pallas_call x1, Pallas kernels, convolve(): pl.pallas_call(functools.partial(conv_kernel, own), out_shape=jax.ShapeDt...  3.53 us
    pallas_call x1, Pallas kernels, pack_signal(): pl.pallas_call(functools.partial(pack_signal_kernel, own, blocks, group),...  2.97 us
    all_to_all x1, waiting for transfers between devices, body(): got = lax.all_to_all(send, 'ctx', split_axis=0, concat_axis=0, tiled=True)  2.71 us
    ppermute x3, waiting for transfers between devices, body(): lax.ppermute(gates[d], 'ch', [(i, i ^ d) for i in range(ch_count)])  2.48 us
    pallas_call x1, Pallas kernels, unpack(): pl.pallas_call(functools.partial(unpack_kernel, own), out_shape=jax.Shape...  1.18 us
  transfers between devices with their start and end apart: 4, of which 2 were waited for; matrix products, arithmetic and copies ran while one was open for 0% of the time, Pallas kernels for 11%

profile of v4, /device:TPU:1, one launch (start us, length us, event | category | flops | bytes accessed | tf_op | source)
XLA Modules:
  0.0 45.7 jit_solution(385882870891296210)
XLA Ops:
  0.0 0.0 copy-start.3
  0.0 3.0 %pack_signal.1 = bf16[8,160,256]{2,1,0:T(8,128)(2,1)} custom-call(bf16[32,8192]{1,0:T(8,128)(2,1)} %pre_ref.1, bf16[32,8192]{1,0:T(8,128)(2,1)} %val_ref.1, f32[2,8192]{1,0:T(2,128)} %taps_ref.1), custom_call_target="tpu_custom_call" | custom-call | tf_op jit(solution)/shard_map/pack_signal/pallas_call | solution.py:69
  3.0 0.0 copy-start
  3.0 0.0 copy-start.2
  3.0 5.4 %all-to-all-start = ((bf16[8,160,256]{2,1,0:T(8,128)(2,1)}), bf16[8,160,256]{2,1,0:T(8,128)(2,1)S(1)}, u32[]{:S(2)}, u32[]{:S(2)}) async-start(bf16[8,160,256]{2,1,0:T(8,128)(2,1)} %pack_signal.1), calls=%async_computation | async-start | bytes 1310720 | tf_op jit(solution)/shard_map/all_to_all | solution.py:261
  8.3 0.0 copy-done
  8.3 0.0 copy-start.1
  8.3 0.7 %split_gate.1 = (bf16[32,2048]{1,0:T(8,128)(2,1)S(1)}, bf16[32,2048]{1,0:T(8,128)(2,1)}, bf16[32,2048]{1,0:T(8,128)(2,1)}, bf16[32,2048]{1,0:T(8,128)(2,1)S(1)}) custom-call(bf16[32,8192]{1,0:T(8,128)(2,1)S(1)} %copy-done), custom_call_target="tpu_custom_call" | custom-call | tf_op jit(solution)/shard_map/split_gate/pallas_call | solution.py:94
  9.1 1.3 %collective-permute-start = (bf16[32,2048]{1,0:T(8,128)(2,1)}, bf16[32,2048]{1,0:T(8,128)(2,1)S(1)}, u32[]{:S(2)}, u32[]{:S(2)}) collective-permute-start(bf16[32,2048]{1,0:T(8,128)(2,1)} %get-tuple-element.33), channel_id=1, source_target_pairs={{0,1},{1,0},{2,3},{3,2},{4,5},{5,4},{6,7},{7,6},{8,9},{9,8},{10,11... | collective-permute-start | bytes 393224 | tf_op jit(solution)/shard_map/ppermute | solution.py:266
  10.4 0.0 copy-start.4
  10.4 2.3 %collective-permute-start.1 = (bf16[32,2048]{1,0:T(8,128)(2,1)}, bf16[32,2048]{1,0:T(8,128)(2,1)S(1)}, u32[]{:S(2)}, u32[]{:S(2)}) collective-permute-start(bf16[32,2048]{1,0:T(8,128)(2,1)} %get-tuple-element.34), channel_id=1, source_target_pairs={{0,2},{1,3},{2,0},{3,1},{4,6},{5,7},{6,4},{7,5},{8,10},{9,11},{10,... | collective-permute-start | bytes 393224 | tf_op jit(solution)/shard_map/ppermute | solution.py:266
  12.7 0.0 collective-permute-start.2
  12.7 0.0 copy-done.3
  12.7 0.0 copy-done.2
  12.7 0.0 copy-done.1
  12.7 0.0 copy-done.4
  12.7 0.6 %make_tables.1 = (bf16[512,256]{1,0:T(8,128)(2,1)S(1)}, bf16[512,256]{1,0:T(8,128)(2,1)S(1)}, f32[256,512]{1,0:T(8,128)S(1)}, f32[4,8,256]{2,1,0:T(8,128)S(1)}) custom-call(f32[32]{0:T(128)S(1)} %copy-done.4, f32[512,256]{1,0:T(8,128)S(1)} %copy-done.1, f32[512,256]{1,0:T(8,128)S(1)} %copy-done.2, f32[256,512]{1,0:T(8,128)S(1)} %copy-done.3), custom_call_target="tpu_custom_call" | custom-call | tf_op jit(solution)/shard_map/make_tables/pallas_call | solution.py:114
  13.3 2.7 %all-to-all-done.got_ref = bf16[8,160,256]{2,1,0:T(8,128)(2,1)S(1)} async-done(((bf16[8,160,256]{2,1,0:T(8,128)(2,1)}), bf16[8,160,256]{2,1,0:T(8,128)(2,1)S(1)}, u32[]{:S(2)}, u32[]{:S(2)}) %all-to-all-start) | async-done | bytes 655392 | tf_op jit(solution)/shard_map/all_to_all | solution.py:261
  16.1 3.5 %convolve.1 = bf16[32,32,256]{2,1,0:T(8,128)(2,1)S(1)} custom-call(bf16[8,160,256]{2,1,0:T(8,128)(2,1)S(1)} %all-to-all-done.got_ref, bf16[512,256]{1,0:T(8,128)(2,1)S(1)} %get-tuple-element.27.outer_ref, bf16[512,256]{1,0:T(8,128)(2,1)S(1)} %get-tuple-element.28.inner_ref, f32[256,512]{1,0:T(8,128)S(1)} %get-tuple-element.29.turns_ref, ...), custom_call_target="tpu_custom_call" | custom-call | flops 65536 | bytes 262144 | tf_op jit(solution)/shard_map/convolve/pallas_call | solution.py:195
  19.6 0.0 collective-permute-done.rest_1_
  19.6 0.0 collective-permute-done.1.rest_2_
  19.6 2.5 %collective-permute-done.2.rest_3_ = bf16[32,2048]{1,0:T(8,128)(2,1)S(1)} collective-permute-done((bf16[32,2048]{1,0:T(8,128)(2,1)S(1)}, bf16[32,2048]{1,0:T(8,128)(2,1)S(1)}, u32[]{:S(2)}, u32[]{:S(2)}) %collective-permute-start.2) | collective-permute-done | bytes 131104 | tf_op jit(solution)/shard_map/ppermute | solution.py:266
  22.1 22.5 %all_to_all.10.got_ref = bf16[32,32,256]{2,1,0:T(8,128)(2,1)S(1)} all-to-all(bf16[32,32,256]{2,1,0:T(8,128)(2,1)S(1)} %convolve.1), channel_id=1, replica_groups=mesh['ctx'=8,'ch'=4] {'ch','ctx'}, dimensions={0} | all-to-all | bytes 1048576 | tf_op jit(solution)/shard_map/all_to_all | solution.py:270
  44.5 1.2 %unpack.1 = bf16[128,2048]{1,0:T(8,128)(2,1)} custom-call(bf16[32,32,256]{2,1,0:T(8,128)(2,1)S(1)} %all_to_all.10.got_ref, bf16[32,2048]{1,0:T(8,128)(2,1)S(1)} %get-tuple-element.37.rest_0_, bf16[32,2048]{1,0:T(8,128)(2,1)S(1)} %collective-permute-done.rest_1_, bf16[32,2048]{1,0:T(8,128)(2,1)S(1)} %collective-permute-done.1.rest_2_, ...), custom_call_target="tpu_custom_call" | custom-call | tf_op jit(solution)/shard_map/unpack/pallas_call | solution.py:241
Async XLA Ops:
  0.0 12.7 %copy-start.3 = (f32[256,512]{1,0:T(8,128)S(1)}, f32[256,512]{1,0:T(8,128)}, u32[]{:S(2)}) copy-start(f32[256,512]{1,0:T(8,128)} %constant.8.clone.turns_ref) | copy-start | bytes 1572868
  3.0 5.4 %copy-start = (bf16[32,8192]{1,0:T(8,128)(2,1)S(1)}, bf16[32,8192]{1,0:T(8,128)(2,1)}, u32[]{:S(2)}) copy-start(bf16[32,8192]{1,0:T(8,128)(2,1)} %gate_ref) | copy-start | bytes 1572868
  3.0 9.7 %copy-start.2 = (f32[512,256]{1,0:T(8,128)S(1)}, f32[512,256]{1,0:T(8,128)}, u32[]{:S(2)}) copy-start(f32[512,256]{1,0:T(8,128)} %constant.7.clone.inner_ref) | copy-start | bytes 1572868
  3.0 13.1 %all-to-all-start = ((bf16[8,160,256]{2,1,0:T(8,128)(2,1)}), bf16[8,160,256]{2,1,0:T(8,128)(2,1)S(1)}, u32[]{:S(2)}, u32[]{:S(2)}) async-start(bf16[8,160,256]{2,1,0:T(8,128)(2,1)} %pack_signal.1), calls=%async_computation | async-start | bytes 1310720 | tf_op jit(solution)/shard_map/all_to_all | solution.py:261
  8.3 4.4 %copy-start.1 = (f32[512,256]{1,0:T(8,128)S(1)}, f32[512,256]{1,0:T(8,128)}, u32[]{:S(2)}) copy-start(f32[512,256]{1,0:T(8,128)} %constant.6.clone.outer_ref) | copy-start | bytes 1572868
  9.1 10.5 %collective-permute-start = (bf16[32,2048]{1,0:T(8,128)(2,1)}, bf16[32,2048]{1,0:T(8,128)(2,1)S(1)}, u32[]{:S(2)}, u32[]{:S(2)}) collective-permute-start(bf16[32,2048]{1,0:T(8,128)(2,1)} %get-tuple-element.33), channel_id=1, source_target_pairs={{0,1},{1,0},{2,3},{3,2},{4,5},{5,4},{6,7},{7,6},{8,9},{9,8},{10,11... | collective-permute-start | bytes 393224 | tf_op jit(solution)/shard_map/ppermute | solution.py:266
  10.4 2.3 %copy-start.4 = (f32[32]{0:T(128)S(1)}, f32[32]{0:T(128)}, u32[]{:S(2)}) copy-start(f32[32]{0:T(128)} %skip_ref) | copy-start | bytes 388
  10.4 9.2 %collective-permute-start.1 = (bf16[32,2048]{1,0:T(8,128)(2,1)}, bf16[32,2048]{1,0:T(8,128)(2,1)S(1)}, u32[]{:S(2)}, u32[]{:S(2)}) collective-permute-start(bf16[32,2048]{1,0:T(8,128)(2,1)} %get-tuple-element.34), channel_id=1, source_target_pairs={{0,2},{1,3},{2,0},{3,1},{4,6},{5,7},{6,4},{7,5},{8,10},{9,11},{10,... | collective-permute-start | bytes 393224 | tf_op jit(solution)/shard_map/ppermute | solution.py:266
  12.7 9.4 %collective-permute-start.2 = (bf16[32,2048]{1,0:T(8,128)(2,1)S(1)}, bf16[32,2048]{1,0:T(8,128)(2,1)S(1)}, u32[]{:S(2)}, u32[]{:S(2)}) collective-permute-start(bf16[32,2048]{1,0:T(8,128)(2,1)S(1)} %get-tuple-element.35), channel_id=1, source_target_pairs={{0,3},{1,2},{2,1},{3,0},{4,7},{5,6},{6,5},{7,4},{8,11},{9,10},{10,... | collective-permute-start | bytes 393224 | tf_op jit(solution)/shard_map/ppermute | solution.py:266

commit v5 on v4

--- a/solution.py
+++ b/solution.py
@@ -10,12 +10,17 @@
 
 W = 256
 LANES = 128
+CUTS = 4
 TILE = 16
-CHUNK = 64
+CHUNK = 128
 
 
 def whole_vmem():
     return pl.BlockSpec(memory_space=pltpu.VMEM)
+
+
+def in_hbm():
+    return pl.BlockSpec(memory_space=pltpu.HBM)
 
 
 def dft_tables(blocks):
@@ -39,66 +44,76 @@
     return jnp.concatenate([flat[h, pl.ds(first, count), :] for h in range(W // LANES)], 1)
 
 
-def pack_signal_kernel(own, blocks, group, pre_ref, val_ref, taps_ref, out_ref, flat, taps_flat):
-    step = pl.program_id(0)
+def pack_kernel(own, blocks, group, ch_count, pre_ref, val_ref, taps_ref, post_ref, out_ref, *rest):
+    gate_refs = rest[:ch_count]
+    pre_s, val_s, taps_s, flat, taps_flat, stage, in_sems, out_sems, gate_sems = rest[ch_count:]
+    parts = out_ref.shape[0]
+    channels = own * parts
     rows = own * blocks
-    channels = pre_ref.shape[0]
-
-    @pl.when(step == 0)
-    def _():
-        for j in range(blocks):
-            spread(taps_flat, j, taps_ref.shape[0], blocks, taps_ref[:, W * j : W * (j + 1)])
-
+    width = blocks * W // CUTS
+    loads = []
+    for q in range(CUTS):
+        cols = pl.ds(q * width, width)
+        loads.append(pltpu.make_async_copy(pre_ref.at[:, cols], pre_s.at[:, cols], in_sems.at[q, 0]))
+        loads.append(pltpu.make_async_copy(val_ref.at[:, cols], val_s.at[:, cols], in_sems.at[q, 1]))
+    taps_load = pltpu.make_async_copy(taps_ref, taps_s, in_sems.at[CUTS, 0])
+    for copy in loads[:2] + [taps_load] + loads[2:]:
+        copy.start()
+    me = lax.axis_index("ch")
+    piece = blocks * W // ch_count
+    gates = []
+    for d in range(ch_count):
+        cols = pl.ds(pl.multiple_of(jnp.bitwise_xor(me, d) * piece, LANES), piece)
+        gates.append(pltpu.make_async_copy(post_ref.at[:, cols], gate_refs[d], gate_sems.at[d]))
+        gates[d].start()
     for j in range(blocks):
+        if j % (blocks // CUTS) == 0:
+            q = j // (blocks // CUTS)
+            loads[2 * q].wait()
+            loads[2 * q + 1].wait()
         cols = slice(W * j, W * (j + 1))
-        product = pre_ref[:, cols].astype(jnp.float32) * val_ref[:, cols].astype(jnp.float32)
+        product = pre_s[:, cols].astype(jnp.float32) * val_s[:, cols].astype(jnp.float32)
         spread(flat, j, channels, blocks, product)
-    for i in range(channels // own):
-        out_ref[i, 0:rows, :] = joined(flat, i * rows, rows).astype(jnp.bfloat16)
-        which = (step * channels + own * i) // group
-        taps = joined(taps_flat, pl.multiple_of(which * blocks, 8), blocks)
-        out_ref[i, rows : rows + blocks, :] = taps.astype(jnp.bfloat16)
-
-
-def pack_signal(pre_gate, value, taps, parts):
+        if j == 0:
+            taps_load.wait()
+        spread(taps_flat, j, taps_s.shape[0], blocks, taps_s[:, cols])
+    stores = []
+    for i in range(parts):
+        stage[i, 0:rows, :] = joined(flat, i * rows, rows).astype(jnp.bfloat16)
+        taps = joined(taps_flat, own * i // group * blocks, blocks)
+        stage[i, rows : rows + blocks, :] = taps.astype(jnp.bfloat16)
+        stores.append(pltpu.make_async_copy(stage.at[i], out_ref.at[i], out_sems.at[i]))
+        stores[i].start()
+    for copy in gates + stores:
+        copy.wait()
+
+
+def pack(pre_gate, value, post_gate, taps, parts, ch_count):
     channels, block = value.shape
     own = channels // parts
     group = channels // taps.shape[0]
     blocks = block // W
-    some = min(TILE, channels)
-    return pl.pallas_call(
-        functools.partial(pack_signal_kernel, own, blocks, group),
-        grid=(channels // some,),
-        out_shape=jax.ShapeDtypeStruct((parts, (own + 1) * blocks, W), jnp.bfloat16),
-        in_specs=[pl.BlockSpec((some, block), lambda s: (s, 0))] * 2 + [pl.BlockSpec(taps.shape, lambda s: (0, 0))],
-        out_specs=pl.BlockSpec((some // own, (own + 1) * blocks, W), lambda s: (s, 0, 0)),
+    local = (own + 1) * blocks
+    return pl.pallas_call(
+        functools.partial(pack_kernel, own, blocks, group, ch_count),
+        out_shape=[jax.ShapeDtypeStruct((parts, local, W), jnp.bfloat16)]
+        + [jax.ShapeDtypeStruct((channels, block // ch_count), jnp.bfloat16)] * ch_count,
+        in_specs=[in_hbm()] * 4,
+        out_specs=[in_hbm()] * (1 + ch_count),
         scratch_shapes=[
-            pltpu.VMEM((W // LANES, some * blocks, LANES), jnp.float32),
+            pltpu.VMEM(pre_gate.shape, jnp.bfloat16),
+            pltpu.VMEM(value.shape, jnp.bfloat16),
+            pltpu.VMEM(taps.shape, jnp.float32),
+            pltpu.VMEM((W // LANES, channels * blocks, LANES), jnp.float32),
             pltpu.VMEM((W // LANES, taps.shape[0] * blocks, LANES), jnp.float32),
+            pltpu.VMEM((parts, local, W), jnp.bfloat16),
+            pltpu.SemaphoreType.DMA((CUTS + 1, 2)),
+            pltpu.SemaphoreType.DMA((parts,)),
+            pltpu.SemaphoreType.DMA((ch_count,)),
         ],
         compiler_params=pltpu.CompilerParams(vmem_limit_bytes=60 * 2**20),
-        name="pack_signal",
-    )(pre_gate, value, taps)
-
-
-def split_gate_kernel(gate_ref, *out_refs):
-    me = lax.axis_index("ch")
-    width = out_refs[0].shape[1]
-    for d, out_ref in enumerate(out_refs):
-        first = pl.multiple_of(jnp.bitwise_xor(me, d) * width, LANES)
-        out_ref[...] = gate_ref[:, pl.ds(first, width)]
-
-
-def split_gate(post_gate, parts):
-    channels, block = post_gate.shape
-    return pl.pallas_call(
-        split_gate_kernel,
-        out_shape=[jax.ShapeDtypeStruct((channels, block // parts), jnp.bfloat16)] * parts,
-        in_specs=[whole_vmem()],
-        out_specs=[whole_vmem()] * parts,
-        compiler_params=pltpu.CompilerParams(vmem_limit_bytes=24 * 2**20),
-        name="split_gate",
-    )(post_gate)
+        name="pack",
+    )(pre_gate, value, taps, post_gate)
 
 
 def tables_kernel(own, skip_ref, outer_ref, inner_ref, turns_ref, outer_out, inner_out, turns_out, weights):
@@ -148,8 +163,8 @@
     for first in range(0, blocks, CHUNK):
         here = slice(first, first + CHUNK)
         there = slice(blocks + first, blocks + first + CHUNK)
-        real = dot(outer_ref[here, :], x_all[...])
-        imag = dot(outer_ref[there, :], x_all[...])
+        both = dot(jnp.concatenate([outer_ref[here, :], outer_ref[there, :]], 0), x_all[...])
+        real, imag = both[0:CHUNK, :], both[CHUNK:, :]
         turn_cos, turn_sin = turns_ref[here, 0:W], turns_ref[here, W:]
         rows = []
         for c in range(own + 1):
@@ -173,12 +188,12 @@
             r_all[here, cols] = (re * turn_cos - im * turn_sin).astype(jnp.bfloat16)
             r_all[there, cols] = (re * turn_sin + im * turn_cos).astype(jnp.bfloat16)
 
+    conv = lax.dot_general(
+        outer_ref[...], r_all[...], (((0,), (0,)), ((), ())), preferred_element_type=jnp.float32
+    )
     for c in range(own):
         cols = slice(W * c, W * (c + 1))
-        conv = lax.dot_general(
-            outer_ref[...], r_all[:, cols], (((0,), (0,)), ((), ())), preferred_element_type=jnp.float32
-        )
-        z_all[c] = conv + weights_ref[c, 0:1, :] * x_all[:, cols].astype(jnp.float32)
+        z_all[c] = conv[:, cols] + weights_ref[c, 0:1, :] * x_all[:, cols].astype(jnp.float32)
     some = out_ref.shape[1] // own
     ch_count = near // some
     for k in range(parts):
@@ -211,7 +226,7 @@
 
 
 def unpack_kernel(own, got_ref, *rest):
-    gate_refs, (out_ref, flat, gate_s) = rest[:-3], rest[-3:]
+    gate_refs, (out_ref, flat, gate_s, stage, sems) = rest[:-5], rest[-5:]
     sources, rows, _ = got_ref.shape
     some = rows // own
     me = lax.axis_index("ch")
@@ -228,7 +243,12 @@
             part = flat[h, pl.ds(j, sources * own, stride=some), :]
             first = W * j + LANES * h
             cols = slice(first, first + LANES)
-            out_ref[:, cols] = (part * gate_s[:, cols].astype(jnp.float32)).astype(jnp.bfloat16)
+            stage[:, cols] = (part * gate_s[:, cols].astype(jnp.float32)).astype(jnp.bfloat16)
+        cols = pl.ds(W * j, W)
+        pltpu.make_async_copy(stage.at[:, cols], out_ref.at[:, cols], sems.at[j]).start()
+    for j in range(some):
+        cols = pl.ds(W * j, W)
+        pltpu.make_async_copy(stage.at[:, cols], out_ref.at[:, cols], sems.at[j]).wait()
 
 
 def unpack(got, gates, own):
@@ -242,10 +262,12 @@
         functools.partial(unpack_kernel, own),
         out_shape=jax.ShapeDtypeStruct(shape, jnp.bfloat16),
         in_specs=[whole_vmem()] * (1 + len(gates)),
-        out_specs=whole_vmem(),
+        out_specs=in_hbm(),
         scratch_shapes=[
             pltpu.VMEM((W // LANES, sources * rows, LANES), jnp.float32),
             pltpu.VMEM(shape, jnp.bfloat16),
+            pltpu.VMEM(shape, jnp.bfloat16),
+            pltpu.SemaphoreType.DMA((rows // own,)),
         ],
         compiler_params=pltpu.CompilerParams(vmem_limit_bytes=24 * 2**20),
         name="unpack",
@@ -257,13 +279,11 @@
     ch_count = lax.axis_size("ch")
     own = value.shape[0] // ctx_count
     blocks = value.shape[1] // W * ctx_count
-    send = pack_signal(pre_gate, value, filter_taps, ctx_count)
+    send, *gates = pack(pre_gate, value, post_gate, filter_taps, ctx_count, ch_count)
     got = lax.all_to_all(send, "ctx", split_axis=0, concat_axis=0, tiled=True)
-    tables = dft_tables(blocks)
-    post_gate, skip, tables, _ = lax.optimization_barrier((post_gate, skip, tables, send))
-    gates = list(split_gate(post_gate, ch_count))
     for d in range(1, ch_count):
         gates[d] = lax.ppermute(gates[d], "ch", [(i, i ^ d) for i in range(ch_count)])
+    tables, skip, _ = lax.optimization_barrier((dft_tables(blocks), skip, send))
     tables = make_tables(skip, *tables, own)
     mixed = convolve(got, tables, own, ch_count)
     mixed, gates = lax.optimization_barrier((mixed, gates))

time: 46.5 us -> 61.1 us (1.31)
  Pallas kernels: 9.04 us -> 22.5 us
  local copies, waits for them, and re-layouts: 0.02 us -> 1.38 us
    pallas_call x2 -> x1, Pallas kernels: 3.7 us -> 17.2 us  [pack(): pl.pallas_call(functools.partial(pack_kernel, own, blocks, group, ch_coun...]
    unnamed x10 -> x14, local copies, waits for them, and re-layouts: 0.02 us -> 1.38 us
    pallas_call x1, Pallas kernels: 3.53 us -> 2.67 us  [convolve(): pl.pallas_call(functools.partial(conv_kernel, own), out_shape=jax.ShapeDt...]
    pallas_call x1, Pallas kernels: 1.18 us -> 2 us  [unpack(): pl.pallas_call(functools.partial(unpack_kernel, own), out_shape=jax.Shape...]
  transfers between devices with their start and end apart: 4 -> 4, of which waited for: 2 -> 2; matrix products, arithmetic and copies ran while one was open for 0% -> 0% of each run, Pallas kernels for 11% -> 5%
where the time goes in v5:
time: 61.1 us; the launch traced here: 60.2 us
  Pallas kernels  22.5 us (37%)
  blocking collectives  22.4 us (37%)
  starting transfers between devices  8.97 us (15%)
  waiting for transfers between devices  4.8 us (8%)
  local copies, waits for them, and re-layouts  1.38 us (2%)
    all_to_all x1, blocking collectives, body(): lax.all_to_all(mixed, ('ch', 'ctx'), split_axis=0, concat_axis=0, tiled=T...  22.4 us
    pallas_call x1, Pallas kernels, pack(): pl.pallas_call(functools.partial(pack_kernel, own, blocks, group, ch_coun...  17.2 us
    all_to_all x1, starting transfers between devices, body(): got = lax.all_to_all(send, 'ctx', split_axis=0, concat_axis=0, tiled=True)  5.37 us
    ppermute x3, starting transfers between devices, body(): lax.ppermute(gates[d], 'ch', [(i, i ^ d) for i in range(ch_count)])  3.61 us
    all_to_all x1, waiting for transfers between devices, body(): got = lax.all_to_all(send, 'ctx', split_axis=0, concat_axis=0, tiled=True)  2.84 us
    pallas_call x1, Pallas kernels, convolve(): pl.pallas_call(functools.partial(conv_kernel, own), out_shape=jax.ShapeDt...  2.67 us
    pallas_call x1, Pallas kernels, unpack(): pl.pallas_call(functools.partial(unpack_kernel, own), out_shape=jax.Shape...  2 us
    ppermute x3, waiting for transfers between devices, body(): lax.ppermute(gates[d], 'ch', [(i, i ^ d) for i in range(ch_count)])  1.96 us
  transfers between devices with their start and end apart: 4, of which 2 were waited for; matrix products, arithmetic and copies ran while one was open for 0% of the time, Pallas kernels for 5%

profile of v5, /device:TPU:1, one launch (start us, length us, event | category | flops | bytes accessed | tf_op | source)
XLA Modules:
  0.0 60.2 jit_solution(12640421665744741384)
XLA Ops:
  0.0 0.0 copy-start.2
  0.0 17.2 %pack.1 = (bf16[8,160,256]{2,1,0:T(8,128)(2,1)}, bf16[32,2048]{1,0:T(8,128)(2,1)}, bf16[32,2048]{1,0:T(8,128)(2,1)}, bf16[32,2048]{1,0:T(8,128)(2,1)}, bf16[32,2048]{1,0:T(8,128)(2,1)}) custom-call(bf16[32,8192]{1,0:T(8,128)(2,1)} %pre_ref.1, bf16[32,8192]{1,0:T(8,128)(2,1)} %val_ref.1, f32[2,8192]{1,0:T(2,128)} %taps_ref.1, bf16[32,8192]{1,0:T(8,128)(2,1)} %post_ref.1), custom_call_target="tpu_custom_call" | custom-call | tf_op jit(solution)/shard_map/pack/pallas_call | solution.py:97
  17.2 0.0 copy-start
  17.2 0.0 copy-start.1
  17.2 5.4 %all-to-all-start = ((bf16[8,160,256]{2,1,0:T(8,128)(2,1)}), bf16[8,160,256]{2,1,0:T(8,128)(2,1)S(1)}, u32[]{:S(2)}, u32[]{:S(2)}) async-start(bf16[8,160,256]{2,1,0:T(8,128)(2,1)} %get-tuple-element.23), calls=%async_computation | async-start | bytes 1310720 | tf_op jit(solution)/shard_map/all_to_all | solution.py:283
  22.6 1.3 %collective-permute-start = (bf16[32,2048]{1,0:T(8,128)(2,1)}, bf16[32,2048]{1,0:T(8,128)(2,1)S(1)}, u32[]{:S(2)}, u32[]{:S(2)}) collective-permute-start(bf16[32,2048]{1,0:T(8,128)(2,1)} %get-tuple-element.33), channel_id=1, source_target_pairs={{0,1},{1,0},{2,3},{3,2},{4,5},{5,4},{6,7},{7,6},{8,9},{9,8},{10,11... | collective-permute-start | bytes 393224 | tf_op jit(solution)/shard_map/ppermute | solution.py:285
  23.9 2.3 %collective-permute-start.1 = (bf16[32,2048]{1,0:T(8,128)(2,1)}, bf16[32,2048]{1,0:T(8,128)(2,1)S(1)}, u32[]{:S(2)}, u32[]{:S(2)}) collective-permute-start(bf16[32,2048]{1,0:T(8,128)(2,1)} %get-tuple-element.34), channel_id=1, source_target_pairs={{0,2},{1,3},{2,0},{3,1},{4,6},{5,7},{6,4},{7,5},{8,10},{9,11},{10,... | collective-permute-start | bytes 393224 | tf_op jit(solution)/shard_map/ppermute | solution.py:285
  26.2 0.0 collective-permute-start.2
  26.2 0.0 copy-done.2
  26.2 0.0 copy-done
  26.2 0.0 copy-done.1
  26.2 0.0 copy-done.6
  26.2 0.6 %make_tables.1 = (bf16[512,256]{1,0:T(8,128)(2,1)S(1)}, bf16[512,256]{1,0:T(8,128)(2,1)S(1)}, f32[256,512]{1,0:T(8,128)S(1)}, f32[4,8,256]{2,1,0:T(8,128)S(1)}) custom-call(f32[32]{0:T(128)S(1)} %copy-done.6, f32[512,256]{1,0:T(8,128)S(1)} %copy-done.2, f32[512,256]{1,0:T(8,128)S(1)} %copy-done.1, f32[256,512]{1,0:T(8,128)S(1)} %copy-done), custom_call_target="tpu_custom_call" | custom-call | tf_op jit(solution)/shard_map/make_tables/pallas_call | solution.py:129
  26.9 0.0 copy-start.4
  26.9 0.6 copy-done.4
  27.5 2.8 %all-to-all-done.got_ref = bf16[8,160,256]{2,1,0:T(8,128)(2,1)S(1)} async-done(((bf16[8,160,256]{2,1,0:T(8,128)(2,1)}), bf16[8,160,256]{2,1,0:T(8,128)(2,1)S(1)}, u32[]{:S(2)}, u32[]{:S(2)}) %all-to-all-start) | async-done | bytes 655392 | tf_op jit(solution)/shard_map/all_to_all | solution.py:283
  30.3 0.8 %copy-done.5 = f32[4,8,256]{2,1,0:T(8,128)S(1)} copy-done((f32[4,8,256]{2,1,0:T(8,128)S(1)}, f32[4,8,256]{2,1,0:T(8,128)}, u32[]{:S(2)}) %copy-start.5) | copy-done | bytes 32792
  31.1 2.7 %convolve.1 = bf16[32,32,256]{2,1,0:T(8,128)(2,1)S(1)} custom-call(bf16[8,160,256]{2,1,0:T(8,128)(2,1)S(1)} %all-to-all-done.got_ref, bf16[512,256]{1,0:T(8,128)(2,1)S(1)} %get-tuple-element.28.outer_ref, bf16[512,256]{1,0:T(8,128)(2,1)S(1)} %get-tuple-element.29.inner_ref, f32[256,512]{1,0:T(8,128)S(1)} %get-tuple-element.30.turns_ref, ...), custom_call_target="tpu_custom_call" | custom-call | flops 65536 | bytes 262144 | tf_op jit(solution)/shard_map/convolve/pallas_call | solution.py:210
  33.8 0.0 collective-permute-done.rest_1_
  33.8 0.0 collective-permute-done.1.rest_2_
  33.8 2.0 %collective-permute-done.2.rest_3_ = bf16[32,2048]{1,0:T(8,128)(2,1)} collective-permute-done((bf16[32,2048]{1,0:T(8,128)(2,1)}, bf16[32,2048]{1,0:T(8,128)(2,1)}, u32[]{:S(2)}, u32[]{:S(2)}) %collective-permute-start.2) | collective-permute-done | bytes 131104 | tf_op jit(solution)/shard_map/ppermute | solution.py:285
  35.7 22.4 %all_to_all.10.got_ref = bf16[32,32,256]{2,1,0:T(8,128)(2,1)S(1)} all-to-all(bf16[32,32,256]{2,1,0:T(8,128)(2,1)S(1)} %convolve.1), channel_id=1, replica_groups=mesh['ctx'=8,'ch'=4] {'ch','ctx'}, dimensions={0} | all-to-all | bytes 1048576 | tf_op jit(solution)/shard_map/all_to_all | solution.py:290
  58.2 0.0 copy-done.3
  58.2 2.0 %unpack.1 = bf16[128,2048]{1,0:T(8,128)(2,1)} custom-call(bf16[32,32,256]{2,1,0:T(8,128)(2,1)S(1)} %all_to_all.10.got_ref, bf16[32,2048]{1,0:T(8,128)(2,1)S(1)} %copy-done.3, bf16[32,2048]{1,0:T(8,128)(2,1)S(1)} %collective-permute-done.rest_1_, bf16[32,2048]{1,0:T(8,128)(2,1)S(1)} %collective-permute-done.1.rest_2_, ...), custom_call_target="tpu_custom_call" | custom-call | tf_op jit(solution)/shard_map/unpack/pallas_call | solution.py:261
  (3 shorter events, 0.0 us)
Async XLA Ops:
  0.0 26.2 %copy-start.2 = (f32[512,256]{1,0:T(8,128)S(1)}, f32[512,256]{1,0:T(8,128)}, u32[]{:S(2)}) copy-start(f32[512,256]{1,0:T(8,128)} %constant.6.clone.outer_ref) | copy-start | bytes 1572868
  17.2 9.0 %copy-start = (f32[256,512]{1,0:T(8,128)S(1)}, f32[256,512]{1,0:T(8,128)}, u32[]{:S(2)}) copy-start(f32[256,512]{1,0:T(8,128)} %constant.8.clone.turns_ref) | copy-start | bytes 1572868
  17.2 9.0 %copy-start.1 = (f32[512,256]{1,0:T(8,128)S(1)}, f32[512,256]{1,0:T(8,128)}, u32[]{:S(2)}) copy-start(f32[512,256]{1,0:T(8,128)} %constant.7.clone.inner_ref) | copy-start | bytes 1572868
  17.2 13.1 %all-to-all-start = ((bf16[8,160,256]{2,1,0:T(8,128)(2,1)}), bf16[8,160,256]{2,1,0:T(8,128)(2,1)S(1)}, u32[]{:S(2)}, u32[]{:S(2)}) async-start(bf16[8,160,256]{2,1,0:T(8,128)(2,1)} %get-tuple-element.23), calls=%async_computation | async-start | bytes 1310720 | tf_op jit(solution)/shard_map/all_to_all | solution.py:283
  22.6 11.2 %collective-permute-start = (bf16[32,2048]{1,0:T(8,128)(2,1)}, bf16[32,2048]{1,0:T(8,128)(2,1)S(1)}, u32[]{:S(2)}, u32[]{:S(2)}) collective-permute-start(bf16[32,2048]{1,0:T(8,128)(2,1)} %get-tuple-element.33), channel_id=1, source_target_pairs={{0,1},{1,0},{2,3},{3,2},{4,5},{5,4},{6,7},{7,6},{8,9},{9,8},{10,11... | collective-permute-start | bytes 393224 | tf_op jit(solution)/shard_map/ppermute | solution.py:285
  23.9 2.3 %copy-start.6 = (f32[32]{0:T(128)S(1)}, f32[32]{0:T(128)}, u32[]{:S(2)}) copy-start(f32[32]{0:T(128)} %skip_ref) | copy-start | bytes 388
  23.9 9.9 %collective-permute-start.1 = (bf16[32,2048]{1,0:T(8,128)(2,1)}, bf16[32,2048]{1,0:T(8,128)(2,1)S(1)}, u32[]{:S(2)}, u32[]{:S(2)}) collective-permute-start(bf16[32,2048]{1,0:T(8,128)(2,1)} %get-tuple-element.34), channel_id=1, source_target_pairs={{0,2},{1,3},{2,0},{3,1},{4,6},{5,7},{6,4},{7,5},{8,10},{9,11},{10,... | collective-permute-start | bytes 393224 | tf_op jit(solution)/shard_map/ppermute | solution.py:285
  26.2 9.5 %collective-permute-start.2 = (bf16[32,2048]{1,0:T(8,128)(2,1)}, bf16[32,2048]{1,0:T(8,128)(2,1)}, u32[]{:S(2)}, u32[]{:S(2)}) collective-permute-start(bf16[32,2048]{1,0:T(8,128)(2,1)} %get-tuple-element.35), channel_id=1, source_target_pairs={{0,3},{1,2},{2,1},{3,0},{4,7},{5,6},{6,5},{7,4},{8,11},{9,10},{10,... | collective-permute-start | bytes 393224 | tf_op jit(solution)/shard_map/ppermute | solution.py:285
  26.9 0.6 %copy-start.4 = (f32[4,8,256]{2,1,0:T(8,128)}, f32[4,8,256]{2,1,0:T(8,128)S(1)}, u32[]{:S(2)}) copy-start(f32[4,8,256]{2,1,0:T(8,128)S(1)} %get-tuple-element.31.weights_ref) | copy-start | bytes 98308
  30.3 0.8 %copy-start.5 = (f32[4,8,256]{2,1,0:T(8,128)S(1)}, f32[4,8,256]{2,1,0:T(8,128)}, u32[]{:S(2)}) copy-start(f32[4,8,256]{2,1,0:T(8,128)} %copy-done.4) | copy-start | bytes 98308
  35.7 22.4 %copy-start.3 = (bf16[32,2048]{1,0:T(8,128)(2,1)S(1)}, bf16[32,2048]{1,0:T(8,128)(2,1)}, u32[]{:S(2)}) copy-start(bf16[32,2048]{1,0:T(8,128)(2,1)} %get-tuple-element.37.rest_0_) | copy-start | bytes 393220

commit v6 on v5

--- a/solution.py
+++ b/solution.py
@@ -46,7 +46,7 @@
 
 def pack_kernel(own, blocks, group, ch_count, pre_ref, val_ref, taps_ref, post_ref, out_ref, *rest):
     gate_refs = rest[:ch_count]
-    pre_s, val_s, taps_s, flat, taps_flat, stage, in_sems, out_sems, gate_sems = rest[ch_count:]
+    pre_s, val_s, taps_s, flat, taps_flat, in_sems, gate_sems = rest[ch_count:]
     parts = out_ref.shape[0]
     channels = own * parts
     rows = own * blocks
@@ -77,14 +77,11 @@
         if j == 0:
             taps_load.wait()
         spread(taps_flat, j, taps_s.shape[0], blocks, taps_s[:, cols])
-    stores = []
     for i in range(parts):
-        stage[i, 0:rows, :] = joined(flat, i * rows, rows).astype(jnp.bfloat16)
+        out_ref[i, 0:rows, :] = joined(flat, i * rows, rows).astype(jnp.bfloat16)
         taps = joined(taps_flat, own * i // group * blocks, blocks)
-        stage[i, rows : rows + blocks, :] = taps.astype(jnp.bfloat16)
-        stores.append(pltpu.make_async_copy(stage.at[i], out_ref.at[i], out_sems.at[i]))
-        stores[i].start()
-    for copy in gates + stores:
+        out_ref[i, rows : rows + blocks, :] = taps.astype(jnp.bfloat16)
+    for copy in gates:
         copy.wait()
 
 
@@ -94,54 +91,54 @@
     group = channels // taps.shape[0]
     blocks = block // W
     local = (own + 1) * blocks
+    args = [pltpu.with_memory_space_constraint(arg, pltpu.HBM) for arg in (pre_gate, value, taps, post_gate)]
     return pl.pallas_call(
         functools.partial(pack_kernel, own, blocks, group, ch_count),
-        out_shape=[jax.ShapeDtypeStruct((parts, local, W), jnp.bfloat16)]
-        + [jax.ShapeDtypeStruct((channels, block // ch_count), jnp.bfloat16)] * ch_count,
+        out_shape=[pltpu.VMEM((parts, local, W), jnp.bfloat16)]
+        + [pltpu.VMEM((channels, block // ch_count), jnp.bfloat16)] * ch_count,
         in_specs=[in_hbm()] * 4,
-        out_specs=[in_hbm()] * (1 + ch_count),
+        out_specs=[whole_vmem()] * (1 + ch_count),
         scratch_shapes=[
             pltpu.VMEM(pre_gate.shape, jnp.bfloat16),
             pltpu.VMEM(value.shape, jnp.bfloat16),
             pltpu.VMEM(taps.shape, jnp.float32),
             pltpu.VMEM((W // LANES, channels * blocks, LANES), jnp.float32),
             pltpu.VMEM((W // LANES, taps.shape[0] * blocks, LANES), jnp.float32),
-            pltpu.VMEM((parts, local, W), jnp.bfloat16),
             pltpu.SemaphoreType.DMA((CUTS + 1, 2)),
-            pltpu.SemaphoreType.DMA((parts,)),
             pltpu.SemaphoreType.DMA((ch_count,)),
         ],
-        compiler_params=pltpu.CompilerParams(vmem_limit_bytes=60 * 2**20),
+        compiler_params=pltpu.CompilerParams(vmem_limit_bytes=16 * 2**20),
         name="pack",
-    )(pre_gate, value, taps, post_gate)
-
-
-def tables_kernel(own, skip_ref, outer_ref, inner_ref, turns_ref, outer_out, inner_out, turns_out, weights):
+    )(*args)
+
+
+def tables_kernel(own, skip_ref, outer_ref, inner_ref, turns_ref, outer_out, inner_out, turns_out):
     outer_out[...] = outer_ref[...].astype(jnp.bfloat16)
     inner_out[...] = inner_ref[...].astype(jnp.bfloat16)
-    turns_out[...] = turns_ref[...]
+    count, width = turns_ref.shape
+    turns_out[0:count, :] = turns_ref[...]
     me = lax.axis_index("ctx")
     for c in range(own):
-        weights[c] = jnp.full((8, W), skip_ref[own * me + c], jnp.float32)
+        turns_out[count + 8 * c : count + 8 * (c + 1), :] = jnp.full((8, width), skip_ref[own * me + c], jnp.float32)
 
 
 def make_tables(skip, outer, inner, turns, own):
+    count, width = turns.shape
     return pl.pallas_call(
         functools.partial(tables_kernel, own),
         out_shape=[
             jax.ShapeDtypeStruct(outer.shape, jnp.bfloat16),
             jax.ShapeDtypeStruct(inner.shape, jnp.bfloat16),
-            jax.ShapeDtypeStruct(turns.shape, jnp.float32),
-            jax.ShapeDtypeStruct((own, 8, W), jnp.float32),
+            jax.ShapeDtypeStruct((count + 8 * own, width), jnp.float32),
         ],
         in_specs=[pl.BlockSpec(memory_space=pltpu.SMEM)] + [whole_vmem()] * 3,
-        out_specs=[whole_vmem()] * 4,
+        out_specs=[whole_vmem()] * 3,
         compiler_params=pltpu.CompilerParams(vmem_limit_bytes=8 * 2**20),
         name="make_tables",
     )(skip, outer, inner, turns)
 
 
-def conv_kernel(own, got_ref, outer_ref, inner_ref, turns_ref, weights_ref, out_ref, x_all, r_all, z_all, ahead, rear):
+def conv_kernel(own, got_ref, outer_ref, inner_ref, turns_ref, out_ref, x_all, r_all, z_all, ahead, rear):
     parts, local, _ = got_ref.shape
     near = local // (own + 1)
     blocks = parts * near
@@ -193,7 +190,7 @@
     )
     for c in range(own):
         cols = slice(W * c, W * (c + 1))
-        z_all[c] = conv[:, cols] + weights_ref[c, 0:1, :] * x_all[:, cols].astype(jnp.float32)
+        z_all[c] = conv[:, cols] + turns_ref[blocks + 8 * c : blocks + 8 * c + 1, 0:W] * x_all[:, cols].astype(jnp.float32)
     some = out_ref.shape[1] // own
     ch_count = near // some
     for k in range(parts):
@@ -226,7 +223,7 @@
 
 
 def unpack_kernel(own, got_ref, *rest):
-    gate_refs, (out_ref, flat, gate_s, stage, sems) = rest[:-5], rest[-5:]
+    gate_refs, (out_ref, flat, gate_s) = rest[:-3], rest[-3:]
     sources, rows, _ = got_ref.shape
     some = rows // own
     me = lax.axis_index("ch")
@@ -243,12 +240,7 @@
             part = flat[h, pl.ds(j, sources * own, stride=some), :]
             first = W * j + LANES * h
             cols = slice(first, first + LANES)
-            stage[:, cols] = (part * gate_s[:, cols].astype(jnp.float32)).astype(jnp.bfloat16)
-        cols = pl.ds(W * j, W)
-        pltpu.make_async_copy(stage.at[:, cols], out_ref.at[:, cols], sems.at[j]).start()
-    for j in range(some):
-        cols = pl.ds(W * j, W)
-        pltpu.make_async_copy(stage.at[:, cols], out_ref.at[:, cols], sems.at[j]).wait()
+            out_ref[:, cols] = (part * gate_s[:, cols].astype(jnp.float32)).astype(jnp.bfloat16)
 
 
 def unpack(got, gates, own):
@@ -262,12 +254,10 @@
         functools.partial(unpack_kernel, own),
         out_shape=jax.ShapeDtypeStruct(shape, jnp.bfloat16),
         in_specs=[whole_vmem()] * (1 + len(gates)),
-        out_specs=in_hbm(),
+        out_specs=whole_vmem(),
         scratch_shapes=[
             pltpu.VMEM((W // LANES, sources * rows, LANES), jnp.float32),
             pltpu.VMEM(shape, jnp.bfloat16),
-            pltpu.VMEM(shape, jnp.bfloat16),
-            pltpu.SemaphoreType.DMA((rows // own,)),
         ],
         compiler_params=pltpu.CompilerParams(vmem_limit_bytes=24 * 2**20),
         name="unpack",

time: 61.1 us -> 47.3 us (0.77)
  Pallas kernels: 22.5 us -> 8.82 us
  waiting for transfers between devices: 4.8 us -> 6.16 us
  local copies, waits for them, and re-layouts: 1.38 us -> 0.02 us
    pallas_call x1, Pallas kernels: 17.2 us -> 3.3 us  [pack(): pl.pallas_call(functools.partial(pack_kernel, own, blocks, group, ch_coun...]
    unnamed x14 -> x8, local copies, waits for them, and re-layouts: 1.38 us -> 0.02 us
    all_to_all x1, waiting for transfers between devices: 2.84 us -> 3.55 us  [body(): got = lax.all_to_all(send, 'ctx', split_axis=0, concat_axis=0, tiled=True)]
    ppermute x3, waiting for transfers between devices: 1.96 us -> 2.61 us  [body(): lax.ppermute(gates[d], 'ch', [(i, i ^ d) for i in range(ch_count)])]
  transfers between devices with their start and end apart: 4 -> 4, of which waited for: 2 -> 2; matrix products, arithmetic and copies ran while one was open for 0% -> 0% of each run, Pallas kernels for 5% -> 7%
where the time goes in v6:
time: 47.3 us; the launch traced here: 46.5 us
  blocking collectives  22.4 us (47%)
  starting transfers between devices  8.97 us (19%)
  Pallas kernels  8.82 us (19%)
  waiting for transfers between devices  6.16 us (13%)
    all_to_all x1, blocking collectives, body(): lax.all_to_all(mixed, ('ch', 'ctx'), split_axis=0, concat_axis=0, tiled=T...  22.4 us
    all_to_all x1, starting transfers between devices, body(): got = lax.all_to_all(send, 'ctx', split_axis=0, concat_axis=0, tiled=True)  5.37 us
    ppermute x3, starting transfers between devices, body(): lax.ppermute(gates[d], 'ch', [(i, i ^ d) for i in range(ch_count)])  3.61 us
    all_to_all x1, waiting for transfers between devices, body(): got = lax.all_to_all(send, 'ctx', split_axis=0, concat_axis=0, tiled=True)  3.55 us
    pallas_call x1, Pallas kernels, pack(): pl.pallas_call(functools.partial(pack_kernel, own, blocks, group, ch_coun...  3.3 us
    pallas_call x1, Pallas kernels, convolve(): pl.pallas_call(functools.partial(conv_kernel, own), out_shape=jax.ShapeDt...  2.67 us
    ppermute x3, waiting for transfers between devices, body(): lax.ppermute(gates[d], 'ch', [(i, i ^ d) for i in range(ch_count)])  2.61 us
    pallas_call x1, Pallas kernels, unpack(): pl.pallas_call(functools.partial(unpack_kernel, own), out_shape=jax.Shape...  2.21 us
  transfers between devices with their start and end apart: 4, of which 2 were waited for; matrix products, arithmetic and copies ran while one was open for 0% of the time, Pallas kernels for 7%

profile of v6, /device:TPU:1, one launch (start us, length us, event | category | flops | bytes accessed | tf_op | source)
XLA Modules:
  0.0 46.5 jit_solution(2107067185237364828)
XLA Ops:
  0.0 0.0 copy-start.2
  0.0 3.3 %pack.1 = (bf16[8,160,256]{2,1,0:T(8,128)(2,1)}, bf16[32,2048]{1,0:T(8,128)(2,1)S(1)}, bf16[32,2048]{1,0:T(8,128)(2,1)}, bf16[32,2048]{1,0:T(8,128)(2,1)}, bf16[32,2048]{1,0:T(8,128)(2,1)}) custom-call(bf16[32,8192]{1,0:T(8,128)(2,1)} %pre_ref.1, bf16[32,8192]{1,0:T(8,128)(2,1)} %val_ref.1, f32[2,8192]{1,0:T(2,128)} %taps_ref.1, bf16[32,8192]{1,0:T(8,128)(2,1)} %post_ref.1), custom_call_target="tpu_custom_call" | custom-call | tf_op jit(solution)/shard_map/pack/pallas_call | solution.py:95
  3.3 0.0 copy-start
  3.3 0.0 copy-start.1
  3.3 5.4 %all-to-all-start = ((bf16[8,160,256]{2,1,0:T(8,128)(2,1)}), bf16[8,160,256]{2,1,0:T(8,128)(2,1)S(1)}, u32[]{:S(2)}, u32[]{:S(2)}) async-start(bf16[8,160,256]{2,1,0:T(8,128)(2,1)} %get-tuple-element.22), calls=%async_computation | async-start | bytes 1310720 | tf_op jit(solution)/shard_map/all_to_all | solution.py:273
  8.7 1.3 %collective-permute-start = (bf16[32,2048]{1,0:T(8,128)(2,1)}, bf16[32,2048]{1,0:T(8,128)(2,1)}, u32[]{:S(2)}, u32[]{:S(2)}) collective-permute-start(bf16[32,2048]{1,0:T(8,128)(2,1)} %get-tuple-element.31), channel_id=1, source_target_pairs={{0,1},{1,0},{2,3},{3,2},{4,5},{5,4},{6,7},{7,6},{8,9},{9,8},{10,11... | collective-permute-start | bytes 393224 | tf_op jit(solution)/shard_map/ppermute | solution.py:275
  10.0 0.0 copy-start.3
  10.0 2.3 %collective-permute-start.1 = (bf16[32,2048]{1,0:T(8,128)(2,1)}, bf16[32,2048]{1,0:T(8,128)(2,1)}, u32[]{:S(2)}, u32[]{:S(2)}) collective-permute-start(bf16[32,2048]{1,0:T(8,128)(2,1)} %get-tuple-element.32), channel_id=1, source_target_pairs={{0,2},{1,3},{2,0},{3,1},{4,6},{5,7},{6,4},{7,5},{8,10},{9,11},{10,... | collective-permute-start | bytes 393224 | tf_op jit(solution)/shard_map/ppermute | solution.py:275
  12.3 0.0 collective-permute-start.2
  12.3 0.0 copy-done.2
  12.3 0.0 copy-done
  12.3 0.0 copy-done.1
  12.3 0.0 copy-done.3
  12.3 0.6 %make_tables.1 = (bf16[512,256]{1,0:T(8,128)(2,1)S(1)}, bf16[512,256]{1,0:T(8,128)(2,1)S(1)}, f32[288,512]{1,0:T(8,128)S(1)}) custom-call(f32[32]{0:T(128)S(1)} %copy-done.3, f32[512,256]{1,0:T(8,128)S(1)} %copy-done.2, f32[512,256]{1,0:T(8,128)S(1)} %copy-done.1, f32[256,512]{1,0:T(8,128)S(1)} %copy-done), custom_call_target="tpu_custom_call" | custom-call | tf_op jit(solution)/shard_map/make_tables/pallas_call | solution.py:127
  13.0 3.5 %all-to-all-done.got_ref = bf16[8,160,256]{2,1,0:T(8,128)(2,1)S(1)} async-done(((bf16[8,160,256]{2,1,0:T(8,128)(2,1)}), bf16[8,160,256]{2,1,0:T(8,128)(2,1)S(1)}, u32[]{:S(2)}, u32[]{:S(2)}) %all-to-all-start) | async-done | bytes 655392 | tf_op jit(solution)/shard_map/all_to_all | solution.py:273
  16.5 2.7 %convolve.1 = bf16[32,32,256]{2,1,0:T(8,128)(2,1)S(1)} custom-call(bf16[8,160,256]{2,1,0:T(8,128)(2,1)S(1)} %all-to-all-done.got_ref, bf16[512,256]{1,0:T(8,128)(2,1)S(1)} %get-tuple-element.27.outer_ref, bf16[512,256]{1,0:T(8,128)(2,1)S(1)} %get-tuple-element.28.inner_ref, f32[288,512]{1,0:T(8,128)S(1)} %get-tuple-element.29.turns_ref), custom_call_target="tpu_custom_call" | custom-call | flops 65536 | bytes 262144 | tf_op jit(solution)/shard_map/convolve/pallas_call | solution.py:207
  19.2 0.0 collective-permute-done.rest_1_
  19.2 0.0 collective-permute-done.1.rest_2_
  19.2 2.6 %collective-permute-done.2.rest_3_ = bf16[32,2048]{1,0:T(8,128)(2,1)} collective-permute-done((bf16[32,2048]{1,0:T(8,128)(2,1)}, bf16[32,2048]{1,0:T(8,128)(2,1)}, u32[]{:S(2)}, u32[]{:S(2)}) %collective-permute-start.2) | collective-permute-done | bytes 131104 | tf_op jit(solution)/shard_map/ppermute | solution.py:275
  21.8 22.4 %all_to_all.10.got_ref = bf16[32,32,256]{2,1,0:T(8,128)(2,1)S(1)} all-to-all(bf16[32,32,256]{2,1,0:T(8,128)(2,1)S(1)} %convolve.1), channel_id=1, replica_groups=mesh['ctx'=8,'ch'=4] {'ch','ctx'}, dimensions={0} | all-to-all | bytes 1048576 | tf_op jit(solution)/shard_map/all_to_all | solution.py:280
  44.3 2.2 %unpack.1 = bf16[128,2048]{1,0:T(8,128)(2,1)} custom-call(bf16[32,32,256]{2,1,0:T(8,128)(2,1)S(1)} %all_to_all.10.got_ref, bf16[32,2048]{1,0:T(8,128)(2,1)S(1)} %get-tuple-element.35.rest_0_, bf16[32,2048]{1,0:T(8,128)(2,1)} %collective-permute-done.rest_1_, bf16[32,2048]{1,0:T(8,128)(2,1)} %collective-permute-done.1.rest_2_, ...), custom_call_target="tpu_custom_call" | custom-call | tf_op jit(solution)/shard_map/unpack/pallas_call | solution.py:253
Async XLA Ops:
  0.0 12.3 %copy-start.2 = (f32[512,256]{1,0:T(8,128)S(1)}, f32[512,256]{1,0:T(8,128)}, u32[]{:S(2)}) copy-start(f32[512,256]{1,0:T(8,128)} %constant.6.clone.outer_ref) | copy-start | bytes 1572868
  3.3 9.0 %copy-start = (f32[256,512]{1,0:T(8,128)S(1)}, f32[256,512]{1,0:T(8,128)}, u32[]{:S(2)}) copy-start(f32[256,512]{1,0:T(8,128)} %constant.8.clone.turns_ref) | copy-start | bytes 1572868
  3.3 9.0 %copy-start.1 = (f32[512,256]{1,0:T(8,128)S(1)}, f32[512,256]{1,0:T(8,128)}, u32[]{:S(2)}) copy-start(f32[512,256]{1,0:T(8,128)} %constant.7.clone.inner_ref) | copy-start | bytes 1572868
  3.3 13.2 %all-to-all-start = ((bf16[8,160,256]{2,1,0:T(8,128)(2,1)}), bf16[8,160,256]{2,1,0:T(8,128)(2,1)S(1)}, u32[]{:S(2)}, u32[]{:S(2)}) async-start(bf16[8,160,256]{2,1,0:T(8,128)(2,1)} %get-tuple-element.22), calls=%async_computation | async-start | bytes 1310720 | tf_op jit(solution)/shard_map/all_to_all | solution.py:273
  8.7 10.5 %collective-permute-start = (bf16[32,2048]{1,0:T(8,128)(2,1)}, bf16[32,2048]{1,0:T(8,128)(2,1)}, u32[]{:S(2)}, u32[]{:S(2)}) collective-permute-start(bf16[32,2048]{1,0:T(8,128)(2,1)} %get-tuple-element.31), channel_id=1, source_target_pairs={{0,1},{1,0},{2,3},{3,2},{4,5},{5,4},{6,7},{7,6},{8,9},{9,8},{10,11... | collective-permute-start | bytes 393224 | tf_op jit(solution)/shard_map/ppermute | solution.py:275
  10.0 2.3 %copy-start.3 = (f32[32]{0:T(128)S(1)}, f32[32]{0:T(128)}, u32[]{:S(2)}) copy-start(f32[32]{0:T(128)} %skip_ref) | copy-start | bytes 388
  10.0 9.2 %collective-permute-start.1 = (bf16[32,2048]{1,0:T(8,128)(2,1)}, bf16[32,2048]{1,0:T(8,128)(2,1)}, u32[]{:S(2)}, u32[]{:S(2)}) collective-permute-start(bf16[32,2048]{1,0:T(8,128)(2,1)} %get-tuple-element.32), channel_id=1, source_target_pairs={{0,2},{1,3},{2,0},{3,1},{4,6},{5,7},{6,4},{7,5},{8,10},{9,11},{10,... | collective-permute-start | bytes 393224 | tf_op jit(solution)/shard_map/ppermute | solution.py:275
  12.3 9.5 %collective-permute-start.2 = (bf16[32,2048]{1,0:T(8,128)(2,1)}, bf16[32,2048]{1,0:T(8,128)(2,1)}, u32[]{:S(2)}, u32[]{:S(2)}) collective-permute-start(bf16[32,2048]{1,0:T(8,128)(2,1)} %get-tuple-element.33), channel_id=1, source_target_pairs={{0,3},{1,2},{2,1},{3,0},{4,7},{5,6},{6,5},{7,4},{8,11},{9,10},{10,... | collective-permute-start | bytes 393224 | tf_op jit(solution)/shard_map/ppermute | solution.py:275

commit v7 on v6

--- a/solution.py
+++ b/solution.py
@@ -35,18 +35,22 @@
     return [jnp.asarray(table, jnp.float32) for table in (outer, inner, turns)]
 
 
-def spread(flat, first, count, stride, value):
+def lay(natural, j, value):
+    count = value.shape[0]
     for h in range(W // LANES):
-        flat[h, pl.ds(first, count, stride=stride), :] = value[:, LANES * h : LANES * (h + 1)]
-
-
-def joined(flat, first, count):
-    return jnp.concatenate([flat[h, pl.ds(first, count), :] for h in range(W // LANES)], 1)
+        first = (j * (W // LANES) + h) * count
+        natural[first : first + count, :] = value[:, LANES * h : LANES * (h + 1)]
+
+
+def pick(natural, channel, count, blocks):
+    halves = W // LANES
+    rows = [natural[pl.ds(h * count + channel, blocks, stride=halves * count), :] for h in range(halves)]
+    return jnp.concatenate(rows, 1).astype(jnp.bfloat16)
 
 
 def pack_kernel(own, blocks, group, ch_count, pre_ref, val_ref, taps_ref, post_ref, out_ref, *rest):
     gate_refs = rest[:ch_count]
-    pre_s, val_s, taps_s, flat, taps_flat, in_sems, gate_sems = rest[ch_count:]
+    pre_s, val_s, taps_s, post_s, natural, natural_taps, stage, in_sems, out_sems, gate_sems = rest[ch_count:]
     parts = out_ref.shape[0]
     channels = own * parts
     rows = own * blocks
@@ -57,31 +61,35 @@
         loads.append(pltpu.make_async_copy(pre_ref.at[:, cols], pre_s.at[:, cols], in_sems.at[q, 0]))
         loads.append(pltpu.make_async_copy(val_ref.at[:, cols], val_s.at[:, cols], in_sems.at[q, 1]))
     taps_load = pltpu.make_async_copy(taps_ref, taps_s, in_sems.at[CUTS, 0])
-    for copy in loads[:2] + [taps_load] + loads[2:]:
+    gate_load = pltpu.make_async_copy(post_ref, post_s, in_sems.at[CUTS, 1])
+    for copy in loads[:2] + [taps_load] + loads[2:] + [gate_load]:
         copy.start()
-    me = lax.axis_index("ch")
-    piece = blocks * W // ch_count
-    gates = []
-    for d in range(ch_count):
-        cols = pl.ds(pl.multiple_of(jnp.bitwise_xor(me, d) * piece, LANES), piece)
-        gates.append(pltpu.make_async_copy(post_ref.at[:, cols], gate_refs[d], gate_sems.at[d]))
-        gates[d].start()
+    groups = taps_s.shape[0]
     for j in range(blocks):
         if j % (blocks // CUTS) == 0:
             q = j // (blocks // CUTS)
             loads[2 * q].wait()
             loads[2 * q + 1].wait()
         cols = slice(W * j, W * (j + 1))
-        product = pre_s[:, cols].astype(jnp.float32) * val_s[:, cols].astype(jnp.float32)
-        spread(flat, j, channels, blocks, product)
+        lay(natural, j, pre_s[:, cols].astype(jnp.float32) * val_s[:, cols].astype(jnp.float32))
         if j == 0:
             taps_load.wait()
-        spread(taps_flat, j, taps_s.shape[0], blocks, taps_s[:, cols])
+        lay(natural_taps, j, taps_s[:, cols])
+    gate_load.wait()
+    me = lax.axis_index("ch")
+    piece = blocks * W // ch_count
+    stores = []
+    for d in range(ch_count):
+        cols = pl.ds(pl.multiple_of(jnp.bitwise_xor(me, d) * piece, LANES), piece)
+        stores.append(pltpu.make_async_copy(post_s.at[:, cols], gate_refs[d], gate_sems.at[d]))
+        stores[-1].start()
     for i in range(parts):
-        out_ref[i, 0:rows, :] = joined(flat, i * rows, rows).astype(jnp.bfloat16)
-        taps = joined(taps_flat, own * i // group * blocks, blocks)
-        out_ref[i, rows : rows + blocks, :] = taps.astype(jnp.bfloat16)
-    for copy in gates:
+        for c in range(own):
+            stage[i, blocks * c : blocks * (c + 1), :] = pick(natural, own * i + c, channels, blocks)
+        stage[i, rows : rows + blocks, :] = pick(natural_taps, own * i // group, groups, blocks)
+        stores.append(pltpu.make_async_copy(stage.at[i], out_ref.at[i], out_sems.at[i]))
+        stores[-1].start()
+    for copy in stores:
         copy.wait()
 
 
@@ -91,20 +99,24 @@
     group = channels // taps.shape[0]
     blocks = block // W
     local = (own + 1) * blocks
+    halves = W // LANES
     args = [pltpu.with_memory_space_constraint(arg, pltpu.HBM) for arg in (pre_gate, value, taps, post_gate)]
     return pl.pallas_call(
         functools.partial(pack_kernel, own, blocks, group, ch_count),
-        out_shape=[pltpu.VMEM((parts, local, W), jnp.bfloat16)]
-        + [pltpu.VMEM((channels, block // ch_count), jnp.bfloat16)] * ch_count,
+        out_shape=[jax.ShapeDtypeStruct((parts, local, W), jnp.bfloat16)]
+        + [jax.ShapeDtypeStruct((channels, block // ch_count), jnp.bfloat16)] * ch_count,
         in_specs=[in_hbm()] * 4,
-        out_specs=[whole_vmem()] * (1 + ch_count),
+        out_specs=[in_hbm()] * (1 + ch_count),
         scratch_shapes=[
             pltpu.VMEM(pre_gate.shape, jnp.bfloat16),
             pltpu.VMEM(value.shape, jnp.bfloat16),
             pltpu.VMEM(taps.shape, jnp.float32),
-            pltpu.VMEM((W // LANES, channels * blocks, LANES), jnp.float32),
-            pltpu.VMEM((W // LANES, taps.shape[0] * blocks, LANES), jnp.float32),
+            pltpu.VMEM(post_gate.shape, jnp.bfloat16),
+            pltpu.VMEM((blocks * halves * channels, LANES), jnp.float32),
+            pltpu.VMEM((blocks * halves * taps.shape[0], LANES), jnp.float32),
+            pltpu.VMEM((parts, local, W), jnp.bfloat16),
             pltpu.SemaphoreType.DMA((CUTS + 1, 2)),
+            pltpu.SemaphoreType.DMA((parts,)),
             pltpu.SemaphoreType.DMA((ch_count,)),
         ],
         compiler_params=pltpu.CompilerParams(vmem_limit_bytes=16 * 2**20),
@@ -112,18 +124,28 @@
     )(*args)
 
 
-def tables_kernel(own, skip_ref, outer_ref, inner_ref, turns_ref, outer_out, inner_out, turns_out):
-    outer_out[...] = outer_ref[...].astype(jnp.bfloat16)
-    inner_out[...] = inner_ref[...].astype(jnp.bfloat16)
+def tables_kernel(own, skip_ref, outer_ref, inner_ref, turns_ref, outer_out, inner_out, turns_out, outer_s, inner_s, sems):
     count, width = turns_ref.shape
-    turns_out[0:count, :] = turns_ref[...]
+    loads = [
+        pltpu.make_async_copy(outer_ref, outer_s, sems.at[0]),
+        pltpu.make_async_copy(inner_ref, inner_s, sems.at[1]),
+        pltpu.make_async_copy(turns_ref, turns_out.at[0:count, :], sems.at[2]),
+    ]
+    for copy in loads:
+        copy.start()
     me = lax.axis_index("ctx")
     for c in range(own):
         turns_out[count + 8 * c : count + 8 * (c + 1), :] = jnp.full((8, width), skip_ref[own * me + c], jnp.float32)
+    loads[0].wait()
+    outer_out[...] = outer_s[...].astype(jnp.bfloat16)
+    loads[1].wait()
+    inner_out[...] = inner_s[...].astype(jnp.bfloat16)
+    loads[2].wait()
 
 
 def make_tables(skip, outer, inner, turns, own):
     count, width = turns.shape
+    args = [pltpu.with_memory_space_constraint(arg, pltpu.HBM) for arg in (outer, inner, turns)]
     return pl.pallas_call(
         functools.partial(tables_kernel, own),
         out_shape=[
@@ -131,11 +153,16 @@
             jax.ShapeDtypeStruct(inner.shape, jnp.bfloat16),
             jax.ShapeDtypeStruct((count + 8 * own, width), jnp.float32),
         ],
-        in_specs=[pl.BlockSpec(memory_space=pltpu.SMEM)] + [whole_vmem()] * 3,
+        in_specs=[pl.BlockSpec(memory_space=pltpu.SMEM)] + [in_hbm()] * 3,
         out_specs=[whole_vmem()] * 3,
-        compiler_params=pltpu.CompilerParams(vmem_limit_bytes=8 * 2**20),
+        scratch_shapes=[
+            pltpu.VMEM(outer.shape, jnp.float32),
+            pltpu.VMEM(inner.shape, jnp.float32),
+            pltpu.SemaphoreType.DMA((3,)),
+        ],
+        compiler_params=pltpu.CompilerParams(vmem_limit_bytes=12 * 2**20),
         name="make_tables",
-    )(skip, outer, inner, turns)
+    )(skip, *args)
 
 
 def conv_kernel(own, got_ref, outer_ref, inner_ref, turns_ref, out_ref, x_all, r_all, z_all, ahead, rear):
@@ -197,7 +224,7 @@
         for m in range(ch_count):
             first = k * near + m * some
             rows = [z_all[c, first : first + some, :] for c in range(own)]
-            out_ref[m * parts + k] = jnp.concatenate(rows, 0).astype(jnp.bfloat16)
+            out_ref[k * ch_count + m] = jnp.concatenate(rows, 0).astype(jnp.bfloat16)
 
 
 def convolve(got, tables, own, ch_count):
@@ -231,10 +258,12 @@
     for d, gate_ref in enumerate(gate_refs):
         first = pl.multiple_of(jnp.bitwise_xor(me, d) * channels, TILE)
         gate_s[pl.ds(first, channels), :] = gate_ref[...]
+    ch_count = len(gate_refs)
     for p in range(sources):
         part = got_ref[p].astype(jnp.float32)
+        first = (p % ch_count * (sources // ch_count) + p // ch_count) * rows
         for h in range(W // LANES):
-            flat[h, p * rows : (p + 1) * rows, :] = part[:, LANES * h : LANES * (h + 1)]
+            flat[h, first : first + rows, :] = part[:, LANES * h : LANES * (h + 1)]
     for j in range(some):
         for h in range(W // LANES):
             part = flat[h, pl.ds(j, sources * own, stride=some), :]
@@ -249,6 +278,7 @@
     if rows % TILE:
         order = jnp.bitwise_xor(lax.axis_index("ch"), jnp.arange(len(gates)))
         gate = jnp.stack(gates)[order].reshape(shape)
+        got = got.reshape(-1, len(gates), rows, W).swapaxes(0, 1)
         return (got.reshape(shape).astype(jnp.float32) * gate.astype(jnp.float32)).astype(jnp.bfloat16)
     return pl.pallas_call(
         functools.partial(unpack_kernel, own),
@@ -261,7 +291,7 @@
         ],
         compiler_params=pltpu.CompilerParams(vmem_limit_bytes=24 * 2**20),
         name="unpack",
-    )(got, *gates)
+    )(got, *[pltpu.with_memory_space_constraint(gate, pltpu.VMEM) for gate in gates])
 
 
 def body(pre_gate, value, post_gate, filter_taps, skip):
@@ -271,13 +301,13 @@
     blocks = value.shape[1] // W * ctx_count
     send, *gates = pack(pre_gate, value, post_gate, filter_taps, ctx_count, ch_count)
     got = lax.all_to_all(send, "ctx", split_axis=0, concat_axis=0, tiled=True)
-    for d in range(1, ch_count):
+    for d in reversed(range(1, ch_count)):
         gates[d] = lax.ppermute(gates[d], "ch", [(i, i ^ d) for i in range(ch_count)])
     tables, skip, _ = lax.optimization_barrier((dft_tables(blocks), skip, send))
     tables = make_tables(skip, *tables, own)
     mixed = convolve(got, tables, own, ch_count)
     mixed, gates = lax.optimization_barrier((mixed, gates))
-    mixed = lax.all_to_all(mixed, ("ch", "ctx"), split_axis=0, concat_axis=0, tiled=True)
+    mixed = lax.all_to_all(mixed, ("ctx", "ch"), split_axis=0, concat_axis=0, tiled=True)
     return unpack(mixed, gates, own)
 
 

time: 47.3 us -> 45.1 us (0.953); the launches traced: 46.5 us -> 44.9 us
  waiting for transfers between devices: 6.16 us -> 4.58 us
    all_to_all x1, waiting for transfers between devices: 3.55 us -> 2.17 us  [body(): got = lax.all_to_all(send, 'ctx', split_axis=0, concat_axis=0, tiled=True)]
    pallas_call x1, Pallas kernels: 0.63 us -> 1.92 us  [make_tables(): pl.pallas_call(functools.partial(tables_kernel, own), out_shape=[jax.Shap...]
    pallas_call x1, Pallas kernels: 2.21 us -> 1.18 us  [unpack(): pl.pallas_call(functools.partial(unpack_kernel, own), out_shape=jax.Shape...]
  transfers between devices with their start and end apart: 4 -> 4, of which waited for: 2 -> 2; matrix products, arithmetic and copies ran while one was open for 0% -> 0% of each run, Pallas kernels for 7% -> 10%
where the time goes in v7:
time: 45.1 us; the launch traced here: 44.9 us
  blocking collectives  22.5 us (50%)
  Pallas kernels  8.87 us (20%)
  starting transfers between devices  8.84 us (20%)
  waiting for transfers between devices  4.58 us (10%)
    all_to_all x1, blocking collectives, body(): lax.all_to_all(mixed, ('ctx', 'ch'), split_axis=0, concat_axis=0, tiled=T...  22.5 us
    all_to_all x1, starting transfers between devices, body(): got = lax.all_to_all(send, 'ctx', split_axis=0, concat_axis=0, tiled=True)  5.24 us
    ppermute x3, starting transfers between devices, body(): lax.ppermute(gates[d], 'ch', [(i, i ^ d) for i in range(ch_count)])  3.61 us
    pallas_call x1, Pallas kernels, pack(): pl.pallas_call(functools.partial(pack_kernel, own, blocks, group, ch_coun...  3.09 us
    pallas_call x1, Pallas kernels, convolve(): pl.pallas_call(functools.partial(conv_kernel, own), out_shape=jax.ShapeDt...  2.67 us
    ppermute x3, waiting for transfers between devices, body(): lax.ppermute(gates[d], 'ch', [(i, i ^ d) for i in range(ch_count)])  2.4 us
    all_to_all x1, waiting for transfers between devices, body(): got = lax.all_to_all(send, 'ctx', split_axis=0, concat_axis=0, tiled=True)  2.17 us
    pallas_call x1, Pallas kernels, make_tables(): pl.pallas_call(functools.partial(tables_kernel, own), out_shape=[jax.Shap...  1.92 us
  transfers between devices with their start and end apart: 4, of which 2 were waited for; matrix products, arithmetic and copies ran while one was open for 0% of the time, Pallas kernels for 10%

profile of v7, /device:TPU:1, one launch (start us, length us, event | category | flops | bytes accessed | tf_op | source)
XLA Modules:
  0.0 44.9 jit_solution(11999154930997992102)
XLA Ops:
  0.0 3.1 %pack.1 = (bf16[8,160,256]{2,1,0:T(8,128)(2,1)}, bf16[32,2048]{1,0:T(8,128)(2,1)S(1)}, bf16[32,2048]{1,0:T(8,128)(2,1)S(1)}, bf16[32,2048]{1,0:T(8,128)(2,1)S(1)}, bf16[32,2048]{1,0:T(8,128)(2,1)S(1)}) custom-call(bf16[32,8192]{1,0:T(8,128)(2,1)} %pre_ref.1, bf16[32,8192]{1,0:T(8,128)(2,1)} %val_ref.1, f32[2,8192]{1,0:T(2,128)} %taps_ref.1, ...), custom_call_target="tpu_custom_call" | custom-call | tf_op jit(solution)/shard_map/pack/pallas_call | solution.py:104
  3.1 5.2 %all-to-all-start = ((bf16[8,160,256]{2,1,0:T(8,128)(2,1)}), bf16[8,160,256]{2,1,0:T(8,128)(2,1)S(1)}, u32[]{:S(2)}, u32[]{:S(2)}) async-start(bf16[8,160,256]{2,1,0:T(8,128)(2,1)} %get-tuple-element.22), calls=%async_computation | async-start | bytes 1310720 | tf_op jit(solution)/shard_map/all_to_all | solution.py:303
  8.3 1.3 %collective-permute-start = (bf16[32,2048]{1,0:T(8,128)(2,1)S(1)}, bf16[32,2048]{1,0:T(8,128)(2,1)S(1)}, u32[]{:S(2)}, u32[]{:S(2)}) collective-permute-start(bf16[32,2048]{1,0:T(8,128)(2,1)S(1)} %get-tuple-element.31), channel_id=1, source_target_pairs={{0,1},{1,0},{2,3},{3,2},{4,5},{5,4},{6,7},{7,6},{8,9},{9,8},{10,11... | collective-permute-start | bytes 393224 | tf_op jit(solution)/shard_map/ppermute | solution.py:305
  9.6 0.0 copy-start
  9.6 2.3 %collective-permute-start.1 = (bf16[32,2048]{1,0:T(8,128)(2,1)S(1)}, bf16[32,2048]{1,0:T(8,128)(2,1)S(1)}, u32[]{:S(2)}, u32[]{:S(2)}) collective-permute-start(bf16[32,2048]{1,0:T(8,128)(2,1)S(1)} %get-tuple-element.32), channel_id=1, source_target_pairs={{0,2},{1,3},{2,0},{3,1},{4,6},{5,7},{6,4},{7,5},{8,10},{9,11},{10,... | collective-permute-start | bytes 393224 | tf_op jit(solution)/shard_map/ppermute | solution.py:305
  11.9 0.0 collective-permute-start.2
  11.9 0.0 copy-done
  12.0 1.9 %make_tables.1 = (bf16[512,256]{1,0:T(8,128)(2,1)S(1)}, bf16[512,256]{1,0:T(8,128)(2,1)S(1)}, f32[288,512]{1,0:T(8,128)S(1)}) custom-call(f32[32]{0:T(128)S(1)} %copy-done, f32[512,256]{1,0:T(8,128)} %constant.6.clone.outer_ref, f32[512,256]{1,0:T(8,128)} %constant.7.clone.inner_ref, f32[256,512]{1,0:T(8,128)} %constant.8.clone.turns_ref), custom_call_target="tpu_custom_call" | custom-call | tf_op jit(solution)/shard_map/make_tables/pallas_call | solution.py:149
  13.9 2.2 %all-to-all-done.got_ref = bf16[8,160,256]{2,1,0:T(8,128)(2,1)S(1)} async-done(((bf16[8,160,256]{2,1,0:T(8,128)(2,1)}), bf16[8,160,256]{2,1,0:T(8,128)(2,1)S(1)}, u32[]{:S(2)}, u32[]{:S(2)}) %all-to-all-start) | async-done | bytes 655392 | tf_op jit(solution)/shard_map/all_to_all | solution.py:303
  16.1 2.7 %convolve.1 = bf16[32,32,256]{2,1,0:T(8,128)(2,1)S(1)} custom-call(bf16[8,160,256]{2,1,0:T(8,128)(2,1)S(1)} %all-to-all-done.got_ref, bf16[512,256]{1,0:T(8,128)(2,1)S(1)} %get-tuple-element.27.outer_ref, bf16[512,256]{1,0:T(8,128)(2,1)S(1)} %get-tuple-element.28.inner_ref, f32[288,512]{1,0:T(8,128)S(1)} %get-tuple-element.29.turns_ref), custom_call_target="tpu_custom_call" | custom-call | flops 65536 | bytes 262144 | tf_op jit(solution)/shard_map/convolve/pallas_call | solution.py:234
  18.7 0.0 collective-permute-done.rest_1_
  18.7 0.0 collective-permute-done.1.rest_2_
  18.8 2.4 %collective-permute-done.2.rest_3_ = bf16[32,2048]{1,0:T(8,128)(2,1)S(1)} collective-permute-done((bf16[32,2048]{1,0:T(8,128)(2,1)S(1)}, bf16[32,2048]{1,0:T(8,128)(2,1)S(1)}, u32[]{:S(2)}, u32[]{:S(2)}) %collective-permute-start.2) | collective-permute-done | bytes 131104 | tf_op jit(solution)/shard_map/ppermute | solution.py:305
  21.2 22.5 %all_to_all.10.got_ref = bf16[32,32,256]{2,1,0:T(8,128)(2,1)S(1)} all-to-all(bf16[32,32,256]{2,1,0:T(8,128)(2,1)S(1)} %convolve.1), channel_id=1, replica_groups=mesh['ctx'=8,'ch'=4] {'ctx','ch'}, dimensions={0} | all-to-all | bytes 1048576 | tf_op jit(solution)/shard_map/all_to_all | solution.py:310
  43.7 1.2 %unpack.1 = bf16[128,2048]{1,0:T(8,128)(2,1)} custom-call(bf16[32,32,256]{2,1,0:T(8,128)(2,1)S(1)} %all_to_all.10.got_ref, bf16[32,2048]{1,0:T(8,128)(2,1)S(1)} %get-tuple-element.35.rest_0_, bf16[32,2048]{1,0:T(8,128)(2,1)S(1)} %collective-permute-done.rest_1_, bf16[32,2048]{1,0:T(8,128)(2,1)S(1)} %collective-permute-done.1.rest_2_, ...), custom_call_target="tpu_custom_call" | custom-call | tf_op jit(solution)/shard_map/unpack/pallas_call | solution.py:283
Async XLA Ops:
  3.1 13.0 %all-to-all-start = ((bf16[8,160,256]{2,1,0:T(8,128)(2,1)}), bf16[8,160,256]{2,1,0:T(8,128)(2,1)S(1)}, u32[]{:S(2)}, u32[]{:S(2)}) async-start(bf16[8,160,256]{2,1,0:T(8,128)(2,1)} %get-tuple-element.22), calls=%async_computation | async-start | bytes 1310720 | tf_op jit(solution)/shard_map/all_to_all | solution.py:303
  8.3 10.4 %collective-permute-start = (bf16[32,2048]{1,0:T(8,128)(2,1)S(1)}, bf16[32,2048]{1,0:T(8,128)(2,1)S(1)}, u32[]{:S(2)}, u32[]{:S(2)}) collective-permute-start(bf16[32,2048]{1,0:T(8,128)(2,1)S(1)} %get-tuple-element.31), channel_id=1, source_target_pairs={{0,1},{1,0},{2,3},{3,2},{4,5},{5,4},{6,7},{7,6},{8,9},{9,8},{10,11... | collective-permute-start | bytes 393224 | tf_op jit(solution)/shard_map/ppermute | solution.py:305
  9.6 2.3 %copy-start = (f32[32]{0:T(128)S(1)}, f32[32]{0:T(128)}, u32[]{:S(2)}) copy-start(f32[32]{0:T(128)} %skip_ref) | copy-start | bytes 388
  9.6 9.1 %collective-permute-start.1 = (bf16[32,2048]{1,0:T(8,128)(2,1)S(1)}, bf16[32,2048]{1,0:T(8,128)(2,1)S(1)}, u32[]{:S(2)}, u32[]{:S(2)}) collective-permute-start(bf16[32,2048]{1,0:T(8,128)(2,1)S(1)} %get-tuple-element.32), channel_id=1, source_target_pairs={{0,2},{1,3},{2,0},{3,1},{4,6},{5,7},{6,4},{7,5},{8,10},{9,11},{10,... | collective-permute-start | bytes 393224 | tf_op jit(solution)/shard_map/ppermute | solution.py:305
  11.9 9.2 %collective-permute-start.2 = (bf16[32,2048]{1,0:T(8,128)(2,1)S(1)}, bf16[32,2048]{1,0:T(8,128)(2,1)S(1)}, u32[]{:S(2)}, u32[]{:S(2)}) collective-permute-start(bf16[32,2048]{1,0:T(8,128)(2,1)S(1)} %get-tuple-element.33), channel_id=1, source_target_pairs={{0,3},{1,2},{2,1},{3,0},{4,7},{5,6},{6,5},{7,4},{8,11},{9,10},{10,... | collective-permute-start | bytes 393224 | tf_op jit(solution)/shard_map/ppermute | solution.py:305

commit v8 on v7

--- a/solution.py
+++ b/solution.py
@@ -10,7 +10,6 @@
 
 W = 256
 LANES = 128
-CUTS = 4
 TILE = 16
 CHUNK = 128
 
@@ -45,50 +44,74 @@
 def pick(natural, channel, count, blocks):
     halves = W // LANES
     rows = [natural[pl.ds(h * count + channel, blocks, stride=halves * count), :] for h in range(halves)]
-    return jnp.concatenate(rows, 1).astype(jnp.bfloat16)
+    return jnp.concatenate(rows, 1)
+
+
+def early_blocks(own, near, ch_count):
+    some = near // ch_count // 2
+    return some if own * some % TILE == 0 else 0
 
 
 def pack_kernel(own, blocks, group, ch_count, pre_ref, val_ref, taps_ref, post_ref, out_ref, *rest):
     gate_refs = rest[:ch_count]
-    pre_s, val_s, taps_s, post_s, natural, natural_taps, stage, in_sems, out_sems, gate_sems = rest[ch_count:]
+    pre_s, val_s, taps_s, post_s, natural, natural_taps, natural_gate, stage, in_sems, out_sems, gate_sems = rest[ch_count:]
     parts = out_ref.shape[0]
     channels = own * parts
+    some = min(TILE, channels)
     rows = own * blocks
-    width = blocks * W // CUTS
+    main = rows + blocks
+    early = early_blocks(own, blocks, ch_count)
     loads = []
-    for q in range(CUTS):
-        cols = pl.ds(q * width, width)
-        loads.append(pltpu.make_async_copy(pre_ref.at[:, cols], pre_s.at[:, cols], in_sems.at[q, 0]))
-        loads.append(pltpu.make_async_copy(val_ref.at[:, cols], val_s.at[:, cols], in_sems.at[q, 1]))
-    taps_load = pltpu.make_async_copy(taps_ref, taps_s, in_sems.at[CUTS, 0])
-    gate_load = pltpu.make_async_copy(post_ref, post_s, in_sems.at[CUTS, 1])
+    for g in range(channels // some):
+        here = pl.ds(g * some, some)
+        loads.append(pltpu.make_async_copy(pre_ref.at[here], pre_s.at[here], in_sems.at[g, 0]))
+        loads.append(pltpu.make_async_copy(val_ref.at[here], val_s.at[here], in_sems.at[g, 1]))
+    taps_load = pltpu.make_async_copy(taps_ref, taps_s, in_sems.at[channels // some, 0])
+    gate_load = pltpu.make_async_copy(post_ref, post_s, in_sems.at[channels // some, 1])
     for copy in loads[:2] + [taps_load] + loads[2:] + [gate_load]:
         copy.start()
     groups = taps_s.shape[0]
+    taps_load.wait()
     for j in range(blocks):
-        if j % (blocks // CUTS) == 0:
-            q = j // (blocks // CUTS)
-            loads[2 * q].wait()
-            loads[2 * q + 1].wait()
-        cols = slice(W * j, W * (j + 1))
-        lay(natural, j, pre_s[:, cols].astype(jnp.float32) * val_s[:, cols].astype(jnp.float32))
-        if j == 0:
-            taps_load.wait()
-        lay(natural_taps, j, taps_s[:, cols])
+        lay(natural_taps, j, taps_s[:, W * j : W * (j + 1)])
+    stores = []
+    for g in range(channels // some):
+        loads[2 * g].wait()
+        loads[2 * g + 1].wait()
+        here = slice(g * some, (g + 1) * some)
+        for j in range(blocks):
+            cols = slice(W * j, W * (j + 1))
+            product = pre_s[here, cols].astype(jnp.float32) * val_s[here, cols].astype(jnp.float32)
+            lay(natural.at[g], j, product)
+        for i in range(g * some // own, (g + 1) * some // own):
+            for c in range(own):
+                mine = pick(natural.at[g], own * i + c - g * some, some, blocks)
+                stage[i, blocks * c : blocks * (c + 1), :] = mine.astype(jnp.bfloat16)
+            taps = pick(natural_taps, own * i // group, groups, blocks)
+            stage[i, rows:main, :] = taps.astype(jnp.bfloat16)
+            stores.append(pltpu.make_async_copy(stage.at[i, 0:main], out_ref.at[i, 0:main], out_sems.at[i, 0]))
+            stores[-1].start()
     gate_load.wait()
     me = lax.axis_index("ch")
     piece = blocks * W // ch_count
-    stores = []
     for d in range(ch_count):
-        cols = pl.ds(pl.multiple_of(jnp.bitwise_xor(me, d) * piece, LANES), piece)
+        first = jnp.bitwise_xor(me, d) * piece
+        width = piece
+        if d == ch_count - 1 and early:
+            for j in range(early):
+                cols = pl.ds(pl.multiple_of(first + W * j, LANES), W)
+                lay(natural_gate, j, post_s[:, cols].astype(jnp.float32))
+            first = first + W * early
+            width = piece - W * early
+        cols = pl.ds(pl.multiple_of(first, LANES), width)
         stores.append(pltpu.make_async_copy(post_s.at[:, cols], gate_refs[d], gate_sems.at[d]))
         stores[-1].start()
-    for i in range(parts):
-        for c in range(own):
-            stage[i, blocks * c : blocks * (c + 1), :] = pick(natural, own * i + c, channels, blocks)
-        stage[i, rows : rows + blocks, :] = pick(natural_taps, own * i // group, groups, blocks)
-        stores.append(pltpu.make_async_copy(stage.at[i], out_ref.at[i], out_sems.at[i]))
-        stores[-1].start()
+    if early:
+        for i in range(parts):
+            gate = [pick(natural_gate, own * i + c, channels, early) for c in range(own)]
+            stage[i, main:, :] = jnp.concatenate(gate, 0).astype(jnp.bfloat16)
+            stores.append(pltpu.make_async_copy(stage.at[i, main:], out_ref.at[i, main:], out_sems.at[i, 1]))
+            stores[-1].start()
     for copy in stores:
         copy.wait()
 
@@ -98,13 +121,17 @@
     own = channels // parts
     group = channels // taps.shape[0]
     blocks = block // W
-    local = (own + 1) * blocks
+    early = early_blocks(own, blocks, ch_count)
+    local = (own + 1) * blocks + own * early
     halves = W // LANES
+    some = min(TILE, channels)
+    piece = block // ch_count
+    widths = [piece] * (ch_count - 1) + [piece - W * early]
     args = [pltpu.with_memory_space_constraint(arg, pltpu.HBM) for arg in (pre_gate, value, taps, post_gate)]
     return pl.pallas_call(
         functools.partial(pack_kernel, own, blocks, group, ch_count),
         out_shape=[jax.ShapeDtypeStruct((parts, local, W), jnp.bfloat16)]
-        + [jax.ShapeDtypeStruct((channels, block // ch_count), jnp.bfloat16)] * ch_count,
+        + [jax.ShapeDtypeStruct((channels, width), jnp.bfloat16) for width in widths],
         in_specs=[in_hbm()] * 4,
         out_specs=[in_hbm()] * (1 + ch_count),
         scratch_shapes=[
@@ -112,11 +139,12 @@
             pltpu.VMEM(value.shape, jnp.bfloat16),
             pltpu.VMEM(taps.shape, jnp.float32),
             pltpu.VMEM(post_gate.shape, jnp.bfloat16),
-            pltpu.VMEM((blocks * halves * channels, LANES), jnp.float32),
+            pltpu.VMEM((channels // some, blocks * halves * some, LANES), jnp.float32),
             pltpu.VMEM((blocks * halves * taps.shape[0], LANES), jnp.float32),
+            pltpu.VMEM((max(early, 1) * halves * channels, LANES), jnp.float32),
             pltpu.VMEM((parts, local, W), jnp.bfloat16),
-            pltpu.SemaphoreType.DMA((CUTS + 1, 2)),
-            pltpu.SemaphoreType.DMA((parts,)),
+            pltpu.SemaphoreType.DMA((channels // some + 1, 2)),
+            pltpu.SemaphoreType.DMA((parts, 2)),
             pltpu.SemaphoreType.DMA((ch_count,)),
         ],
         compiler_params=pltpu.CompilerParams(vmem_limit_bytes=16 * 2**20),
@@ -165,9 +193,8 @@
     )(skip, *args)
 
 
-def conv_kernel(own, got_ref, outer_ref, inner_ref, turns_ref, out_ref, x_all, r_all, z_all, ahead, rear):
-    parts, local, _ = got_ref.shape
-    near = local // (own + 1)
+def conv_kernel(own, near, ch_count, got_ref, outer_ref, inner_ref, turns_ref, out_ref, x_all, r_all, z_all, ahead, rear):
+    parts = got_ref.shape[0]
     blocks = parts * near
     length = blocks * W
     for p in range(parts):
@@ -219,20 +246,29 @@
         cols = slice(W * c, W * (c + 1))
         z_all[c] = conv[:, cols] + turns_ref[blocks + 8 * c : blocks + 8 * c + 1, 0:W] * x_all[:, cols].astype(jnp.float32)
     some = out_ref.shape[1] // own
-    ch_count = near // some
+    early = early_blocks(own, near, ch_count)
+    far = jnp.bitwise_xor(lax.axis_index("ch"), ch_count - 1)
     for k in range(parts):
+        factors = []
+        if early:
+            gate = got_ref[k, (own + 1) * near :, :].astype(jnp.float32)
+            for c in range(own):
+                rest = jnp.ones((some - early, W), jnp.float32)
+                factors.append(jnp.concatenate([gate[early * c : early * (c + 1), :], rest], 0))
         for m in range(ch_count):
             first = k * near + m * some
             rows = [z_all[c, first : first + some, :] for c in range(own)]
+            if early:
+                rows = [jnp.where(far == m, factors[c], 1.0) * rows[c] for c in range(own)]
             out_ref[k * ch_count + m] = jnp.concatenate(rows, 0).astype(jnp.bfloat16)
 
 
-def convolve(got, tables, own, ch_count):
-    parts, local, _ = got.shape
-    blocks = parts * (local // (own + 1))
+def convolve(got, tables, own, near, ch_count):
+    parts = got.shape[0]
+    blocks = parts * near
     owners = parts * ch_count
     return pl.pallas_call(
-        functools.partial(conv_kernel, own),
+        functools.partial(conv_kernel, own, near, ch_count),
         out_shape=jax.ShapeDtypeStruct((owners, own * blocks // owners, W), jnp.bfloat16),
         in_specs=[whole_vmem()] * (1 + len(tables)),
         out_specs=whole_vmem(),
@@ -256,8 +292,11 @@
     me = lax.axis_index("ch")
     channels = gate_refs[0].shape[0]
     for d, gate_ref in enumerate(gate_refs):
-        first = pl.multiple_of(jnp.bitwise_xor(me, d) * channels, TILE)
-        gate_s[pl.ds(first, channels), :] = gate_ref[...]
+        here = pl.ds(pl.multiple_of(jnp.bitwise_xor(me, d) * channels, TILE), channels)
+        early = gate_s.shape[1] - gate_ref.shape[1]
+        if early:
+            gate_s[here, 0:early] = jnp.ones((channels, early), jnp.bfloat16)
+        gate_s[here, early:] = gate_ref[...]
     ch_count = len(gate_refs)
     for p in range(sources):
         part = got_ref[p].astype(jnp.float32)
@@ -305,7 +344,7 @@
         gates[d] = lax.ppermute(gates[d], "ch", [(i, i ^ d) for i in range(ch_count)])
     tables, skip, _ = lax.optimization_barrier((dft_tables(blocks), skip, send))
     tables = make_tables(skip, *tables, own)
-    mixed = convolve(got, tables, own, ch_count)
+    mixed = convolve(got, tables, own, blocks // ctx_count, ch_count)
     mixed, gates = lax.optimization_barrier((mixed, gates))
     mixed = lax.all_to_all(mixed, ("ctx", "ch"), split_axis=0, concat_axis=0, tiled=True)
     return unpack(mixed, gates, own)

time: 45.1 us -> 42.9 us (0.951)
  waiting for transfers between devices: 4.58 us -> 3.19 us
  blocking collectives: 22.5 us -> 22 us
    ppermute x3, waiting for transfers between devices: 2.4 us -> 0.33 us  [body(): lax.ppermute(gates[d], 'ch', [(i, i ^ d) for i in range(ch_count)])]
    all_to_all x1, waiting for transfers between devices: 2.17 us -> 2.86 us  [body(): got = lax.all_to_all(send, 'ctx', split_axis=0, concat_axis=0, tiled=True)]
    all_to_all x1, blocking collectives: 22.5 us -> 22 us  [body(): lax.all_to_all(mixed, ('ctx', 'ch'), split_axis=0, concat_axis=0, tiled=T...]
  transfers between devices with their start and end apart: 4 -> 4, of which waited for: 2 -> 2; matrix products, arithmetic and copies ran while one was open for 0% -> 0% of each run, Pallas kernels for 10% -> 11%
where the time goes in v8:
time: 42.9 us; the launch traced here: 42.7 us
  blocking collectives  22 us (51%)
  starting transfers between devices  8.84 us (21%)
  Pallas kernels  8.58 us (20%)
  waiting for transfers between devices  3.19 us (7%)
    all_to_all x1, blocking collectives, body(): lax.all_to_all(mixed, ('ctx', 'ch'), split_axis=0, concat_axis=0, tiled=T...  22 us
    all_to_all x1, starting transfers between devices, body(): got = lax.all_to_all(send, 'ctx', split_axis=0, concat_axis=0, tiled=True)  5.24 us
    ppermute x3, starting transfers between devices, body(): lax.ppermute(gates[d], 'ch', [(i, i ^ d) for i in range(ch_count)])  3.61 us
    all_to_all x1, waiting for transfers between devices, body(): got = lax.all_to_all(send, 'ctx', split_axis=0, concat_axis=0, tiled=True)  2.86 us
    pallas_call x1, Pallas kernels, pack(): pl.pallas_call(functools.partial(pack_kernel, own, blocks, group, ch_coun...  2.79 us
    pallas_call x1, Pallas kernels, convolve(): pl.pallas_call(functools.partial(conv_kernel, own, near, ch_count), out_s...  2.68 us
    pallas_call x1, Pallas kernels, make_tables(): pl.pallas_call(functools.partial(tables_kernel, own), out_shape=[jax.Shap...  1.92 us
    pallas_call x1, Pallas kernels, unpack(): pl.pallas_call(functools.partial(unpack_kernel, own), out_shape=jax.Shape...  1.19 us
  transfers between devices with their start and end apart: 4, of which 2 were waited for; matrix products, arithmetic and copies ran while one was open for 0% of the time, Pallas kernels for 11%

profile of v8, /device:TPU:1, one launch (start us, length us, event | category | flops | bytes accessed | tf_op | source)
XLA Modules:
  0.0 42.7 jit_solution(10982251569187923909)
XLA Ops:
  0.0 2.8 %pack.1 = (bf16[8,176,256]{2,1,0:T(8,128)(2,1)}, bf16[32,2048]{1,0:T(8,128)(2,1)S(1)}, bf16[32,2048]{1,0:T(8,128)(2,1)S(1)}, bf16[32,2048]{1,0:T(8,128)(2,1)S(1)}, bf16[32,1024]{1,0:T(8,128)(2,1)S(1)}) custom-call(bf16[32,8192]{1,0:T(8,128)(2,1)} %pre_ref.1, bf16[32,8192]{1,0:T(8,128)(2,1)} %val_ref.1, f32[2,8192]{1,0:T(2,128)} %taps_ref.1, ...), custom_call_target="tpu_custom_call" | custom-call | tf_op jit(solution)/shard_map/pack/pallas_call | solution.py:131
  2.8 5.2 %all-to-all-start = ((bf16[8,176,256]{2,1,0:T(8,128)(2,1)}), bf16[8,176,256]{2,1,0:T(8,128)(2,1)S(1)}, u32[]{:S(2)}, u32[]{:S(2)}) async-start(bf16[8,176,256]{2,1,0:T(8,128)(2,1)} %get-tuple-element.22), calls=%async_computation | async-start | bytes 1441792 | tf_op jit(solution)/shard_map/all_to_all | solution.py:342
  8.0 1.3 %collective-permute-start = (bf16[32,2048]{1,0:T(8,128)(2,1)S(1)}, bf16[32,2048]{1,0:T(8,128)(2,1)S(1)}, u32[]{:S(2)}, u32[]{:S(2)}) collective-permute-start(bf16[32,2048]{1,0:T(8,128)(2,1)S(1)} %get-tuple-element.31), channel_id=1, source_target_pairs={{0,1},{1,0},{2,3},{3,2},{4,5},{5,4},{6,7},{7,6},{8,9},{9,8},{10,11... | collective-permute-start | bytes 393224 | tf_op jit(solution)/shard_map/ppermute | solution.py:344
  9.3 0.0 copy-start
  9.3 2.3 %collective-permute-start.1 = (bf16[32,2048]{1,0:T(8,128)(2,1)S(1)}, bf16[32,2048]{1,0:T(8,128)(2,1)S(1)}, u32[]{:S(2)}, u32[]{:S(2)}) collective-permute-start(bf16[32,2048]{1,0:T(8,128)(2,1)S(1)} %get-tuple-element.32), channel_id=1, source_target_pairs={{0,2},{1,3},{2,0},{3,1},{4,6},{5,7},{6,4},{7,5},{8,10},{9,11},{10,... | collective-permute-start | bytes 393224 | tf_op jit(solution)/shard_map/ppermute | solution.py:344
  11.6 0.0 collective-permute-start.2
  11.6 0.0 copy-done
  11.7 1.9 %make_tables.1 = (bf16[512,256]{1,0:T(8,128)(2,1)S(1)}, bf16[512,256]{1,0:T(8,128)(2,1)S(1)}, f32[288,512]{1,0:T(8,128)S(1)}) custom-call(f32[32]{0:T(128)S(1)} %copy-done, f32[512,256]{1,0:T(8,128)} %constant.6.clone.outer_ref, f32[512,256]{1,0:T(8,128)} %constant.7.clone.inner_ref, f32[256,512]{1,0:T(8,128)} %constant.8.clone.turns_ref), custom_call_target="tpu_custom_call" | custom-call | tf_op jit(solution)/shard_map/make_tables/pallas_call | solution.py:177
  13.6 2.9 %all-to-all-done.got_ref = bf16[8,176,256]{2,1,0:T(8,128)(2,1)S(1)} async-done(((bf16[8,176,256]{2,1,0:T(8,128)(2,1)}), bf16[8,176,256]{2,1,0:T(8,128)(2,1)S(1)}, u32[]{:S(2)}, u32[]{:S(2)}) %all-to-all-start) | async-done | bytes 720928 | tf_op jit(solution)/shard_map/all_to_all | solution.py:342
  16.4 2.7 %convolve.1 = bf16[32,32,256]{2,1,0:T(8,128)(2,1)S(1)} custom-call(bf16[8,176,256]{2,1,0:T(8,128)(2,1)S(1)} %all-to-all-done.got_ref, bf16[512,256]{1,0:T(8,128)(2,1)S(1)} %get-tuple-element.27.outer_ref, bf16[512,256]{1,0:T(8,128)(2,1)S(1)} %get-tuple-element.28.inner_ref, f32[288,512]{1,0:T(8,128)S(1)} %get-tuple-element.29.turns_ref), custom_call_target="tpu_custom_call" | custom-call | flops 65536 | bytes 262144 | tf_op jit(solution)/shard_map/convolve/pallas_call | solution.py:270
  19.1 0.3 collective-permute-done.2.rest_3_
  19.5 0.0 collective-permute-done.rest_1_
  19.5 0.0 collective-permute-done.1.rest_2_
  19.5 22.0 %all_to_all.10.got_ref = bf16[32,32,256]{2,1,0:T(8,128)(2,1)S(1)} all-to-all(bf16[32,32,256]{2,1,0:T(8,128)(2,1)S(1)} %convolve.1), channel_id=1, replica_groups=mesh['ctx'=8,'ch'=4] {'ctx','ch'}, dimensions={0} | all-to-all | bytes 1048576 | tf_op jit(solution)/shard_map/all_to_all | solution.py:349
  41.5 1.2 %unpack.1 = bf16[128,2048]{1,0:T(8,128)(2,1)} custom-call(bf16[32,32,256]{2,1,0:T(8,128)(2,1)S(1)} %all_to_all.10.got_ref, bf16[32,2048]{1,0:T(8,128)(2,1)S(1)} %get-tuple-element.35.rest_0_, bf16[32,2048]{1,0:T(8,128)(2,1)S(1)} %collective-permute-done.rest_1_, bf16[32,2048]{1,0:T(8,128)(2,1)S(1)} %collective-permute-done.1.rest_2_, ...), custom_call_target="tpu_custom_call" | custom-call | tf_op jit(solution)/shard_map/unpack/pallas_call | solution.py:322
Async XLA Ops:
  2.8 13.6 %all-to-all-start = ((bf16[8,176,256]{2,1,0:T(8,128)(2,1)}), bf16[8,176,256]{2,1,0:T(8,128)(2,1)S(1)}, u32[]{:S(2)}, u32[]{:S(2)}) async-start(bf16[8,176,256]{2,1,0:T(8,128)(2,1)} %get-tuple-element.22), calls=%async_computation | async-start | bytes 1441792 | tf_op jit(solution)/shard_map/all_to_all | solution.py:342
  8.0 11.4 %collective-permute-start = (bf16[32,2048]{1,0:T(8,128)(2,1)S(1)}, bf16[32,2048]{1,0:T(8,128)(2,1)S(1)}, u32[]{:S(2)}, u32[]{:S(2)}) collective-permute-start(bf16[32,2048]{1,0:T(8,128)(2,1)S(1)} %get-tuple-element.31), channel_id=1, source_target_pairs={{0,1},{1,0},{2,3},{3,2},{4,5},{5,4},{6,7},{7,6},{8,9},{9,8},{10,11... | collective-permute-start | bytes 393224 | tf_op jit(solution)/shard_map/ppermute | solution.py:344
  9.3 2.3 %copy-start = (f32[32]{0:T(128)S(1)}, f32[32]{0:T(128)}, u32[]{:S(2)}) copy-start(f32[32]{0:T(128)} %skip_ref) | copy-start | bytes 388
  9.3 10.1 %collective-permute-start.1 = (bf16[32,2048]{1,0:T(8,128)(2,1)S(1)}, bf16[32,2048]{1,0:T(8,128)(2,1)S(1)}, u32[]{:S(2)}, u32[]{:S(2)}) collective-permute-start(bf16[32,2048]{1,0:T(8,128)(2,1)S(1)} %get-tuple-element.32), channel_id=1, source_target_pairs={{0,2},{1,3},{2,0},{3,1},{4,6},{5,7},{6,4},{7,5},{8,10},{9,11},{10,... | collective-permute-start | bytes 393224 | tf_op jit(solution)/shard_map/ppermute | solution.py:344
  11.6 7.8 %collective-permute-start.2 = (bf16[32,1024]{1,0:T(8,128)(2,1)S(1)}, bf16[32,1024]{1,0:T(8,128)(2,1)S(1)}, u32[]{:S(2)}, u32[]{:S(2)}) collective-permute-start(bf16[32,1024]{1,0:T(8,128)(2,1)S(1)} %get-tuple-element.33), channel_id=1, source_target_pairs={{0,3},{1,2},{2,1},{3,0},{4,7},{5,6},{6,5},{7,4},{8,11},{9,10},{10,... | collective-permute-start | bytes 196616 | tf_op jit(solution)/shard_map/ppermute | solution.py:344

commit v9 on v8

--- a/solution.py
+++ b/solution.py
@@ -47,20 +47,13 @@
     return jnp.concatenate(rows, 1)
 
 
-def early_blocks(own, near, ch_count):
-    some = near // ch_count // 2
-    return some if own * some % TILE == 0 else 0
-
-
-def pack_kernel(own, blocks, group, ch_count, pre_ref, val_ref, taps_ref, post_ref, out_ref, *rest):
-    gate_refs = rest[:ch_count]
-    pre_s, val_s, taps_s, post_s, natural, natural_taps, natural_gate, stage, in_sems, out_sems, gate_sems = rest[ch_count:]
-    parts = out_ref.shape[0]
+def pack_kernel(own, blocks, group, ch_count, parts, pre_ref, val_ref, taps_ref, post_ref, *rest):
+    out_refs, gate_refs = rest[:parts], rest[parts : parts + ch_count // 2]
+    pre_s, val_s, taps_s, post_s, natural, natural_taps, natural_gate, stage, in_sems = rest[parts + ch_count // 2 :]
     channels = own * parts
     some = min(TILE, channels)
     rows = own * blocks
     main = rows + blocks
-    early = early_blocks(own, blocks, ch_count)
     loads = []
     for g in range(channels // some):
         here = pl.ds(g * some, some)
@@ -74,7 +67,6 @@
     taps_load.wait()
     for j in range(blocks):
         lay(natural_taps, j, taps_s[:, W * j : W * (j + 1)])
-    stores = []
     for g in range(channels // some):
         loads[2 * g].wait()
         loads[2 * g + 1].wait()
@@ -89,31 +81,24 @@
                 stage[i, blocks * c : blocks * (c + 1), :] = mine.astype(jnp.bfloat16)
             taps = pick(natural_taps, own * i // group, groups, blocks)
             stage[i, rows:main, :] = taps.astype(jnp.bfloat16)
-            stores.append(pltpu.make_async_copy(stage.at[i, 0:main], out_ref.at[i, 0:main], out_sems.at[i, 0]))
-            stores[-1].start()
     gate_load.wait()
-    me = lax.axis_index("ch")
-    piece = blocks * W // ch_count
+    place = lax.axis_index("ch")
+    piece = blocks // ch_count
     for d in range(ch_count):
-        first = jnp.bitwise_xor(me, d) * piece
-        width = piece
-        if d == ch_count - 1 and early:
-            for j in range(early):
+        first = jnp.bitwise_xor(place, d) * (piece * W)
+        if d < ch_count // 2:
+            gate_refs[d][...] = post_s[:, pl.ds(pl.multiple_of(first, LANES), piece * W)]
+        else:
+            for j in range(piece):
                 cols = pl.ds(pl.multiple_of(first + W * j, LANES), W)
-                lay(natural_gate, j, post_s[:, cols].astype(jnp.float32))
-            first = first + W * early
-            width = piece - W * early
-        cols = pl.ds(pl.multiple_of(first, LANES), width)
-        stores.append(pltpu.make_async_copy(post_s.at[:, cols], gate_refs[d], gate_sems.at[d]))
-        stores[-1].start()
-    if early:
-        for i in range(parts):
-            gate = [pick(natural_gate, own * i + c, channels, early) for c in range(own)]
-            stage[i, main:, :] = jnp.concatenate(gate, 0).astype(jnp.bfloat16)
-            stores.append(pltpu.make_async_copy(stage.at[i, main:], out_ref.at[i, main:], out_sems.at[i, 1]))
-            stores[-1].start()
-    for copy in stores:
-        copy.wait()
+                lay(natural_gate, (d - ch_count // 2) * piece + j, post_s[:, cols].astype(jnp.float32))
+    early = piece * (ch_count - ch_count // 2)
+    for i in range(parts):
+        gate = [pick(natural_gate, own * i + c, channels, early) for c in range(own)]
+        stage[i, main:, :] = jnp.concatenate(gate, 0).astype(jnp.bfloat16)
+    me = lax.axis_index("ctx")
+    for d in range(parts):
+        out_refs[d][...] = stage[jnp.bitwise_xor(me, d)]
 
 
 def pack(pre_gate, value, post_gate, taps, parts, ch_count):
@@ -121,19 +106,18 @@
     own = channels // parts
     group = channels // taps.shape[0]
     blocks = block // W
-    early = early_blocks(own, blocks, ch_count)
+    piece = blocks // ch_count
+    early = piece * (ch_count - ch_count // 2)
     local = (own + 1) * blocks + own * early
     halves = W // LANES
     some = min(TILE, channels)
-    piece = block // ch_count
-    widths = [piece] * (ch_count - 1) + [piece - W * early]
     args = [pltpu.with_memory_space_constraint(arg, pltpu.HBM) for arg in (pre_gate, value, taps, post_gate)]
-    return pl.pallas_call(
-        functools.partial(pack_kernel, own, blocks, group, ch_count),
-        out_shape=[jax.ShapeDtypeStruct((parts, local, W), jnp.bfloat16)]
-        + [jax.ShapeDtypeStruct((channels, width), jnp.bfloat16) for width in widths],
+    out = pl.pallas_call(
+        functools.partial(pack_kernel, own, blocks, group, ch_count, parts),
+        out_shape=[jax.ShapeDtypeStruct((local, W), jnp.bfloat16)] * parts
+        + [jax.ShapeDtypeStruct((channels, piece * W), jnp.bfloat16)] * (ch_count // 2),
         in_specs=[in_hbm()] * 4,
-        out_specs=[in_hbm()] * (1 + ch_count),
+        out_specs=[whole_vmem()] * (parts + ch_count // 2),
         scratch_shapes=[
             pltpu.VMEM(pre_gate.shape, jnp.bfloat16),
             pltpu.VMEM(value.shape, jnp.bfloat16),
@@ -141,15 +125,18 @@
             pltpu.VMEM(post_gate.shape, jnp.bfloat16),
             pltpu.VMEM((channels // some, blocks * halves * some, LANES), jnp.float32),
             pltpu.VMEM((blocks * halves * taps.shape[0], LANES), jnp.float32),
-            pltpu.VMEM((max(early, 1) * halves * channels, LANES), jnp.float32),
+            pltpu.VMEM((early * halves * channels, LANES), jnp.float32),
             pltpu.VMEM((parts, local, W), jnp.bfloat16),
             pltpu.SemaphoreType.DMA((channels // some + 1, 2)),
-            pltpu.SemaphoreType.DMA((parts, 2)),
-            pltpu.SemaphoreType.DMA((ch_count,)),
         ],
         compiler_params=pltpu.CompilerParams(vmem_limit_bytes=16 * 2**20),
         name="pack",
     )(*args)
+    return list(out[:parts]), list(out[parts:])
+
+
+def swap(piece, axis, count, d):
+    return lax.ppermute(piece, axis, [(i, i ^ d) for i in range(count)])
 
 
 def tables_kernel(own, skip_ref, outer_ref, inner_ref, turns_ref, outer_out, inner_out, turns_out, outer_s, inner_s, sems):
@@ -193,13 +180,16 @@
     )(skip, *args)
 
 
-def conv_kernel(own, near, ch_count, got_ref, outer_ref, inner_ref, turns_ref, out_ref, x_all, r_all, z_all, ahead, rear):
-    parts = got_ref.shape[0]
+def conv_kernel(own, near, ch_count, parts, *rest):
+    got_refs = rest[:parts]
+    outer_ref, inner_ref, turns_ref, out_ref, x_all, r_all, z_all, ahead, rear = rest[parts:]
     blocks = parts * near
     length = blocks * W
-    for p in range(parts):
+    me = lax.axis_index("ctx")
+    for d in range(parts):
+        here = pl.ds(pl.multiple_of(jnp.bitwise_xor(me, d) * near, TILE), near)
         for c in range(own + 1):
-            x_all[p * near : (p + 1) * near, W * c : W * (c + 1)] = got_ref[p, c * near : (c + 1) * near, :]
+            x_all[here, W * c : W * (c + 1)] = got_refs[d][c * near : (c + 1) * near, :]
 
     near_cos, near_sin = inner_ref[0:W, :], inner_ref[W:, :]
     for table, sign in ((ahead, -1), (rear, 1)):
@@ -246,31 +236,30 @@
         cols = slice(W * c, W * (c + 1))
         z_all[c] = conv[:, cols] + turns_ref[blocks + 8 * c : blocks + 8 * c + 1, 0:W] * x_all[:, cols].astype(jnp.float32)
     some = out_ref.shape[1] // own
-    early = early_blocks(own, near, ch_count)
-    far = jnp.bitwise_xor(lax.axis_index("ch"), ch_count - 1)
-    for k in range(parts):
-        factors = []
-        if early:
-            gate = got_ref[k, (own + 1) * near :, :].astype(jnp.float32)
-            for c in range(own):
-                rest = jnp.ones((some - early, W), jnp.float32)
-                factors.append(jnp.concatenate([gate[early * c : early * (c + 1), :], rest], 0))
+    early = some * (ch_count - ch_count // 2)
+    place = lax.axis_index("ch")
+    for d in range(parts):
+        k = jnp.bitwise_xor(me, d)
+        gate = got_refs[d][(own + 1) * near :, :].astype(jnp.float32)
+        mine = [z_all[c, pl.ds(pl.multiple_of(k * near, TILE), near), :] for c in range(own)]
         for m in range(ch_count):
-            first = k * near + m * some
-            rows = [z_all[c, first : first + some, :] for c in range(own)]
-            if early:
-                rows = [jnp.where(far == m, factors[c], 1.0) * rows[c] for c in range(own)]
+            rows = [part[m * some : (m + 1) * some, :] for part in mine]
+            for e in range(ch_count // 2, ch_count):
+                at = (e - ch_count // 2) * some
+                for c in range(own):
+                    factor = jnp.where(jnp.bitwise_xor(place, e) == m, gate[c * early + at : c * early + at + some, :], 1.0)
+                    rows[c] = rows[c] * factor
             out_ref[k * ch_count + m] = jnp.concatenate(rows, 0).astype(jnp.bfloat16)
 
 
 def convolve(got, tables, own, near, ch_count):
-    parts = got.shape[0]
+    parts = len(got)
     blocks = parts * near
     owners = parts * ch_count
     return pl.pallas_call(
-        functools.partial(conv_kernel, own, near, ch_count),
+        functools.partial(conv_kernel, own, near, ch_count, parts),
         out_shape=jax.ShapeDtypeStruct((owners, own * blocks // owners, W), jnp.bfloat16),
-        in_specs=[whole_vmem()] * (1 + len(tables)),
+        in_specs=[whole_vmem()] * (parts + len(tables)),
         out_specs=whole_vmem(),
         scratch_shapes=[
             pltpu.VMEM((blocks, W * (own + 1)), jnp.bfloat16),
@@ -282,22 +271,19 @@
         compiler_params=pltpu.CompilerParams(vmem_limit_bytes=32 * 2**20),
         cost_estimate=pl.CostEstimate(flops=blocks * W, bytes_accessed=4 * blocks * W, transcendentals=0),
         name="convolve",
-    )(got, *tables)
+    )(*got, *tables)
 
 
 def unpack_kernel(own, got_ref, *rest):
     gate_refs, (out_ref, flat, gate_s) = rest[:-3], rest[-3:]
     sources, rows, _ = got_ref.shape
     some = rows // own
-    me = lax.axis_index("ch")
-    channels = gate_refs[0].shape[0]
-    for d, gate_ref in enumerate(gate_refs):
-        here = pl.ds(pl.multiple_of(jnp.bitwise_xor(me, d) * channels, TILE), channels)
-        early = gate_s.shape[1] - gate_ref.shape[1]
-        if early:
-            gate_s[here, 0:early] = jnp.ones((channels, early), jnp.bfloat16)
-        gate_s[here, early:] = gate_ref[...]
-    ch_count = len(gate_refs)
+    place = lax.axis_index("ch")
+    channels, width = gate_refs[0].shape
+    ch_count = out_ref.shape[0] // channels
+    for d in range(ch_count):
+        here = pl.ds(pl.multiple_of(jnp.bitwise_xor(place, d) * channels, TILE), channels)
+        gate_s[here, :] = gate_refs[d][...] if d < len(gate_refs) else jnp.ones((channels, width), jnp.bfloat16)
     for p in range(sources):
         part = got_ref[p].astype(jnp.float32)
         first = (p % ch_count * (sources // ch_count) + p // ch_count) * rows
@@ -311,13 +297,14 @@
             out_ref[:, cols] = (part * gate_s[:, cols].astype(jnp.float32)).astype(jnp.bfloat16)
 
 
-def unpack(got, gates, own):
+def unpack(got, gates, own, ch_count):
     sources, rows, _ = got.shape
     shape = (sources * own, rows // own * W)
     if rows % TILE:
-        order = jnp.bitwise_xor(lax.axis_index("ch"), jnp.arange(len(gates)))
-        gate = jnp.stack(gates)[order].reshape(shape)
-        got = got.reshape(-1, len(gates), rows, W).swapaxes(0, 1)
+        ones = [jnp.ones_like(gates[0])] * (ch_count - len(gates))
+        order = jnp.bitwise_xor(lax.axis_index("ch"), jnp.arange(ch_count))
+        gate = jnp.stack(gates + ones)[order].reshape(shape)
+        got = got.reshape(-1, ch_count, rows, W).swapaxes(0, 1)
         return (got.reshape(shape).astype(jnp.float32) * gate.astype(jnp.float32)).astype(jnp.bfloat16)
     return pl.pallas_call(
         functools.partial(unpack_kernel, own),
@@ -337,17 +324,18 @@
     ctx_count = lax.axis_size("ctx")
     ch_count = lax.axis_size("ch")
     own = value.shape[0] // ctx_count
-    blocks = value.shape[1] // W * ctx_count
-    send, *gates = pack(pre_gate, value, post_gate, filter_taps, ctx_count, ch_count)
-    got = lax.all_to_all(send, "ctx", split_axis=0, concat_axis=0, tiled=True)
-    for d in reversed(range(1, ch_count)):
-        gates[d] = lax.ppermute(gates[d], "ch", [(i, i ^ d) for i in range(ch_count)])
-    tables, skip, _ = lax.optimization_barrier((dft_tables(blocks), skip, send))
-    tables = make_tables(skip, *tables, own)
-    mixed = convolve(got, tables, own, blocks // ctx_count, ch_count)
+    near = value.shape[1] // W
+    got, gates = pack(pre_gate, value, post_gate, filter_taps, ctx_count, ch_count)
+    tables, skip, _ = lax.optimization_barrier((dft_tables(near * ctx_count), skip, got[0]))
+    for d in range(1, ctx_count):
+        got[d] = swap(got[d], "ctx", ctx_count, d)
+    for d in range(1, ch_count // 2):
+        gates[d] = swap(gates[d], "ch", ch_count, d)
+    tables = list(make_tables(skip, *tables, own))
+    mixed = convolve(got, tables, own, near, ch_count)
     mixed, gates = lax.optimization_barrier((mixed, gates))
     mixed = lax.all_to_all(mixed, ("ctx", "ch"), split_axis=0, concat_axis=0, tiled=True)
-    return unpack(mixed, gates, own)
+    return unpack(mixed, gates, own, ch_count)
 
 
 def solution(mesh):

time: 42.9 us -> 43.1 us (level)
  starting transfers between devices: 8.84 us -> 11.1 us
  blocking collectives: 22 us -> 19.8 us
  waiting for transfers between devices: 3.19 us -> 3.8 us
    ppermute x3 -> x8, starting transfers between devices: 3.61 us -> 11.1 us  [swap(): return lax.ppermute(piece, axis, [(i, i ^ d) for i in range(count)])]
    all_to_all x1 -> x0, starting transfers between devices: 5.24 us -> none  [body(): got = lax.all_to_all(send, 'ctx', split_axis=0, concat_axis=0, tiled=True)]
    ppermute x3 -> x8, waiting for transfers between devices: 0.33 us -> 3.8 us  [swap(): return lax.ppermute(piece, axis, [(i, i ^ d) for i in range(count)])]
    all_to_all x1 -> x0, waiting for transfers between devices: 2.86 us -> none  [body(): got = lax.all_to_all(send, 'ctx', split_axis=0, concat_axis=0, tiled=True)]
    all_to_all x1, blocking collectives: 22 us -> 19.8 us  [body(): lax.all_to_all(mixed, ('ctx', 'ch'), split_axis=0, concat_axis=0, tiled=T...]
    pallas_call x1, Pallas kernels: 2.79 us -> 2.18 us  [pack(): pl.pallas_call(functools.partial(pack_kernel, own, blocks, group, ch_coun...]
  transfers between devices with their start and end apart: 4 -> 8, of which waited for: 2 -> 2; matrix products, arithmetic and copies ran while one was open for 0% -> 0% of each run, Pallas kernels for 11% -> 11%
where the time goes in v9:
time: 43.1 us; the launch traced here: 42.9 us
  blocking collectives  19.8 us (46%)
  starting transfers between devices  11.1 us (26%)
  Pallas kernels  8.17 us (19%)
  waiting for transfers between devices  3.8 us (9%)
    all_to_all x1, blocking collectives, body(): lax.all_to_all(mixed, ('ctx', 'ch'), split_axis=0, concat_axis=0, tiled=T...  19.8 us
    ppermute x8, starting transfers between devices, swap(): return lax.ppermute(piece, axis, [(i, i ^ d) for i in range(count)])  11.1 us
    ppermute x8, waiting for transfers between devices, swap(): return lax.ppermute(piece, axis, [(i, i ^ d) for i in range(count)])  3.8 us
    pallas_call x1, Pallas kernels, convolve(): pl.pallas_call(functools.partial(conv_kernel, own, near, ch_count, parts)...  2.88 us
    pallas_call x1, Pallas kernels, pack(): pl.pallas_call(functools.partial(pack_kernel, own, blocks, group, ch_coun...  2.18 us
    pallas_call x1, Pallas kernels, make_tables(): pl.pallas_call(functools.partial(tables_kernel, own), out_shape=[jax.Shap...  1.92 us
    pallas_call x1, Pallas kernels, unpack(): pl.pallas_call(functools.partial(unpack_kernel, own), out_shape=jax.Shape...  1.19 us
  transfers between devices with their start and end apart: 8, of which 2 were waited for; matrix products, arithmetic and copies ran while one was open for 0% of the time, Pallas kernels for 11%

profile of v9, /device:TPU:1, one launch (start us, length us, event | category | flops | bytes accessed | tf_op | source)
XLA Modules:
  0.0 42.9 jit_solution(16004904792869126618)
XLA Ops:
  0.0 2.2 %pack.1 = (bf16[224,256]{1,0:T(8,128)(2,1)S(1)}, bf16[224,256]{1,0:T(8,128)(2,1)S(1)}, bf16[224,256]{1,0:T(8,128)(2,1)S(1)}, bf16[224,256]{1,0:T(8,128)(2,1)S(1)...) custom-call(bf16[32,8192]{1,0:T(8,128)(2,1)} %pre_ref.1, ...), custom_call_target="tpu_custom_call" | custom-call | tf_op jit(solution)/shard_map/pack/pallas_call | solution.py:115
  2.2 0.1 collective-permute-start
  2.3 2.7 %collective-permute-start.1 = (bf16[224,256]{1,0:T(8,128)(2,1)S(1)}, bf16[224,256]{1,0:T(8,128)(2,1)S(1)}, u32[]{:S(2)}, u32[]{:S(2)}) collective-permute-start(bf16[224,256]{1,0:T(8,128)(2,1)S(1)} %get-tuple-element.27), channel_id=1, source_target_pairs={{0,8},{4,12},{8,0},{12,4},{16,24},{20,28},{24,16},{28,20},{1,9},{5... | collective-permute-start | bytes 344072 | tf_op jit(solution)/shard_map/ppermute | solution.py:139
  5.0 0.0 collective-permute-start.2
  5.0 1.7 %collective-permute-start.7 = (bf16[32,2048]{1,0:T(8,128)(2,1)S(1)}, bf16[32,2048]{1,0:T(8,128)(2,1)S(1)}, u32[]{:S(2)}, u32[]{:S(2)}) collective-permute-start(bf16[32,2048]{1,0:T(8,128)(2,1)S(1)} %get-tuple-element.41), channel_id=1, source_target_pairs={{0,1},{1,0},{2,3},{3,2},{4,5},{5,4},{6,7},{7,6},{8,9},{9,8},{10,11... | collective-permute-start | bytes 393224 | tf_op jit(solution)/shard_map/ppermute | solution.py:139
  6.8 1.2 %collective-permute-start.3 = (bf16[224,256]{1,0:T(8,128)(2,1)S(1)}, bf16[224,256]{1,0:T(8,128)(2,1)S(1)}, u32[]{:S(2)}, u32[]{:S(2)}) collective-permute-start(bf16[224,256]{1,0:T(8,128)(2,1)S(1)} %get-tuple-element.29), channel_id=1, source_target_pairs={{0,16},{4,20},{8,24},{12,28},{16,0},{20,4},{24,8},{28,12},{1,17},{... | collective-permute-start | bytes 344072 | tf_op jit(solution)/shard_map/ppermute | solution.py:139
  8.0 0.0 collective-permute-done.rest_1_
  8.0 0.8 %collective-permute-start.4 = (bf16[224,256]{1,0:T(8,128)(2,1)S(1)}, bf16[224,256]{1,0:T(8,128)(2,1)S(1)}, u32[]{:S(2)}, u32[]{:S(2)}) collective-permute-start(bf16[224,256]{1,0:T(8,128)(2,1)S(1)} %get-tuple-element.30), channel_id=1, source_target_pairs={{0,20},{4,16},{8,28},{12,24},{16,4},{20,0},{24,12},{28,8},{1,21},{... | collective-permute-start | bytes 344072 | tf_op jit(solution)/shard_map/ppermute | solution.py:139
  8.8 0.0 collective-permute-done.1.rest_2_
  8.8 2.2 %collective-permute-start.5 = (bf16[224,256]{1,0:T(8,128)(2,1)S(1)}, bf16[224,256]{1,0:T(8,128)(2,1)S(1)}, u32[]{:S(2)}, u32[]{:S(2)}) collective-permute-start(bf16[224,256]{1,0:T(8,128)(2,1)S(1)} %get-tuple-element.31), channel_id=1, source_target_pairs={{0,24},{4,28},{8,16},{12,20},{16,8},{20,12},{24,0},{28,4},{1,25},{... | collective-permute-start | bytes 344072 | tf_op jit(solution)/shard_map/ppermute | solution.py:139
  11.0 0.1 collective-permute-done.2.rest_3_
  11.1 0.0 copy-start
  11.1 2.3 %collective-permute-start.6 = (bf16[224,256]{1,0:T(8,128)(2,1)S(1)}, bf16[224,256]{1,0:T(8,128)(2,1)S(1)}, u32[]{:S(2)}, u32[]{:S(2)}) collective-permute-start(bf16[224,256]{1,0:T(8,128)(2,1)S(1)} %get-tuple-element.32), channel_id=1, source_target_pairs={{0,28},{4,24},{8,20},{12,16},{16,12},{20,8},{24,4},{28,0},{1,29},{... | collective-permute-start | bytes 344072 | tf_op jit(solution)/shard_map/ppermute | solution.py:139
  13.4 0.0 copy-done
  13.4 1.9 %make_tables.1 = (bf16[512,256]{1,0:T(8,128)(2,1)S(1)}, bf16[512,256]{1,0:T(8,128)(2,1)S(1)}, f32[288,512]{1,0:T(8,128)S(1)}) custom-call(f32[32]{0:T(128)S(1)} %copy-done, f32[512,256]{1,0:T(8,128)} %constant.6.clone.outer_ref, f32[512,256]{1,0:T(8,128)} %constant.7.clone.inner_ref, f32[256,512]{1,0:T(8,128)} %constant.8.clone.turns_ref), custom_call_target="tpu_custom_call" | custom-call | tf_op jit(solution)/shard_map/make_tables/pallas_call | solution.py:164
  15.3 0.0 collective-permute-done.3.rest_4_
  15.3 3.7 %collective-permute-done.4.rest_5_ = bf16[224,256]{1,0:T(8,128)(2,1)S(1)} collective-permute-done((bf16[224,256]{1,0:T(8,128)(2,1)S(1)}, bf16[224,256]{1,0:T(8,128)(2,1)S(1)}, u32[]{:S(2)}, u32[]{:S(2)}) %collective-permute-start.4) | collective-permute-done | bytes 114720 | tf_op jit(solution)/shard_map/ppermute | solution.py:139
  19.0 0.0 collective-permute-done.5.rest_6_
  19.0 0.0 collective-permute-done.6.rest_7_
  19.0 2.9 %convolve.1 = bf16[32,32,256]{2,1,0:T(8,128)(2,1)S(1)} custom-call(bf16[224,256]{1,0:T(8,128)(2,1)S(1)} %get-tuple-element.25.rest_0_, bf16[224,256]{1,0:T(8,128)(2,1)S(1)} %collective-permute-done.rest_1_, bf16[224,256]{1,0:T(8,128)(2,1)S(1)} %collective-permute-done.1.rest_2_, bf16[224,256]{1,0:T(8,128)(2,1)S(1)} %collective-permute-done.2.rest_3_, ...), custom_call_target="tpu_custom_call" | custom-call | flops 65536 | bytes 262144 | tf_op jit(solution)/shard_map/convolve/pallas_call | solution.py:259
  21.9 0.0 collective-permute-done.7.rest_1_
  21.9 19.8 %all_to_all.5.got_ref = bf16[32,32,256]{2,1,0:T(8,128)(2,1)S(1)} all-to-all(bf16[32,32,256]{2,1,0:T(8,128)(2,1)S(1)} %convolve.1), channel_id=1, replica_groups=mesh['ctx'=8,'ch'=4] {'ctx','ch'}, dimensions={0} | all-to-all | bytes 1048576 | tf_op jit(solution)/shard_map/all_to_all | solution.py:337
  41.7 1.2 %unpack.1 = bf16[128,2048]{1,0:T(8,128)(2,1)} custom-call(bf16[32,32,256]{2,1,0:T(8,128)(2,1)S(1)} %all_to_all.5.got_ref, bf16[32,2048]{1,0:T(8,128)(2,1)S(1)} %get-tuple-element.43.rest_0_, bf16[32,2048]{1,0:T(8,128)(2,1)S(1)} %collective-permute-done.7.rest_1_), custom_call_target="tpu_custom_call" | custom-call | tf_op jit(solution)/shard_map/unpack/pallas_call | solution.py:309
Async XLA Ops:
  2.2 5.8 %collective-permute-start = (bf16[224,256]{1,0:T(8,128)(2,1)S(1)}, bf16[224,256]{1,0:T(8,128)(2,1)S(1)}, u32[]{:S(2)}, u32[]{:S(2)}) collective-permute-start(bf16[224,256]{1,0:T(8,128)(2,1)S(1)} %get-tuple-element.26), channel_id=1, source_target_pairs={{0,4},{4,0},{8,12},{12,8},{16,20},{20,16},{24,28},{28,24},{1,5},{5... | collective-permute-start | bytes 344072 | tf_op jit(solution)/shard_map/ppermute | solution.py:139
  2.3 6.5 %collective-permute-start.1 = (bf16[224,256]{1,0:T(8,128)(2,1)S(1)}, bf16[224,256]{1,0:T(8,128)(2,1)S(1)}, u32[]{:S(2)}, u32[]{:S(2)}) collective-permute-start(bf16[224,256]{1,0:T(8,128)(2,1)S(1)} %get-tuple-element.27), channel_id=1, source_target_pairs={{0,8},{4,12},{8,0},{12,4},{16,24},{20,28},{24,16},{28,20},{1,9},{5... | collective-permute-start | bytes 344072 | tf_op jit(solution)/shard_map/ppermute | solution.py:139
  5.0 6.1 %collective-permute-start.2 = (bf16[224,256]{1,0:T(8,128)(2,1)S(1)}, bf16[224,256]{1,0:T(8,128)(2,1)S(1)}, u32[]{:S(2)}, u32[]{:S(2)}) collective-permute-start(bf16[224,256]{1,0:T(8,128)(2,1)S(1)} %get-tuple-element.28), channel_id=1, source_target_pairs={{0,12},{4,8},{8,4},{12,0},{16,28},{20,24},{24,20},{28,16},{1,13},{... | collective-permute-start | bytes 344072 | tf_op jit(solution)/shard_map/ppermute | solution.py:139
  5.0 16.9 %collective-permute-start.7 = (bf16[32,2048]{1,0:T(8,128)(2,1)S(1)}, bf16[32,2048]{1,0:T(8,128)(2,1)S(1)}, u32[]{:S(2)}, u32[]{:S(2)}) collective-permute-start(bf16[32,2048]{1,0:T(8,128)(2,1)S(1)} %get-tuple-element.41), channel_id=1, source_target_pairs={{0,1},{1,0},{2,3},{3,2},{4,5},{5,4},{6,7},{7,6},{8,9},{9,8},{10,11... | collective-permute-start | bytes 393224 | tf_op jit(solution)/shard_map/ppermute | solution.py:139
  6.8 8.6 %collective-permute-start.3 = (bf16[224,256]{1,0:T(8,128)(2,1)S(1)}, bf16[224,256]{1,0:T(8,128)(2,1)S(1)}, u32[]{:S(2)}, u32[]{:S(2)}) collective-permute-start(bf16[224,256]{1,0:T(8,128)(2,1)S(1)} %get-tuple-element.29), channel_id=1, source_target_pairs={{0,16},{4,20},{8,24},{12,28},{16,0},{20,4},{24,8},{28,12},{1,17},{... | collective-permute-start | bytes 344072 | tf_op jit(solution)/shard_map/ppermute | solution.py:139
  8.0 11.0 %collective-permute-start.4 = (bf16[224,256]{1,0:T(8,128)(2,1)S(1)}, bf16[224,256]{1,0:T(8,128)(2,1)S(1)}, u32[]{:S(2)}, u32[]{:S(2)}) collective-permute-start(bf16[224,256]{1,0:T(8,128)(2,1)S(1)} %get-tuple-element.30), channel_id=1, source_target_pairs={{0,20},{4,16},{8,28},{12,24},{16,4},{20,0},{24,12},{28,8},{1,21},{... | collective-permute-start | bytes 344072 | tf_op jit(solution)/shard_map/ppermute | solution.py:139
  8.8 10.2 %collective-permute-start.5 = (bf16[224,256]{1,0:T(8,128)(2,1)S(1)}, bf16[224,256]{1,0:T(8,128)(2,1)S(1)}, u32[]{:S(2)}, u32[]{:S(2)}) collective-permute-start(bf16[224,256]{1,0:T(8,128)(2,1)S(1)} %get-tuple-element.31), channel_id=1, source_target_pairs={{0,24},{4,28},{8,16},{12,20},{16,8},{20,12},{24,0},{28,4},{1,25},{... | collective-permute-start | bytes 344072 | tf_op jit(solution)/shard_map/ppermute | solution.py:139
  11.1 2.3 %copy-start = (f32[32]{0:T(128)S(1)}, f32[32]{0:T(128)}, u32[]{:S(2)}) copy-start(f32[32]{0:T(128)} %skip_ref) | copy-start | bytes 388
  11.1 7.9 %collective-permute-start.6 = (bf16[224,256]{1,0:T(8,128)(2,1)S(1)}, bf16[224,256]{1,0:T(8,128)(2,1)S(1)}, u32[]{:S(2)}, u32[]{:S(2)}) collective-permute-start(bf16[224,256]{1,0:T(8,128)(2,1)S(1)} %get-tuple-element.32), channel_id=1, source_target_pairs={{0,28},{4,24},{8,20},{12,16},{16,12},{20,8},{24,4},{28,0},{1,29},{... | collective-permute-start | bytes 344072 | tf_op jit(solution)/shard_map/ppermute | solution.py:139

commit v10 on v9

--- a/solution.py
+++ b/solution.py
@@ -135,6 +135,15 @@
     return list(out[:parts]), list(out[parts:])
 
 
+def partner_order(count):
+    corners = [d for d in range(1, count) if bin(d >> 1).count("1") > 1]
+    straight = [d for d in range(count - 1, 1, -1) if bin(d >> 1).count("1") == 1 and d % 2 == 0]
+    order = [0]
+    for n in range(max(len(corners), len(straight))):
+        order += straight[n : n + 1] + corners[n : n + 1]
+    return order + [d for d in range(count - 1, 0, -1) if d not in order][::-1][1:] + [1]
+
+
 def swap(piece, axis, count, d):
     return lax.ppermute(piece, axis, [(i, i ^ d) for i in range(count)])
 
@@ -186,10 +195,11 @@
     blocks = parts * near
     length = blocks * W
     me = lax.axis_index("ctx")
-    for d in range(parts):
+    order = partner_order(parts)
+    for d, got_ref in zip(order, got_refs):
         here = pl.ds(pl.multiple_of(jnp.bitwise_xor(me, d) * near, TILE), near)
         for c in range(own + 1):
-            x_all[here, W * c : W * (c + 1)] = got_refs[d][c * near : (c + 1) * near, :]
+            x_all[here, W * c : W * (c + 1)] = got_ref[c * near : (c + 1) * near, :]
 
     near_cos, near_sin = inner_ref[0:W, :], inner_ref[W:, :]
     for table, sign in ((ahead, -1), (rear, 1)):
@@ -238,9 +248,9 @@
     some = out_ref.shape[1] // own
     early = some * (ch_count - ch_count // 2)
     place = lax.axis_index("ch")
-    for d in range(parts):
+    for d, got_ref in zip(order, got_refs):
         k = jnp.bitwise_xor(me, d)
-        gate = got_refs[d][(own + 1) * near :, :].astype(jnp.float32)
+        gate = got_ref[(own + 1) * near :, :].astype(jnp.float32)
         mine = [z_all[c, pl.ds(pl.multiple_of(k * near, TILE), near), :] for c in range(own)]
         for m in range(ch_count):
             rows = [part[m * some : (m + 1) * some, :] for part in mine]
@@ -327,8 +337,7 @@
     near = value.shape[1] // W
     got, gates = pack(pre_gate, value, post_gate, filter_taps, ctx_count, ch_count)
     tables, skip, _ = lax.optimization_barrier((dft_tables(near * ctx_count), skip, got[0]))
-    for d in range(1, ctx_count):
-        got[d] = swap(got[d], "ctx", ctx_count, d)
+    got = [swap(got[d], "ctx", ctx_count, d) if d else got[d] for d in partner_order(ctx_count)]
     for d in range(1, ch_count // 2):
         gates[d] = swap(gates[d], "ch", ch_count, d)
     tables = list(make_tables(skip, *tables, own))

time: 43.1 us -> 41.9 us (0.972)
  waiting for transfers between devices: 3.8 us -> 2 us
  starting transfers between devices: 11.1 us -> 11.6 us
    ppermute x8, waiting for transfers between devices: 3.8 us -> 2 us  [swap(): return lax.ppermute(piece, axis, [(i, i ^ d) for i in range(count)])]
    ppermute x8, starting transfers between devices: 11.1 us -> 11.6 us  [swap(): return lax.ppermute(piece, axis, [(i, i ^ d) for i in range(count)])]
where the time goes in v10:
time: 41.9 us; the launch traced here: 41.8 us
  blocking collectives  19.9 us (47%)
  starting transfers between devices  11.6 us (28%)
  Pallas kernels  8.16 us (19%)
  waiting for transfers between devices  2 us (5%)
    all_to_all x1, blocking collectives, body(): lax.all_to_all(mixed, ('ctx', 'ch'), split_axis=0, concat_axis=0, tiled=T...  19.9 us
    ppermute x8, starting transfers between devices, swap(): return lax.ppermute(piece, axis, [(i, i ^ d) for i in range(count)])  11.6 us
    pallas_call x1, Pallas kernels, convolve(): pl.pallas_call(functools.partial(conv_kernel, own, near, ch_count, parts)...  2.88 us
    pallas_call x1, Pallas kernels, pack(): pl.pallas_call(functools.partial(pack_kernel, own, blocks, group, ch_coun...  2.18 us
    ppermute x8, waiting for transfers between devices, swap(): return lax.ppermute(piece, axis, [(i, i ^ d) for i in range(count)])  2 us
    pallas_call x1, Pallas kernels, make_tables(): pl.pallas_call(functools.partial(tables_kernel, own), out_shape=[jax.Shap...  1.92 us
    pallas_call x1, Pallas kernels, unpack(): pl.pallas_call(functools.partial(unpack_kernel, own), out_shape=jax.Shape...  1.19 us
  transfers between devices with their start and end apart: 8, of which 2 were waited for; matrix products, arithmetic and copies ran while one was open for 0% of the time, Pallas kernels for 11%

profile of v10, /device:TPU:1, one launch (start us, length us, event | category | flops | bytes accessed | tf_op | source)
XLA Modules:
  0.0 41.8 jit_solution(3354590883637320114)
XLA Ops:
  0.0 2.2 %pack.1 = (bf16[224,256]{1,0:T(8,128)(2,1)S(1)}, bf16[224,256]{1,0:T(8,128)(2,1)S(1)}, bf16[224,256]{1,0:T(8,128)(2,1)S(1)}, bf16[224,256]{1,0:T(8,128)(2,1)S(1)...) custom-call(bf16[32,8192]{1,0:T(8,128)(2,1)} %pre_ref.1, ...), custom_call_target="tpu_custom_call" | custom-call | tf_op jit(solution)/shard_map/pack/pallas_call | solution.py:115
  2.2 2.1 %collective-permute-start = (bf16[224,256]{1,0:T(8,128)(2,1)S(1)}, bf16[224,256]{1,0:T(8,128)(2,1)S(1)}, u32[]{:S(2)}, u32[]{:S(2)}) collective-permute-start(bf16[224,256]{1,0:T(8,128)(2,1)S(1)} %get-tuple-element.26), channel_id=1, source_target_pairs={{0,16},{4,20},{8,24},{12,28},{16,0},{20,4},{24,8},{28,12},{1,17},{... | collective-permute-start | bytes 344072 | tf_op jit(solution)/shard_map/ppermute | solution.py:148
  4.3 1.2 %collective-permute-start.1 = (bf16[224,256]{1,0:T(8,128)(2,1)S(1)}, bf16[224,256]{1,0:T(8,128)(2,1)S(1)}, u32[]{:S(2)}, u32[]{:S(2)}) collective-permute-start(bf16[224,256]{1,0:T(8,128)(2,1)S(1)} %get-tuple-element.27), channel_id=1, source_target_pairs={{0,24},{4,28},{8,16},{12,20},{16,8},{20,12},{24,0},{28,4},{1,25},{... | collective-permute-start | bytes 344072 | tf_op jit(solution)/shard_map/ppermute | solution.py:148
  5.5 0.1 collective-permute-start.2
  5.6 1.4 %collective-permute-start.7 = (bf16[32,2048]{1,0:T(8,128)(2,1)S(1)}, bf16[32,2048]{1,0:T(8,128)(2,1)S(1)}, u32[]{:S(2)}, u32[]{:S(2)}) collective-permute-start(bf16[32,2048]{1,0:T(8,128)(2,1)S(1)} %get-tuple-element.41), channel_id=1, source_target_pairs={{0,1},{1,0},{2,3},{3,2},{4,5},{5,4},{6,7},{7,6},{8,9},{9,8},{10,11... | collective-permute-start | bytes 393224 | tf_op jit(solution)/shard_map/ppermute | solution.py:148
  7.0 3.8 %collective-permute-start.3 = (bf16[224,256]{1,0:T(8,128)(2,1)S(1)}, bf16[224,256]{1,0:T(8,128)(2,1)S(1)}, u32[]{:S(2)}, u32[]{:S(2)}) collective-permute-start(bf16[224,256]{1,0:T(8,128)(2,1)S(1)} %get-tuple-element.29), channel_id=1, source_target_pairs={{0,28},{4,24},{8,20},{12,16},{16,12},{20,8},{24,4},{28,0},{1,29},{... | collective-permute-start | bytes 344072 | tf_op jit(solution)/shard_map/ppermute | solution.py:148
  10.9 0.0 collective-permute-done.rest_1_
  10.9 0.2 collective-permute-start.4
  11.0 0.0 collective-permute-done.1.rest_2_
  11.0 1.2 %collective-permute-start.5 = (bf16[224,256]{1,0:T(8,128)(2,1)S(1)}, bf16[224,256]{1,0:T(8,128)(2,1)S(1)}, u32[]{:S(2)}, u32[]{:S(2)}) collective-permute-start(bf16[224,256]{1,0:T(8,128)(2,1)S(1)} %get-tuple-element.31), channel_id=1, source_target_pairs={{0,20},{4,16},{8,28},{12,24},{16,4},{20,0},{24,12},{28,8},{1,21},{... | collective-permute-start | bytes 344072 | tf_op jit(solution)/shard_map/ppermute | solution.py:148
  12.2 0.0 collective-permute-done.2.rest_3_
  12.2 0.0 copy-start
  12.2 1.6 %collective-permute-start.6 = (bf16[224,256]{1,0:T(8,128)(2,1)S(1)}, bf16[224,256]{1,0:T(8,128)(2,1)S(1)}, u32[]{:S(2)}, u32[]{:S(2)}) collective-permute-start(bf16[224,256]{1,0:T(8,128)(2,1)S(1)} %get-tuple-element.32), channel_id=1, source_target_pairs={{0,4},{4,0},{8,12},{12,8},{16,20},{20,16},{24,28},{28,24},{1,5},{5... | collective-permute-start | bytes 344072 | tf_op jit(solution)/shard_map/ppermute | solution.py:148
  13.8 0.0 copy-done
  13.8 1.9 %make_tables.1 = (bf16[512,256]{1,0:T(8,128)(2,1)S(1)}, bf16[512,256]{1,0:T(8,128)(2,1)S(1)}, f32[288,512]{1,0:T(8,128)S(1)}) custom-call(f32[32]{0:T(128)S(1)} %copy-done, f32[512,256]{1,0:T(8,128)} %constant.6.clone.outer_ref, f32[512,256]{1,0:T(8,128)} %constant.7.clone.inner_ref, f32[256,512]{1,0:T(8,128)} %constant.8.clone.turns_ref), custom_call_target="tpu_custom_call" | custom-call | tf_op jit(solution)/shard_map/make_tables/pallas_call | solution.py:173
  15.8 0.0 collective-permute-done.3.rest_4_
  15.8 0.9 %collective-permute-done.4.rest_5_ = bf16[224,256]{1,0:T(8,128)(2,1)S(1)} collective-permute-done((bf16[224,256]{1,0:T(8,128)(2,1)S(1)}, bf16[224,256]{1,0:T(8,128)(2,1)S(1)}, u32[]{:S(2)}, u32[]{:S(2)}) %collective-permute-start.4) | collective-permute-done | bytes 114720 | tf_op jit(solution)/shard_map/ppermute | solution.py:148
  16.7 1.1 %collective-permute-done.5.rest_6_ = bf16[224,256]{1,0:T(8,128)(2,1)S(1)} collective-permute-done((bf16[224,256]{1,0:T(8,128)(2,1)S(1)}, bf16[224,256]{1,0:T(8,128)(2,1)S(1)}, u32[]{:S(2)}, u32[]{:S(2)}) %collective-permute-start.5) | collective-permute-done | bytes 114720 | tf_op jit(solution)/shard_map/ppermute | solution.py:148
  17.8 0.0 collective-permute-done.6.rest_7_
  17.8 2.9 %convolve.1 = bf16[32,32,256]{2,1,0:T(8,128)(2,1)S(1)} custom-call(bf16[224,256]{1,0:T(8,128)(2,1)S(1)} %get-tuple-element.25.rest_0_, bf16[224,256]{1,0:T(8,128)(2,1)S(1)} %collective-permute-done.rest_1_, bf16[224,256]{1,0:T(8,128)(2,1)S(1)} %collective-permute-done.1.rest_2_, bf16[224,256]{1,0:T(8,128)(2,1)S(1)} %collective-permute-done.2.rest_3_, ...), custom_call_target="tpu_custom_call" | custom-call | flops 65536 | bytes 262144 | tf_op jit(solution)/shard_map/convolve/pallas_call | solution.py:269
  20.7 0.0 collective-permute-done.7.rest_1_
  20.7 19.9 %all_to_all.5.got_ref = bf16[32,32,256]{2,1,0:T(8,128)(2,1)S(1)} all-to-all(bf16[32,32,256]{2,1,0:T(8,128)(2,1)S(1)} %convolve.1), channel_id=1, replica_groups=mesh['ctx'=8,'ch'=4] {'ctx','ch'}, dimensions={0} | all-to-all | bytes 1048576 | tf_op jit(solution)/shard_map/all_to_all | solution.py:346
  40.6 1.2 %unpack.1 = bf16[128,2048]{1,0:T(8,128)(2,1)} custom-call(bf16[32,32,256]{2,1,0:T(8,128)(2,1)S(1)} %all_to_all.5.got_ref, bf16[32,2048]{1,0:T(8,128)(2,1)S(1)} %get-tuple-element.43.rest_0_, bf16[32,2048]{1,0:T(8,128)(2,1)S(1)} %collective-permute-done.7.rest_1_), custom_call_target="tpu_custom_call" | custom-call | tf_op jit(solution)/shard_map/unpack/pallas_call | solution.py:319
Async XLA Ops:
  2.2 8.7 %collective-permute-start = (bf16[224,256]{1,0:T(8,128)(2,1)S(1)}, bf16[224,256]{1,0:T(8,128)(2,1)S(1)}, u32[]{:S(2)}, u32[]{:S(2)}) collective-permute-start(bf16[224,256]{1,0:T(8,128)(2,1)S(1)} %get-tuple-element.26), channel_id=1, source_target_pairs={{0,16},{4,20},{8,24},{12,28},{16,0},{20,4},{24,8},{28,12},{1,17},{... | collective-permute-start | bytes 344072 | tf_op jit(solution)/shard_map/ppermute | solution.py:148
  4.3 6.7 %collective-permute-start.1 = (bf16[224,256]{1,0:T(8,128)(2,1)S(1)}, bf16[224,256]{1,0:T(8,128)(2,1)S(1)}, u32[]{:S(2)}, u32[]{:S(2)}) collective-permute-start(bf16[224,256]{1,0:T(8,128)(2,1)S(1)} %get-tuple-element.27), channel_id=1, source_target_pairs={{0,24},{4,28},{8,16},{12,20},{16,8},{20,12},{24,0},{28,4},{1,25},{... | collective-permute-start | bytes 344072 | tf_op jit(solution)/shard_map/ppermute | solution.py:148
  5.5 6.8 %collective-permute-start.2 = (bf16[224,256]{1,0:T(8,128)(2,1)S(1)}, bf16[224,256]{1,0:T(8,128)(2,1)S(1)}, u32[]{:S(2)}, u32[]{:S(2)}) collective-permute-start(bf16[224,256]{1,0:T(8,128)(2,1)S(1)} %get-tuple-element.28), channel_id=1, source_target_pairs={{0,8},{4,12},{8,0},{12,4},{16,24},{20,28},{24,16},{28,20},{1,9},{5... | collective-permute-start | bytes 344072 | tf_op jit(solution)/shard_map/ppermute | solution.py:148
  5.6 15.1 %collective-permute-start.7 = (bf16[32,2048]{1,0:T(8,128)(2,1)S(1)}, bf16[32,2048]{1,0:T(8,128)(2,1)S(1)}, u32[]{:S(2)}, u32[]{:S(2)}) collective-permute-start(bf16[32,2048]{1,0:T(8,128)(2,1)S(1)} %get-tuple-element.41), channel_id=1, source_target_pairs={{0,1},{1,0},{2,3},{3,2},{4,5},{5,4},{6,7},{7,6},{8,9},{9,8},{10,11... | collective-permute-start | bytes 393224 | tf_op jit(solution)/shard_map/ppermute | solution.py:148
  7.0 8.8 %collective-permute-start.3 = (bf16[224,256]{1,0:T(8,128)(2,1)S(1)}, bf16[224,256]{1,0:T(8,128)(2,1)S(1)}, u32[]{:S(2)}, u32[]{:S(2)}) collective-permute-start(bf16[224,256]{1,0:T(8,128)(2,1)S(1)} %get-tuple-element.29), channel_id=1, source_target_pairs={{0,28},{4,24},{8,20},{12,16},{16,12},{20,8},{24,4},{28,0},{1,29},{... | collective-permute-start | bytes 344072 | tf_op jit(solution)/shard_map/ppermute | solution.py:148
  10.9 5.8 %collective-permute-start.4 = (bf16[224,256]{1,0:T(8,128)(2,1)S(1)}, bf16[224,256]{1,0:T(8,128)(2,1)S(1)}, u32[]{:S(2)}, u32[]{:S(2)}) collective-permute-start(bf16[224,256]{1,0:T(8,128)(2,1)S(1)} %get-tuple-element.30), channel_id=1, source_target_pairs={{0,12},{4,8},{8,4},{12,0},{16,28},{20,24},{24,20},{28,16},{1,13},{... | collective-permute-start | bytes 344072 | tf_op jit(solution)/shard_map/ppermute | solution.py:148
  11.0 6.7 %collective-permute-start.5 = (bf16[224,256]{1,0:T(8,128)(2,1)S(1)}, bf16[224,256]{1,0:T(8,128)(2,1)S(1)}, u32[]{:S(2)}, u32[]{:S(2)}) collective-permute-start(bf16[224,256]{1,0:T(8,128)(2,1)S(1)} %get-tuple-element.31), channel_id=1, source_target_pairs={{0,20},{4,16},{8,28},{12,24},{16,4},{20,0},{24,12},{28,8},{1,21},{... | collective-permute-start | bytes 344072 | tf_op jit(solution)/shard_map/ppermute | solution.py:148
  12.2 1.6 %copy-start = (f32[32]{0:T(128)S(1)}, f32[32]{0:T(128)}, u32[]{:S(2)}) copy-start(f32[32]{0:T(128)} %skip_ref) | copy-start | bytes 388
  12.2 5.5 %collective-permute-start.6 = (bf16[224,256]{1,0:T(8,128)(2,1)S(1)}, bf16[224,256]{1,0:T(8,128)(2,1)S(1)}, u32[]{:S(2)}, u32[]{:S(2)}) collective-permute-start(bf16[224,256]{1,0:T(8,128)(2,1)S(1)} %get-tuple-element.32), channel_id=1, source_target_pairs={{0,4},{4,0},{8,12},{12,8},{16,20},{20,16},{24,28},{28,24},{1,5},{5... | collective-permute-start | bytes 344072 | tf_op jit(solution)/shard_map/ppermute | solution.py:148

commit v11 on v10

--- a/solution.py
+++ b/solution.py
@@ -11,7 +11,7 @@
 W = 256
 LANES = 128
 TILE = 16
-CHUNK = 128
+CHUNK = 256
 
 
 def whole_vmem():
@@ -31,7 +31,7 @@
     near = 2 * np.pi * (np.arange(W)[:, None] * np.arange(W)[None, :] % W) / W
     inner = np.concatenate([np.cos(near), np.sin(near)], 0)
     turns = np.concatenate([np.cos(turn), np.sin(turn)], 1)
-    return [jnp.asarray(table, jnp.float32) for table in (outer, inner, turns)]
+    return [jnp.asarray(table, jnp.float32) for table in (outer, outer.T, inner, turns)]
 
 
 def lay(natural, j, value):
@@ -141,19 +141,23 @@
     order = [0]
     for n in range(max(len(corners), len(straight))):
         order += straight[n : n + 1] + corners[n : n + 1]
-    return order + [d for d in range(count - 1, 0, -1) if d not in order][::-1][1:] + [1]
+    order += [d for d in range(2, count) if d not in order]
+    return order + [1]
 
 
 def swap(piece, axis, count, d):
     return lax.ppermute(piece, axis, [(i, i ^ d) for i in range(count)])
 
 
-def tables_kernel(own, skip_ref, outer_ref, inner_ref, turns_ref, outer_out, inner_out, turns_out, outer_s, inner_s, sems):
+def tables_kernel(own, skip_ref, *rest):
+    outer_ref, back_ref, inner_ref, turns_ref, outer_out, back_out, ahead, rear, turns_out = rest[:9]
+    outer_s, back_s, inner_s, sems = rest[9:]
     count, width = turns_ref.shape
     loads = [
-        pltpu.make_async_copy(outer_ref, outer_s, sems.at[0]),
-        pltpu.make_async_copy(inner_ref, inner_s, sems.at[1]),
-        pltpu.make_async_copy(turns_ref, turns_out.at[0:count, :], sems.at[2]),
+        pltpu.make_async_copy(inner_ref, inner_s, sems.at[0]),
+        pltpu.make_async_copy(outer_ref, outer_s, sems.at[1]),
+        pltpu.make_async_copy(back_ref, back_s, sems.at[2]),
+        pltpu.make_async_copy(turns_ref, turns_out.at[0:count, :], sems.at[3]),
     ]
     for copy in loads:
         copy.start()
@@ -161,37 +165,43 @@
     for c in range(own):
         turns_out[count + 8 * c : count + 8 * (c + 1), :] = jnp.full((8, width), skip_ref[own * me + c], jnp.float32)
     loads[0].wait()
+    near_cos, near_sin = inner_s[0:W, :].astype(jnp.bfloat16), inner_s[W:, :].astype(jnp.bfloat16)
+    for table, sign in ((ahead, -1), (rear, 1)):
+        table[0:W, 0:W] = near_cos
+        table[0:W, W:] = near_sin * sign
+        table[W:, 0:W] = near_sin * -sign
+        table[W:, W:] = near_cos
+    loads[1].wait()
     outer_out[...] = outer_s[...].astype(jnp.bfloat16)
-    loads[1].wait()
-    inner_out[...] = inner_s[...].astype(jnp.bfloat16)
     loads[2].wait()
-
-
-def make_tables(skip, outer, inner, turns, own):
+    back_out[...] = back_s[...].astype(jnp.bfloat16)
+    loads[3].wait()
+
+
+def make_tables(skip, outer, back, inner, turns, own):
     count, width = turns.shape
-    args = [pltpu.with_memory_space_constraint(arg, pltpu.HBM) for arg in (outer, inner, turns)]
+    args = [pltpu.with_memory_space_constraint(arg, pltpu.HBM) for arg in (outer, back, inner, turns)]
+    narrow = (outer.shape, back.shape, (2 * W, 2 * W), (2 * W, 2 * W))
     return pl.pallas_call(
         functools.partial(tables_kernel, own),
-        out_shape=[
-            jax.ShapeDtypeStruct(outer.shape, jnp.bfloat16),
-            jax.ShapeDtypeStruct(inner.shape, jnp.bfloat16),
-            jax.ShapeDtypeStruct((count + 8 * own, width), jnp.float32),
-        ],
-        in_specs=[pl.BlockSpec(memory_space=pltpu.SMEM)] + [in_hbm()] * 3,
-        out_specs=[whole_vmem()] * 3,
+        out_shape=[jax.ShapeDtypeStruct(shape, jnp.bfloat16) for shape in narrow]
+        + [jax.ShapeDtypeStruct((count + 8 * own, width), jnp.float32)],
+        in_specs=[pl.BlockSpec(memory_space=pltpu.SMEM)] + [in_hbm()] * 4,
+        out_specs=[whole_vmem()] * 5,
         scratch_shapes=[
             pltpu.VMEM(outer.shape, jnp.float32),
+            pltpu.VMEM(back.shape, jnp.float32),
             pltpu.VMEM(inner.shape, jnp.float32),
-            pltpu.SemaphoreType.DMA((3,)),
+            pltpu.SemaphoreType.DMA((4,)),
         ],
-        compiler_params=pltpu.CompilerParams(vmem_limit_bytes=12 * 2**20),
+        compiler_params=pltpu.CompilerParams(vmem_limit_bytes=16 * 2**20),
         name="make_tables",
     )(skip, *args)
 
 
 def conv_kernel(own, near, ch_count, parts, *rest):
     got_refs = rest[:parts]
-    outer_ref, inner_ref, turns_ref, out_ref, x_all, r_all, z_all, ahead, rear = rest[parts:]
+    outer_ref, back_ref, ahead, rear, turns_ref, out_ref, x_all, r_all, z_all = rest[parts:]
     blocks = parts * near
     length = blocks * W
     me = lax.axis_index("ctx")
@@ -200,13 +210,6 @@
         here = pl.ds(pl.multiple_of(jnp.bitwise_xor(me, d) * near, TILE), near)
         for c in range(own + 1):
             x_all[here, W * c : W * (c + 1)] = got_ref[c * near : (c + 1) * near, :]
-
-    near_cos, near_sin = inner_ref[0:W, :], inner_ref[W:, :]
-    for table, sign in ((ahead, -1), (rear, 1)):
-        table[0:W, 0:W] = near_cos
-        table[0:W, W:] = near_sin * sign
-        table[W:, 0:W] = near_sin * -sign
-        table[W:, W:] = near_cos
 
     def dot(left, right):
         return jnp.dot(left, right, preferred_element_type=jnp.float32)
@@ -239,9 +242,7 @@
             r_all[here, cols] = (re * turn_cos - im * turn_sin).astype(jnp.bfloat16)
             r_all[there, cols] = (re * turn_sin + im * turn_cos).astype(jnp.bfloat16)
 
-    conv = lax.dot_general(
-        outer_ref[...], r_all[...], (((0,), (0,)), ((), ())), preferred_element_type=jnp.float32
-    )
+    conv = dot(back_ref[...], r_all[...])
     for c in range(own):
         cols = slice(W * c, W * (c + 1))
         z_all[c] = conv[:, cols] + turns_ref[blocks + 8 * c : blocks + 8 * c + 1, 0:W] * x_all[:, cols].astype(jnp.float32)
@@ -275,8 +276,6 @@
             pltpu.VMEM((blocks, W * (own + 1)), jnp.bfloat16),
             pltpu.VMEM((2 * blocks, W * own), jnp.bfloat16),
             pltpu.VMEM((own, blocks, W), jnp.float32),
-            pltpu.VMEM((2 * W, 2 * W), jnp.bfloat16),
-            pltpu.VMEM((2 * W, 2 * W), jnp.bfloat16),
         ],
         compiler_params=pltpu.CompilerParams(vmem_limit_bytes=32 * 2**20),
         cost_estimate=pl.CostEstimate(flops=blocks * W, bytes_accessed=4 * blocks * W, transcendentals=0),
@@ -285,7 +284,7 @@
 
 
 def unpack_kernel(own, got_ref, *rest):
-    gate_refs, (out_ref, flat, gate_s) = rest[:-3], rest[-3:]
+    gate_refs, (out_ref, flat, gate_s, stage, sems) = rest[:-5], rest[-5:]
     sources, rows, _ = got_ref.shape
     some = rows // own
     place = lax.axis_index("ch")
@@ -294,17 +293,24 @@
     for d in range(ch_count):
         here = pl.ds(pl.multiple_of(jnp.bitwise_xor(place, d) * channels, TILE), channels)
         gate_s[here, :] = gate_refs[d][...] if d < len(gate_refs) else jnp.ones((channels, width), jnp.bfloat16)
-    for p in range(sources):
-        part = got_ref[p].astype(jnp.float32)
-        first = (p % ch_count * (sources // ch_count) + p // ch_count) * rows
-        for h in range(W // LANES):
-            flat[h, first : first + rows, :] = part[:, LANES * h : LANES * (h + 1)]
-    for j in range(some):
-        for h in range(W // LANES):
-            part = flat[h, pl.ds(j, sources * own, stride=some), :]
-            first = W * j + LANES * h
-            cols = slice(first, first + LANES)
-            out_ref[:, cols] = (part * gate_s[:, cols].astype(jnp.float32)).astype(jnp.bfloat16)
+    copies = []
+    for m in range(ch_count):
+        here = slice(m * channels, (m + 1) * channels)
+        for k in range(sources // ch_count):
+            part = got_ref[k * ch_count + m].astype(jnp.float32)
+            first = m * channels * some + k * rows
+            for h in range(W // LANES):
+                flat[h, first : first + rows, :] = part[:, LANES * h : LANES * (h + 1)]
+        for j in range(some):
+            for h in range(W // LANES):
+                part = flat[h, pl.ds(m * channels * some + j, channels, stride=some), :]
+                first = W * j + LANES * h
+                cols = slice(first, first + LANES)
+                stage[here, cols] = (part * gate_s[here, cols].astype(jnp.float32)).astype(jnp.bfloat16)
+        copies.append(pltpu.make_async_copy(stage.at[here], out_ref.at[here], sems.at[m]))
+        copies[m].start()
+    for copy in copies:
+        copy.wait()
 
 
 def unpack(got, gates, own, ch_count):
@@ -320,10 +326,12 @@
         functools.partial(unpack_kernel, own),
         out_shape=jax.ShapeDtypeStruct(shape, jnp.bfloat16),
         in_specs=[whole_vmem()] * (1 + len(gates)),
-        out_specs=whole_vmem(),
+        out_specs=in_hbm(),
         scratch_shapes=[
             pltpu.VMEM((W // LANES, sources * rows, LANES), jnp.float32),
             pltpu.VMEM(shape, jnp.bfloat16),
+            pltpu.VMEM(shape, jnp.bfloat16),
+            pltpu.SemaphoreType.DMA((ch_count,)),
         ],
         compiler_params=pltpu.CompilerParams(vmem_limit_bytes=24 * 2**20),
         name="unpack",

time: 41.9 us -> 41.5 us (level)
  no operation moved by 1% of the time
where the time goes in v11:
time: 41.5 us; the launch traced here: 41.3 us
  blocking collectives  19.9 us (48%)
  starting transfers between devices  11.6 us (28%)
  Pallas kernels  7.89 us (19%)
  waiting for transfers between devices  1.83 us (4%)
    all_to_all x1, blocking collectives, body(): lax.all_to_all(mixed, ('ctx', 'ch'), split_axis=0, concat_axis=0, tiled=T...  19.9 us
    ppermute x8, starting transfers between devices, swap(): return lax.ppermute(piece, axis, [(i, i ^ d) for i in range(count)])  11.6 us
    pallas_call x1, Pallas kernels, convolve(): pl.pallas_call(functools.partial(conv_kernel, own, near, ch_count, parts)...  2.61 us
    pallas_call x1, Pallas kernels, pack(): pl.pallas_call(functools.partial(pack_kernel, own, blocks, group, ch_coun...  2.18 us
    pallas_call x1, Pallas kernels, make_tables(): pl.pallas_call(functools.partial(tables_kernel, own), out_shape=[jax.Shap...  2.09 us
    ppermute x8, waiting for transfers between devices, swap(): return lax.ppermute(piece, axis, [(i, i ^ d) for i in range(count)])  1.83 us
    pallas_call x1, Pallas kernels, unpack(): pl.pallas_call(functools.partial(unpack_kernel, own), out_shape=jax.Shape...  1.01 us
  transfers between devices with their start and end apart: 8, of which 2 were waited for; matrix products, arithmetic and copies ran while one was open for 0% of the time, Pallas kernels for 11%

profile of v11, /device:TPU:1, one launch (start us, length us, event | category | flops | bytes accessed | tf_op | source)
XLA Modules:
  0.0 41.3 jit_solution(462994908021196556)
XLA Ops:
  0.0 2.2 %pack.1 = (bf16[224,256]{1,0:T(8,128)(2,1)S(1)}, bf16[224,256]{1,0:T(8,128)(2,1)S(1)}, bf16[224,256]{1,0:T(8,128)(2,1)S(1)}, bf16[224,256]{1,0:T(8,128)(2,1)S(1)...) custom-call(bf16[32,8192]{1,0:T(8,128)(2,1)} %pre_ref.1, ...), custom_call_target="tpu_custom_call" | custom-call | tf_op jit(solution)/shard_map/pack/pallas_call | solution.py:115
  2.2 2.1 %collective-permute-start = (bf16[224,256]{1,0:T(8,128)(2,1)S(1)}, bf16[224,256]{1,0:T(8,128)(2,1)S(1)}, u32[]{:S(2)}, u32[]{:S(2)}) collective-permute-start(bf16[224,256]{1,0:T(8,128)(2,1)S(1)} %get-tuple-element.29), channel_id=1, source_target_pairs={{0,16},{4,20},{8,24},{12,28},{16,0},{20,4},{24,8},{28,12},{1,17},{... | collective-permute-start | bytes 344072 | tf_op jit(solution)/shard_map/ppermute | solution.py:149
  4.3 1.2 %collective-permute-start.1 = (bf16[224,256]{1,0:T(8,128)(2,1)S(1)}, bf16[224,256]{1,0:T(8,128)(2,1)S(1)}, u32[]{:S(2)}, u32[]{:S(2)}) collective-permute-start(bf16[224,256]{1,0:T(8,128)(2,1)S(1)} %get-tuple-element.30), channel_id=1, source_target_pairs={{0,24},{4,28},{8,16},{12,20},{16,8},{20,12},{24,0},{28,4},{1,25},{... | collective-permute-start | bytes 344072 | tf_op jit(solution)/shard_map/ppermute | solution.py:149
  5.5 0.1 collective-permute-start.2
  5.6 1.4 %collective-permute-start.7 = (bf16[32,2048]{1,0:T(8,128)(2,1)S(1)}, bf16[32,2048]{1,0:T(8,128)(2,1)S(1)}, u32[]{:S(2)}, u32[]{:S(2)}) collective-permute-start(bf16[32,2048]{1,0:T(8,128)(2,1)S(1)} %get-tuple-element.47), channel_id=1, source_target_pairs={{0,1},{1,0},{2,3},{3,2},{4,5},{5,4},{6,7},{7,6},{8,9},{9,8},{10,11... | collective-permute-start | bytes 393224 | tf_op jit(solution)/shard_map/ppermute | solution.py:149
  7.0 3.8 %collective-permute-start.3 = (bf16[224,256]{1,0:T(8,128)(2,1)S(1)}, bf16[224,256]{1,0:T(8,128)(2,1)S(1)}, u32[]{:S(2)}, u32[]{:S(2)}) collective-permute-start(bf16[224,256]{1,0:T(8,128)(2,1)S(1)} %get-tuple-element.32), channel_id=1, source_target_pairs={{0,28},{4,24},{8,20},{12,16},{16,12},{20,8},{24,4},{28,0},{1,29},{... | collective-permute-start | bytes 344072 | tf_op jit(solution)/shard_map/ppermute | solution.py:149
  10.9 0.0 collective-permute-done.rest_1_
  10.9 0.2 collective-permute-start.4
  11.0 0.0 collective-permute-done.1.rest_2_
  11.0 1.2 %collective-permute-start.5 = (bf16[224,256]{1,0:T(8,128)(2,1)S(1)}, bf16[224,256]{1,0:T(8,128)(2,1)S(1)}, u32[]{:S(2)}, u32[]{:S(2)}) collective-permute-start(bf16[224,256]{1,0:T(8,128)(2,1)S(1)} %get-tuple-element.34), channel_id=1, source_target_pairs={{0,20},{4,16},{8,28},{12,24},{16,4},{20,0},{24,12},{28,8},{1,21},{... | collective-permute-start | bytes 344072 | tf_op jit(solution)/shard_map/ppermute | solution.py:149
  12.2 0.0 collective-permute-done.2.rest_3_
  12.2 0.0 copy-start
  12.2 1.6 %collective-permute-start.6 = (bf16[224,256]{1,0:T(8,128)(2,1)S(1)}, bf16[224,256]{1,0:T(8,128)(2,1)S(1)}, u32[]{:S(2)}, u32[]{:S(2)}) collective-permute-start(bf16[224,256]{1,0:T(8,128)(2,1)S(1)} %get-tuple-element.35), channel_id=1, source_target_pairs={{0,4},{4,0},{8,12},{12,8},{16,20},{20,16},{24,28},{28,24},{1,5},{5... | collective-permute-start | bytes 344072 | tf_op jit(solution)/shard_map/ppermute | solution.py:149
  13.8 0.0 copy-done
  13.8 2.1 %make_tables.1 = (bf16[512,256]{1,0:T(8,128)(2,1)S(1)}, bf16[256,512]{1,0:T(8,128)(2,1)S(1)}, bf16[512,512]{1,0:T(8,128)(2,1)S(1)}, bf16[512,512]{1,0:T(8,128)(2,1)S(1)}, f32[288,512]{1,0:T(8,128)S(1)}) custom-call(f32[32]{0:T(128)S(1)} %copy-done, f32[512,256]{1,0:T(8,128)} %constant.8.clone.rest_0_, f32[256,512]{1,0:T(8,128)} %constant.9.clone.rest_1_, ...), custom_call_target="tpu_custom_call" | custom-call | tf_op jit(solution)/shard_map/make_tables/pallas_call | solution.py:185
  15.9 0.0 collective-permute-done.3.rest_4_
  16.0 0.7 %collective-permute-done.4.rest_5_ = bf16[224,256]{1,0:T(8,128)(2,1)S(1)} collective-permute-done((bf16[224,256]{1,0:T(8,128)(2,1)S(1)}, bf16[224,256]{1,0:T(8,128)(2,1)S(1)}, u32[]{:S(2)}, u32[]{:S(2)}) %collective-permute-start.4) | collective-permute-done | bytes 114720 | tf_op jit(solution)/shard_map/ppermute | solution.py:149
  16.7 1.1 %collective-permute-done.5.rest_6_ = bf16[224,256]{1,0:T(8,128)(2,1)S(1)} collective-permute-done((bf16[224,256]{1,0:T(8,128)(2,1)S(1)}, bf16[224,256]{1,0:T(8,128)(2,1)S(1)}, u32[]{:S(2)}, u32[]{:S(2)}) %collective-permute-start.5) | collective-permute-done | bytes 114720 | tf_op jit(solution)/shard_map/ppermute | solution.py:149
  17.8 0.0 collective-permute-done.6.rest_7_
  17.8 2.6 %convolve.1 = bf16[32,32,256]{2,1,0:T(8,128)(2,1)S(1)} custom-call(bf16[224,256]{1,0:T(8,128)(2,1)S(1)} %get-tuple-element.28.rest_0_, bf16[224,256]{1,0:T(8,128)(2,1)S(1)} %collective-permute-done.rest_1_, bf16[224,256]{1,0:T(8,128)(2,1)S(1)} %collective-permute-done.1.rest_2_, bf16[224,256]{1,0:T(8,128)(2,1)S(1)} %collective-permute-done.2.rest_3_, ...), custom_call_target="tpu_custom_call" | custom-call | flops 65536 | bytes 262144 | tf_op jit(solution)/shard_map/convolve/pallas_call | solution.py:270
  20.4 0.0 collective-permute-done.7.rest_1_
  20.4 19.9 %all_to_all.5.got_ref = bf16[32,32,256]{2,1,0:T(8,128)(2,1)S(1)} all-to-all(bf16[32,32,256]{2,1,0:T(8,128)(2,1)S(1)} %convolve.1), channel_id=1, replica_groups=mesh['ctx'=8,'ch'=4] {'ctx','ch'}, dimensions={0} | all-to-all | bytes 1048576 | tf_op jit(solution)/shard_map/all_to_all | solution.py:354
  40.3 1.0 %unpack.1 = bf16[128,2048]{1,0:T(8,128)(2,1)} custom-call(bf16[32,32,256]{2,1,0:T(8,128)(2,1)S(1)} %all_to_all.5.got_ref, bf16[32,2048]{1,0:T(8,128)(2,1)S(1)} %get-tuple-element.49.rest_0_, bf16[32,2048]{1,0:T(8,128)(2,1)S(1)} %collective-permute-done.7.rest_1_), custom_call_target="tpu_custom_call" | custom-call | tf_op jit(solution)/shard_map/unpack/pallas_call | solution.py:325
Async XLA Ops:
  2.2 8.7 %collective-permute-start = (bf16[224,256]{1,0:T(8,128)(2,1)S(1)}, bf16[224,256]{1,0:T(8,128)(2,1)S(1)}, u32[]{:S(2)}, u32[]{:S(2)}) collective-permute-start(bf16[224,256]{1,0:T(8,128)(2,1)S(1)} %get-tuple-element.29), channel_id=1, source_target_pairs={{0,16},{4,20},{8,24},{12,28},{16,0},{20,4},{24,8},{28,12},{1,17},{... | collective-permute-start | bytes 344072 | tf_op jit(solution)/shard_map/ppermute | solution.py:149
  4.3 6.7 %collective-permute-start.1 = (bf16[224,256]{1,0:T(8,128)(2,1)S(1)}, bf16[224,256]{1,0:T(8,128)(2,1)S(1)}, u32[]{:S(2)}, u32[]{:S(2)}) collective-permute-start(bf16[224,256]{1,0:T(8,128)(2,1)S(1)} %get-tuple-element.30), channel_id=1, source_target_pairs={{0,24},{4,28},{8,16},{12,20},{16,8},{20,12},{24,0},{28,4},{1,25},{... | collective-permute-start | bytes 344072 | tf_op jit(solution)/shard_map/ppermute | solution.py:149
  5.5 6.8 %collective-permute-start.2 = (bf16[224,256]{1,0:T(8,128)(2,1)S(1)}, bf16[224,256]{1,0:T(8,128)(2,1)S(1)}, u32[]{:S(2)}, u32[]{:S(2)}) collective-permute-start(bf16[224,256]{1,0:T(8,128)(2,1)S(1)} %get-tuple-element.31), channel_id=1, source_target_pairs={{0,8},{4,12},{8,0},{12,4},{16,24},{20,28},{24,16},{28,20},{1,9},{5... | collective-permute-start | bytes 344072 | tf_op jit(solution)/shard_map/ppermute | solution.py:149
  5.6 14.8 %collective-permute-start.7 = (bf16[32,2048]{1,0:T(8,128)(2,1)S(1)}, bf16[32,2048]{1,0:T(8,128)(2,1)S(1)}, u32[]{:S(2)}, u32[]{:S(2)}) collective-permute-start(bf16[32,2048]{1,0:T(8,128)(2,1)S(1)} %get-tuple-element.47), channel_id=1, source_target_pairs={{0,1},{1,0},{2,3},{3,2},{4,5},{5,4},{6,7},{7,6},{8,9},{9,8},{10,11... | collective-permute-start | bytes 393224 | tf_op jit(solution)/shard_map/ppermute | solution.py:149
  7.0 8.9 %collective-permute-start.3 = (bf16[224,256]{1,0:T(8,128)(2,1)S(1)}, bf16[224,256]{1,0:T(8,128)(2,1)S(1)}, u32[]{:S(2)}, u32[]{:S(2)}) collective-permute-start(bf16[224,256]{1,0:T(8,128)(2,1)S(1)} %get-tuple-element.32), channel_id=1, source_target_pairs={{0,28},{4,24},{8,20},{12,16},{16,12},{20,8},{24,4},{28,0},{1,29},{... | collective-permute-start | bytes 344072 | tf_op jit(solution)/shard_map/ppermute | solution.py:149
  10.9 5.8 %collective-permute-start.4 = (bf16[224,256]{1,0:T(8,128)(2,1)S(1)}, bf16[224,256]{1,0:T(8,128)(2,1)S(1)}, u32[]{:S(2)}, u32[]{:S(2)}) collective-permute-start(bf16[224,256]{1,0:T(8,128)(2,1)S(1)} %get-tuple-element.33), channel_id=1, source_target_pairs={{0,12},{4,8},{8,4},{12,0},{16,28},{20,24},{24,20},{28,16},{1,13},{... | collective-permute-start | bytes 344072 | tf_op jit(solution)/shard_map/ppermute | solution.py:149
  11.0 6.7 %collective-permute-start.5 = (bf16[224,256]{1,0:T(8,128)(2,1)S(1)}, bf16[224,256]{1,0:T(8,128)(2,1)S(1)}, u32[]{:S(2)}, u32[]{:S(2)}) collective-permute-start(bf16[224,256]{1,0:T(8,128)(2,1)S(1)} %get-tuple-element.34), channel_id=1, source_target_pairs={{0,20},{4,16},{8,28},{12,24},{16,4},{20,0},{24,12},{28,8},{1,21},{... | collective-permute-start | bytes 344072 | tf_op jit(solution)/shard_map/ppermute | solution.py:149
  12.2 1.6 %copy-start = (f32[32]{0:T(128)S(1)}, f32[32]{0:T(128)}, u32[]{:S(2)}) copy-start(f32[32]{0:T(128)} %skip_ref) | copy-start | bytes 388
  12.2 5.5 %collective-permute-start.6 = (bf16[224,256]{1,0:T(8,128)(2,1)S(1)}, bf16[224,256]{1,0:T(8,128)(2,1)S(1)}, u32[]{:S(2)}, u32[]{:S(2)}) collective-permute-start(bf16[224,256]{1,0:T(8,128)(2,1)S(1)} %get-tuple-element.35), channel_id=1, source_target_pairs={{0,4},{4,0},{8,12},{12,8},{16,20},{20,16},{24,28},{28,24},{1,5},{5... | collective-permute-start | bytes 344072 | tf_op jit(solution)/shard_map/ppermute | solution.py:149

commit v12 on v11

--- a/solution.py
+++ b/solution.py
@@ -1,4 +1,5 @@
 import functools
+import math
 
 import jax
 import jax.numpy as jnp
@@ -137,12 +138,9 @@
 
 def partner_order(count):
     corners = [d for d in range(1, count) if bin(d >> 1).count("1") > 1]
-    straight = [d for d in range(count - 1, 1, -1) if bin(d >> 1).count("1") == 1 and d % 2 == 0]
-    order = [0]
-    for n in range(max(len(corners), len(straight))):
-        order += straight[n : n + 1] + corners[n : n + 1]
-    order += [d for d in range(2, count) if d not in order]
-    return order + [1]
+    straight = [d for d in range(2, count, 2) if d not in corners]
+    order = [0] + corners[:1] + straight + corners[1:]
+    return order + [d for d in range(2, count) if d not in order] + [1]
 
 
 def swap(piece, axis, count, d):
@@ -204,6 +202,7 @@
     outer_ref, back_ref, ahead, rear, turns_ref, out_ref, x_all, r_all, z_all = rest[parts:]
     blocks = parts * near
     length = blocks * W
+    chunk = math.gcd(blocks, CHUNK)
     me = lax.axis_index("ctx")
     order = partner_order(parts)
     for d, got_ref in zip(order, got_refs):
@@ -214,11 +213,11 @@
     def dot(left, right):
         return jnp.dot(left, right, preferred_element_type=jnp.float32)
 
-    for first in range(0, blocks, CHUNK):
-        here = slice(first, first + CHUNK)
-        there = slice(blocks + first, blocks + first + CHUNK)
+    for first in range(0, blocks, chunk):
+        here = slice(first, first + chunk)
+        there = slice(blocks + first, blocks + first + chunk)
         both = dot(jnp.concatenate([outer_ref[here, :], outer_ref[there, :]], 0), x_all[...])
-        real, imag = both[0:CHUNK, :], both[CHUNK:, :]
+        real, imag = both[0:chunk, :], both[chunk:, :]
         turn_cos, turn_sin = turns_ref[here, 0:W], turns_ref[here, W:]
         rows = []
         for c in range(own + 1):
@@ -226,17 +225,17 @@
             pair = [re * turn_cos + im * turn_sin, im * turn_cos - re * turn_sin]
             rows.append(jnp.concatenate(pair, 1).astype(jnp.bfloat16))
         spectrum = dot(jnp.concatenate(rows, 0), ahead[...])
-        filt_re = spectrum[CHUNK * own :, 0:W] * (1.0 / length)
-        filt_im = spectrum[CHUNK * own :, W:] * (1.0 / length)
+        filt_re = spectrum[chunk * own :, 0:W] * (1.0 / length)
+        filt_im = spectrum[chunk * own :, W:] * (1.0 / length)
         rows = []
         for c in range(own):
-            part = spectrum[CHUNK * c : CHUNK * (c + 1), :]
+            part = spectrum[chunk * c : chunk * (c + 1), :]
             re, im = part[:, 0:W], part[:, W:]
             pair = [re * filt_re - im * filt_im, re * filt_im + im * filt_re]
             rows.append(jnp.concatenate(pair, 1).astype(jnp.bfloat16))
         middle = dot(jnp.concatenate(rows, 0), rear[...])
         for c in range(own):
-            part = middle[CHUNK * c : CHUNK * (c + 1), :]
+            part = middle[chunk * c : chunk * (c + 1), :]
             re, im = part[:, 0:W], part[:, W:]
             cols = slice(W * c, W * (c + 1))
             r_all[here, cols] = (re * turn_cos - im * turn_sin).astype(jnp.bfloat16)

time: 41.5 us -> 41.5 us (level)
  blocking collectives: 19.9 us -> 20.7 us
  waiting for transfers between devices: 1.83 us -> 1.41 us
    all_to_all x1, blocking collectives: 19.9 us -> 20.7 us  [body(): lax.all_to_all(mixed, ('ctx', 'ch'), split_axis=0, concat_axis=0, tiled=T...]
    ppermute x8, waiting for transfers between devices: 1.83 us -> 1.41 us  [swap(): return lax.ppermute(piece, axis, [(i, i ^ d) for i in range(count)])]
where the time goes in v12:
time: 41.5 us; the launch traced here: 41.3 us
  blocking collectives  20.7 us (50%)
  starting transfers between devices  11.2 us (27%)
  Pallas kernels  7.88 us (19%)
  waiting for transfers between devices  1.41 us (3%)
    all_to_all x1, blocking collectives, body(): lax.all_to_all(mixed, ('ctx', 'ch'), split_axis=0, concat_axis=0, tiled=T...  20.7 us
    ppermute x8, starting transfers between devices, swap(): return lax.ppermute(piece, axis, [(i, i ^ d) for i in range(count)])  11.2 us
    pallas_call x1, Pallas kernels, convolve(): pl.pallas_call(functools.partial(conv_kernel, own, near, ch_count, parts)...  2.6 us
    pallas_call x1, Pallas kernels, pack(): pl.pallas_call(functools.partial(pack_kernel, own, blocks, group, ch_coun...  2.18 us
    pallas_call x1, Pallas kernels, make_tables(): pl.pallas_call(functools.partial(tables_kernel, own), out_shape=[jax.Shap...  2.09 us
    ppermute x8, waiting for transfers between devices, swap(): return lax.ppermute(piece, axis, [(i, i ^ d) for i in range(count)])  1.41 us
    pallas_call x1, Pallas kernels, unpack(): pl.pallas_call(functools.partial(unpack_kernel, own), out_shape=jax.Shape...  1.01 us
  transfers between devices with their start and end apart: 8, of which 2 were waited for; matrix products, arithmetic and copies ran while one was open for 0% of the time, Pallas kernels for 11%

profile of v12, /device:TPU:1, one launch (start us, length us, event | category | flops | bytes accessed | tf_op | source)
XLA Modules:
  0.0 41.3 jit_solution(2650998924716766509)
XLA Ops:
  0.0 2.2 %pack.1 = (bf16[224,256]{1,0:T(8,128)(2,1)S(1)}, bf16[224,256]{1,0:T(8,128)(2,1)S(1)}, bf16[224,256]{1,0:T(8,128)(2,1)S(1)}, bf16[224,256]{1,0:T(8,128)(2,1)S(1)...) custom-call(bf16[32,8192]{1,0:T(8,128)(2,1)} %pre_ref.1, ...), custom_call_target="tpu_custom_call" | custom-call | tf_op jit(solution)/shard_map/pack/pallas_call | solution.py:116
  2.2 3.1 %collective-permute-start = (bf16[224,256]{1,0:T(8,128)(2,1)S(1)}, bf16[224,256]{1,0:T(8,128)(2,1)S(1)}, u32[]{:S(2)}, u32[]{:S(2)}) collective-permute-start(bf16[224,256]{1,0:T(8,128)(2,1)S(1)} %get-tuple-element.29), channel_id=1, source_target_pairs={{0,24},{4,28},{8,16},{12,20},{16,8},{20,12},{24,0},{28,4},{1,25},{... | collective-permute-start | bytes 344072 | tf_op jit(solution)/shard_map/ppermute | solution.py:147
  5.2 0.3 collective-permute-start.1
  5.5 0.1 collective-permute-start.2
  5.6 1.4 %collective-permute-start.7 = (bf16[32,2048]{1,0:T(8,128)(2,1)S(1)}, bf16[32,2048]{1,0:T(8,128)(2,1)S(1)}, u32[]{:S(2)}, u32[]{:S(2)}) collective-permute-start(bf16[32,2048]{1,0:T(8,128)(2,1)S(1)} %get-tuple-element.47), channel_id=1, source_target_pairs={{0,1},{1,0},{2,3},{3,2},{4,5},{5,4},{6,7},{7,6},{8,9},{9,8},{10,11... | collective-permute-start | bytes 393224 | tf_op jit(solution)/shard_map/ppermute | solution.py:147
  7.0 3.8 %collective-permute-start.3 = (bf16[224,256]{1,0:T(8,128)(2,1)S(1)}, bf16[224,256]{1,0:T(8,128)(2,1)S(1)}, u32[]{:S(2)}, u32[]{:S(2)}) collective-permute-start(bf16[224,256]{1,0:T(8,128)(2,1)S(1)} %get-tuple-element.32), channel_id=1, source_target_pairs={{0,28},{4,24},{8,20},{12,16},{16,12},{20,8},{24,4},{28,0},{1,29},{... | collective-permute-start | bytes 344072 | tf_op jit(solution)/shard_map/ppermute | solution.py:147
  10.9 0.0 collective-permute-done.rest_1_
  10.9 0.9 %collective-permute-start.4 = (bf16[224,256]{1,0:T(8,128)(2,1)S(1)}, bf16[224,256]{1,0:T(8,128)(2,1)S(1)}, u32[]{:S(2)}, u32[]{:S(2)}) collective-permute-start(bf16[224,256]{1,0:T(8,128)(2,1)S(1)} %get-tuple-element.33), channel_id=1, source_target_pairs={{0,12},{4,8},{8,4},{12,0},{16,28},{20,24},{24,20},{28,16},{1,13},{... | collective-permute-start | bytes 344072 | tf_op jit(solution)/shard_map/ppermute | solution.py:147
  11.8 0.0 collective-permute-done.1.rest_2_
  11.8 0.2 collective-permute-start.5
  12.0 0.0 collective-permute-done.2.rest_3_
  12.0 0.0 copy-start
  12.0 1.4 %collective-permute-start.6 = (bf16[224,256]{1,0:T(8,128)(2,1)S(1)}, bf16[224,256]{1,0:T(8,128)(2,1)S(1)}, u32[]{:S(2)}, u32[]{:S(2)}) collective-permute-start(bf16[224,256]{1,0:T(8,128)(2,1)S(1)} %get-tuple-element.35), channel_id=1, source_target_pairs={{0,4},{4,0},{8,12},{12,8},{16,20},{20,16},{24,28},{28,24},{1,5},{5... | collective-permute-start | bytes 344072 | tf_op jit(solution)/shard_map/ppermute | solution.py:147
  13.4 0.0 copy-done
  13.4 2.1 %make_tables.1 = (bf16[512,256]{1,0:T(8,128)(2,1)S(1)}, bf16[256,512]{1,0:T(8,128)(2,1)S(1)}, bf16[512,512]{1,0:T(8,128)(2,1)S(1)}, bf16[512,512]{1,0:T(8,128)(2,1)S(1)}, f32[288,512]{1,0:T(8,128)S(1)}) custom-call(f32[32]{0:T(128)S(1)} %copy-done, f32[512,256]{1,0:T(8,128)} %constant.8.clone.rest_0_, f32[256,512]{1,0:T(8,128)} %constant.9.clone.rest_1_, ...), custom_call_target="tpu_custom_call" | custom-call | tf_op jit(solution)/shard_map/make_tables/pallas_call | solution.py:183
  15.5 0.0 collective-permute-done.3.rest_4_
  15.5 1.0 %collective-permute-done.4.rest_5_ = bf16[224,256]{1,0:T(8,128)(2,1)S(1)} collective-permute-done((bf16[224,256]{1,0:T(8,128)(2,1)S(1)}, bf16[224,256]{1,0:T(8,128)(2,1)S(1)}, u32[]{:S(2)}, u32[]{:S(2)}) %collective-permute-start.4) | collective-permute-done | bytes 114720 | tf_op jit(solution)/shard_map/ppermute | solution.py:147
  16.6 0.4 collective-permute-done.5.rest_6_
  16.9 0.0 collective-permute-done.6.rest_7_
  16.9 2.6 %convolve.1 = bf16[32,32,256]{2,1,0:T(8,128)(2,1)S(1)} custom-call(bf16[224,256]{1,0:T(8,128)(2,1)S(1)} %get-tuple-element.28.rest_0_, bf16[224,256]{1,0:T(8,128)(2,1)S(1)} %collective-permute-done.rest_1_, bf16[224,256]{1,0:T(8,128)(2,1)S(1)} %collective-permute-done.1.rest_2_, bf16[224,256]{1,0:T(8,128)(2,1)S(1)} %collective-permute-done.2.rest_3_, ...), custom_call_target="tpu_custom_call" | custom-call | flops 65536 | bytes 262144 | tf_op jit(solution)/shard_map/convolve/pallas_call | solution.py:269
  19.6 0.0 collective-permute-done.7.rest_1_
  19.6 20.7 %all_to_all.5.got_ref = bf16[32,32,256]{2,1,0:T(8,128)(2,1)S(1)} all-to-all(bf16[32,32,256]{2,1,0:T(8,128)(2,1)S(1)} %convolve.1), channel_id=1, replica_groups=mesh['ctx'=8,'ch'=4] {'ctx','ch'}, dimensions={0} | all-to-all | bytes 1048576 | tf_op jit(solution)/shard_map/all_to_all | solution.py:353
  40.3 1.0 %unpack.1 = bf16[128,2048]{1,0:T(8,128)(2,1)} custom-call(bf16[32,32,256]{2,1,0:T(8,128)(2,1)S(1)} %all_to_all.5.got_ref, bf16[32,2048]{1,0:T(8,128)(2,1)S(1)} %get-tuple-element.49.rest_0_, bf16[32,2048]{1,0:T(8,128)(2,1)S(1)} %collective-permute-done.7.rest_1_), custom_call_target="tpu_custom_call" | custom-call | tf_op jit(solution)/shard_map/unpack/pallas_call | solution.py:324
Async XLA Ops:
  2.2 8.7 %collective-permute-start = (bf16[224,256]{1,0:T(8,128)(2,1)S(1)}, bf16[224,256]{1,0:T(8,128)(2,1)S(1)}, u32[]{:S(2)}, u32[]{:S(2)}) collective-permute-start(bf16[224,256]{1,0:T(8,128)(2,1)S(1)} %get-tuple-element.29), channel_id=1, source_target_pairs={{0,24},{4,28},{8,16},{12,20},{16,8},{20,12},{24,0},{28,4},{1,25},{... | collective-permute-start | bytes 344072 | tf_op jit(solution)/shard_map/ppermute | solution.py:147
  5.2 6.5 %collective-permute-start.1 = (bf16[224,256]{1,0:T(8,128)(2,1)S(1)}, bf16[224,256]{1,0:T(8,128)(2,1)S(1)}, u32[]{:S(2)}, u32[]{:S(2)}) collective-permute-start(bf16[224,256]{1,0:T(8,128)(2,1)S(1)} %get-tuple-element.30), channel_id=1, source_target_pairs={{0,8},{4,12},{8,0},{12,4},{16,24},{20,28},{24,16},{28,20},{1,9},{5... | collective-permute-start | bytes 344072 | tf_op jit(solution)/shard_map/ppermute | solution.py:147
  5.5 6.5 %collective-permute-start.2 = (bf16[224,256]{1,0:T(8,128)(2,1)S(1)}, bf16[224,256]{1,0:T(8,128)(2,1)S(1)}, u32[]{:S(2)}, u32[]{:S(2)}) collective-permute-start(bf16[224,256]{1,0:T(8,128)(2,1)S(1)} %get-tuple-element.31), channel_id=1, source_target_pairs={{0,16},{4,20},{8,24},{12,28},{16,0},{20,4},{24,8},{28,12},{1,17},{... | collective-permute-start | bytes 344072 | tf_op jit(solution)/shard_map/ppermute | solution.py:147
  5.6 13.9 %collective-permute-start.7 = (bf16[32,2048]{1,0:T(8,128)(2,1)S(1)}, bf16[32,2048]{1,0:T(8,128)(2,1)S(1)}, u32[]{:S(2)}, u32[]{:S(2)}) collective-permute-start(bf16[32,2048]{1,0:T(8,128)(2,1)S(1)} %get-tuple-element.47), channel_id=1, source_target_pairs={{0,1},{1,0},{2,3},{3,2},{4,5},{5,4},{6,7},{7,6},{8,9},{9,8},{10,11... | collective-permute-start | bytes 393224 | tf_op jit(solution)/shard_map/ppermute | solution.py:147
  7.0 8.5 %collective-permute-start.3 = (bf16[224,256]{1,0:T(8,128)(2,1)S(1)}, bf16[224,256]{1,0:T(8,128)(2,1)S(1)}, u32[]{:S(2)}, u32[]{:S(2)}) collective-permute-start(bf16[224,256]{1,0:T(8,128)(2,1)S(1)} %get-tuple-element.32), channel_id=1, source_target_pairs={{0,28},{4,24},{8,20},{12,16},{16,12},{20,8},{24,4},{28,0},{1,29},{... | collective-permute-start | bytes 344072 | tf_op jit(solution)/shard_map/ppermute | solution.py:147
  10.9 5.7 %collective-permute-start.4 = (bf16[224,256]{1,0:T(8,128)(2,1)S(1)}, bf16[224,256]{1,0:T(8,128)(2,1)S(1)}, u32[]{:S(2)}, u32[]{:S(2)}) collective-permute-start(bf16[224,256]{1,0:T(8,128)(2,1)S(1)} %get-tuple-element.33), channel_id=1, source_target_pairs={{0,12},{4,8},{8,4},{12,0},{16,28},{20,24},{24,20},{28,16},{1,13},{... | collective-permute-start | bytes 344072 | tf_op jit(solution)/shard_map/ppermute | solution.py:147
  11.8 5.1 %collective-permute-start.5 = (bf16[224,256]{1,0:T(8,128)(2,1)S(1)}, bf16[224,256]{1,0:T(8,128)(2,1)S(1)}, u32[]{:S(2)}, u32[]{:S(2)}) collective-permute-start(bf16[224,256]{1,0:T(8,128)(2,1)S(1)} %get-tuple-element.34), channel_id=1, source_target_pairs={{0,20},{4,16},{8,28},{12,24},{16,4},{20,0},{24,12},{28,8},{1,21},{... | collective-permute-start | bytes 344072 | tf_op jit(solution)/shard_map/ppermute | solution.py:147
  12.0 1.5 %copy-start = (f32[32]{0:T(128)S(1)}, f32[32]{0:T(128)}, u32[]{:S(2)}) copy-start(f32[32]{0:T(128)} %skip_ref) | copy-start | bytes 388
  12.0 5.0 %collective-permute-start.6 = (bf16[224,256]{1,0:T(8,128)(2,1)S(1)}, bf16[224,256]{1,0:T(8,128)(2,1)S(1)}, u32[]{:S(2)}, u32[]{:S(2)}) collective-permute-start(bf16[224,256]{1,0:T(8,128)(2,1)S(1)} %get-tuple-element.35), channel_id=1, source_target_pairs={{0,4},{4,0},{8,12},{12,8},{16,20},{20,16},{24,28},{28,24},{1,5},{5... | collective-permute-start | bytes 344072 | tf_op jit(solution)/shard_map/ppermute | solution.py:147

commit v13 on v12

--- a/solution.py
+++ b/solution.py
@@ -343,11 +343,15 @@
     own = value.shape[0] // ctx_count
     near = value.shape[1] // W
     got, gates = pack(pre_gate, value, post_gate, filter_taps, ctx_count, ch_count)
+    order = partner_order(ctx_count)
+    got = [got[d] for d in order]
     tables, skip, _ = lax.optimization_barrier((dft_tables(near * ctx_count), skip, got[0]))
-    got = [swap(got[d], "ctx", ctx_count, d) if d else got[d] for d in partner_order(ctx_count)]
+    tables = list(make_tables(skip, *tables, own))
+    half = ctx_count // 2 + 1
+    tables, got[half:] = lax.optimization_barrier((tables, got[half:]))
+    got = [swap(piece, "ctx", ctx_count, d) if d else piece for piece, d in zip(got, order)]
     for d in range(1, ch_count // 2):
         gates[d] = swap(gates[d], "ch", ch_count, d)
-    tables = list(make_tables(skip, *tables, own))
     mixed = convolve(got, tables, own, near, ch_count)
     mixed, gates = lax.optimization_barrier((mixed, gates))
     mixed = lax.all_to_all(mixed, ("ctx", "ch"), split_axis=0, concat_axis=0, tiled=True)

time: 41.5 us -> 41.6 us (level)
  waiting for transfers between devices: 1.41 us -> 4.25 us
  blocking collectives: 20.7 us -> 19.2 us
  starting transfers between devices: 11.2 us -> 10.1 us
    ppermute x8, waiting for transfers between devices: 1.41 us -> 4.25 us  [swap(): return lax.ppermute(piece, axis, [(i, i ^ d) for i in range(count)])]
    all_to_all x1, blocking collectives: 20.7 us -> 19.2 us  [body(): lax.all_to_all(mixed, ('ctx', 'ch'), split_axis=0, concat_axis=0, tiled=T...]
    ppermute x8, starting transfers between devices: 11.2 us -> 10.1 us  [swap(): return lax.ppermute(piece, axis, [(i, i ^ d) for i in range(count)])]
  transfers between devices with their start and end apart: 8 -> 8, of which waited for: 2 -> 3; matrix products, arithmetic and copies ran while one was open for 0% -> 0% of each run, Pallas kernels for 11% -> 11%
where the time goes in v13:
time: 41.6 us; the launch traced here: 41.4 us
  blocking collectives  19.2 us (46%)
  starting transfers between devices  10.1 us (24%)
  Pallas kernels  7.89 us (19%)
  waiting for transfers between devices  4.25 us (10%)
    all_to_all x1, blocking collectives, body(): lax.all_to_all(mixed, ('ctx', 'ch'), split_axis=0, concat_axis=0, tiled=T...  19.2 us
    ppermute x8, starting transfers between devices, swap(): return lax.ppermute(piece, axis, [(i, i ^ d) for i in range(count)])  10.1 us
    ppermute x8, waiting for transfers between devices, swap(): return lax.ppermute(piece, axis, [(i, i ^ d) for i in range(count)])  4.25 us
    pallas_call x1, Pallas kernels, convolve(): pl.pallas_call(functools.partial(conv_kernel, own, near, ch_count, parts)...  2.61 us
    pallas_call x1, Pallas kernels, pack(): pl.pallas_call(functools.partial(pack_kernel, own, blocks, group, ch_coun...  2.18 us
    pallas_call x1, Pallas kernels, make_tables(): pl.pallas_call(functools.partial(tables_kernel, own), out_shape=[jax.Shap...  2.09 us
    pallas_call x1, Pallas kernels, unpack(): pl.pallas_call(functools.partial(unpack_kernel, own), out_shape=jax.Shape...  1.01 us
  transfers between devices with their start and end apart: 8, of which 3 were waited for; matrix products, arithmetic and copies ran while one was open for 0% of the time, Pallas kernels for 11%

profile of v13, /device:TPU:1, one launch (start us, length us, event | category | flops | bytes accessed | tf_op | source)
XLA Modules:
  0.0 41.4 jit_solution(14702580528744650281)
XLA Ops:
  0.0 2.2 %pack.1 = (bf16[224,256]{1,0:T(8,128)(2,1)S(1)}, bf16[224,256]{1,0:T(8,128)(2,1)S(1)}, bf16[224,256]{1,0:T(8,128)(2,1)S(1)}, bf16[224,256]{1,0:T(8,128)(2,1)S(1)...) custom-call(bf16[32,8192]{1,0:T(8,128)(2,1)} %pre_ref.1, ...), custom_call_target="tpu_custom_call" | custom-call | tf_op jit(solution)/shard_map/pack/pallas_call | solution.py:116
  2.2 3.1 %collective-permute-start = (bf16[224,256]{1,0:T(8,128)(2,1)S(1)}, bf16[224,256]{1,0:T(8,128)(2,1)S(1)}, u32[]{:S(2)}, u32[]{:S(2)}) collective-permute-start(bf16[224,256]{1,0:T(8,128)(2,1)S(1)} %get-tuple-element.37), channel_id=1, source_target_pairs={{0,24},{4,28},{8,16},{12,20},{16,8},{20,12},{24,0},{28,4},{1,25},{... | collective-permute-start | bytes 344072 | tf_op jit(solution)/shard_map/ppermute | solution.py:147
  5.2 0.3 collective-permute-start.1
  5.5 0.1 collective-permute-start.2
  5.6 1.4 %collective-permute-start.7 = (bf16[32,2048]{1,0:T(8,128)(2,1)S(1)}, bf16[32,2048]{1,0:T(8,128)(2,1)S(1)}, u32[]{:S(2)}, u32[]{:S(2)}) collective-permute-start(bf16[32,2048]{1,0:T(8,128)(2,1)S(1)} %get-tuple-element.63), channel_id=1, source_target_pairs={{0,1},{1,0},{2,3},{3,2},{4,5},{5,4},{6,7},{7,6},{8,9},{9,8},{10,11... | collective-permute-start | bytes 393224 | tf_op jit(solution)/shard_map/ppermute | solution.py:147
  7.0 0.0 copy-start
  7.0 3.8 %collective-permute-start.3 = (bf16[224,256]{1,0:T(8,128)(2,1)S(1)}, bf16[224,256]{1,0:T(8,128)(2,1)S(1)}, u32[]{:S(2)}, u32[]{:S(2)}) collective-permute-start(bf16[224,256]{1,0:T(8,128)(2,1)S(1)} %get-tuple-element.40), channel_id=1, source_target_pairs={{0,28},{4,24},{8,20},{12,16},{16,12},{20,8},{24,4},{28,0},{1,29},{... | collective-permute-start | bytes 344072 | tf_op jit(solution)/shard_map/ppermute | solution.py:147
  10.9 0.0 copy-done
  10.9 2.1 %make_tables.1 = (bf16[512,256]{1,0:T(8,128)(2,1)S(1)}, bf16[256,512]{1,0:T(8,128)(2,1)S(1)}, bf16[512,512]{1,0:T(8,128)(2,1)S(1)}, bf16[512,512]{1,0:T(8,128)(2,1)S(1)}, f32[288,512]{1,0:T(8,128)S(1)}) custom-call(f32[32]{0:T(128)S(1)} %copy-done, f32[512,256]{1,0:T(8,128)} %constant.8.clone.rest_0_, f32[256,512]{1,0:T(8,128)} %constant.9.clone.rest_1_, ...), custom_call_target="tpu_custom_call" | custom-call | tf_op jit(solution)/shard_map/make_tables/pallas_call | solution.py:183
  13.0 0.0 collective-permute-done.rest_1_
  13.0 0.1 collective-permute-start.4
  13.1 0.0 collective-permute-done.1.rest_2_
  13.1 0.7 %collective-permute-start.5 = (bf16[224,256]{1,0:T(8,128)(2,1)S(1)}, bf16[224,256]{1,0:T(8,128)(2,1)S(1)}, u32[]{:S(2)}, u32[]{:S(2)}) collective-permute-start(bf16[224,256]{1,0:T(8,128)(2,1)S(1)} %get-tuple-element.55), channel_id=1, source_target_pairs={{0,20},{4,16},{8,28},{12,24},{16,4},{20,0},{24,12},{28,8},{1,21},{... | collective-permute-start | bytes 344072 | tf_op jit(solution)/shard_map/ppermute | solution.py:147
  13.8 0.0 collective-permute-done.2.rest_3_
  13.8 0.6 %collective-permute-start.6 = (bf16[224,256]{1,0:T(8,128)(2,1)S(1)}, bf16[224,256]{1,0:T(8,128)(2,1)S(1)}, u32[]{:S(2)}, u32[]{:S(2)}) collective-permute-start(bf16[224,256]{1,0:T(8,128)(2,1)S(1)} %get-tuple-element.56), channel_id=1, source_target_pairs={{0,4},{4,0},{8,12},{12,8},{16,20},{20,16},{24,28},{28,24},{1,5},{5... | collective-permute-start | bytes 344072 | tf_op jit(solution)/shard_map/ppermute | solution.py:147
  14.4 0.3 collective-permute-done.3.rest_4_
  14.7 2.9 %collective-permute-done.4.rest_5_ = bf16[224,256]{1,0:T(8,128)(2,1)S(1)} collective-permute-done((bf16[224,256]{1,0:T(8,128)(2,1)S(1)}, bf16[224,256]{1,0:T(8,128)(2,1)S(1)}, u32[]{:S(2)}, u32[]{:S(2)}) %collective-permute-start.4) | collective-permute-done | bytes 114720 | tf_op jit(solution)/shard_map/ppermute | solution.py:147
  17.6 1.1 %collective-permute-done.5.rest_6_ = bf16[224,256]{1,0:T(8,128)(2,1)S(1)} collective-permute-done((bf16[224,256]{1,0:T(8,128)(2,1)S(1)}, bf16[224,256]{1,0:T(8,128)(2,1)S(1)}, u32[]{:S(2)}, u32[]{:S(2)}) %collective-permute-start.5) | collective-permute-done | bytes 114720 | tf_op jit(solution)/shard_map/ppermute | solution.py:147
  18.6 0.0 collective-permute-done.6.rest_7_
  18.6 2.6 %convolve.1 = bf16[32,32,256]{2,1,0:T(8,128)(2,1)S(1)} custom-call(bf16[224,256]{1,0:T(8,128)(2,1)S(1)} %get-tuple-element.36.rest_0_, bf16[224,256]{1,0:T(8,128)(2,1)S(1)} %collective-permute-done.rest_1_, bf16[224,256]{1,0:T(8,128)(2,1)S(1)} %collective-permute-done.1.rest_2_, bf16[224,256]{1,0:T(8,128)(2,1)S(1)} %collective-permute-done.2.rest_3_, ...), custom_call_target="tpu_custom_call" | custom-call | flops 65536 | bytes 262144 | tf_op jit(solution)/shard_map/convolve/pallas_call | solution.py:269
  21.3 0.0 collective-permute-done.7.rest_1_
  21.3 19.2 %all_to_all.5.got_ref = bf16[32,32,256]{2,1,0:T(8,128)(2,1)S(1)} all-to-all(bf16[32,32,256]{2,1,0:T(8,128)(2,1)S(1)} %convolve.1), channel_id=1, replica_groups=mesh['ctx'=8,'ch'=4] {'ctx','ch'}, dimensions={0} | all-to-all | bytes 1048576 | tf_op jit(solution)/shard_map/all_to_all | solution.py:357
  40.4 1.0 %unpack.1 = bf16[128,2048]{1,0:T(8,128)(2,1)} custom-call(bf16[32,32,256]{2,1,0:T(8,128)(2,1)S(1)} %all_to_all.5.got_ref, bf16[32,2048]{1,0:T(8,128)(2,1)S(1)} %get-tuple-element.65.rest_0_, bf16[32,2048]{1,0:T(8,128)(2,1)S(1)} %collective-permute-done.7.rest_1_), custom_call_target="tpu_custom_call" | custom-call | tf_op jit(solution)/shard_map/unpack/pallas_call | solution.py:324
Async XLA Ops:
  2.2 10.8 %collective-permute-start = (bf16[224,256]{1,0:T(8,128)(2,1)S(1)}, bf16[224,256]{1,0:T(8,128)(2,1)S(1)}, u32[]{:S(2)}, u32[]{:S(2)}) collective-permute-start(bf16[224,256]{1,0:T(8,128)(2,1)S(1)} %get-tuple-element.37), channel_id=1, source_target_pairs={{0,24},{4,28},{8,16},{12,20},{16,8},{20,12},{24,0},{28,4},{1,25},{... | collective-permute-start | bytes 344072 | tf_op jit(solution)/shard_map/ppermute | solution.py:147
  5.2 7.8 %collective-permute-start.1 = (bf16[224,256]{1,0:T(8,128)(2,1)S(1)}, bf16[224,256]{1,0:T(8,128)(2,1)S(1)}, u32[]{:S(2)}, u32[]{:S(2)}) collective-permute-start(bf16[224,256]{1,0:T(8,128)(2,1)S(1)} %get-tuple-element.38), channel_id=1, source_target_pairs={{0,8},{4,12},{8,0},{12,4},{16,24},{20,28},{24,16},{28,20},{1,9},{5... | collective-permute-start | bytes 344072 | tf_op jit(solution)/shard_map/ppermute | solution.py:147
  5.5 8.3 %collective-permute-start.2 = (bf16[224,256]{1,0:T(8,128)(2,1)S(1)}, bf16[224,256]{1,0:T(8,128)(2,1)S(1)}, u32[]{:S(2)}, u32[]{:S(2)}) collective-permute-start(bf16[224,256]{1,0:T(8,128)(2,1)S(1)} %get-tuple-element.39), channel_id=1, source_target_pairs={{0,16},{4,20},{8,24},{12,28},{16,0},{20,4},{24,8},{28,12},{1,17},{... | collective-permute-start | bytes 344072 | tf_op jit(solution)/shard_map/ppermute | solution.py:147
  5.6 15.6 %collective-permute-start.7 = (bf16[32,2048]{1,0:T(8,128)(2,1)S(1)}, bf16[32,2048]{1,0:T(8,128)(2,1)S(1)}, u32[]{:S(2)}, u32[]{:S(2)}) collective-permute-start(bf16[32,2048]{1,0:T(8,128)(2,1)S(1)} %get-tuple-element.63), channel_id=1, source_target_pairs={{0,1},{1,0},{2,3},{3,2},{4,5},{5,4},{6,7},{7,6},{8,9},{9,8},{10,11... | collective-permute-start | bytes 393224 | tf_op jit(solution)/shard_map/ppermute | solution.py:147
  7.0 3.9 %copy-start = (f32[32]{0:T(128)S(1)}, f32[32]{0:T(128)}, u32[]{:S(2)}) copy-start(f32[32]{0:T(128)} %skip_ref) | copy-start | bytes 388
  7.0 7.6 %collective-permute-start.3 = (bf16[224,256]{1,0:T(8,128)(2,1)S(1)}, bf16[224,256]{1,0:T(8,128)(2,1)S(1)}, u32[]{:S(2)}, u32[]{:S(2)}) collective-permute-start(bf16[224,256]{1,0:T(8,128)(2,1)S(1)} %get-tuple-element.40), channel_id=1, source_target_pairs={{0,28},{4,24},{8,20},{12,16},{16,12},{20,8},{24,4},{28,0},{1,29},{... | collective-permute-start | bytes 344072 | tf_op jit(solution)/shard_map/ppermute | solution.py:147
  13.0 4.6 %collective-permute-start.4 = (bf16[224,256]{1,0:T(8,128)(2,1)S(1)}, bf16[224,256]{1,0:T(8,128)(2,1)S(1)}, u32[]{:S(2)}, u32[]{:S(2)}) collective-permute-start(bf16[224,256]{1,0:T(8,128)(2,1)S(1)} %get-tuple-element.54), channel_id=1, source_target_pairs={{0,12},{4,8},{8,4},{12,0},{16,28},{20,24},{24,20},{28,16},{1,13},{... | collective-permute-start | bytes 344072 | tf_op jit(solution)/shard_map/ppermute | solution.py:147
  13.1 5.6 %collective-permute-start.5 = (bf16[224,256]{1,0:T(8,128)(2,1)S(1)}, bf16[224,256]{1,0:T(8,128)(2,1)S(1)}, u32[]{:S(2)}, u32[]{:S(2)}) collective-permute-start(bf16[224,256]{1,0:T(8,128)(2,1)S(1)} %get-tuple-element.55), channel_id=1, source_target_pairs={{0,20},{4,16},{8,28},{12,24},{16,4},{20,0},{24,12},{28,8},{1,21},{... | collective-permute-start | bytes 344072 | tf_op jit(solution)/shard_map/ppermute | solution.py:147
  13.8 4.8 %collective-permute-start.6 = (bf16[224,256]{1,0:T(8,128)(2,1)S(1)}, bf16[224,256]{1,0:T(8,128)(2,1)S(1)}, u32[]{:S(2)}, u32[]{:S(2)}) collective-permute-start(bf16[224,256]{1,0:T(8,128)(2,1)S(1)} %get-tuple-element.56), channel_id=1, source_target_pairs={{0,4},{4,0},{8,12},{12,8},{16,20},{20,16},{24,28},{28,24},{1,5},{5... | collective-permute-start | bytes 344072 | tf_op jit(solution)/shard_map/ppermute | solution.py:147

commit v14 on v12

--- a/solution.py
+++ b/solution.py
@@ -49,8 +49,8 @@
 
 
 def pack_kernel(own, blocks, group, ch_count, parts, pre_ref, val_ref, taps_ref, post_ref, *rest):
-    out_refs, gate_refs = rest[:parts], rest[parts : parts + ch_count // 2]
-    pre_s, val_s, taps_s, post_s, natural, natural_taps, natural_gate, stage, in_sems = rest[parts + ch_count // 2 :]
+    even_refs, odd_ref, gate_refs = rest[: parts // 2], rest[parts // 2], rest[parts // 2 + 1 : parts // 2 + 1 + ch_count]
+    pre_s, val_s, taps_s, natural, natural_taps, stage, in_sems, gate_sems = rest[parts // 2 + 1 + ch_count :]
     channels = own * parts
     some = min(TILE, channels)
     rows = own * blocks
@@ -61,8 +61,13 @@
         loads.append(pltpu.make_async_copy(pre_ref.at[here], pre_s.at[here], in_sems.at[g, 0]))
         loads.append(pltpu.make_async_copy(val_ref.at[here], val_s.at[here], in_sems.at[g, 1]))
     taps_load = pltpu.make_async_copy(taps_ref, taps_s, in_sems.at[channels // some, 0])
-    gate_load = pltpu.make_async_copy(post_ref, post_s, in_sems.at[channels // some, 1])
-    for copy in loads[:2] + [taps_load] + loads[2:] + [gate_load]:
+    place = lax.axis_index("ch")
+    piece = blocks // ch_count * W
+    gates = []
+    for d in range(ch_count):
+        cols = pl.ds(pl.multiple_of(jnp.bitwise_xor(place, d) * piece, LANES), piece)
+        gates.append(pltpu.make_async_copy(post_ref.at[:, cols], gate_refs[d], gate_sems.at[d]))
+    for copy in loads[:2] + [taps_load] + loads[2:] + gates[::-1]:
         copy.start()
     groups = taps_s.shape[0]
     taps_load.wait()
@@ -82,24 +87,14 @@
                 stage[i, blocks * c : blocks * (c + 1), :] = mine.astype(jnp.bfloat16)
             taps = pick(natural_taps, own * i // group, groups, blocks)
             stage[i, rows:main, :] = taps.astype(jnp.bfloat16)
-    gate_load.wait()
-    place = lax.axis_index("ch")
-    piece = blocks // ch_count
-    for d in range(ch_count):
-        first = jnp.bitwise_xor(place, d) * (piece * W)
-        if d < ch_count // 2:
-            gate_refs[d][...] = post_s[:, pl.ds(pl.multiple_of(first, LANES), piece * W)]
-        else:
-            for j in range(piece):
-                cols = pl.ds(pl.multiple_of(first + W * j, LANES), W)
-                lay(natural_gate, (d - ch_count // 2) * piece + j, post_s[:, cols].astype(jnp.float32))
-    early = piece * (ch_count - ch_count // 2)
-    for i in range(parts):
-        gate = [pick(natural_gate, own * i + c, channels, early) for c in range(own)]
-        stage[i, main:, :] = jnp.concatenate(gate, 0).astype(jnp.bfloat16)
     me = lax.axis_index("ctx")
     for d in range(parts):
-        out_refs[d][...] = stage[jnp.bitwise_xor(me, d)]
+        if d % 2:
+            odd_ref[d // 2] = stage[jnp.bitwise_xor(me, d)]
+        else:
+            even_refs[d // 2][...] = stage[jnp.bitwise_xor(me, d)]
+    for copy in gates:
+        copy.wait()
 
 
 def pack(pre_gate, value, post_gate, taps, parts, ch_count):
@@ -107,40 +102,57 @@
     own = channels // parts
     group = channels // taps.shape[0]
     blocks = block // W
-    piece = blocks // ch_count
-    early = piece * (ch_count - ch_count // 2)
-    local = (own + 1) * blocks + own * early
+    local = (own + 1) * blocks
     halves = W // LANES
     some = min(TILE, channels)
     args = [pltpu.with_memory_space_constraint(arg, pltpu.HBM) for arg in (pre_gate, value, taps, post_gate)]
     out = pl.pallas_call(
         functools.partial(pack_kernel, own, blocks, group, ch_count, parts),
-        out_shape=[jax.ShapeDtypeStruct((local, W), jnp.bfloat16)] * parts
-        + [jax.ShapeDtypeStruct((channels, piece * W), jnp.bfloat16)] * (ch_count // 2),
+        out_shape=[jax.ShapeDtypeStruct((local, W), jnp.bfloat16)] * (parts // 2)
+        + [jax.ShapeDtypeStruct((parts // 2, local, W), jnp.bfloat16)]
+        + [jax.ShapeDtypeStruct((channels, block // ch_count), jnp.bfloat16)] * ch_count,
         in_specs=[in_hbm()] * 4,
-        out_specs=[whole_vmem()] * (parts + ch_count // 2),
+        out_specs=[whole_vmem()] * (parts // 2 + 1 + ch_count),
         scratch_shapes=[
             pltpu.VMEM(pre_gate.shape, jnp.bfloat16),
             pltpu.VMEM(value.shape, jnp.bfloat16),
             pltpu.VMEM(taps.shape, jnp.float32),
-            pltpu.VMEM(post_gate.shape, jnp.bfloat16),
             pltpu.VMEM((channels // some, blocks * halves * some, LANES), jnp.float32),
             pltpu.VMEM((blocks * halves * taps.shape[0], LANES), jnp.float32),
-            pltpu.VMEM((early * halves * channels, LANES), jnp.float32),
             pltpu.VMEM((parts, local, W), jnp.bfloat16),
             pltpu.SemaphoreType.DMA((channels // some + 1, 2)),
+            pltpu.SemaphoreType.DMA((ch_count,)),
         ],
         compiler_params=pltpu.CompilerParams(vmem_limit_bytes=16 * 2**20),
         name="pack",
     )(*args)
-    return list(out[:parts]), list(out[parts:])
-
-
-def partner_order(count):
-    corners = [d for d in range(1, count) if bin(d >> 1).count("1") > 1]
-    straight = [d for d in range(2, count, 2) if d not in corners]
-    order = [0] + corners[:1] + straight + corners[1:]
-    return order + [d for d in range(2, count) if d not in order] + [1]
+    return list(out[: parts // 2]), out[parts // 2], list(out[parts // 2 + 1 :])
+
+
+def chip_order(chips):
+    corners = [n for n in range(1, chips) if bin(n).count("1") > 1]
+    return corners + [n for n in range(1, chips) if n not in corners]
+
+
+def merge_kernel(order, other_ref, *refs):
+    count = len(refs) // 2
+    rows = other_ref.shape[1]
+    for n in range(count):
+        refs[count + n][0:rows, :] = refs[n][...]
+        refs[count + n][rows:, :] = other_ref[order[n]]
+
+
+def merge(even, other, order):
+    local, width = even[0].shape
+    count = len(even) - 1
+    return pl.pallas_call(
+        functools.partial(merge_kernel, order),
+        out_shape=[jax.ShapeDtypeStruct((2 * local, width), jnp.bfloat16)] * count,
+        in_specs=[whole_vmem()] * (1 + count),
+        out_specs=[whole_vmem()] * count,
+        compiler_params=pltpu.CompilerParams(vmem_limit_bytes=8 * 2**20),
+        name="merge",
+    )(other, *even[1:])
 
 
 def swap(piece, axis, count, d):
@@ -197,18 +209,27 @@
     )(skip, *args)
 
 
-def conv_kernel(own, near, ch_count, parts, *rest):
-    got_refs = rest[:parts]
-    outer_ref, back_ref, ahead, rear, turns_ref, out_ref, x_all, r_all, z_all = rest[parts:]
+def conv_kernel(own, near, parts, mine_ref, other_ref, *rest):
+    pair_refs = rest[: parts // 2 - 1]
+    outer_ref, back_ref, ahead, rear, turns_ref, out_ref, x_all, r_all, z_all = rest[parts // 2 - 1 :]
     blocks = parts * near
     length = blocks * W
     chunk = math.gcd(blocks, CHUNK)
+    local = mine_ref.shape[0]
     me = lax.axis_index("ctx")
-    order = partner_order(parts)
-    for d, got_ref in zip(order, got_refs):
+    order = chip_order(parts // 2)
+    for d in range(parts):
         here = pl.ds(pl.multiple_of(jnp.bitwise_xor(me, d) * near, TILE), near)
         for c in range(own + 1):
-            x_all[here, W * c : W * (c + 1)] = got_ref[c * near : (c + 1) * near, :]
+            first = c * near
+            if d == 0:
+                part = mine_ref[first : first + near, :]
+            elif d == 1:
+                part = other_ref[0, first : first + near, :]
+            else:
+                first += d % 2 * local
+                part = pair_refs[order.index(d // 2)][first : first + near, :]
+            x_all[here, W * c : W * (c + 1)] = part
 
     def dot(left, right):
         return jnp.dot(left, right, preferred_element_type=jnp.float32)
@@ -246,30 +267,19 @@
         cols = slice(W * c, W * (c + 1))
         z_all[c] = conv[:, cols] + turns_ref[blocks + 8 * c : blocks + 8 * c + 1, 0:W] * x_all[:, cols].astype(jnp.float32)
     some = out_ref.shape[1] // own
-    early = some * (ch_count - ch_count // 2)
-    place = lax.axis_index("ch")
-    for d, got_ref in zip(order, got_refs):
-        k = jnp.bitwise_xor(me, d)
-        gate = got_ref[(own + 1) * near :, :].astype(jnp.float32)
-        mine = [z_all[c, pl.ds(pl.multiple_of(k * near, TILE), near), :] for c in range(own)]
-        for m in range(ch_count):
-            rows = [part[m * some : (m + 1) * some, :] for part in mine]
-            for e in range(ch_count // 2, ch_count):
-                at = (e - ch_count // 2) * some
-                for c in range(own):
-                    factor = jnp.where(jnp.bitwise_xor(place, e) == m, gate[c * early + at : c * early + at + some, :], 1.0)
-                    rows[c] = rows[c] * factor
-            out_ref[k * ch_count + m] = jnp.concatenate(rows, 0).astype(jnp.bfloat16)
-
-
-def convolve(got, tables, own, near, ch_count):
-    parts = len(got)
+    for n in range(out_ref.shape[0]):
+        rows = [z_all[c, n * some : (n + 1) * some, :] for c in range(own)]
+        out_ref[n] = jnp.concatenate(rows, 0).astype(jnp.bfloat16)
+
+
+def convolve(mine, other, pairs, tables, own, near, ch_count):
+    parts = 2 * len(pairs) + 2
     blocks = parts * near
     owners = parts * ch_count
     return pl.pallas_call(
-        functools.partial(conv_kernel, own, near, ch_count, parts),
+        functools.partial(conv_kernel, own, near, parts),
         out_shape=jax.ShapeDtypeStruct((owners, own * blocks // owners, W), jnp.bfloat16),
-        in_specs=[whole_vmem()] * (parts + len(tables)),
+        in_specs=[whole_vmem()] * (2 + len(pairs) + len(tables)),
         out_specs=whole_vmem(),
         scratch_shapes=[
             pltpu.VMEM((blocks, W * (own + 1)), jnp.bfloat16),
@@ -279,7 +289,7 @@
         compiler_params=pltpu.CompilerParams(vmem_limit_bytes=32 * 2**20),
         cost_estimate=pl.CostEstimate(flops=blocks * W, bytes_accessed=4 * blocks * W, transcendentals=0),
         name="convolve",
-    )(*got, *tables)
+    )(mine, other, *pairs, *tables)
 
 
 def unpack_kernel(own, got_ref, *rest):
@@ -287,11 +297,11 @@
     sources, rows, _ = got_ref.shape
     some = rows // own
     place = lax.axis_index("ch")
-    channels, width = gate_refs[0].shape
+    channels = gate_refs[0].shape[0]
     ch_count = out_ref.shape[0] // channels
     for d in range(ch_count):
         here = pl.ds(pl.multiple_of(jnp.bitwise_xor(place, d) * channels, TILE), channels)
-        gate_s[here, :] = gate_refs[d][...] if d < len(gate_refs) else jnp.ones((channels, width), jnp.bfloat16)
+        gate_s[here, :] = gate_refs[d][...]
     copies = []
     for m in range(ch_count):
         here = slice(m * channels, (m + 1) * channels)
@@ -316,9 +326,8 @@
     sources, rows, _ = got.shape
     shape = (sources * own, rows // own * W)
     if rows % TILE:
-        ones = [jnp.ones_like(gates[0])] * (ch_count - len(gates))
         order = jnp.bitwise_xor(lax.axis_index("ch"), jnp.arange(ch_count))
-        gate = jnp.stack(gates + ones)[order].reshape(shape)
+        gate = jnp.stack(gates)[order].reshape(shape)
         got = got.reshape(-1, ch_count, rows, W).swapaxes(0, 1)
         return (got.reshape(shape).astype(jnp.float32) * gate.astype(jnp.float32)).astype(jnp.bfloat16)
     return pl.pallas_call(
@@ -342,14 +351,19 @@
     ch_count = lax.axis_size("ch")
     own = value.shape[0] // ctx_count
     near = value.shape[1] // W
-    got, gates = pack(pre_gate, value, post_gate, filter_taps, ctx_count, ch_count)
-    tables, skip, _ = lax.optimization_barrier((dft_tables(near * ctx_count), skip, got[0]))
-    got = [swap(got[d], "ctx", ctx_count, d) if d else got[d] for d in partner_order(ctx_count)]
-    for d in range(1, ch_count // 2):
+    even, odd, gates = pack(pre_gate, value, post_gate, filter_taps, ctx_count, ch_count)
+    other = swap(odd, "ctx", ctx_count, 1)
+    for d in reversed(range(1, ch_count)):
         gates[d] = swap(gates[d], "ch", ch_count, d)
+    order = chip_order(ctx_count // 2)
+    pairs = merge([even[n] for n in [0] + order], other, order)
+    pairs = [swap(pair, "ctx", ctx_count, 2 * n) for n, pair in zip(order, pairs)]
+    tables, skip, _ = lax.optimization_barrier((dft_tables(near * ctx_count), skip, odd))
     tables = list(make_tables(skip, *tables, own))
-    mixed = convolve(got, tables, own, near, ch_count)
-    mixed, gates = lax.optimization_barrier((mixed, gates))
+    gates[-1], pairs = lax.optimization_barrier((gates[-1], pairs))
+    mixed = convolve(even[0], other, pairs, tables, own, near, ch_count)
+    mixed, gates = lax.optimization_barrier((mixed, gates[::-1]))
+    gates = gates[::-1]
     mixed = lax.all_to_all(mixed, ("ctx", "ch"), split_axis=0, concat_axis=0, tiled=True)
     return unpack(mixed, gates, own, ch_count)
 

time: 41.5 us -> 42.4 us (1.022)
  waiting for transfers between devices: 1.41 us -> 2.52 us
  Pallas kernels: 7.88 us -> 7.43 us
    ppermute x8 -> x7, waiting for transfers between devices: 1.41 us -> 2.52 us  [swap(): return lax.ppermute(piece, axis, [(i, i ^ d) for i in range(count)])]
    pallas_call x1 -> x2, Pallas kernels: 2.6 us -> 2.48 us  [the longest x1 2.44 us: convolve(): pl.pallas_call(functools.partial(conv_kernel, own, near, parts), out_shap...]
    ppermute x8 -> x7, starting transfers between devices: 11.2 us -> 11.3 us  [swap(): return lax.ppermute(piece, axis, [(i, i ^ d) for i in range(count)])]
  transfers between devices with their start and end apart: 8 -> 7, of which waited for: 2 -> 4; matrix products, arithmetic and copies ran while one was open for 0% -> 0% of each run, Pallas kernels for 11% -> 11%
where the time goes in v14:
time: 42.4 us; the launch traced here: 42.2 us
  blocking collectives  20.9 us (49%)
  starting transfers between devices  11.3 us (27%)
  Pallas kernels  7.43 us (18%)
  waiting for transfers between devices  2.52 us (6%)
    all_to_all x1, blocking collectives, body(): lax.all_to_all(mixed, ('ctx', 'ch'), split_axis=0, concat_axis=0, tiled=T...  20.9 us
    ppermute x7, starting transfers between devices, swap(): return lax.ppermute(piece, axis, [(i, i ^ d) for i in range(count)])  11.3 us
    ppermute x7, waiting for transfers between devices, swap(): return lax.ppermute(piece, axis, [(i, i ^ d) for i in range(count)])  2.52 us
    pallas_call x1, Pallas kernels, convolve(): pl.pallas_call(functools.partial(conv_kernel, own, near, parts), out_shap...  2.44 us
    pallas_call x1, Pallas kernels, make_tables(): pl.pallas_call(functools.partial(tables_kernel, own), out_shape=[jax.Shap...  2.09 us
    pallas_call x1, Pallas kernels, pack(): pl.pallas_call(functools.partial(pack_kernel, own, blocks, group, ch_coun...  1.86 us
    pallas_call x1, Pallas kernels, unpack(): pl.pallas_call(functools.partial(unpack_kernel, own), out_shape=jax.Shape...  1.01 us
  transfers between devices with their start and end apart: 7, of which 4 were waited for; matrix products, arithmetic and copies ran while one was open for 0% of the time, Pallas kernels for 11%

profile of v14, /device:TPU:1, one launch (start us, length us, event | category | flops | bytes accessed | tf_op | source)
XLA Modules:
  0.0 42.2 jit_solution(14378707234133352571)
XLA Ops:
  0.0 1.9 %pack.1 = (bf16[160,256]{1,0:T(8,128)(2,1)S(1)}, bf16[160,256]{1,0:T(8,128)(2,1)S(1)}, bf16[160,256]{1,0:T(8,128)(2,1)S(1)}, bf16[160,256]{1,0:T(8,128)(2,1)S(1)...) custom-call(bf16[32,8192]{1,0:T(8,128)(2,1)} %pre_ref.1, ...), custom_call_target="tpu_custom_call" | custom-call | tf_op jit(solution)/shard_map/pack/pallas_call | solution.py:109
  1.9 0.1 collective-permute-start
  2.0 4.8 %collective-permute-start.1 = (bf16[32,2048]{1,0:T(8,128)(2,1)S(1)}, bf16[32,2048]{1,0:T(8,128)(2,1)S(1)}, u32[]{:S(2)}, u32[]{:S(2)}) collective-permute-start(bf16[32,2048]{1,0:T(8,128)(2,1)S(1)} %get-tuple-element.38), channel_id=1, source_target_pairs={{0,3},{1,2},{2,1},{3,0},{4,7},{5,6},{6,5},{7,4},{8,11},{9,10},{10,... | collective-permute-start | bytes 393224 | tf_op jit(solution)/shard_map/ppermute | solution.py:159
  6.8 0.0 collective-permute-done.other_ref
  6.8 2.2 %collective-permute-start.2 = (bf16[320,256]{1,0:T(8,128)(2,1)S(1)}, bf16[320,256]{1,0:T(8,128)(2,1)S(1)}, u32[]{:S(2)}, u32[]{:S(2)}) collective-permute-start(bf16[320,256]{1,0:T(8,128)(2,1)S(1)} %get-tuple-element.42), channel_id=1, source_target_pairs={{0,24},{4,28},{8,16},{12,20},{16,8},{20,12},{24,0},{28,4},{1,25},{... | collective-permute-start | bytes 491528 | tf_op jit(solution)/shard_map/ppermute | solution.py:159
  9.0 0.3 collective-permute-start.3
  9.3 0.2 collective-permute-start.4
  9.5 0.0 copy-start
  9.5 0.2 collective-permute-start.5
  9.8 0.8 %collective-permute-done.1.rest_3_ = bf16[32,2048]{1,0:T(8,128)(2,1)S(1)} collective-permute-done((bf16[32,2048]{1,0:T(8,128)(2,1)S(1)}, bf16[32,2048]{1,0:T(8,128)(2,1)S(1)}, u32[]{:S(2)}, u32[]{:S(2)}) %collective-permute-start.1) | collective-permute-done | bytes 131104 | tf_op jit(solution)/shard_map/ppermute | solution.py:159
  10.6 3.4 %collective-permute-start.6 = (bf16[32,2048]{1,0:T(8,128)(2,1)S(1)}, bf16[32,2048]{1,0:T(8,128)(2,1)S(1)}, u32[]{:S(2)}, u32[]{:S(2)}) collective-permute-start(bf16[32,2048]{1,0:T(8,128)(2,1)S(1)} %get-tuple-element.60), channel_id=1, source_target_pairs={{0,1},{1,0},{2,3},{3,2},{4,5},{5,4},{6,7},{7,6},{8,9},{9,8},{10,11... | collective-permute-start | bytes 393224 | tf_op jit(solution)/shard_map/ppermute | solution.py:159
  14.0 0.0 copy-done
  14.0 2.1 %make_tables.1 = (bf16[512,256]{1,0:T(8,128)(2,1)S(1)}, bf16[256,512]{1,0:T(8,128)(2,1)S(1)}, bf16[512,512]{1,0:T(8,128)(2,1)S(1)}, bf16[512,512]{1,0:T(8,128)(2,1)S(1)}, f32[288,512]{1,0:T(8,128)S(1)}) custom-call(f32[32]{0:T(128)S(1)} %copy-done, f32[512,256]{1,0:T(8,128)} %constant.8.clone.rest_0_, f32[256,512]{1,0:T(8,128)} %constant.9.clone.rest_1_, ...), custom_call_target="tpu_custom_call" | custom-call | tf_op jit(solution)/shard_map/make_tables/pallas_call | solution.py:195
  16.1 0.0 collective-permute-done.2.rest_0_
  16.1 0.7 %collective-permute-done.3.rest_1_ = bf16[320,256]{1,0:T(8,128)(2,1)S(1)} collective-permute-done((bf16[320,256]{1,0:T(8,128)(2,1)S(1)}, bf16[320,256]{1,0:T(8,128)(2,1)S(1)}, u32[]{:S(2)}, u32[]{:S(2)}) %collective-permute-start.3) | collective-permute-done | bytes 163872 | tf_op jit(solution)/shard_map/ppermute | solution.py:159
  16.8 0.6 %collective-permute-done.4.rest_2_ = bf16[320,256]{1,0:T(8,128)(2,1)S(1)} collective-permute-done((bf16[320,256]{1,0:T(8,128)(2,1)S(1)}, bf16[320,256]{1,0:T(8,128)(2,1)S(1)}, u32[]{:S(2)}, u32[]{:S(2)}) %collective-permute-start.4) | collective-permute-done | bytes 163872 | tf_op jit(solution)/shard_map/ppermute | solution.py:159
  17.4 2.4 %convolve.1 = bf16[32,32,256]{2,1,0:T(8,128)(2,1)S(1)} custom-call(bf16[160,256]{1,0:T(8,128)(2,1)S(1)} %get-tuple-element.36.mine_ref, bf16[4,160,256]{2,1,0:T(8,128)(2,1)S(1)} %collective-permute-done.other_ref, bf16[320,256]{1,0:T(8,128)(2,1)S(1)} %collective-permute-done.2.rest_0_, bf16[320,256]{1,0:T(8,128)(2,1)S(1)} %collective-permute-done.3.rest_1_, ...), custom_call_target="tpu_custom_call" | custom-call | flops 65536 | bytes 262144 | tf_op jit(solution)/shard_map/convolve/pallas_call | solution.py:279
  19.9 0.0 collective-permute-done.5.rest_2_
  19.9 0.4 collective-permute-done.6.rest_1_
  20.3 20.9 %all_to_all.5.got_ref = bf16[32,32,256]{2,1,0:T(8,128)(2,1)S(1)} all-to-all(bf16[32,32,256]{2,1,0:T(8,128)(2,1)S(1)} %convolve.1), channel_id=1, replica_groups=mesh['ctx'=8,'ch'=4] {'ctx','ch'}, dimensions={0} | all-to-all | bytes 1048576 | tf_op jit(solution)/shard_map/all_to_all | solution.py:367
  41.2 1.0 %unpack.1 = bf16[128,2048]{1,0:T(8,128)(2,1)} custom-call(bf16[32,32,256]{2,1,0:T(8,128)(2,1)S(1)} %all_to_all.5.got_ref, bf16[32,2048]{1,0:T(8,128)(2,1)S(1)} %get-tuple-element.63.rest_0_, bf16[32,2048]{1,0:T(8,128)(2,1)S(1)} %collective-permute-done.6.rest_1_, bf16[32,2048]{1,0:T(8,128)(2,1)S(1)} %collective-permute-done.5.rest_2_, ...), custom_call_target="tpu_custom_call" | custom-call | tf_op jit(solution)/shard_map/unpack/pallas_call | solution.py:333
  (1 shorter events, 0.0 us)
Async XLA Ops:
  1.9 4.9 %collective-permute-start = (bf16[4,160,256]{2,1,0:T(8,128)(2,1)S(1)}, bf16[4,160,256]{2,1,0:T(8,128)(2,1)S(1)}, u32[]{:S(2)}, u32[]{:S(2)}) collective-permute-start(bf16[4,160,256]{2,1,0:T(8,128)(2,1)S(1)} %get-tuple-element.37), channel_id=1, source_target_pairs={{0,4},{4,0},{8,12},{12,8},{16,20},{20,16},{24,28},{28,24},{1,5},{5... | collective-permute-start | bytes 983048 | tf_op jit(solution)/shard_map/ppermute | solution.py:159
  2.0 8.6 %collective-permute-start.1 = (bf16[32,2048]{1,0:T(8,128)(2,1)S(1)}, bf16[32,2048]{1,0:T(8,128)(2,1)S(1)}, u32[]{:S(2)}, u32[]{:S(2)}) collective-permute-start(bf16[32,2048]{1,0:T(8,128)(2,1)S(1)} %get-tuple-element.38), channel_id=1, source_target_pairs={{0,3},{1,2},{2,1},{3,0},{4,7},{5,6},{6,5},{7,4},{8,11},{9,10},{10,... | collective-permute-start | bytes 393224 | tf_op jit(solution)/shard_map/ppermute | solution.py:159
  6.8 9.3 %collective-permute-start.2 = (bf16[320,256]{1,0:T(8,128)(2,1)S(1)}, bf16[320,256]{1,0:T(8,128)(2,1)S(1)}, u32[]{:S(2)}, u32[]{:S(2)}) collective-permute-start(bf16[320,256]{1,0:T(8,128)(2,1)S(1)} %get-tuple-element.42), channel_id=1, source_target_pairs={{0,24},{4,28},{8,16},{12,20},{16,8},{20,12},{24,0},{28,4},{1,25},{... | collective-permute-start | bytes 491528 | tf_op jit(solution)/shard_map/ppermute | solution.py:159
  9.0 7.8 %collective-permute-start.3 = (bf16[320,256]{1,0:T(8,128)(2,1)S(1)}, bf16[320,256]{1,0:T(8,128)(2,1)S(1)}, u32[]{:S(2)}, u32[]{:S(2)}) collective-permute-start(bf16[320,256]{1,0:T(8,128)(2,1)S(1)} %get-tuple-element.43), channel_id=1, source_target_pairs={{0,8},{4,12},{8,0},{12,4},{16,24},{20,28},{24,16},{28,20},{1,9},{5... | collective-permute-start | bytes 491528 | tf_op jit(solution)/shard_map/ppermute | solution.py:159
  9.3 8.1 %collective-permute-start.4 = (bf16[320,256]{1,0:T(8,128)(2,1)S(1)}, bf16[320,256]{1,0:T(8,128)(2,1)S(1)}, u32[]{:S(2)}, u32[]{:S(2)}) collective-permute-start(bf16[320,256]{1,0:T(8,128)(2,1)S(1)} %get-tuple-element.44), channel_id=1, source_target_pairs={{0,16},{4,20},{8,24},{12,28},{16,0},{20,4},{24,8},{28,12},{1,17},{... | collective-permute-start | bytes 491528 | tf_op jit(solution)/shard_map/ppermute | solution.py:159
  9.5 4.5 %copy-start = (f32[32]{0:T(128)S(1)}, f32[32]{0:T(128)}, u32[]{:S(2)}) copy-start(f32[32]{0:T(128)} %skip_ref) | copy-start | bytes 388
  9.5 10.3 %collective-permute-start.5 = (bf16[32,2048]{1,0:T(8,128)(2,1)S(1)}, bf16[32,2048]{1,0:T(8,128)(2,1)S(1)}, u32[]{:S(2)}, u32[]{:S(2)}) collective-permute-start(bf16[32,2048]{1,0:T(8,128)(2,1)S(1)} %get-tuple-element.59), channel_id=1, source_target_pairs={{0,2},{1,3},{2,0},{3,1},{4,6},{5,7},{6,4},{7,5},{8,10},{9,11},{10,... | collective-permute-start | bytes 393224 | tf_op jit(solution)/shard_map/ppermute | solution.py:159
  10.6 9.7 %collective-permute-start.6 = (bf16[32,2048]{1,0:T(8,128)(2,1)S(1)}, bf16[32,2048]{1,0:T(8,128)(2,1)S(1)}, u32[]{:S(2)}, u32[]{:S(2)}) collective-permute-start(bf16[32,2048]{1,0:T(8,128)(2,1)S(1)} %get-tuple-element.60), channel_id=1, source_target_pairs={{0,1},{1,0},{2,3},{3,2},{4,5},{5,4},{6,7},{7,6},{8,9},{9,8},{10,11... | collective-permute-start | bytes 393224 | tf_op jit(solution)/shard_map/ppermute | solution.py:159

commit v15 on v13

--- a/solution.py
+++ b/solution.py
@@ -50,24 +50,32 @@
 
 def pack_kernel(own, blocks, group, ch_count, parts, pre_ref, val_ref, taps_ref, post_ref, *rest):
     out_refs, gate_refs = rest[:parts], rest[parts : parts + ch_count // 2]
-    pre_s, val_s, taps_s, post_s, natural, natural_taps, natural_gate, stage, in_sems = rest[parts + ch_count // 2 :]
+    pre_s, val_s, taps_s, far_s, natural, natural_taps, natural_gate, stage, in_sems, gate_sems = rest[
+        parts + ch_count // 2 :
+    ]
     channels = own * parts
     some = min(TILE, channels)
     rows = own * blocks
-    main = rows + blocks
+    piece = blocks // ch_count
+    early = piece * (ch_count // 2)
+    main = rows + own * early
+    place = lax.axis_index("ch")
     loads = []
     for g in range(channels // some):
         here = pl.ds(g * some, some)
         loads.append(pltpu.make_async_copy(pre_ref.at[here], pre_s.at[here], in_sems.at[g, 0]))
         loads.append(pltpu.make_async_copy(val_ref.at[here], val_s.at[here], in_sems.at[g, 1]))
     taps_load = pltpu.make_async_copy(taps_ref, taps_s, in_sems.at[channels // some, 0])
-    gate_load = pltpu.make_async_copy(post_ref, post_s, in_sems.at[channels // some, 1])
-    for copy in loads[:2] + [taps_load] + loads[2:] + [gate_load]:
+    other_half = (1 - place // (ch_count // 2)) * (early * W)
+    cols = pl.ds(pl.multiple_of(other_half, LANES), early * W)
+    far_load = pltpu.make_async_copy(post_ref.at[:, cols], far_s, in_sems.at[channels // some, 1])
+    gates = []
+    for d in range(ch_count // 2):
+        cols = pl.ds(pl.multiple_of(jnp.bitwise_xor(place, d) * (piece * W), LANES), piece * W)
+        gates.append(pltpu.make_async_copy(post_ref.at[:, cols], gate_refs[d], gate_sems.at[d]))
+    for copy in loads[:2] + [taps_load, far_load] + loads[2:] + gates[::-1]:
         copy.start()
     groups = taps_s.shape[0]
-    taps_load.wait()
-    for j in range(blocks):
-        lay(natural_taps, j, taps_s[:, W * j : W * (j + 1)])
     for g in range(channels // some):
         loads[2 * g].wait()
         loads[2 * g + 1].wait()
@@ -80,26 +88,26 @@
             for c in range(own):
                 mine = pick(natural.at[g], own * i + c - g * some, some, blocks)
                 stage[i, blocks * c : blocks * (c + 1), :] = mine.astype(jnp.bfloat16)
-            taps = pick(natural_taps, own * i // group, groups, blocks)
-            stage[i, rows:main, :] = taps.astype(jnp.bfloat16)
-    gate_load.wait()
-    place = lax.axis_index("ch")
-    piece = blocks // ch_count
-    for d in range(ch_count):
-        first = jnp.bitwise_xor(place, d) * (piece * W)
-        if d < ch_count // 2:
-            gate_refs[d][...] = post_s[:, pl.ds(pl.multiple_of(first, LANES), piece * W)]
-        else:
-            for j in range(piece):
-                cols = pl.ds(pl.multiple_of(first + W * j, LANES), W)
-                lay(natural_gate, (d - ch_count // 2) * piece + j, post_s[:, cols].astype(jnp.float32))
-    early = piece * (ch_count - ch_count // 2)
-    for i in range(parts):
-        gate = [pick(natural_gate, own * i + c, channels, early) for c in range(own)]
-        stage[i, main:, :] = jnp.concatenate(gate, 0).astype(jnp.bfloat16)
+        if g == 0:
+            taps_load.wait()
+            for j in range(blocks):
+                lay(natural_taps, j, taps_s[:, W * j : W * (j + 1)])
+            for i in range(parts):
+                stage[i, main:, :] = pick(natural_taps, own * i // group, groups, blocks).astype(jnp.bfloat16)
+            far_load.wait()
+            for d in range(ch_count // 2, ch_count):
+                first = jnp.bitwise_xor(place, d) % (ch_count // 2) * (piece * W)
+                for j in range(piece):
+                    cols = pl.ds(pl.multiple_of(first + W * j, LANES), W)
+                    lay(natural_gate, (d - ch_count // 2) * piece + j, far_s[:, cols].astype(jnp.float32))
+            for i in range(parts):
+                gate = [pick(natural_gate, own * i + c, channels, early) for c in range(own)]
+                stage[i, rows:main, :] = jnp.concatenate(gate, 0).astype(jnp.bfloat16)
     me = lax.axis_index("ctx")
     for d in range(parts):
         out_refs[d][...] = stage[jnp.bitwise_xor(me, d)]
+    for copy in gates:
+        copy.wait()
 
 
 def pack(pre_gate, value, post_gate, taps, parts, ch_count):
@@ -108,8 +116,8 @@
     group = channels // taps.shape[0]
     blocks = block // W
     piece = blocks // ch_count
-    early = piece * (ch_count - ch_count // 2)
-    local = (own + 1) * blocks + own * early
+    early = piece * (ch_count // 2)
+    local = own * (blocks + early) + blocks
     halves = W // LANES
     some = min(TILE, channels)
     args = [pltpu.with_memory_space_constraint(arg, pltpu.HBM) for arg in (pre_gate, value, taps, post_gate)]
@@ -123,12 +131,13 @@
             pltpu.VMEM(pre_gate.shape, jnp.bfloat16),
             pltpu.VMEM(value.shape, jnp.bfloat16),
             pltpu.VMEM(taps.shape, jnp.float32),
-            pltpu.VMEM(post_gate.shape, jnp.bfloat16),
+            pltpu.VMEM((channels, early * W), jnp.bfloat16),
             pltpu.VMEM((channels // some, blocks * halves * some, LANES), jnp.float32),
             pltpu.VMEM((blocks * halves * taps.shape[0], LANES), jnp.float32),
             pltpu.VMEM((early * halves * channels, LANES), jnp.float32),
             pltpu.VMEM((parts, local, W), jnp.bfloat16),
             pltpu.SemaphoreType.DMA((channels // some + 1, 2)),
+            pltpu.SemaphoreType.DMA((ch_count // 2,)),
         ],
         compiler_params=pltpu.CompilerParams(vmem_limit_bytes=16 * 2**20),
         name="pack",
@@ -205,10 +214,14 @@
     chunk = math.gcd(blocks, CHUNK)
     me = lax.axis_index("ctx")
     order = partner_order(parts)
+    some = out_ref.shape[1] // own
+    early = some * (ch_count // 2)
+    main = own * (near + early)
     for d, got_ref in zip(order, got_refs):
         here = pl.ds(pl.multiple_of(jnp.bitwise_xor(me, d) * near, TILE), near)
-        for c in range(own + 1):
+        for c in range(own):
             x_all[here, W * c : W * (c + 1)] = got_ref[c * near : (c + 1) * near, :]
+        x_all[here, W * own :] = got_ref[main:, :]
 
     def dot(left, right):
         return jnp.dot(left, right, preferred_element_type=jnp.float32)
@@ -245,12 +258,10 @@
     for c in range(own):
         cols = slice(W * c, W * (c + 1))
         z_all[c] = conv[:, cols] + turns_ref[blocks + 8 * c : blocks + 8 * c + 1, 0:W] * x_all[:, cols].astype(jnp.float32)
-    some = out_ref.shape[1] // own
-    early = some * (ch_count - ch_count // 2)
     place = lax.axis_index("ch")
     for d, got_ref in zip(order, got_refs):
         k = jnp.bitwise_xor(me, d)
-        gate = got_ref[(own + 1) * near :, :].astype(jnp.float32)
+        gate = got_ref[own * near : main, :].astype(jnp.float32)
         mine = [z_all[c, pl.ds(pl.multiple_of(k * near, TILE), near), :] for c in range(own)]
         for m in range(ch_count):
             rows = [part[m * some : (m + 1) * some, :] for part in mine]

time: 41.6 us -> 41.6 us (level)
  no operation moved by 1% of the time
where the time goes in v15:
time: 41.6 us; the launch traced here: 41.5 us
  blocking collectives  19.2 us (46%)
  starting transfers between devices  10.1 us (24%)
  Pallas kernels  7.92 us (19%)
  waiting for transfers between devices  4.25 us (10%)
    all_to_all x1, blocking collectives, body(): lax.all_to_all(mixed, ('ctx', 'ch'), split_axis=0, concat_axis=0, tiled=T...  19.2 us
    ppermute x8, starting transfers between devices, swap(): return lax.ppermute(piece, axis, [(i, i ^ d) for i in range(count)])  10.1 us
    ppermute x8, waiting for transfers between devices, swap(): return lax.ppermute(piece, axis, [(i, i ^ d) for i in range(count)])  4.25 us
    pallas_call x1, Pallas kernels, convolve(): pl.pallas_call(functools.partial(conv_kernel, own, near, ch_count, parts)...  2.61 us
    pallas_call x1, Pallas kernels, pack(): pl.pallas_call(functools.partial(pack_kernel, own, blocks, group, ch_coun...  2.2 us
    pallas_call x1, Pallas kernels, make_tables(): pl.pallas_call(functools.partial(tables_kernel, own), out_shape=[jax.Shap...  2.09 us
    pallas_call x1, Pallas kernels, unpack(): pl.pallas_call(functools.partial(unpack_kernel, own), out_shape=jax.Shape...  1.01 us
  transfers between devices with their start and end apart: 8, of which 3 were waited for; matrix products, arithmetic and copies ran while one was open for 0% of the time, Pallas kernels for 11%

profile of v15, /device:TPU:1, one launch (start us, length us, event | category | flops | bytes accessed | tf_op | source)
XLA Modules:
  0.0 41.5 jit_solution(5275285697990435480)
XLA Ops:
  0.0 2.2 %pack.1 = (bf16[224,256]{1,0:T(8,128)(2,1)S(1)}, bf16[224,256]{1,0:T(8,128)(2,1)S(1)}, bf16[224,256]{1,0:T(8,128)(2,1)S(1)}, bf16[224,256]{1,0:T(8,128)(2,1)S(1)...) custom-call(bf16[32,8192]{1,0:T(8,128)(2,1)} %pre_ref.1, ...), custom_call_target="tpu_custom_call" | custom-call | tf_op jit(solution)/shard_map/pack/pallas_call | solution.py:124
  2.2 3.1 %collective-permute-start = (bf16[224,256]{1,0:T(8,128)(2,1)S(1)}, bf16[224,256]{1,0:T(8,128)(2,1)S(1)}, u32[]{:S(2)}, u32[]{:S(2)}) collective-permute-start(bf16[224,256]{1,0:T(8,128)(2,1)S(1)} %get-tuple-element.37), channel_id=1, source_target_pairs={{0,24},{4,28},{8,16},{12,20},{16,8},{20,12},{24,0},{28,4},{1,25},{... | collective-permute-start | bytes 344072 | tf_op jit(solution)/shard_map/ppermute | solution.py:156
  5.3 0.3 collective-permute-start.1
  5.5 0.1 collective-permute-start.2
  5.6 1.4 %collective-permute-start.7 = (bf16[32,2048]{1,0:T(8,128)(2,1)S(1)}, bf16[32,2048]{1,0:T(8,128)(2,1)S(1)}, u32[]{:S(2)}, u32[]{:S(2)}) collective-permute-start(bf16[32,2048]{1,0:T(8,128)(2,1)S(1)} %get-tuple-element.63), channel_id=1, source_target_pairs={{0,1},{1,0},{2,3},{3,2},{4,5},{5,4},{6,7},{7,6},{8,9},{9,8},{10,11... | collective-permute-start | bytes 393224 | tf_op jit(solution)/shard_map/ppermute | solution.py:156
  7.1 0.0 copy-start
  7.1 3.8 %collective-permute-start.3 = (bf16[224,256]{1,0:T(8,128)(2,1)S(1)}, bf16[224,256]{1,0:T(8,128)(2,1)S(1)}, u32[]{:S(2)}, u32[]{:S(2)}) collective-permute-start(bf16[224,256]{1,0:T(8,128)(2,1)S(1)} %get-tuple-element.40), channel_id=1, source_target_pairs={{0,28},{4,24},{8,20},{12,16},{16,12},{20,8},{24,4},{28,0},{1,29},{... | collective-permute-start | bytes 344072 | tf_op jit(solution)/shard_map/ppermute | solution.py:156
  10.9 0.0 copy-done
  10.9 2.1 %make_tables.1 = (bf16[512,256]{1,0:T(8,128)(2,1)S(1)}, bf16[256,512]{1,0:T(8,128)(2,1)S(1)}, bf16[512,512]{1,0:T(8,128)(2,1)S(1)}, bf16[512,512]{1,0:T(8,128)(2,1)S(1)}, f32[288,512]{1,0:T(8,128)S(1)}) custom-call(f32[32]{0:T(128)S(1)} %copy-done, f32[512,256]{1,0:T(8,128)} %constant.8.clone.rest_0_, f32[256,512]{1,0:T(8,128)} %constant.9.clone.rest_1_, ...), custom_call_target="tpu_custom_call" | custom-call | tf_op jit(solution)/shard_map/make_tables/pallas_call | solution.py:192
  13.0 0.0 collective-permute-done.rest_1_
  13.0 0.1 collective-permute-start.4
  13.1 0.0 collective-permute-done.1.rest_2_
  13.1 0.7 %collective-permute-start.5 = (bf16[224,256]{1,0:T(8,128)(2,1)S(1)}, bf16[224,256]{1,0:T(8,128)(2,1)S(1)}, u32[]{:S(2)}, u32[]{:S(2)}) collective-permute-start(bf16[224,256]{1,0:T(8,128)(2,1)S(1)} %get-tuple-element.55), channel_id=1, source_target_pairs={{0,20},{4,16},{8,28},{12,24},{16,4},{20,0},{24,12},{28,8},{1,21},{... | collective-permute-start | bytes 344072 | tf_op jit(solution)/shard_map/ppermute | solution.py:156
  13.8 0.0 collective-permute-done.2.rest_3_
  13.8 0.6 %collective-permute-start.6 = (bf16[224,256]{1,0:T(8,128)(2,1)S(1)}, bf16[224,256]{1,0:T(8,128)(2,1)S(1)}, u32[]{:S(2)}, u32[]{:S(2)}) collective-permute-start(bf16[224,256]{1,0:T(8,128)(2,1)S(1)} %get-tuple-element.56), channel_id=1, source_target_pairs={{0,4},{4,0},{8,12},{12,8},{16,20},{20,16},{24,28},{28,24},{1,5},{5... | collective-permute-start | bytes 344072 | tf_op jit(solution)/shard_map/ppermute | solution.py:156
  14.4 0.3 collective-permute-done.3.rest_4_
  14.7 2.9 %collective-permute-done.4.rest_5_ = bf16[224,256]{1,0:T(8,128)(2,1)S(1)} collective-permute-done((bf16[224,256]{1,0:T(8,128)(2,1)S(1)}, bf16[224,256]{1,0:T(8,128)(2,1)S(1)}, u32[]{:S(2)}, u32[]{:S(2)}) %collective-permute-start.4) | collective-permute-done | bytes 114720 | tf_op jit(solution)/shard_map/ppermute | solution.py:156
  17.6 1.1 %collective-permute-done.5.rest_6_ = bf16[224,256]{1,0:T(8,128)(2,1)S(1)} collective-permute-done((bf16[224,256]{1,0:T(8,128)(2,1)S(1)}, bf16[224,256]{1,0:T(8,128)(2,1)S(1)}, u32[]{:S(2)}, u32[]{:S(2)}) %collective-permute-start.5) | collective-permute-done | bytes 114720 | tf_op jit(solution)/shard_map/ppermute | solution.py:156
  18.7 0.0 collective-permute-done.6.rest_7_
  18.7 2.6 %convolve.1 = bf16[32,32,256]{2,1,0:T(8,128)(2,1)S(1)} custom-call(bf16[224,256]{1,0:T(8,128)(2,1)S(1)} %get-tuple-element.36.rest_0_, bf16[224,256]{1,0:T(8,128)(2,1)S(1)} %collective-permute-done.rest_1_, bf16[224,256]{1,0:T(8,128)(2,1)S(1)} %collective-permute-done.1.rest_2_, bf16[224,256]{1,0:T(8,128)(2,1)S(1)} %collective-permute-done.2.rest_3_, ...), custom_call_target="tpu_custom_call" | custom-call | flops 65536 | bytes 262144 | tf_op jit(solution)/shard_map/convolve/pallas_call | solution.py:280
  21.3 0.0 collective-permute-done.7.rest_1_
  21.3 19.2 %all_to_all.5.got_ref = bf16[32,32,256]{2,1,0:T(8,128)(2,1)S(1)} all-to-all(bf16[32,32,256]{2,1,0:T(8,128)(2,1)S(1)} %convolve.1), channel_id=1, replica_groups=mesh['ctx'=8,'ch'=4] {'ctx','ch'}, dimensions={0} | all-to-all | bytes 1048576 | tf_op jit(solution)/shard_map/all_to_all | solution.py:368
  40.4 1.0 %unpack.1 = bf16[128,2048]{1,0:T(8,128)(2,1)} custom-call(bf16[32,32,256]{2,1,0:T(8,128)(2,1)S(1)} %all_to_all.5.got_ref, bf16[32,2048]{1,0:T(8,128)(2,1)S(1)} %get-tuple-element.65.rest_0_, bf16[32,2048]{1,0:T(8,128)(2,1)S(1)} %collective-permute-done.7.rest_1_), custom_call_target="tpu_custom_call" | custom-call | tf_op jit(solution)/shard_map/unpack/pallas_call | solution.py:335
Async XLA Ops:
  2.2 10.8 %collective-permute-start = (bf16[224,256]{1,0:T(8,128)(2,1)S(1)}, bf16[224,256]{1,0:T(8,128)(2,1)S(1)}, u32[]{:S(2)}, u32[]{:S(2)}) collective-permute-start(bf16[224,256]{1,0:T(8,128)(2,1)S(1)} %get-tuple-element.37), channel_id=1, source_target_pairs={{0,24},{4,28},{8,16},{12,20},{16,8},{20,12},{24,0},{28,4},{1,25},{... | collective-permute-start | bytes 344072 | tf_op jit(solution)/shard_map/ppermute | solution.py:156
  5.3 7.8 %collective-permute-start.1 = (bf16[224,256]{1,0:T(8,128)(2,1)S(1)}, bf16[224,256]{1,0:T(8,128)(2,1)S(1)}, u32[]{:S(2)}, u32[]{:S(2)}) collective-permute-start(bf16[224,256]{1,0:T(8,128)(2,1)S(1)} %get-tuple-element.38), channel_id=1, source_target_pairs={{0,8},{4,12},{8,0},{12,4},{16,24},{20,28},{24,16},{28,20},{1,9},{5... | collective-permute-start | bytes 344072 | tf_op jit(solution)/shard_map/ppermute | solution.py:156
  5.5 8.3 %collective-permute-start.2 = (bf16[224,256]{1,0:T(8,128)(2,1)S(1)}, bf16[224,256]{1,0:T(8,128)(2,1)S(1)}, u32[]{:S(2)}, u32[]{:S(2)}) collective-permute-start(bf16[224,256]{1,0:T(8,128)(2,1)S(1)} %get-tuple-element.39), channel_id=1, source_target_pairs={{0,16},{4,20},{8,24},{12,28},{16,0},{20,4},{24,8},{28,12},{1,17},{... | collective-permute-start | bytes 344072 | tf_op jit(solution)/shard_map/ppermute | solution.py:156
  5.6 15.6 %collective-permute-start.7 = (bf16[32,2048]{1,0:T(8,128)(2,1)S(1)}, bf16[32,2048]{1,0:T(8,128)(2,1)S(1)}, u32[]{:S(2)}, u32[]{:S(2)}) collective-permute-start(bf16[32,2048]{1,0:T(8,128)(2,1)S(1)} %get-tuple-element.63), channel_id=1, source_target_pairs={{0,1},{1,0},{2,3},{3,2},{4,5},{5,4},{6,7},{7,6},{8,9},{9,8},{10,11... | collective-permute-start | bytes 393224 | tf_op jit(solution)/shard_map/ppermute | solution.py:156
  7.1 3.9 %copy-start = (f32[32]{0:T(128)S(1)}, f32[32]{0:T(128)}, u32[]{:S(2)}) copy-start(f32[32]{0:T(128)} %skip_ref) | copy-start | bytes 388
  7.1 7.6 %collective-permute-start.3 = (bf16[224,256]{1,0:T(8,128)(2,1)S(1)}, bf16[224,256]{1,0:T(8,128)(2,1)S(1)}, u32[]{:S(2)}, u32[]{:S(2)}) collective-permute-start(bf16[224,256]{1,0:T(8,128)(2,1)S(1)} %get-tuple-element.40), channel_id=1, source_target_pairs={{0,28},{4,24},{8,20},{12,16},{16,12},{20,8},{24,4},{28,0},{1,29},{... | collective-permute-start | bytes 344072 | tf_op jit(solution)/shard_map/ppermute | solution.py:156
  13.0 4.6 %collective-permute-start.4 = (bf16[224,256]{1,0:T(8,128)(2,1)S(1)}, bf16[224,256]{1,0:T(8,128)(2,1)S(1)}, u32[]{:S(2)}, u32[]{:S(2)}) collective-permute-start(bf16[224,256]{1,0:T(8,128)(2,1)S(1)} %get-tuple-element.54), channel_id=1, source_target_pairs={{0,12},{4,8},{8,4},{12,0},{16,28},{20,24},{24,20},{28,16},{1,13},{... | collective-permute-start | bytes 344072 | tf_op jit(solution)/shard_map/ppermute | solution.py:156
  13.1 5.6 %collective-permute-start.5 = (bf16[224,256]{1,0:T(8,128)(2,1)S(1)}, bf16[224,256]{1,0:T(8,128)(2,1)S(1)}, u32[]{:S(2)}, u32[]{:S(2)}) collective-permute-start(bf16[224,256]{1,0:T(8,128)(2,1)S(1)} %get-tuple-element.55), channel_id=1, source_target_pairs={{0,20},{4,16},{8,28},{12,24},{16,4},{20,0},{24,12},{28,8},{1,21},{... | collective-permute-start | bytes 344072 | tf_op jit(solution)/shard_map/ppermute | solution.py:156
  13.8 4.8 %collective-permute-start.6 = (bf16[224,256]{1,0:T(8,128)(2,1)S(1)}, bf16[224,256]{1,0:T(8,128)(2,1)S(1)}, u32[]{:S(2)}, u32[]{:S(2)}) collective-permute-start(bf16[224,256]{1,0:T(8,128)(2,1)S(1)} %get-tuple-element.56), channel_id=1, source_target_pairs={{0,4},{4,0},{8,12},{12,8},{16,20},{20,16},{24,28},{28,24},{1,5},{5... | collective-permute-start | bytes 344072 | tf_op jit(solution)/shard_map/ppermute | solution.py:156

commit v16 on v13

--- a/solution.py
+++ b/solution.py
@@ -259,7 +259,7 @@
                 for c in range(own):
                     factor = jnp.where(jnp.bitwise_xor(place, e) == m, gate[c * early + at : c * early + at + some, :], 1.0)
                     rows[c] = rows[c] * factor
-            out_ref[k * ch_count + m] = jnp.concatenate(rows, 0).astype(jnp.bfloat16)
+            out_ref[parts * ch_count - 1 - (k * ch_count + m)] = jnp.concatenate(rows, 0).astype(jnp.bfloat16)
 
 
 def convolve(got, tables, own, near, ch_count):
@@ -296,7 +296,7 @@
     for m in range(ch_count):
         here = slice(m * channels, (m + 1) * channels)
         for k in range(sources // ch_count):
-            part = got_ref[k * ch_count + m].astype(jnp.float32)
+            part = got_ref[sources - 1 - (k * ch_count + m)].astype(jnp.float32)
             first = m * channels * some + k * rows
             for h in range(W // LANES):
                 flat[h, first : first + rows, :] = part[:, LANES * h : LANES * (h + 1)]
@@ -319,7 +319,7 @@
         ones = [jnp.ones_like(gates[0])] * (ch_count - len(gates))
         order = jnp.bitwise_xor(lax.axis_index("ch"), jnp.arange(ch_count))
         gate = jnp.stack(gates + ones)[order].reshape(shape)
-        got = got.reshape(-1, ch_count, rows, W).swapaxes(0, 1)
+        got = got[::-1].reshape(-1, ch_count, rows, W).swapaxes(0, 1)
         return (got.reshape(shape).astype(jnp.float32) * gate.astype(jnp.float32)).astype(jnp.bfloat16)
     return pl.pallas_call(
         functools.partial(unpack_kernel, own),
@@ -354,7 +354,8 @@
         gates[d] = swap(gates[d], "ch", ch_count, d)
     mixed = convolve(got, tables, own, near, ch_count)
     mixed, gates = lax.optimization_barrier((mixed, gates))
-    mixed = lax.all_to_all(mixed, ("ctx", "ch"), split_axis=0, concat_axis=0, tiled=True)
+    places = list(range(ctx_count * ch_count))[::-1]
+    mixed = lax.all_to_all(mixed, ("ctx", "ch"), split_axis=0, concat_axis=0, tiled=True, axis_index_groups=[places])
     return unpack(mixed, gates, own, ch_count)
 
 

time: 41.6 us -> 43.2 us (1.038)
  the two profiles are of different devices: /device:TPU:1 before, /device:TPU:0 now
where the time goes in v16:
time: 43.2 us; the launch traced here: 43 us
  blocking collectives  20.4 us (47%)
  starting transfers between devices  10 us (23%)
  Pallas kernels  7.88 us (18%)
  waiting for transfers between devices  4.65 us (11%)
    all_to_all x1, blocking collectives, body(): lax.all_to_all(mixed, ('ctx', 'ch'), split_axis=0, concat_axis=0, tiled=T...  20.4 us
    ppermute x8, starting transfers between devices, swap(): return lax.ppermute(piece, axis, [(i, i ^ d) for i in range(count)])  10 us
    ppermute x8, waiting for transfers between devices, swap(): return lax.ppermute(piece, axis, [(i, i ^ d) for i in range(count)])  4.65 us
    pallas_call x1, Pallas kernels, convolve(): pl.pallas_call(functools.partial(conv_kernel, own, near, ch_count, parts)...  2.6 us
    pallas_call x1, Pallas kernels, pack(): pl.pallas_call(functools.partial(pack_kernel, own, blocks, group, ch_coun...  2.18 us
    pallas_call x1, Pallas kernels, make_tables(): pl.pallas_call(functools.partial(tables_kernel, own), out_shape=[jax.Shap...  2.09 us
    pallas_call x1, Pallas kernels, unpack(): pl.pallas_call(functools.partial(unpack_kernel, own), out_shape=jax.Shape...  1.01 us
  transfers between devices with their start and end apart: 8, of which 3 were waited for; matrix products, arithmetic and copies ran while one was open for 0% of the time, Pallas kernels for 11%

profile of v16, /device:TPU:0, one launch (start us, length us, event | category | flops | bytes accessed | tf_op | source)
XLA Modules:
  0.0 43.0 jit_solution(8751008185326200592)
XLA Ops:
  0.0 2.2 %pack.1 = (bf16[224,256]{1,0:T(8,128)(2,1)S(1)}, bf16[224,256]{1,0:T(8,128)(2,1)S(1)}, bf16[224,256]{1,0:T(8,128)(2,1)S(1)}, bf16[224,256]{1,0:T(8,128)(2,1)S(1)...) custom-call(bf16[32,8192]{1,0:T(8,128)(2,1)} %pre_ref.1, ...), custom_call_target="tpu_custom_call" | custom-call | tf_op jit(solution)/shard_map/pack/pallas_call | solution.py:116
  2.2 4.0 %collective-permute-start = (bf16[224,256]{1,0:T(8,128)(2,1)S(1)}, bf16[224,256]{1,0:T(8,128)(2,1)S(1)}, u32[]{:S(2)}, u32[]{:S(2)}) collective-permute-start(bf16[224,256]{1,0:T(8,128)(2,1)S(1)} %get-tuple-element.37), channel_id=1, source_target_pairs={{0,24},{4,28},{8,16},{12,20},{16,8},{20,12},{24,0},{28,4},{1,25},{... | collective-permute-start | bytes 344072 | tf_op jit(solution)/shard_map/ppermute | solution.py:147
  6.1 0.5 %collective-permute-start.1 = (bf16[224,256]{1,0:T(8,128)(2,1)S(1)}, bf16[224,256]{1,0:T(8,128)(2,1)S(1)}, u32[]{:S(2)}, u32[]{:S(2)}) collective-permute-start(bf16[224,256]{1,0:T(8,128)(2,1)S(1)} %get-tuple-element.38), channel_id=1, source_target_pairs={{0,8},{4,12},{8,0},{12,4},{16,24},{20,28},{24,16},{28,20},{1,9},{5... | collective-permute-start | bytes 344072 | tf_op jit(solution)/shard_map/ppermute | solution.py:147
  6.7 0.1 collective-permute-start.2
  6.8 2.0 %collective-permute-start.7 = (bf16[32,2048]{1,0:T(8,128)(2,1)S(1)}, bf16[32,2048]{1,0:T(8,128)(2,1)S(1)}, u32[]{:S(2)}, u32[]{:S(2)}) collective-permute-start(bf16[32,2048]{1,0:T(8,128)(2,1)S(1)} %get-tuple-element.63), channel_id=1, source_target_pairs={{0,1},{1,0},{2,3},{3,2},{4,5},{5,4},{6,7},{7,6},{8,9},{9,8},{10,11... | collective-permute-start | bytes 393224 | tf_op jit(solution)/shard_map/ppermute | solution.py:147
  8.8 0.0 copy-start
  8.8 0.8 %collective-permute-start.3 = (bf16[224,256]{1,0:T(8,128)(2,1)S(1)}, bf16[224,256]{1,0:T(8,128)(2,1)S(1)}, u32[]{:S(2)}, u32[]{:S(2)}) collective-permute-start(bf16[224,256]{1,0:T(8,128)(2,1)S(1)} %get-tuple-element.40), channel_id=1, source_target_pairs={{0,28},{4,24},{8,20},{12,16},{16,12},{20,8},{24,4},{28,0},{1,29},{... | collective-permute-start | bytes 344072 | tf_op jit(solution)/shard_map/ppermute | solution.py:147
  9.5 0.0 copy-done
  9.5 2.1 %make_tables.1 = (bf16[512,256]{1,0:T(8,128)(2,1)S(1)}, bf16[256,512]{1,0:T(8,128)(2,1)S(1)}, bf16[512,512]{1,0:T(8,128)(2,1)S(1)}, bf16[512,512]{1,0:T(8,128)(2,1)S(1)}, f32[288,512]{1,0:T(8,128)S(1)}) custom-call(f32[32]{0:T(128)S(1)} %copy-done, f32[512,256]{1,0:T(8,128)} %constant.8.clone.rest_0_, f32[256,512]{1,0:T(8,128)} %constant.9.clone.rest_1_, ...), custom_call_target="tpu_custom_call" | custom-call | tf_op jit(solution)/shard_map/make_tables/pallas_call | solution.py:183
  11.6 0.0 collective-permute-done.rest_1_
  11.6 2.0 %collective-permute-start.4 = (bf16[224,256]{1,0:T(8,128)(2,1)S(1)}, bf16[224,256]{1,0:T(8,128)(2,1)S(1)}, u32[]{:S(2)}, u32[]{:S(2)}) collective-permute-start(bf16[224,256]{1,0:T(8,128)(2,1)S(1)} %get-tuple-element.54), channel_id=1, source_target_pairs={{0,12},{4,8},{8,4},{12,0},{16,28},{20,24},{24,20},{28,16},{1,13},{... | collective-permute-start | bytes 344072 | tf_op jit(solution)/shard_map/ppermute | solution.py:147
  13.6 0.0 collective-permute-done.1.rest_2_
  13.6 0.7 %collective-permute-start.5 = (bf16[224,256]{1,0:T(8,128)(2,1)S(1)}, bf16[224,256]{1,0:T(8,128)(2,1)S(1)}, u32[]{:S(2)}, u32[]{:S(2)}) collective-permute-start(bf16[224,256]{1,0:T(8,128)(2,1)S(1)} %get-tuple-element.55), channel_id=1, source_target_pairs={{0,20},{4,16},{8,28},{12,24},{16,4},{20,0},{24,12},{28,8},{1,21},{... | collective-permute-start | bytes 344072 | tf_op jit(solution)/shard_map/ppermute | solution.py:147
  14.3 0.0 collective-permute-done.2.rest_3_
  14.3 0.0 collective-permute-start.6
  14.3 0.7 %collective-permute-done.3.rest_4_ = bf16[224,256]{1,0:T(8,128)(2,1)S(1)} collective-permute-done((bf16[224,256]{1,0:T(8,128)(2,1)S(1)}, bf16[224,256]{1,0:T(8,128)(2,1)S(1)}, u32[]{:S(2)}, u32[]{:S(2)}) %collective-permute-start.3) | collective-permute-done | bytes 114720 | tf_op jit(solution)/shard_map/ppermute | solution.py:147
  15.0 1.4 %collective-permute-done.4.rest_5_ = bf16[224,256]{1,0:T(8,128)(2,1)S(1)} collective-permute-done((bf16[224,256]{1,0:T(8,128)(2,1)S(1)}, bf16[224,256]{1,0:T(8,128)(2,1)S(1)}, u32[]{:S(2)}, u32[]{:S(2)}) %collective-permute-start.4) | collective-permute-done | bytes 114720 | tf_op jit(solution)/shard_map/ppermute | solution.py:147
  16.4 2.6 %collective-permute-done.5.rest_6_ = bf16[224,256]{1,0:T(8,128)(2,1)S(1)} collective-permute-done((bf16[224,256]{1,0:T(8,128)(2,1)S(1)}, bf16[224,256]{1,0:T(8,128)(2,1)S(1)}, u32[]{:S(2)}, u32[]{:S(2)}) %collective-permute-start.5) | collective-permute-done | bytes 114720 | tf_op jit(solution)/shard_map/ppermute | solution.py:147
  19.0 0.0 collective-permute-done.6.rest_7_
  19.0 2.6 %convolve.1 = bf16[32,32,256]{2,1,0:T(8,128)(2,1)S(1)} custom-call(bf16[224,256]{1,0:T(8,128)(2,1)S(1)} %get-tuple-element.36.rest_0_, bf16[224,256]{1,0:T(8,128)(2,1)S(1)} %collective-permute-done.rest_1_, bf16[224,256]{1,0:T(8,128)(2,1)S(1)} %collective-permute-done.1.rest_2_, bf16[224,256]{1,0:T(8,128)(2,1)S(1)} %collective-permute-done.2.rest_3_, ...), custom_call_target="tpu_custom_call" | custom-call | flops 65536 | bytes 262144 | tf_op jit(solution)/shard_map/convolve/pallas_call | solution.py:269
  21.6 0.0 collective-permute-done.7.rest_1_
  21.6 20.4 %all_to_all.5.got_ref = bf16[32,32,256]{2,1,0:T(8,128)(2,1)S(1)} all-to-all(bf16[32,32,256]{2,1,0:T(8,128)(2,1)S(1)} %convolve.1), channel_id=1, replica_groups={{31,30,29,28,27,26,25,24,23,22,21,20,19,18,17,16,15,14,13,12,11,10,9,8,..., dimensions={0} | all-to-all | bytes 1048576 | tf_op jit(solution)/shard_map/all_to_all | solution.py:358
  42.0 1.0 %unpack.1 = bf16[128,2048]{1,0:T(8,128)(2,1)} custom-call(bf16[32,32,256]{2,1,0:T(8,128)(2,1)S(1)} %all_to_all.5.got_ref, bf16[32,2048]{1,0:T(8,128)(2,1)S(1)} %get-tuple-element.65.rest_0_, bf16[32,2048]{1,0:T(8,128)(2,1)S(1)} %collective-permute-done.7.rest_1_), custom_call_target="tpu_custom_call" | custom-call | tf_op jit(solution)/shard_map/unpack/pallas_call | solution.py:324
Async XLA Ops:
  2.2 9.5 %collective-permute-start = (bf16[224,256]{1,0:T(8,128)(2,1)S(1)}, bf16[224,256]{1,0:T(8,128)(2,1)S(1)}, u32[]{:S(2)}, u32[]{:S(2)}) collective-permute-start(bf16[224,256]{1,0:T(8,128)(2,1)S(1)} %get-tuple-element.37), channel_id=1, source_target_pairs={{0,24},{4,28},{8,16},{12,20},{16,8},{20,12},{24,0},{28,4},{1,25},{... | collective-permute-start | bytes 344072 | tf_op jit(solution)/shard_map/ppermute | solution.py:147
  6.1 7.5 %collective-permute-start.1 = (bf16[224,256]{1,0:T(8,128)(2,1)S(1)}, bf16[224,256]{1,0:T(8,128)(2,1)S(1)}, u32[]{:S(2)}, u32[]{:S(2)}) collective-permute-start(bf16[224,256]{1,0:T(8,128)(2,1)S(1)} %get-tuple-element.38), channel_id=1, source_target_pairs={{0,8},{4,12},{8,0},{12,4},{16,24},{20,28},{24,16},{28,20},{1,9},{5... | collective-permute-start | bytes 344072 | tf_op jit(solution)/shard_map/ppermute | solution.py:147
  6.7 7.6 %collective-permute-start.2 = (bf16[224,256]{1,0:T(8,128)(2,1)S(1)}, bf16[224,256]{1,0:T(8,128)(2,1)S(1)}, u32[]{:S(2)}, u32[]{:S(2)}) collective-permute-start(bf16[224,256]{1,0:T(8,128)(2,1)S(1)} %get-tuple-element.39), channel_id=1, source_target_pairs={{0,16},{4,20},{8,24},{12,28},{16,0},{20,4},{24,8},{28,12},{1,17},{... | collective-permute-start | bytes 344072 | tf_op jit(solution)/shard_map/ppermute | solution.py:147
  6.8 14.8 %collective-permute-start.7 = (bf16[32,2048]{1,0:T(8,128)(2,1)S(1)}, bf16[32,2048]{1,0:T(8,128)(2,1)S(1)}, u32[]{:S(2)}, u32[]{:S(2)}) collective-permute-start(bf16[32,2048]{1,0:T(8,128)(2,1)S(1)} %get-tuple-element.63), channel_id=1, source_target_pairs={{0,1},{1,0},{2,3},{3,2},{4,5},{5,4},{6,7},{7,6},{8,9},{9,8},{10,11... | collective-permute-start | bytes 393224 | tf_op jit(solution)/shard_map/ppermute | solution.py:147
  8.8 0.8 %copy-start = (f32[32]{0:T(128)S(1)}, f32[32]{0:T(128)}, u32[]{:S(2)}) copy-start(f32[32]{0:T(128)} %skip_ref) | copy-start | bytes 388
  8.8 6.2 %collective-permute-start.3 = (bf16[224,256]{1,0:T(8,128)(2,1)S(1)}, bf16[224,256]{1,0:T(8,128)(2,1)S(1)}, u32[]{:S(2)}, u32[]{:S(2)}) collective-permute-start(bf16[224,256]{1,0:T(8,128)(2,1)S(1)} %get-tuple-element.40), channel_id=1, source_target_pairs={{0,28},{4,24},{8,20},{12,16},{16,12},{20,8},{24,4},{28,0},{1,29},{... | collective-permute-start | bytes 344072 | tf_op jit(solution)/shard_map/ppermute | solution.py:147
  11.6 4.7 %collective-permute-start.4 = (bf16[224,256]{1,0:T(8,128)(2,1)S(1)}, bf16[224,256]{1,0:T(8,128)(2,1)S(1)}, u32[]{:S(2)}, u32[]{:S(2)}) collective-permute-start(bf16[224,256]{1,0:T(8,128)(2,1)S(1)} %get-tuple-element.54), channel_id=1, source_target_pairs={{0,12},{4,8},{8,4},{12,0},{16,28},{20,24},{24,20},{28,16},{1,13},{... | collective-permute-start | bytes 344072 | tf_op jit(solution)/shard_map/ppermute | solution.py:147
  13.6 5.3 %collective-permute-start.5 = (bf16[224,256]{1,0:T(8,128)(2,1)S(1)}, bf16[224,256]{1,0:T(8,128)(2,1)S(1)}, u32[]{:S(2)}, u32[]{:S(2)}) collective-permute-start(bf16[224,256]{1,0:T(8,128)(2,1)S(1)} %get-tuple-element.55), channel_id=1, source_target_pairs={{0,20},{4,16},{8,28},{12,24},{16,4},{20,0},{24,12},{28,8},{1,21},{... | collective-permute-start | bytes 344072 | tf_op jit(solution)/shard_map/ppermute | solution.py:147
  14.3 4.6 %collective-permute-start.6 = (bf16[224,256]{1,0:T(8,128)(2,1)S(1)}, bf16[224,256]{1,0:T(8,128)(2,1)S(1)}, u32[]{:S(2)}, u32[]{:S(2)}) collective-permute-start(bf16[224,256]{1,0:T(8,128)(2,1)S(1)} %get-tuple-element.56), channel_id=1, source_target_pairs={{0,4},{4,0},{8,12},{12,8},{16,20},{20,16},{24,28},{28,24},{1,5},{5... | collective-permute-start | bytes 344072 | tf_op jit(solution)/shard_map/ppermute | solution.py:147

commit v17 on v13

--- a/solution.py
+++ b/solution.py
@@ -48,9 +48,18 @@
     return jnp.concatenate(rows, 1)
 
 
+def late_pieces(own, piece, ch_count):
+    early = max(1, ch_count // 4)
+    if own * piece * early % TILE:
+        early = ch_count // 2
+    return ch_count - early
+
+
 def pack_kernel(own, blocks, group, ch_count, parts, pre_ref, val_ref, taps_ref, post_ref, *rest):
-    out_refs, gate_refs = rest[:parts], rest[parts : parts + ch_count // 2]
-    pre_s, val_s, taps_s, post_s, natural, natural_taps, natural_gate, stage, in_sems = rest[parts + ch_count // 2 :]
+    piece = blocks // ch_count
+    late = late_pieces(own, piece, ch_count)
+    out_refs, gate_refs = rest[:parts], rest[parts : parts + late]
+    pre_s, val_s, taps_s, post_s, natural, natural_taps, natural_gate, stage, in_sems = rest[parts + late :]
     channels = own * parts
     some = min(TILE, channels)
     rows = own * blocks
@@ -84,16 +93,15 @@
             stage[i, rows:main, :] = taps.astype(jnp.bfloat16)
     gate_load.wait()
     place = lax.axis_index("ch")
-    piece = blocks // ch_count
     for d in range(ch_count):
         first = jnp.bitwise_xor(place, d) * (piece * W)
-        if d < ch_count // 2:
+        if d < late:
             gate_refs[d][...] = post_s[:, pl.ds(pl.multiple_of(first, LANES), piece * W)]
         else:
             for j in range(piece):
                 cols = pl.ds(pl.multiple_of(first + W * j, LANES), W)
-                lay(natural_gate, (d - ch_count // 2) * piece + j, post_s[:, cols].astype(jnp.float32))
-    early = piece * (ch_count - ch_count // 2)
+                lay(natural_gate, (d - late) * piece + j, post_s[:, cols].astype(jnp.float32))
+    early = piece * (ch_count - late)
     for i in range(parts):
         gate = [pick(natural_gate, own * i + c, channels, early) for c in range(own)]
         stage[i, main:, :] = jnp.concatenate(gate, 0).astype(jnp.bfloat16)
@@ -108,7 +116,8 @@
     group = channels // taps.shape[0]
     blocks = block // W
     piece = blocks // ch_count
-    early = piece * (ch_count - ch_count // 2)
+    late = late_pieces(own, piece, ch_count)
+    early = piece * (ch_count - late)
     local = (own + 1) * blocks + own * early
     halves = W // LANES
     some = min(TILE, channels)
@@ -116,9 +125,9 @@
     out = pl.pallas_call(
         functools.partial(pack_kernel, own, blocks, group, ch_count, parts),
         out_shape=[jax.ShapeDtypeStruct((local, W), jnp.bfloat16)] * parts
-        + [jax.ShapeDtypeStruct((channels, piece * W), jnp.bfloat16)] * (ch_count // 2),
+        + [jax.ShapeDtypeStruct((channels, piece * W), jnp.bfloat16)] * late,
         in_specs=[in_hbm()] * 4,
-        out_specs=[whole_vmem()] * (parts + ch_count // 2),
+        out_specs=[whole_vmem()] * (parts + late),
         scratch_shapes=[
             pltpu.VMEM(pre_gate.shape, jnp.bfloat16),
             pltpu.VMEM(value.shape, jnp.bfloat16),
@@ -246,7 +255,8 @@
         cols = slice(W * c, W * (c + 1))
         z_all[c] = conv[:, cols] + turns_ref[blocks + 8 * c : blocks + 8 * c + 1, 0:W] * x_all[:, cols].astype(jnp.float32)
     some = out_ref.shape[1] // own
-    early = some * (ch_count - ch_count // 2)
+    late = late_pieces(own, some, ch_count)
+    early = some * (ch_count - late)
     place = lax.axis_index("ch")
     for d, got_ref in zip(order, got_refs):
         k = jnp.bitwise_xor(me, d)
@@ -254,8 +264,8 @@
         mine = [z_all[c, pl.ds(pl.multiple_of(k * near, TILE), near), :] for c in range(own)]
         for m in range(ch_count):
             rows = [part[m * some : (m + 1) * some, :] for part in mine]
-            for e in range(ch_count // 2, ch_count):
-                at = (e - ch_count // 2) * some
+            for e in range(late, ch_count):
+                at = (e - late) * some
                 for c in range(own):
                     factor = jnp.where(jnp.bitwise_xor(place, e) == m, gate[c * early + at : c * early + at + some, :], 1.0)
                     rows[c] = rows[c] * factor
@@ -347,13 +357,12 @@
     got = [got[d] for d in order]
     tables, skip, _ = lax.optimization_barrier((dft_tables(near * ctx_count), skip, got[0]))
     tables = list(make_tables(skip, *tables, own))
-    half = ctx_count // 2 + 1
-    tables, got[half:] = lax.optimization_barrier((tables, got[half:]))
     got = [swap(piece, "ctx", ctx_count, d) if d else piece for piece, d in zip(got, order)]
-    for d in range(1, ch_count // 2):
+    for d in range(1, len(gates)):
         gates[d] = swap(gates[d], "ch", ch_count, d)
     mixed = convolve(got, tables, own, near, ch_count)
-    mixed, gates = lax.optimization_barrier((mixed, gates))
+    mixed, gates = lax.optimization_barrier((mixed, gates[::-1]))
+    gates = gates[::-1]
     mixed = lax.all_to_all(mixed, ("ctx", "ch"), split_axis=0, concat_axis=0, tiled=True)
     return unpack(mixed, gates, own, ch_count)
 

time: 41.6 us -> 41.1 us (0.988)
  waiting for transfers between devices: 4.25 us -> 1.61 us
  starting transfers between devices: 10.1 us -> 12.4 us
    ppermute x8 -> x9, waiting for transfers between devices: 4.25 us -> 1.61 us  [swap(): return lax.ppermute(piece, axis, [(i, i ^ d) for i in range(count)])]
    ppermute x8 -> x9, starting transfers between devices: 10.1 us -> 12.4 us  [swap(): return lax.ppermute(piece, axis, [(i, i ^ d) for i in range(count)])]
  transfers between devices with their start and end apart: 8 -> 9, of which waited for: 3 -> 2; matrix products, arithmetic and copies ran while one was open for 0% -> 0% of each run, Pallas kernels for 11% -> 11%
where the time goes in v17:
time: 41.1 us; the launch traced here: 40.9 us
  blocking collectives  19.2 us (47%)
  starting transfers between devices  12.4 us (30%)
  Pallas kernels  7.65 us (19%)
  waiting for transfers between devices  1.61 us (4%)
    all_to_all x1, blocking collectives, body(): lax.all_to_all(mixed, ('ctx', 'ch'), split_axis=0, concat_axis=0, tiled=T...  19.2 us
    ppermute x9, starting transfers between devices, swap(): return lax.ppermute(piece, axis, [(i, i ^ d) for i in range(count)])  12.4 us
    pallas_call x1, Pallas kernels, convolve(): pl.pallas_call(functools.partial(conv_kernel, own, near, ch_count, parts)...  2.53 us
    pallas_call x1, Pallas kernels, make_tables(): pl.pallas_call(functools.partial(tables_kernel, own), out_shape=[jax.Shap...  2.09 us
    pallas_call x1, Pallas kernels, pack(): pl.pallas_call(functools.partial(pack_kernel, own, blocks, group, ch_coun...  2.02 us
    ppermute x9, waiting for transfers between devices, swap(): return lax.ppermute(piece, axis, [(i, i ^ d) for i in range(count)])  1.61 us
    pallas_call x1, Pallas kernels, unpack(): pl.pallas_call(functools.partial(unpack_kernel, own), out_shape=jax.Shape...  1.01 us
  transfers between devices with their start and end apart: 9, of which 2 were waited for; matrix products, arithmetic and copies ran while one was open for 0% of the time, Pallas kernels for 11%

profile of v17, /device:TPU:1, one launch (start us, length us, event | category | flops | bytes accessed | tf_op | source)
XLA Modules:
  0.0 40.9 jit_solution(11787927309251494103)
XLA Ops:
  0.0 2.0 %pack.1 = (bf16[192,256]{1,0:T(8,128)(2,1)S(1)}, bf16[192,256]{1,0:T(8,128)(2,1)S(1)}, bf16[192,256]{1,0:T(8,128)(2,1)S(1)}, bf16[192,256]{1,0:T(8,128)(2,1)S(1)...) custom-call(bf16[32,8192]{1,0:T(8,128)(2,1)} %pre_ref.1, ...), custom_call_target="tpu_custom_call" | custom-call | tf_op jit(solution)/shard_map/pack/pallas_call | solution.py:125
  2.0 3.1 %collective-permute-start = (bf16[192,256]{1,0:T(8,128)(2,1)S(1)}, bf16[192,256]{1,0:T(8,128)(2,1)S(1)}, u32[]{:S(2)}, u32[]{:S(2)}) collective-permute-start(bf16[192,256]{1,0:T(8,128)(2,1)S(1)} %get-tuple-element.31), channel_id=1, source_target_pairs={{0,24},{4,28},{8,16},{12,20},{16,8},{20,12},{24,0},{28,4},{1,25},{... | collective-permute-start | bytes 294920 | tf_op jit(solution)/shard_map/ppermute | solution.py:156
  5.1 0.3 collective-permute-start.1
  5.3 0.1 collective-permute-start.2
  5.5 3.7 %collective-permute-start.3 = (bf16[192,256]{1,0:T(8,128)(2,1)S(1)}, bf16[192,256]{1,0:T(8,128)(2,1)S(1)}, u32[]{:S(2)}, u32[]{:S(2)}) collective-permute-start(bf16[192,256]{1,0:T(8,128)(2,1)S(1)} %get-tuple-element.34), channel_id=1, source_target_pairs={{0,28},{4,24},{8,20},{12,16},{16,12},{20,8},{24,4},{28,0},{1,29},{... | collective-permute-start | bytes 294920 | tf_op jit(solution)/shard_map/ppermute | solution.py:156
  9.1 2.3 %collective-permute-start.7 = (bf16[32,2048]{1,0:T(8,128)(2,1)S(1)}, bf16[32,2048]{1,0:T(8,128)(2,1)S(1)}, u32[]{:S(2)}, u32[]{:S(2)}) collective-permute-start(bf16[32,2048]{1,0:T(8,128)(2,1)S(1)} %get-tuple-element.48), channel_id=1, source_target_pairs={{0,2},{1,3},{2,0},{3,1},{4,6},{5,7},{6,4},{7,5},{8,10},{9,11},{10,... | collective-permute-start | bytes 393224 | tf_op jit(solution)/shard_map/ppermute | solution.py:156
  11.4 0.0 collective-permute-done.rest_1_
  11.5 1.3 %collective-permute-start.8 = (bf16[32,2048]{1,0:T(8,128)(2,1)S(1)}, bf16[32,2048]{1,0:T(8,128)(2,1)S(1)}, u32[]{:S(2)}, u32[]{:S(2)}) collective-permute-start(bf16[32,2048]{1,0:T(8,128)(2,1)S(1)} %get-tuple-element.49), channel_id=1, source_target_pairs={{0,1},{1,0},{2,3},{3,2},{4,5},{5,4},{6,7},{7,6},{8,9},{9,8},{10,11... | collective-permute-start | bytes 393224 | tf_op jit(solution)/shard_map/ppermute | solution.py:156
  12.7 0.0 collective-permute-done.1.rest_2_
  12.8 0.1 collective-permute-start.4
  12.9 0.0 collective-permute-done.2.rest_3_
  12.9 0.6 %collective-permute-start.5 = (bf16[192,256]{1,0:T(8,128)(2,1)S(1)}, bf16[192,256]{1,0:T(8,128)(2,1)S(1)}, u32[]{:S(2)}, u32[]{:S(2)}) collective-permute-start(bf16[192,256]{1,0:T(8,128)(2,1)S(1)} %get-tuple-element.36), channel_id=1, source_target_pairs={{0,20},{4,16},{8,28},{12,24},{16,4},{20,0},{24,12},{28,8},{1,21},{... | collective-permute-start | bytes 294920 | tf_op jit(solution)/shard_map/ppermute | solution.py:156
  13.5 0.0 collective-permute-done.3.rest_4_
  13.5 0.9 %collective-permute-start.6 = (bf16[192,256]{1,0:T(8,128)(2,1)S(1)}, bf16[192,256]{1,0:T(8,128)(2,1)S(1)}, u32[]{:S(2)}, u32[]{:S(2)}) collective-permute-start(bf16[192,256]{1,0:T(8,128)(2,1)S(1)} %get-tuple-element.37), channel_id=1, source_target_pairs={{0,4},{4,0},{8,12},{12,8},{16,20},{20,16},{24,28},{28,24},{1,5},{5... | collective-permute-start | bytes 294920 | tf_op jit(solution)/shard_map/ppermute | solution.py:156
  14.4 0.0 copy-done
  14.4 2.1 %make_tables.1 = (bf16[512,256]{1,0:T(8,128)(2,1)S(1)}, bf16[256,512]{1,0:T(8,128)(2,1)S(1)}, bf16[512,512]{1,0:T(8,128)(2,1)S(1)}, bf16[512,512]{1,0:T(8,128)(2,1)S(1)}, f32[288,512]{1,0:T(8,128)S(1)}) custom-call(f32[32]{0:T(128)S(1)} %copy-done, f32[512,256]{1,0:T(8,128)} %constant.8.clone.rest_0_, f32[256,512]{1,0:T(8,128)} %constant.9.clone.rest_1_, ...), custom_call_target="tpu_custom_call" | custom-call | tf_op jit(solution)/shard_map/make_tables/pallas_call | solution.py:192
  16.5 0.6 %collective-permute-done.4.rest_5_ = bf16[192,256]{1,0:T(8,128)(2,1)S(1)} collective-permute-done((bf16[192,256]{1,0:T(8,128)(2,1)S(1)}, bf16[192,256]{1,0:T(8,128)(2,1)S(1)}, u32[]{:S(2)}, u32[]{:S(2)}) %collective-permute-start.4) | collective-permute-done | bytes 98336 | tf_op jit(solution)/shard_map/ppermute | solution.py:156
  17.1 1.0 %collective-permute-done.5.rest_6_ = bf16[192,256]{1,0:T(8,128)(2,1)S(1)} collective-permute-done((bf16[192,256]{1,0:T(8,128)(2,1)S(1)}, bf16[192,256]{1,0:T(8,128)(2,1)S(1)}, u32[]{:S(2)}, u32[]{:S(2)}) %collective-permute-start.5) | collective-permute-done | bytes 98336 | tf_op jit(solution)/shard_map/ppermute | solution.py:156
  18.1 0.0 collective-permute-done.6.rest_7_
  18.1 2.5 %convolve.1 = bf16[32,32,256]{2,1,0:T(8,128)(2,1)S(1)} custom-call(bf16[192,256]{1,0:T(8,128)(2,1)S(1)} %get-tuple-element.30.rest_0_, bf16[192,256]{1,0:T(8,128)(2,1)S(1)} %collective-permute-done.rest_1_, bf16[192,256]{1,0:T(8,128)(2,1)S(1)} %collective-permute-done.1.rest_2_, bf16[192,256]{1,0:T(8,128)(2,1)S(1)} %collective-permute-done.2.rest_3_, ...), custom_call_target="tpu_custom_call" | custom-call | flops 65536 | bytes 262144 | tf_op jit(solution)/shard_map/convolve/pallas_call | solution.py:279
  20.6 0.0 collective-permute-done.7.rest_2_
  20.7 0.0 collective-permute-done.8.rest_1_
  20.7 19.2 %all_to_all.5.got_ref = bf16[32,32,256]{2,1,0:T(8,128)(2,1)S(1)} all-to-all(bf16[32,32,256]{2,1,0:T(8,128)(2,1)S(1)} %convolve.1), channel_id=1, replica_groups=mesh['ctx'=8,'ch'=4] {'ctx','ch'}, dimensions={0} | all-to-all | bytes 1048576 | tf_op jit(solution)/shard_map/all_to_all | solution.py:366
  39.9 1.0 %unpack.1 = bf16[128,2048]{1,0:T(8,128)(2,1)} custom-call(bf16[32,32,256]{2,1,0:T(8,128)(2,1)S(1)} %all_to_all.5.got_ref, bf16[32,2048]{1,0:T(8,128)(2,1)S(1)} %get-tuple-element.52.rest_0_, bf16[32,2048]{1,0:T(8,128)(2,1)S(1)} %collective-permute-done.8.rest_1_, bf16[32,2048]{1,0:T(8,128)(2,1)S(1)} %collective-permute-done.7.rest_2_), custom_call_target="tpu_custom_call" | custom-call | tf_op jit(solution)/shard_map/unpack/pallas_call | solution.py:334
  (1 shorter events, 0.0 us)
Async XLA Ops:
  2.0 9.4 %collective-permute-start = (bf16[192,256]{1,0:T(8,128)(2,1)S(1)}, bf16[192,256]{1,0:T(8,128)(2,1)S(1)}, u32[]{:S(2)}, u32[]{:S(2)}) collective-permute-start(bf16[192,256]{1,0:T(8,128)(2,1)S(1)} %get-tuple-element.31), channel_id=1, source_target_pairs={{0,24},{4,28},{8,16},{12,20},{16,8},{20,12},{24,0},{28,4},{1,25},{... | collective-permute-start | bytes 294920 | tf_op jit(solution)/shard_map/ppermute | solution.py:156
  5.1 7.7 %collective-permute-start.1 = (bf16[192,256]{1,0:T(8,128)(2,1)S(1)}, bf16[192,256]{1,0:T(8,128)(2,1)S(1)}, u32[]{:S(2)}, u32[]{:S(2)}) collective-permute-start(bf16[192,256]{1,0:T(8,128)(2,1)S(1)} %get-tuple-element.32), channel_id=1, source_target_pairs={{0,8},{4,12},{8,0},{12,4},{16,24},{20,28},{24,16},{28,20},{1,9},{5... | collective-permute-start | bytes 294920 | tf_op jit(solution)/shard_map/ppermute | solution.py:156
  5.3 7.5 %collective-permute-start.2 = (bf16[192,256]{1,0:T(8,128)(2,1)S(1)}, bf16[192,256]{1,0:T(8,128)(2,1)S(1)}, u32[]{:S(2)}, u32[]{:S(2)}) collective-permute-start(bf16[192,256]{1,0:T(8,128)(2,1)S(1)} %get-tuple-element.33), channel_id=1, source_target_pairs={{0,16},{4,20},{8,24},{12,28},{16,0},{20,4},{24,8},{28,12},{1,17},{... | collective-permute-start | bytes 294920 | tf_op jit(solution)/shard_map/ppermute | solution.py:156
  5.5 8.1 %collective-permute-start.3 = (bf16[192,256]{1,0:T(8,128)(2,1)S(1)}, bf16[192,256]{1,0:T(8,128)(2,1)S(1)}, u32[]{:S(2)}, u32[]{:S(2)}) collective-permute-start(bf16[192,256]{1,0:T(8,128)(2,1)S(1)} %get-tuple-element.34), channel_id=1, source_target_pairs={{0,28},{4,24},{8,20},{12,16},{16,12},{20,8},{24,4},{28,0},{1,29},{... | collective-permute-start | bytes 294920 | tf_op jit(solution)/shard_map/ppermute | solution.py:156
  9.1 11.5 %collective-permute-start.7 = (bf16[32,2048]{1,0:T(8,128)(2,1)S(1)}, bf16[32,2048]{1,0:T(8,128)(2,1)S(1)}, u32[]{:S(2)}, u32[]{:S(2)}) collective-permute-start(bf16[32,2048]{1,0:T(8,128)(2,1)S(1)} %get-tuple-element.48), channel_id=1, source_target_pairs={{0,2},{1,3},{2,0},{3,1},{4,6},{5,7},{6,4},{7,5},{8,10},{9,11},{10,... | collective-permute-start | bytes 393224 | tf_op jit(solution)/shard_map/ppermute | solution.py:156
  11.5 9.2 %collective-permute-start.8 = (bf16[32,2048]{1,0:T(8,128)(2,1)S(1)}, bf16[32,2048]{1,0:T(8,128)(2,1)S(1)}, u32[]{:S(2)}, u32[]{:S(2)}) collective-permute-start(bf16[32,2048]{1,0:T(8,128)(2,1)S(1)} %get-tuple-element.49), channel_id=1, source_target_pairs={{0,1},{1,0},{2,3},{3,2},{4,5},{5,4},{6,7},{7,6},{8,9},{9,8},{10,11... | collective-permute-start | bytes 393224 | tf_op jit(solution)/shard_map/ppermute | solution.py:156
  12.8 4.3 %collective-permute-start.4 = (bf16[192,256]{1,0:T(8,128)(2,1)S(1)}, bf16[192,256]{1,0:T(8,128)(2,1)S(1)}, u32[]{:S(2)}, u32[]{:S(2)}) collective-permute-start(bf16[192,256]{1,0:T(8,128)(2,1)S(1)} %get-tuple-element.35), channel_id=1, source_target_pairs={{0,12},{4,8},{8,4},{12,0},{16,28},{20,24},{24,20},{28,16},{1,13},{... | collective-permute-start | bytes 294920 | tf_op jit(solution)/shard_map/ppermute | solution.py:156
  12.9 5.2 %collective-permute-start.5 = (bf16[192,256]{1,0:T(8,128)(2,1)S(1)}, bf16[192,256]{1,0:T(8,128)(2,1)S(1)}, u32[]{:S(2)}, u32[]{:S(2)}) collective-permute-start(bf16[192,256]{1,0:T(8,128)(2,1)S(1)} %get-tuple-element.36), channel_id=1, source_target_pairs={{0,20},{4,16},{8,28},{12,24},{16,4},{20,0},{24,12},{28,8},{1,21},{... | collective-permute-start | bytes 294920 | tf_op jit(solution)/shard_map/ppermute | solution.py:156
  13.5 0.9 %copy-start = (f32[32]{0:T(128)S(1)}, f32[32]{0:T(128)}, u32[]{:S(2)}) copy-start(f32[32]{0:T(128)} %skip_ref) | copy-start | bytes 388
  13.5 4.6 %collective-permute-start.6 = (bf16[192,256]{1,0:T(8,128)(2,1)S(1)}, bf16[192,256]{1,0:T(8,128)(2,1)S(1)}, u32[]{:S(2)}, u32[]{:S(2)}) collective-permute-start(bf16[192,256]{1,0:T(8,128)(2,1)S(1)} %get-tuple-element.37), channel_id=1, source_target_pairs={{0,4},{4,0},{8,12},{12,8},{16,20},{20,16},{24,28},{28,24},{1,5},{5... | collective-permute-start | bytes 294920 | tf_op jit(solution)/shard_map/ppermute | solution.py:156

commit v18 on v17

--- a/solution.py
+++ b/solution.py
@@ -287,7 +287,7 @@
             pltpu.VMEM((own, blocks, W), jnp.float32),
         ],
         compiler_params=pltpu.CompilerParams(vmem_limit_bytes=32 * 2**20),
-        cost_estimate=pl.CostEstimate(flops=blocks * W, bytes_accessed=4 * blocks * W, transcendentals=0),
+        cost_estimate=pl.CostEstimate(flops=16000 * blocks * W, bytes_accessed=4 * blocks * W, transcendentals=0),
         name="convolve",
     )(*got, *tables)
 
@@ -360,6 +360,7 @@
     got = [swap(piece, "ctx", ctx_count, d) if d else piece for piece, d in zip(got, order)]
     for d in range(1, len(gates)):
         gates[d] = swap(gates[d], "ch", ch_count, d)
+    got[1:], gates[2:] = lax.optimization_barrier((got[1:], gates[2:]))
     mixed = convolve(got, tables, own, near, ch_count)
     mixed, gates = lax.optimization_barrier((mixed, gates[::-1]))
     gates = gates[::-1]

time: 41.1 us -> 40.7 us (level)
  blocking collectives: 19.2 us -> 18.4 us
  waiting for transfers between devices: 1.61 us -> 2.36 us
    all_to_all x1, blocking collectives: 19.2 us -> 18.4 us  [body(): lax.all_to_all(mixed, ('ctx', 'ch'), split_axis=0, concat_axis=0, tiled=T...]
    ppermute x9, waiting for transfers between devices: 1.61 us -> 2.36 us  [swap(): return lax.ppermute(piece, axis, [(i, i ^ d) for i in range(count)])]
  transfers between devices with their start and end apart: 9 -> 9, of which waited for: 2 -> 1; matrix products, arithmetic and copies ran while one was open for 0% -> 0% of each run, Pallas kernels for 11% -> 11%
where the time goes in v18:
time: 40.7 us; the launch traced here: 40.5 us
  blocking collectives  18.4 us (45%)
  starting transfers between devices  12.1 us (30%)
  Pallas kernels  7.65 us (19%)
  waiting for transfers between devices  2.36 us (6%)
    all_to_all x1, blocking collectives, body(): lax.all_to_all(mixed, ('ctx', 'ch'), split_axis=0, concat_axis=0, tiled=T...  18.4 us
    ppermute x9, starting transfers between devices, swap(): return lax.ppermute(piece, axis, [(i, i ^ d) for i in range(count)])  12.1 us
    pallas_call x1, Pallas kernels, convolve(): pl.pallas_call(functools.partial(conv_kernel, own, near, ch_count, parts)...  2.53 us
    ppermute x9, waiting for transfers between devices, swap(): return lax.ppermute(piece, axis, [(i, i ^ d) for i in range(count)])  2.36 us
    pallas_call x1, Pallas kernels, make_tables(): pl.pallas_call(functools.partial(tables_kernel, own), out_shape=[jax.Shap...  2.09 us
    pallas_call x1, Pallas kernels, pack(): pl.pallas_call(functools.partial(pack_kernel, own, blocks, group, ch_coun...  2.02 us
    pallas_call x1, Pallas kernels, unpack(): pl.pallas_call(functools.partial(unpack_kernel, own), out_shape=jax.Shape...  1.01 us
  transfers between devices with their start and end apart: 9, of which 1 were waited for; matrix products, arithmetic and copies ran while one was open for 0% of the time, Pallas kernels for 11%

profile of v18, /device:TPU:1, one launch (start us, length us, event | category | flops | bytes accessed | tf_op | source)
XLA Modules:
  0.0 40.5 jit_solution(9827339158586774739)
XLA Ops:
  0.0 2.0 %pack.1 = (bf16[192,256]{1,0:T(8,128)(2,1)S(1)}, bf16[192,256]{1,0:T(8,128)(2,1)S(1)}, bf16[192,256]{1,0:T(8,128)(2,1)S(1)}, bf16[192,256]{1,0:T(8,128)(2,1)S(1)...) custom-call(bf16[32,8192]{1,0:T(8,128)(2,1)} %pre_ref.1, ...), custom_call_target="tpu_custom_call" | custom-call | tf_op jit(solution)/shard_map/pack/pallas_call | solution.py:125
  2.0 3.1 %collective-permute-start = (bf16[192,256]{1,0:T(8,128)(2,1)S(1)}, bf16[192,256]{1,0:T(8,128)(2,1)S(1)}, u32[]{:S(2)}, u32[]{:S(2)}) collective-permute-start(bf16[192,256]{1,0:T(8,128)(2,1)S(1)} %get-tuple-element.39), channel_id=1, source_target_pairs={{0,24},{4,28},{8,16},{12,20},{16,8},{20,12},{24,0},{28,4},{1,25},{... | collective-permute-start | bytes 294920 | tf_op jit(solution)/shard_map/ppermute | solution.py:156
  5.1 0.3 collective-permute-start.1
  5.3 0.1 collective-permute-start.2
  5.5 2.4 %collective-permute-start.7 = (bf16[32,2048]{1,0:T(8,128)(2,1)S(1)}, bf16[32,2048]{1,0:T(8,128)(2,1)S(1)}, u32[]{:S(2)}, u32[]{:S(2)}) collective-permute-start(bf16[32,2048]{1,0:T(8,128)(2,1)S(1)} %get-tuple-element.46), channel_id=1, source_target_pairs={{0,2},{1,3},{2,0},{3,1},{4,6},{5,7},{6,4},{7,5},{8,10},{9,11},{10,... | collective-permute-start | bytes 393224 | tf_op jit(solution)/shard_map/ppermute | solution.py:156
  7.9 3.8 %collective-permute-start.3 = (bf16[192,256]{1,0:T(8,128)(2,1)S(1)}, bf16[192,256]{1,0:T(8,128)(2,1)S(1)}, u32[]{:S(2)}, u32[]{:S(2)}) collective-permute-start(bf16[192,256]{1,0:T(8,128)(2,1)S(1)} %get-tuple-element.42), channel_id=1, source_target_pairs={{0,28},{4,24},{8,20},{12,16},{16,12},{20,8},{24,4},{28,0},{1,29},{... | collective-permute-start | bytes 294920 | tf_op jit(solution)/shard_map/ppermute | solution.py:156
  11.7 0.0 collective-permute-done.rest_1_
  11.7 0.0 collective-permute-start.4
  11.7 0.0 collective-permute-done.1.rest_2_
  11.7 0.8 %collective-permute-start.5 = (bf16[192,256]{1,0:T(8,128)(2,1)S(1)}, bf16[192,256]{1,0:T(8,128)(2,1)S(1)}, u32[]{:S(2)}, u32[]{:S(2)}) collective-permute-start(bf16[192,256]{1,0:T(8,128)(2,1)S(1)} %get-tuple-element.44), channel_id=1, source_target_pairs={{0,20},{4,16},{8,28},{12,24},{16,4},{20,0},{24,12},{28,8},{1,21},{... | collective-permute-start | bytes 294920 | tf_op jit(solution)/shard_map/ppermute | solution.py:156
  12.5 0.0 collective-permute-done.2.rest_3_
  12.5 0.3 collective-permute-start.6
  12.8 2.3 %collective-permute-done.3.rest_4_ = bf16[192,256]{1,0:T(8,128)(2,1)S(1)} collective-permute-done((bf16[192,256]{1,0:T(8,128)(2,1)S(1)}, bf16[192,256]{1,0:T(8,128)(2,1)S(1)}, u32[]{:S(2)}, u32[]{:S(2)}) %collective-permute-start.3) | collective-permute-done | bytes 98336 | tf_op jit(solution)/shard_map/ppermute | solution.py:156
  15.2 1.3 %collective-permute-start.8 = (bf16[32,2048]{1,0:T(8,128)(2,1)S(1)}, bf16[32,2048]{1,0:T(8,128)(2,1)S(1)}, u32[]{:S(2)}, u32[]{:S(2)}) collective-permute-start(bf16[32,2048]{1,0:T(8,128)(2,1)S(1)} %get-tuple-element.65), channel_id=1, source_target_pairs={{0,1},{1,0},{2,3},{3,2},{4,5},{5,4},{6,7},{7,6},{8,9},{9,8},{10,11... | collective-permute-start | bytes 393224 | tf_op jit(solution)/shard_map/ppermute | solution.py:156
  16.5 0.0 copy-done
  16.5 2.1 %make_tables.1 = (bf16[512,256]{1,0:T(8,128)(2,1)S(1)}, bf16[256,512]{1,0:T(8,128)(2,1)S(1)}, bf16[512,512]{1,0:T(8,128)(2,1)S(1)}, bf16[512,512]{1,0:T(8,128)(2,1)S(1)}, f32[288,512]{1,0:T(8,128)S(1)}) custom-call(f32[32]{0:T(128)S(1)} %copy-done, f32[512,256]{1,0:T(8,128)} %constant.8.clone.rest_0_, f32[256,512]{1,0:T(8,128)} %constant.9.clone.rest_1_, ...), custom_call_target="tpu_custom_call" | custom-call | tf_op jit(solution)/shard_map/make_tables/pallas_call | solution.py:192
  18.6 0.0 collective-permute-done.4.rest_5_
  18.6 0.0 collective-permute-done.5.rest_6_
  18.6 0.0 collective-permute-done.6.rest_7_
  18.6 0.0 collective-permute-done.7.rest_2_
  18.6 2.5 %convolve.1 = bf16[32,32,256]{2,1,0:T(8,128)(2,1)S(1)} custom-call(bf16[192,256]{1,0:T(8,128)(2,1)S(1)} %get-tuple-element.38.rest_0_, bf16[192,256]{1,0:T(8,128)(2,1)S(1)} %collective-permute-done.rest_1_, bf16[192,256]{1,0:T(8,128)(2,1)S(1)} %collective-permute-done.1.rest_2_, bf16[192,256]{1,0:T(8,128)(2,1)S(1)} %collective-permute-done.2.rest_3_, ...), custom_call_target="tpu_custom_call" | custom-call | flops 1048576000 | bytes 262144 | tf_op jit(solution)/shard_map/convolve/pallas_call | solution.py:279
  21.2 0.0 collective-permute-done.8.rest_1_
  21.2 18.4 %all_to_all.5.got_ref = bf16[32,32,256]{2,1,0:T(8,128)(2,1)S(1)} all-to-all(bf16[32,32,256]{2,1,0:T(8,128)(2,1)S(1)} %convolve.1), channel_id=1, replica_groups=mesh['ctx'=8,'ch'=4] {'ctx','ch'}, dimensions={0} | all-to-all | bytes 1048576 | tf_op jit(solution)/shard_map/all_to_all | solution.py:367
  39.5 1.0 %unpack.1 = bf16[128,2048]{1,0:T(8,128)(2,1)} custom-call(bf16[32,32,256]{2,1,0:T(8,128)(2,1)S(1)} %all_to_all.5.got_ref, bf16[32,2048]{1,0:T(8,128)(2,1)S(1)} %get-tuple-element.68.rest_0_, bf16[32,2048]{1,0:T(8,128)(2,1)S(1)} %collective-permute-done.8.rest_1_, bf16[32,2048]{1,0:T(8,128)(2,1)S(1)} %collective-permute-done.7.rest_2_), custom_call_target="tpu_custom_call" | custom-call | tf_op jit(solution)/shard_map/unpack/pallas_call | solution.py:334
  (1 shorter events, 0.0 us)
Async XLA Ops:
  2.0 9.7 %collective-permute-start = (bf16[192,256]{1,0:T(8,128)(2,1)S(1)}, bf16[192,256]{1,0:T(8,128)(2,1)S(1)}, u32[]{:S(2)}, u32[]{:S(2)}) collective-permute-start(bf16[192,256]{1,0:T(8,128)(2,1)S(1)} %get-tuple-element.39), channel_id=1, source_target_pairs={{0,24},{4,28},{8,16},{12,20},{16,8},{20,12},{24,0},{28,4},{1,25},{... | collective-permute-start | bytes 294920 | tf_op jit(solution)/shard_map/ppermute | solution.py:156
  5.1 6.6 %collective-permute-start.1 = (bf16[192,256]{1,0:T(8,128)(2,1)S(1)}, bf16[192,256]{1,0:T(8,128)(2,1)S(1)}, u32[]{:S(2)}, u32[]{:S(2)}) collective-permute-start(bf16[192,256]{1,0:T(8,128)(2,1)S(1)} %get-tuple-element.40), channel_id=1, source_target_pairs={{0,8},{4,12},{8,0},{12,4},{16,24},{20,28},{24,16},{28,20},{1,9},{5... | collective-permute-start | bytes 294920 | tf_op jit(solution)/shard_map/ppermute | solution.py:156
  5.3 7.2 %collective-permute-start.2 = (bf16[192,256]{1,0:T(8,128)(2,1)S(1)}, bf16[192,256]{1,0:T(8,128)(2,1)S(1)}, u32[]{:S(2)}, u32[]{:S(2)}) collective-permute-start(bf16[192,256]{1,0:T(8,128)(2,1)S(1)} %get-tuple-element.41), channel_id=1, source_target_pairs={{0,16},{4,20},{8,24},{12,28},{16,0},{20,4},{24,8},{28,12},{1,17},{... | collective-permute-start | bytes 294920 | tf_op jit(solution)/shard_map/ppermute | solution.py:156
  5.5 13.2 %collective-permute-start.7 = (bf16[32,2048]{1,0:T(8,128)(2,1)S(1)}, bf16[32,2048]{1,0:T(8,128)(2,1)S(1)}, u32[]{:S(2)}, u32[]{:S(2)}) collective-permute-start(bf16[32,2048]{1,0:T(8,128)(2,1)S(1)} %get-tuple-element.46), channel_id=1, source_target_pairs={{0,2},{1,3},{2,0},{3,1},{4,6},{5,7},{6,4},{7,5},{8,10},{9,11},{10,... | collective-permute-start | bytes 393224 | tf_op jit(solution)/shard_map/ppermute | solution.py:156
  7.9 7.3 %collective-permute-start.3 = (bf16[192,256]{1,0:T(8,128)(2,1)S(1)}, bf16[192,256]{1,0:T(8,128)(2,1)S(1)}, u32[]{:S(2)}, u32[]{:S(2)}) collective-permute-start(bf16[192,256]{1,0:T(8,128)(2,1)S(1)} %get-tuple-element.42), channel_id=1, source_target_pairs={{0,28},{4,24},{8,20},{12,16},{16,12},{20,8},{24,4},{28,0},{1,29},{... | collective-permute-start | bytes 294920 | tf_op jit(solution)/shard_map/ppermute | solution.py:156
  11.7 6.8 %collective-permute-start.4 = (bf16[192,256]{1,0:T(8,128)(2,1)S(1)}, bf16[192,256]{1,0:T(8,128)(2,1)S(1)}, u32[]{:S(2)}, u32[]{:S(2)}) collective-permute-start(bf16[192,256]{1,0:T(8,128)(2,1)S(1)} %get-tuple-element.43), channel_id=1, source_target_pairs={{0,12},{4,8},{8,4},{12,0},{16,28},{20,24},{24,20},{28,16},{1,13},{... | collective-permute-start | bytes 294920 | tf_op jit(solution)/shard_map/ppermute | solution.py:156
  11.7 6.8 %collective-permute-start.5 = (bf16[192,256]{1,0:T(8,128)(2,1)S(1)}, bf16[192,256]{1,0:T(8,128)(2,1)S(1)}, u32[]{:S(2)}, u32[]{:S(2)}) collective-permute-start(bf16[192,256]{1,0:T(8,128)(2,1)S(1)} %get-tuple-element.44), channel_id=1, source_target_pairs={{0,20},{4,16},{8,28},{12,24},{16,4},{20,0},{24,12},{28,8},{1,21},{... | collective-permute-start | bytes 294920 | tf_op jit(solution)/shard_map/ppermute | solution.py:156
  12.5 6.1 %collective-permute-start.6 = (bf16[192,256]{1,0:T(8,128)(2,1)S(1)}, bf16[192,256]{1,0:T(8,128)(2,1)S(1)}, u32[]{:S(2)}, u32[]{:S(2)}) collective-permute-start(bf16[192,256]{1,0:T(8,128)(2,1)S(1)} %get-tuple-element.45), channel_id=1, source_target_pairs={{0,4},{4,0},{8,12},{12,8},{16,20},{20,16},{24,28},{28,24},{1,5},{5... | collective-permute-start | bytes 294920 | tf_op jit(solution)/shard_map/ppermute | solution.py:156
  15.2 1.3 %copy-start = (f32[32]{0:T(128)S(1)}, f32[32]{0:T(128)}, u32[]{:S(2)}) copy-start(f32[32]{0:T(128)} %skip_ref) | copy-start | bytes 388
  15.2 6.0 %collective-permute-start.8 = (bf16[32,2048]{1,0:T(8,128)(2,1)S(1)}, bf16[32,2048]{1,0:T(8,128)(2,1)S(1)}, u32[]{:S(2)}, u32[]{:S(2)}) collective-permute-start(bf16[32,2048]{1,0:T(8,128)(2,1)S(1)} %get-tuple-element.65), channel_id=1, source_target_pairs={{0,1},{1,0},{2,3},{3,2},{4,5},{5,4},{6,7},{7,6},{8,9},{9,8},{10,11... | collective-permute-start | bytes 393224 | tf_op jit(solution)/shard_map/ppermute | solution.py:156

commit v19 on v18

--- a/solution.py
+++ b/solution.py
@@ -357,6 +357,8 @@
     got = [got[d] for d in order]
     tables, skip, _ = lax.optimization_barrier((dft_tables(near * ctx_count), skip, got[0]))
     tables = list(make_tables(skip, *tables, own))
+    half = ctx_count // 2 + 1
+    tables, got[half:] = lax.optimization_barrier((tables, got[half:]))
     got = [swap(piece, "ctx", ctx_count, d) if d else piece for piece, d in zip(got, order)]
     for d in range(1, len(gates)):
         gates[d] = swap(gates[d], "ch", ch_count, d)

time: 40.7 us -> 41 us (level)
  transfers between devices with their start and end apart: 9 -> 9, of which waited for: 1 -> 2; matrix products, arithmetic and copies ran while one was open for 0% -> 0% of each run, Pallas kernels for 11% -> 11%
where the time goes in v19:
time: 41 us; the launch traced here: 40.8 us
  blocking collectives  18 us (44%)
  starting transfers between devices  12.4 us (30%)
  Pallas kernels  7.65 us (19%)
  waiting for transfers between devices  2.74 us (7%)
    all_to_all x1, blocking collectives, body(): lax.all_to_all(mixed, ('ctx', 'ch'), split_axis=0, concat_axis=0, tiled=T...  18 us
    ppermute x9, starting transfers between devices, swap(): return lax.ppermute(piece, axis, [(i, i ^ d) for i in range(count)])  12.4 us
    ppermute x9, waiting for transfers between devices, swap(): return lax.ppermute(piece, axis, [(i, i ^ d) for i in range(count)])  2.74 us
    pallas_call x1, Pallas kernels, convolve(): pl.pallas_call(functools.partial(conv_kernel, own, near, ch_count, parts)...  2.53 us
    pallas_call x1, Pallas kernels, make_tables(): pl.pallas_call(functools.partial(tables_kernel, own), out_shape=[jax.Shap...  2.09 us
    pallas_call x1, Pallas kernels, pack(): pl.pallas_call(functools.partial(pack_kernel, own, blocks, group, ch_coun...  2.02 us
    pallas_call x1, Pallas kernels, unpack(): pl.pallas_call(functools.partial(unpack_kernel, own), out_shape=jax.Shape...  1.01 us
  transfers between devices with their start and end apart: 9, of which 2 were waited for; matrix products, arithmetic and copies ran while one was open for 0% of the time, Pallas kernels for 11%

profile of v19, /device:TPU:1, one launch (start us, length us, event | category | flops | bytes accessed | tf_op | source)
XLA Modules:
  0.0 40.8 jit_solution(1078038903042206735)
XLA Ops:
  0.0 2.0 %pack.1 = (bf16[192,256]{1,0:T(8,128)(2,1)S(1)}, bf16[192,256]{1,0:T(8,128)(2,1)S(1)}, bf16[192,256]{1,0:T(8,128)(2,1)S(1)}, bf16[192,256]{1,0:T(8,128)(2,1)S(1)...) custom-call(bf16[32,8192]{1,0:T(8,128)(2,1)} %pre_ref.1, ...), custom_call_target="tpu_custom_call" | custom-call | tf_op jit(solution)/shard_map/pack/pallas_call | solution.py:125
  2.0 3.1 %collective-permute-start = (bf16[192,256]{1,0:T(8,128)(2,1)S(1)}, bf16[192,256]{1,0:T(8,128)(2,1)S(1)}, u32[]{:S(2)}, u32[]{:S(2)}) collective-permute-start(bf16[192,256]{1,0:T(8,128)(2,1)S(1)} %get-tuple-element.47), channel_id=1, source_target_pairs={{0,24},{4,28},{8,16},{12,20},{16,8},{20,12},{24,0},{28,4},{1,25},{... | collective-permute-start | bytes 294920 | tf_op jit(solution)/shard_map/ppermute | solution.py:156
  5.1 0.3 collective-permute-start.1
  5.3 0.1 collective-permute-start.2
  5.5 2.4 %collective-permute-start.7 = (bf16[32,2048]{1,0:T(8,128)(2,1)S(1)}, bf16[32,2048]{1,0:T(8,128)(2,1)S(1)}, u32[]{:S(2)}, u32[]{:S(2)}) collective-permute-start(bf16[32,2048]{1,0:T(8,128)(2,1)S(1)} %get-tuple-element.67), channel_id=1, source_target_pairs={{0,2},{1,3},{2,0},{3,1},{4,6},{5,7},{6,4},{7,5},{8,10},{9,11},{10,... | collective-permute-start | bytes 393224 | tf_op jit(solution)/shard_map/ppermute | solution.py:156
  7.9 3.8 %collective-permute-start.3 = (bf16[192,256]{1,0:T(8,128)(2,1)S(1)}, bf16[192,256]{1,0:T(8,128)(2,1)S(1)}, u32[]{:S(2)}, u32[]{:S(2)}) collective-permute-start(bf16[192,256]{1,0:T(8,128)(2,1)S(1)} %get-tuple-element.50), channel_id=1, source_target_pairs={{0,28},{4,24},{8,20},{12,16},{16,12},{20,8},{24,4},{28,0},{1,29},{... | collective-permute-start | bytes 294920 | tf_op jit(solution)/shard_map/ppermute | solution.py:156
  11.7 0.0 copy-done
  11.7 2.1 %make_tables.1 = (bf16[512,256]{1,0:T(8,128)(2,1)S(1)}, bf16[256,512]{1,0:T(8,128)(2,1)S(1)}, bf16[512,512]{1,0:T(8,128)(2,1)S(1)}, bf16[512,512]{1,0:T(8,128)(2,1)S(1)}, f32[288,512]{1,0:T(8,128)S(1)}) custom-call(f32[32]{0:T(128)S(1)} %copy-done, f32[512,256]{1,0:T(8,128)} %constant.8.clone.rest_0_, f32[256,512]{1,0:T(8,128)} %constant.9.clone.rest_1_, ...), custom_call_target="tpu_custom_call" | custom-call | tf_op jit(solution)/shard_map/make_tables/pallas_call | solution.py:192
  13.8 0.0 collective-permute-done.rest_1_
  13.8 0.1 collective-permute-start.4
  13.9 0.0 collective-permute-done.1.rest_2_
  13.9 0.7 %collective-permute-start.5 = (bf16[192,256]{1,0:T(8,128)(2,1)S(1)}, bf16[192,256]{1,0:T(8,128)(2,1)S(1)}, u32[]{:S(2)}, u32[]{:S(2)}) collective-permute-start(bf16[192,256]{1,0:T(8,128)(2,1)S(1)} %get-tuple-element.65), channel_id=1, source_target_pairs={{0,20},{4,16},{8,28},{12,24},{16,4},{20,0},{24,12},{28,8},{1,21},{... | collective-permute-start | bytes 294920 | tf_op jit(solution)/shard_map/ppermute | solution.py:156
  14.7 0.0 collective-permute-done.2.rest_3_
  14.7 0.6 %collective-permute-start.6 = (bf16[192,256]{1,0:T(8,128)(2,1)S(1)}, bf16[192,256]{1,0:T(8,128)(2,1)S(1)}, u32[]{:S(2)}, u32[]{:S(2)}) collective-permute-start(bf16[192,256]{1,0:T(8,128)(2,1)S(1)} %get-tuple-element.66), channel_id=1, source_target_pairs={{0,4},{4,0},{8,12},{12,8},{16,20},{20,16},{24,28},{28,24},{1,5},{5... | collective-permute-start | bytes 294920 | tf_op jit(solution)/shard_map/ppermute | solution.py:156
  15.2 0.0 collective-permute-done.3.rest_4_
  15.2 1.3 %collective-permute-start.8 = (bf16[32,2048]{1,0:T(8,128)(2,1)S(1)}, bf16[32,2048]{1,0:T(8,128)(2,1)S(1)}, u32[]{:S(2)}, u32[]{:S(2)}) collective-permute-start(bf16[32,2048]{1,0:T(8,128)(2,1)S(1)} %get-tuple-element.81), channel_id=1, source_target_pairs={{0,1},{1,0},{2,3},{3,2},{4,5},{5,4},{6,7},{7,6},{8,9},{9,8},{10,11... | collective-permute-start | bytes 393224 | tf_op jit(solution)/shard_map/ppermute | solution.py:156
  16.5 1.7 %collective-permute-done.4.rest_5_ = bf16[192,256]{1,0:T(8,128)(2,1)S(1)} collective-permute-done((bf16[192,256]{1,0:T(8,128)(2,1)S(1)}, bf16[192,256]{1,0:T(8,128)(2,1)S(1)}, u32[]{:S(2)}, u32[]{:S(2)}) %collective-permute-start.4) | collective-permute-done | bytes 98336 | tf_op jit(solution)/shard_map/ppermute | solution.py:156
  18.2 1.0 %collective-permute-done.5.rest_6_ = bf16[192,256]{1,0:T(8,128)(2,1)S(1)} collective-permute-done((bf16[192,256]{1,0:T(8,128)(2,1)S(1)}, bf16[192,256]{1,0:T(8,128)(2,1)S(1)}, u32[]{:S(2)}, u32[]{:S(2)}) %collective-permute-start.5) | collective-permute-done | bytes 98336 | tf_op jit(solution)/shard_map/ppermute | solution.py:156
  19.3 0.0 collective-permute-done.6.rest_7_
  19.3 0.0 collective-permute-done.7.rest_2_
  19.3 2.5 %convolve.1 = bf16[32,32,256]{2,1,0:T(8,128)(2,1)S(1)} custom-call(bf16[192,256]{1,0:T(8,128)(2,1)S(1)} %get-tuple-element.46.rest_0_, bf16[192,256]{1,0:T(8,128)(2,1)S(1)} %collective-permute-done.rest_1_, bf16[192,256]{1,0:T(8,128)(2,1)S(1)} %collective-permute-done.1.rest_2_, bf16[192,256]{1,0:T(8,128)(2,1)S(1)} %collective-permute-done.2.rest_3_, ...), custom_call_target="tpu_custom_call" | custom-call | flops 1048576000 | bytes 262144 | tf_op jit(solution)/shard_map/convolve/pallas_call | solution.py:279
  21.8 0.0 collective-permute-done.8.rest_1_
  21.8 18.0 %all_to_all.5.got_ref = bf16[32,32,256]{2,1,0:T(8,128)(2,1)S(1)} all-to-all(bf16[32,32,256]{2,1,0:T(8,128)(2,1)S(1)} %convolve.1), channel_id=1, replica_groups=mesh['ctx'=8,'ch'=4] {'ctx','ch'}, dimensions={0} | all-to-all | bytes 1048576 | tf_op jit(solution)/shard_map/all_to_all | solution.py:369
  39.8 1.0 %unpack.1 = bf16[128,2048]{1,0:T(8,128)(2,1)} custom-call(bf16[32,32,256]{2,1,0:T(8,128)(2,1)S(1)} %all_to_all.5.got_ref, bf16[32,2048]{1,0:T(8,128)(2,1)S(1)} %get-tuple-element.84.rest_0_, bf16[32,2048]{1,0:T(8,128)(2,1)S(1)} %collective-permute-done.8.rest_1_, bf16[32,2048]{1,0:T(8,128)(2,1)S(1)} %collective-permute-done.7.rest_2_), custom_call_target="tpu_custom_call" | custom-call | tf_op jit(solution)/shard_map/unpack/pallas_call | solution.py:334
  (1 shorter events, 0.0 us)
Async XLA Ops:
  2.0 11.8 %collective-permute-start = (bf16[192,256]{1,0:T(8,128)(2,1)S(1)}, bf16[192,256]{1,0:T(8,128)(2,1)S(1)}, u32[]{:S(2)}, u32[]{:S(2)}) collective-permute-start(bf16[192,256]{1,0:T(8,128)(2,1)S(1)} %get-tuple-element.47), channel_id=1, source_target_pairs={{0,24},{4,28},{8,16},{12,20},{16,8},{20,12},{24,0},{28,4},{1,25},{... | collective-permute-start | bytes 294920 | tf_op jit(solution)/shard_map/ppermute | solution.py:156
  5.1 8.8 %collective-permute-start.1 = (bf16[192,256]{1,0:T(8,128)(2,1)S(1)}, bf16[192,256]{1,0:T(8,128)(2,1)S(1)}, u32[]{:S(2)}, u32[]{:S(2)}) collective-permute-start(bf16[192,256]{1,0:T(8,128)(2,1)S(1)} %get-tuple-element.48), channel_id=1, source_target_pairs={{0,8},{4,12},{8,0},{12,4},{16,24},{20,28},{24,16},{28,20},{1,9},{5... | collective-permute-start | bytes 294920 | tf_op jit(solution)/shard_map/ppermute | solution.py:156
  5.3 9.3 %collective-permute-start.2 = (bf16[192,256]{1,0:T(8,128)(2,1)S(1)}, bf16[192,256]{1,0:T(8,128)(2,1)S(1)}, u32[]{:S(2)}, u32[]{:S(2)}) collective-permute-start(bf16[192,256]{1,0:T(8,128)(2,1)S(1)} %get-tuple-element.49), channel_id=1, source_target_pairs={{0,16},{4,20},{8,24},{12,28},{16,0},{20,4},{24,8},{28,12},{1,17},{... | collective-permute-start | bytes 294920 | tf_op jit(solution)/shard_map/ppermute | solution.py:156
  5.5 13.8 %collective-permute-start.7 = (bf16[32,2048]{1,0:T(8,128)(2,1)S(1)}, bf16[32,2048]{1,0:T(8,128)(2,1)S(1)}, u32[]{:S(2)}, u32[]{:S(2)}) collective-permute-start(bf16[32,2048]{1,0:T(8,128)(2,1)S(1)} %get-tuple-element.67), channel_id=1, source_target_pairs={{0,2},{1,3},{2,0},{3,1},{4,6},{5,7},{6,4},{7,5},{8,10},{9,11},{10,... | collective-permute-start | bytes 393224 | tf_op jit(solution)/shard_map/ppermute | solution.py:156
  7.9 3.9 %copy-start = (f32[32]{0:T(128)S(1)}, f32[32]{0:T(128)}, u32[]{:S(2)}) copy-start(f32[32]{0:T(128)} %skip_ref) | copy-start | bytes 388
  7.9 7.4 %collective-permute-start.3 = (bf16[192,256]{1,0:T(8,128)(2,1)S(1)}, bf16[192,256]{1,0:T(8,128)(2,1)S(1)}, u32[]{:S(2)}, u32[]{:S(2)}) collective-permute-start(bf16[192,256]{1,0:T(8,128)(2,1)S(1)} %get-tuple-element.50), channel_id=1, source_target_pairs={{0,28},{4,24},{8,20},{12,16},{16,12},{20,8},{24,4},{28,0},{1,29},{... | collective-permute-start | bytes 294920 | tf_op jit(solution)/shard_map/ppermute | solution.py:156
  13.8 4.4 %collective-permute-start.4 = (bf16[192,256]{1,0:T(8,128)(2,1)S(1)}, bf16[192,256]{1,0:T(8,128)(2,1)S(1)}, u32[]{:S(2)}, u32[]{:S(2)}) collective-permute-start(bf16[192,256]{1,0:T(8,128)(2,1)S(1)} %get-tuple-element.64), channel_id=1, source_target_pairs={{0,12},{4,8},{8,4},{12,0},{16,28},{20,24},{24,20},{28,16},{1,13},{... | collective-permute-start | bytes 294920 | tf_op jit(solution)/shard_map/ppermute | solution.py:156
  13.9 5.3 %collective-permute-start.5 = (bf16[192,256]{1,0:T(8,128)(2,1)S(1)}, bf16[192,256]{1,0:T(8,128)(2,1)S(1)}, u32[]{:S(2)}, u32[]{:S(2)}) collective-permute-start(bf16[192,256]{1,0:T(8,128)(2,1)S(1)} %get-tuple-element.65), channel_id=1, source_target_pairs={{0,20},{4,16},{8,28},{12,24},{16,4},{20,0},{24,12},{28,8},{1,21},{... | collective-permute-start | bytes 294920 | tf_op jit(solution)/shard_map/ppermute | solution.py:156
  14.7 4.6 %collective-permute-start.6 = (bf16[192,256]{1,0:T(8,128)(2,1)S(1)}, bf16[192,256]{1,0:T(8,128)(2,1)S(1)}, u32[]{:S(2)}, u32[]{:S(2)}) collective-permute-start(bf16[192,256]{1,0:T(8,128)(2,1)S(1)} %get-tuple-element.66), channel_id=1, source_target_pairs={{0,4},{4,0},{8,12},{12,8},{16,20},{20,16},{24,28},{28,24},{1,5},{5... | collective-permute-start | bytes 294920 | tf_op jit(solution)/shard_map/ppermute | solution.py:156
  15.2 6.6 %collective-permute-start.8 = (bf16[32,2048]{1,0:T(8,128)(2,1)S(1)}, bf16[32,2048]{1,0:T(8,128)(2,1)S(1)}, u32[]{:S(2)}, u32[]{:S(2)}) collective-permute-start(bf16[32,2048]{1,0:T(8,128)(2,1)S(1)} %get-tuple-element.81), channel_id=1, source_target_pairs={{0,1},{1,0},{2,3},{3,2},{4,5},{5,4},{6,7},{7,6},{8,9},{9,8},{10,11... | collective-permute-start | bytes 393224 | tf_op jit(solution)/shard_map/ppermute | solution.py:156

commit v20 on v18

--- a/solution.py
+++ b/solution.py
@@ -32,7 +32,7 @@
     near = 2 * np.pi * (np.arange(W)[:, None] * np.arange(W)[None, :] % W) / W
     inner = np.concatenate([np.cos(near), np.sin(near)], 0)
     turns = np.concatenate([np.cos(turn), np.sin(turn)], 1)
-    return [jnp.asarray(table, jnp.float32) for table in (outer, outer.T, inner, turns)]
+    return [jnp.asarray(table, jnp.float32) for table in (outer, inner, turns)]
 
 
 def lay(natural, j, value):
@@ -156,15 +156,13 @@
     return lax.ppermute(piece, axis, [(i, i ^ d) for i in range(count)])
 
 
-def tables_kernel(own, skip_ref, *rest):
-    outer_ref, back_ref, inner_ref, turns_ref, outer_out, back_out, ahead, rear, turns_out = rest[:9]
-    outer_s, back_s, inner_s, sems = rest[9:]
+def tables_kernel(own, skip_ref, outer_ref, inner_ref, turns_ref, outer_out, back_out, ahead, rear, turns_out, *rest):
+    outer_s, inner_s, sems = rest
     count, width = turns_ref.shape
     loads = [
-        pltpu.make_async_copy(inner_ref, inner_s, sems.at[0]),
-        pltpu.make_async_copy(outer_ref, outer_s, sems.at[1]),
-        pltpu.make_async_copy(back_ref, back_s, sems.at[2]),
-        pltpu.make_async_copy(turns_ref, turns_out.at[0:count, :], sems.at[3]),
+        pltpu.make_async_copy(outer_ref, outer_s, sems.at[0]),
+        pltpu.make_async_copy(inner_ref, inner_s, sems.at[1]),
+        pltpu.make_async_copy(turns_ref, turns_out.at[0:count, :], sems.at[2]),
     ]
     for copy in loads:
         copy.start()
@@ -172,34 +170,32 @@
     for c in range(own):
         turns_out[count + 8 * c : count + 8 * (c + 1), :] = jnp.full((8, width), skip_ref[own * me + c], jnp.float32)
     loads[0].wait()
+    outer_out[...] = outer_s[...].astype(jnp.bfloat16)
+    back_out[...] = outer_s[...].T.astype(jnp.bfloat16)
+    loads[1].wait()
     near_cos, near_sin = inner_s[0:W, :].astype(jnp.bfloat16), inner_s[W:, :].astype(jnp.bfloat16)
     for table, sign in ((ahead, -1), (rear, 1)):
         table[0:W, 0:W] = near_cos
         table[0:W, W:] = near_sin * sign
         table[W:, 0:W] = near_sin * -sign
         table[W:, W:] = near_cos
-    loads[1].wait()
-    outer_out[...] = outer_s[...].astype(jnp.bfloat16)
     loads[2].wait()
-    back_out[...] = back_s[...].astype(jnp.bfloat16)
-    loads[3].wait()
-
-
-def make_tables(skip, outer, back, inner, turns, own):
+
+
+def make_tables(skip, outer, inner, turns, own):
     count, width = turns.shape
-    args = [pltpu.with_memory_space_constraint(arg, pltpu.HBM) for arg in (outer, back, inner, turns)]
-    narrow = (outer.shape, back.shape, (2 * W, 2 * W), (2 * W, 2 * W))
+    args = [pltpu.with_memory_space_constraint(arg, pltpu.HBM) for arg in (outer, inner, turns)]
+    narrow = (outer.shape, outer.shape[::-1], (2 * W, 2 * W), (2 * W, 2 * W))
     return pl.pallas_call(
         functools.partial(tables_kernel, own),
         out_shape=[jax.ShapeDtypeStruct(shape, jnp.bfloat16) for shape in narrow]
         + [jax.ShapeDtypeStruct((count + 8 * own, width), jnp.float32)],
-        in_specs=[pl.BlockSpec(memory_space=pltpu.SMEM)] + [in_hbm()] * 4,
+        in_specs=[pl.BlockSpec(memory_space=pltpu.SMEM)] + [in_hbm()] * 3,
         out_specs=[whole_vmem()] * 5,
         scratch_shapes=[
             pltpu.VMEM(outer.shape, jnp.float32),
-            pltpu.VMEM(back.shape, jnp.float32),
             pltpu.VMEM(inner.shape, jnp.float32),
-            pltpu.SemaphoreType.DMA((4,)),
+            pltpu.SemaphoreType.DMA((3,)),
         ],
         compiler_params=pltpu.CompilerParams(vmem_limit_bytes=16 * 2**20),
         name="make_tables",

time: 40.7 us -> 40.5 us (level)
  no operation moved by 1% of the time
where the time goes in v20:
time: 40.5 us; the launch traced here: 40.4 us
  blocking collectives  18.4 us (45%)
  starting transfers between devices  12.1 us (30%)
  Pallas kernels  7.49 us (18%)
  waiting for transfers between devices  2.36 us (6%)
    all_to_all x1, blocking collectives, body(): lax.all_to_all(mixed, ('ctx', 'ch'), split_axis=0, concat_axis=0, tiled=T...  18.4 us
    ppermute x9, starting transfers between devices, swap(): return lax.ppermute(piece, axis, [(i, i ^ d) for i in range(count)])  12.1 us
    pallas_call x1, Pallas kernels, convolve(): pl.pallas_call(functools.partial(conv_kernel, own, near, ch_count, parts)...  2.54 us
    ppermute x9, waiting for transfers between devices, swap(): return lax.ppermute(piece, axis, [(i, i ^ d) for i in range(count)])  2.36 us
    pallas_call x1, Pallas kernels, pack(): pl.pallas_call(functools.partial(pack_kernel, own, blocks, group, ch_coun...  2.02 us
    pallas_call x1, Pallas kernels, make_tables(): pl.pallas_call(functools.partial(tables_kernel, own), out_shape=[jax.Shap...  1.92 us
    pallas_call x1, Pallas kernels, unpack(): pl.pallas_call(functools.partial(unpack_kernel, own), out_shape=jax.Shape...  1.01 us
  transfers between devices with their start and end apart: 9, of which 1 were waited for; matrix products, arithmetic and copies ran while one was open for 0% of the time, Pallas kernels for 11%

profile of v20, /device:TPU:1, one launch (start us, length us, event | category | flops | bytes accessed | tf_op | source)
XLA Modules:
  0.0 40.4 jit_solution(13569954403367121217)
XLA Ops:
  0.0 2.0 %pack.1 = (bf16[192,256]{1,0:T(8,128)(2,1)S(1)}, bf16[192,256]{1,0:T(8,128)(2,1)S(1)}, bf16[192,256]{1,0:T(8,128)(2,1)S(1)}, bf16[192,256]{1,0:T(8,128)(2,1)S(1)...) custom-call(bf16[32,8192]{1,0:T(8,128)(2,1)} %pre_ref.1, ...), custom_call_target="tpu_custom_call" | custom-call | tf_op jit(solution)/shard_map/pack/pallas_call | solution.py:125
  2.0 3.1 %collective-permute-start = (bf16[192,256]{1,0:T(8,128)(2,1)S(1)}, bf16[192,256]{1,0:T(8,128)(2,1)S(1)}, u32[]{:S(2)}, u32[]{:S(2)}) collective-permute-start(bf16[192,256]{1,0:T(8,128)(2,1)S(1)} %get-tuple-element.38), channel_id=1, source_target_pairs={{0,24},{4,28},{8,16},{12,20},{16,8},{20,12},{24,0},{28,4},{1,25},{... | collective-permute-start | bytes 294920 | tf_op jit(solution)/shard_map/ppermute | solution.py:156
  5.1 0.3 collective-permute-start.1
  5.3 0.1 collective-permute-start.2
  5.5 2.4 %collective-permute-start.7 = (bf16[32,2048]{1,0:T(8,128)(2,1)S(1)}, bf16[32,2048]{1,0:T(8,128)(2,1)S(1)}, u32[]{:S(2)}, u32[]{:S(2)}) collective-permute-start(bf16[32,2048]{1,0:T(8,128)(2,1)S(1)} %get-tuple-element.45), channel_id=1, source_target_pairs={{0,2},{1,3},{2,0},{3,1},{4,6},{5,7},{6,4},{7,5},{8,10},{9,11},{10,... | collective-permute-start | bytes 393224 | tf_op jit(solution)/shard_map/ppermute | solution.py:156
  7.9 3.8 %collective-permute-start.3 = (bf16[192,256]{1,0:T(8,128)(2,1)S(1)}, bf16[192,256]{1,0:T(8,128)(2,1)S(1)}, u32[]{:S(2)}, u32[]{:S(2)}) collective-permute-start(bf16[192,256]{1,0:T(8,128)(2,1)S(1)} %get-tuple-element.41), channel_id=1, source_target_pairs={{0,28},{4,24},{8,20},{12,16},{16,12},{20,8},{24,4},{28,0},{1,29},{... | collective-permute-start | bytes 294920 | tf_op jit(solution)/shard_map/ppermute | solution.py:156
  11.7 0.0 collective-permute-done.rest_1_
  11.7 0.0 collective-permute-start.4
  11.7 0.0 collective-permute-done.1.rest_2_
  11.7 0.8 %collective-permute-start.5 = (bf16[192,256]{1,0:T(8,128)(2,1)S(1)}, bf16[192,256]{1,0:T(8,128)(2,1)S(1)}, u32[]{:S(2)}, u32[]{:S(2)}) collective-permute-start(bf16[192,256]{1,0:T(8,128)(2,1)S(1)} %get-tuple-element.43), channel_id=1, source_target_pairs={{0,20},{4,16},{8,28},{12,24},{16,4},{20,0},{24,12},{28,8},{1,21},{... | collective-permute-start | bytes 294920 | tf_op jit(solution)/shard_map/ppermute | solution.py:156
  12.5 0.0 collective-permute-done.2.rest_3_
  12.5 0.3 collective-permute-start.6
  12.8 2.3 %collective-permute-done.3.rest_4_ = bf16[192,256]{1,0:T(8,128)(2,1)S(1)} collective-permute-done((bf16[192,256]{1,0:T(8,128)(2,1)S(1)}, bf16[192,256]{1,0:T(8,128)(2,1)S(1)}, u32[]{:S(2)}, u32[]{:S(2)}) %collective-permute-start.3) | collective-permute-done | bytes 98336 | tf_op jit(solution)/shard_map/ppermute | solution.py:156
  15.2 1.3 %collective-permute-start.8 = (bf16[32,2048]{1,0:T(8,128)(2,1)S(1)}, bf16[32,2048]{1,0:T(8,128)(2,1)S(1)}, u32[]{:S(2)}, u32[]{:S(2)}) collective-permute-start(bf16[32,2048]{1,0:T(8,128)(2,1)S(1)} %get-tuple-element.63), channel_id=1, source_target_pairs={{0,1},{1,0},{2,3},{3,2},{4,5},{5,4},{6,7},{7,6},{8,9},{9,8},{10,11... | collective-permute-start | bytes 393224 | tf_op jit(solution)/shard_map/ppermute | solution.py:156
  16.5 0.0 copy-done
  16.5 1.9 %make_tables.1 = (bf16[512,256]{1,0:T(8,128)(2,1)S(1)}, bf16[256,512]{1,0:T(8,128)(2,1)S(1)}, bf16[512,512]{1,0:T(8,128)(2,1)S(1)}, bf16[512,512]{1,0:T(8,128)(2,1)S(1)}, f32[288,512]{1,0:T(8,128)S(1)}) custom-call(f32[32]{0:T(128)S(1)} %copy-done, f32[512,256]{1,0:T(8,128)} %constant.6.clone.outer_ref, f32[512,256]{1,0:T(8,128)} %constant.7.clone.inner_ref, ...), custom_call_target="tpu_custom_call" | custom-call | tf_op jit(solution)/shard_map/make_tables/pallas_call | solution.py:189
  18.4 0.0 collective-permute-done.4.rest_5_
  18.4 0.0 collective-permute-done.5.rest_6_
  18.4 0.0 collective-permute-done.6.rest_7_
  18.4 0.0 collective-permute-done.7.rest_2_
  18.4 2.5 %convolve.1 = bf16[32,32,256]{2,1,0:T(8,128)(2,1)S(1)} custom-call(bf16[192,256]{1,0:T(8,128)(2,1)S(1)} %get-tuple-element.37.rest_0_, bf16[192,256]{1,0:T(8,128)(2,1)S(1)} %collective-permute-done.rest_1_, bf16[192,256]{1,0:T(8,128)(2,1)S(1)} %collective-permute-done.1.rest_2_, bf16[192,256]{1,0:T(8,128)(2,1)S(1)} %collective-permute-done.2.rest_3_, ...), custom_call_target="tpu_custom_call" | custom-call | flops 1048576000 | bytes 262144 | tf_op jit(solution)/shard_map/convolve/pallas_call | solution.py:275
  21.0 0.0 collective-permute-done.8.rest_1_
  21.0 18.4 %all_to_all.5.got_ref = bf16[32,32,256]{2,1,0:T(8,128)(2,1)S(1)} all-to-all(bf16[32,32,256]{2,1,0:T(8,128)(2,1)S(1)} %convolve.1), channel_id=1, replica_groups=mesh['ctx'=8,'ch'=4] {'ctx','ch'}, dimensions={0} | all-to-all | bytes 1048576 | tf_op jit(solution)/shard_map/all_to_all | solution.py:363
  39.4 1.0 %unpack.1 = bf16[128,2048]{1,0:T(8,128)(2,1)} custom-call(bf16[32,32,256]{2,1,0:T(8,128)(2,1)S(1)} %all_to_all.5.got_ref, bf16[32,2048]{1,0:T(8,128)(2,1)S(1)} %get-tuple-element.66.rest_0_, bf16[32,2048]{1,0:T(8,128)(2,1)S(1)} %collective-permute-done.8.rest_1_, bf16[32,2048]{1,0:T(8,128)(2,1)S(1)} %collective-permute-done.7.rest_2_), custom_call_target="tpu_custom_call" | custom-call | tf_op jit(solution)/shard_map/unpack/pallas_call | solution.py:330
  (1 shorter events, 0.0 us)
Async XLA Ops:
  2.0 9.7 %collective-permute-start = (bf16[192,256]{1,0:T(8,128)(2,1)S(1)}, bf16[192,256]{1,0:T(8,128)(2,1)S(1)}, u32[]{:S(2)}, u32[]{:S(2)}) collective-permute-start(bf16[192,256]{1,0:T(8,128)(2,1)S(1)} %get-tuple-element.38), channel_id=1, source_target_pairs={{0,24},{4,28},{8,16},{12,20},{16,8},{20,12},{24,0},{28,4},{1,25},{... | collective-permute-start | bytes 294920 | tf_op jit(solution)/shard_map/ppermute | solution.py:156
  5.1 6.6 %collective-permute-start.1 = (bf16[192,256]{1,0:T(8,128)(2,1)S(1)}, bf16[192,256]{1,0:T(8,128)(2,1)S(1)}, u32[]{:S(2)}, u32[]{:S(2)}) collective-permute-start(bf16[192,256]{1,0:T(8,128)(2,1)S(1)} %get-tuple-element.39), channel_id=1, source_target_pairs={{0,8},{4,12},{8,0},{12,4},{16,24},{20,28},{24,16},{28,20},{1,9},{5... | collective-permute-start | bytes 294920 | tf_op jit(solution)/shard_map/ppermute | solution.py:156
  5.3 7.2 %collective-permute-start.2 = (bf16[192,256]{1,0:T(8,128)(2,1)S(1)}, bf16[192,256]{1,0:T(8,128)(2,1)S(1)}, u32[]{:S(2)}, u32[]{:S(2)}) collective-permute-start(bf16[192,256]{1,0:T(8,128)(2,1)S(1)} %get-tuple-element.40), channel_id=1, source_target_pairs={{0,16},{4,20},{8,24},{12,28},{16,0},{20,4},{24,8},{28,12},{1,17},{... | collective-permute-start | bytes 294920 | tf_op jit(solution)/shard_map/ppermute | solution.py:156
  5.5 13.0 %collective-permute-start.7 = (bf16[32,2048]{1,0:T(8,128)(2,1)S(1)}, bf16[32,2048]{1,0:T(8,128)(2,1)S(1)}, u32[]{:S(2)}, u32[]{:S(2)}) collective-permute-start(bf16[32,2048]{1,0:T(8,128)(2,1)S(1)} %get-tuple-element.45), channel_id=1, source_target_pairs={{0,2},{1,3},{2,0},{3,1},{4,6},{5,7},{6,4},{7,5},{8,10},{9,11},{10,... | collective-permute-start | bytes 393224 | tf_op jit(solution)/shard_map/ppermute | solution.py:156
  7.9 7.3 %collective-permute-start.3 = (bf16[192,256]{1,0:T(8,128)(2,1)S(1)}, bf16[192,256]{1,0:T(8,128)(2,1)S(1)}, u32[]{:S(2)}, u32[]{:S(2)}) collective-permute-start(bf16[192,256]{1,0:T(8,128)(2,1)S(1)} %get-tuple-element.41), channel_id=1, source_target_pairs={{0,28},{4,24},{8,20},{12,16},{16,12},{20,8},{24,4},{28,0},{1,29},{... | collective-permute-start | bytes 294920 | tf_op jit(solution)/shard_map/ppermute | solution.py:156
  11.7 6.7 %collective-permute-start.4 = (bf16[192,256]{1,0:T(8,128)(2,1)S(1)}, bf16[192,256]{1,0:T(8,128)(2,1)S(1)}, u32[]{:S(2)}, u32[]{:S(2)}) collective-permute-start(bf16[192,256]{1,0:T(8,128)(2,1)S(1)} %get-tuple-element.42), channel_id=1, source_target_pairs={{0,12},{4,8},{8,4},{12,0},{16,28},{20,24},{24,20},{28,16},{1,13},{... | collective-permute-start | bytes 294920 | tf_op jit(solution)/shard_map/ppermute | solution.py:156
  11.7 6.7 %collective-permute-start.5 = (bf16[192,256]{1,0:T(8,128)(2,1)S(1)}, bf16[192,256]{1,0:T(8,128)(2,1)S(1)}, u32[]{:S(2)}, u32[]{:S(2)}) collective-permute-start(bf16[192,256]{1,0:T(8,128)(2,1)S(1)} %get-tuple-element.43), channel_id=1, source_target_pairs={{0,20},{4,16},{8,28},{12,24},{16,4},{20,0},{24,12},{28,8},{1,21},{... | collective-permute-start | bytes 294920 | tf_op jit(solution)/shard_map/ppermute | solution.py:156
  12.5 5.9 %collective-permute-start.6 = (bf16[192,256]{1,0:T(8,128)(2,1)S(1)}, bf16[192,256]{1,0:T(8,128)(2,1)S(1)}, u32[]{:S(2)}, u32[]{:S(2)}) collective-permute-start(bf16[192,256]{1,0:T(8,128)(2,1)S(1)} %get-tuple-element.44), channel_id=1, source_target_pairs={{0,4},{4,0},{8,12},{12,8},{16,20},{20,16},{24,28},{28,24},{1,5},{5... | collective-permute-start | bytes 294920 | tf_op jit(solution)/shard_map/ppermute | solution.py:156
  15.2 1.3 %copy-start = (f32[32]{0:T(128)S(1)}, f32[32]{0:T(128)}, u32[]{:S(2)}) copy-start(f32[32]{0:T(128)} %skip_ref) | copy-start | bytes 388
  15.2 5.8 %collective-permute-start.8 = (bf16[32,2048]{1,0:T(8,128)(2,1)S(1)}, bf16[32,2048]{1,0:T(8,128)(2,1)S(1)}, u32[]{:S(2)}, u32[]{:S(2)}) collective-permute-start(bf16[32,2048]{1,0:T(8,128)(2,1)S(1)} %get-tuple-element.63), channel_id=1, source_target_pairs={{0,1},{1,0},{2,3},{3,2},{4,5},{5,4},{6,7},{7,6},{8,9},{9,8},{10,11... | collective-permute-start | bytes 393224 | tf_op jit(solution)/shard_map/ppermute | solution.py:156

commit v21 on v20

--- a/solution.py
+++ b/solution.py
@@ -157,18 +157,20 @@
 
 
 def tables_kernel(own, skip_ref, outer_ref, inner_ref, turns_ref, outer_out, back_out, ahead, rear, turns_out, *rest):
-    outer_s, inner_s, sems = rest
+    outer_s, inner_s, skip_s, sems = rest
     count, width = turns_ref.shape
     loads = [
         pltpu.make_async_copy(outer_ref, outer_s, sems.at[0]),
         pltpu.make_async_copy(inner_ref, inner_s, sems.at[1]),
         pltpu.make_async_copy(turns_ref, turns_out.at[0:count, :], sems.at[2]),
+        pltpu.make_async_copy(skip_ref, skip_s, sems.at[3]),
     ]
-    for copy in loads:
+    for copy in loads[::-1]:
         copy.start()
+    loads[3].wait()
     me = lax.axis_index("ctx")
     for c in range(own):
-        turns_out[count + 8 * c : count + 8 * (c + 1), :] = jnp.full((8, width), skip_ref[own * me + c], jnp.float32)
+        turns_out[count + 8 * c : count + 8 * (c + 1), :] = jnp.full((8, width), skip_s[own * me + c], jnp.float32)
     loads[0].wait()
     outer_out[...] = outer_s[...].astype(jnp.bfloat16)
     back_out[...] = outer_s[...].T.astype(jnp.bfloat16)
@@ -184,22 +186,23 @@
 
 def make_tables(skip, outer, inner, turns, own):
     count, width = turns.shape
-    args = [pltpu.with_memory_space_constraint(arg, pltpu.HBM) for arg in (outer, inner, turns)]
+    args = [pltpu.with_memory_space_constraint(arg, pltpu.HBM) for arg in (skip, outer, inner, turns)]
     narrow = (outer.shape, outer.shape[::-1], (2 * W, 2 * W), (2 * W, 2 * W))
     return pl.pallas_call(
         functools.partial(tables_kernel, own),
         out_shape=[jax.ShapeDtypeStruct(shape, jnp.bfloat16) for shape in narrow]
         + [jax.ShapeDtypeStruct((count + 8 * own, width), jnp.float32)],
-        in_specs=[pl.BlockSpec(memory_space=pltpu.SMEM)] + [in_hbm()] * 3,
+        in_specs=[in_hbm()] * 4,
         out_specs=[whole_vmem()] * 5,
         scratch_shapes=[
             pltpu.VMEM(outer.shape, jnp.float32),
             pltpu.VMEM(inner.shape, jnp.float32),
-            pltpu.SemaphoreType.DMA((3,)),
+            pltpu.SMEM(skip.shape, jnp.float32),
+            pltpu.SemaphoreType.DMA((4,)),
         ],
         compiler_params=pltpu.CompilerParams(vmem_limit_bytes=16 * 2**20),
         name="make_tables",
-    )(skip, *args)
+    )(*args)
 
 
 def conv_kernel(own, near, ch_count, parts, *rest):

time: 40.5 us -> 40.4 us (level)
  transfers between devices with their start and end apart: 9 -> 9, of which waited for: 1 -> 1; matrix products, arithmetic and copies ran while one was open for 0% -> 0% of each run, Pallas kernels for 11% -> 10%
where the time goes in v21:
time: 40.4 us; the launch traced here: 40.2 us
  blocking collectives  18.5 us (46%)
  starting transfers between devices  12.1 us (30%)
  Pallas kernels  7.17 us (18%)
  waiting for transfers between devices  2.36 us (6%)
    all_to_all x1, blocking collectives, body(): lax.all_to_all(mixed, ('ctx', 'ch'), split_axis=0, concat_axis=0, tiled=T...  18.5 us
    ppermute x9, starting transfers between devices, swap(): return lax.ppermute(piece, axis, [(i, i ^ d) for i in range(count)])  12.1 us
    pallas_call x1, Pallas kernels, convolve(): pl.pallas_call(functools.partial(conv_kernel, own, near, ch_count, parts)...  2.53 us
    ppermute x9, waiting for transfers between devices, swap(): return lax.ppermute(piece, axis, [(i, i ^ d) for i in range(count)])  2.36 us
    pallas_call x1, Pallas kernels, pack(): pl.pallas_call(functools.partial(pack_kernel, own, blocks, group, ch_coun...  2.02 us
    pallas_call x1, Pallas kernels, make_tables(): pl.pallas_call(functools.partial(tables_kernel, own), out_shape=[jax.Shap...  1.61 us
    pallas_call x1, Pallas kernels, unpack(): pl.pallas_call(functools.partial(unpack_kernel, own), out_shape=jax.Shape...  1.01 us
  transfers between devices with their start and end apart: 9, of which 1 were waited for; matrix products, arithmetic and copies ran while one was open for 0% of the time, Pallas kernels for 10%

profile of v21, /device:TPU:1, one launch (start us, length us, event | category | flops | bytes accessed | tf_op | source)
XLA Modules:
  0.0 40.2 jit_solution(11206999010408136666)
XLA Ops:
  0.0 2.0 %pack.1 = (bf16[192,256]{1,0:T(8,128)(2,1)S(1)}, bf16[192,256]{1,0:T(8,128)(2,1)S(1)}, bf16[192,256]{1,0:T(8,128)(2,1)S(1)}, bf16[192,256]{1,0:T(8,128)(2,1)S(1)...) custom-call(bf16[32,8192]{1,0:T(8,128)(2,1)} %pre_ref.1, ...), custom_call_target="tpu_custom_call" | custom-call | tf_op jit(solution)/shard_map/pack/pallas_call | solution.py:125
  2.0 3.1 %collective-permute-start = (bf16[192,256]{1,0:T(8,128)(2,1)S(1)}, bf16[192,256]{1,0:T(8,128)(2,1)S(1)}, u32[]{:S(2)}, u32[]{:S(2)}) collective-permute-start(bf16[192,256]{1,0:T(8,128)(2,1)S(1)} %get-tuple-element.38), channel_id=1, source_target_pairs={{0,24},{4,28},{8,16},{12,20},{16,8},{20,12},{24,0},{28,4},{1,25},{... | collective-permute-start | bytes 294920 | tf_op jit(solution)/shard_map/ppermute | solution.py:156
  5.1 0.3 collective-permute-start.1
  5.3 0.1 collective-permute-start.2
  5.5 2.4 %collective-permute-start.7 = (bf16[32,2048]{1,0:T(8,128)(2,1)S(1)}, bf16[32,2048]{1,0:T(8,128)(2,1)S(1)}, u32[]{:S(2)}, u32[]{:S(2)}) collective-permute-start(bf16[32,2048]{1,0:T(8,128)(2,1)S(1)} %get-tuple-element.45), channel_id=1, source_target_pairs={{0,2},{1,3},{2,0},{3,1},{4,6},{5,7},{6,4},{7,5},{8,10},{9,11},{10,... | collective-permute-start | bytes 393224 | tf_op jit(solution)/shard_map/ppermute | solution.py:156
  7.9 3.8 %collective-permute-start.3 = (bf16[192,256]{1,0:T(8,128)(2,1)S(1)}, bf16[192,256]{1,0:T(8,128)(2,1)S(1)}, u32[]{:S(2)}, u32[]{:S(2)}) collective-permute-start(bf16[192,256]{1,0:T(8,128)(2,1)S(1)} %get-tuple-element.41), channel_id=1, source_target_pairs={{0,28},{4,24},{8,20},{12,16},{16,12},{20,8},{24,4},{28,0},{1,29},{... | collective-permute-start | bytes 294920 | tf_op jit(solution)/shard_map/ppermute | solution.py:156
  11.7 0.0 collective-permute-done.rest_1_
  11.7 0.0 collective-permute-start.4
  11.7 0.0 collective-permute-done.1.rest_2_
  11.7 0.8 %collective-permute-start.5 = (bf16[192,256]{1,0:T(8,128)(2,1)S(1)}, bf16[192,256]{1,0:T(8,128)(2,1)S(1)}, u32[]{:S(2)}, u32[]{:S(2)}) collective-permute-start(bf16[192,256]{1,0:T(8,128)(2,1)S(1)} %get-tuple-element.43), channel_id=1, source_target_pairs={{0,20},{4,16},{8,28},{12,24},{16,4},{20,0},{24,12},{28,8},{1,21},{... | collective-permute-start | bytes 294920 | tf_op jit(solution)/shard_map/ppermute | solution.py:156
  12.5 0.0 collective-permute-done.2.rest_3_
  12.5 0.3 collective-permute-start.6
  12.8 2.3 %collective-permute-done.3.rest_4_ = bf16[192,256]{1,0:T(8,128)(2,1)S(1)} collective-permute-done((bf16[192,256]{1,0:T(8,128)(2,1)S(1)}, bf16[192,256]{1,0:T(8,128)(2,1)S(1)}, u32[]{:S(2)}, u32[]{:S(2)}) %collective-permute-start.3) | collective-permute-done | bytes 98336 | tf_op jit(solution)/shard_map/ppermute | solution.py:156
  15.2 1.3 %collective-permute-start.8 = (bf16[32,2048]{1,0:T(8,128)(2,1)S(1)}, bf16[32,2048]{1,0:T(8,128)(2,1)S(1)}, u32[]{:S(2)}, u32[]{:S(2)}) collective-permute-start(bf16[32,2048]{1,0:T(8,128)(2,1)S(1)} %get-tuple-element.63), channel_id=1, source_target_pairs={{0,1},{1,0},{2,3},{3,2},{4,5},{5,4},{6,7},{7,6},{8,9},{9,8},{10,11... | collective-permute-start | bytes 393224 | tf_op jit(solution)/shard_map/ppermute | solution.py:156
  16.5 1.6 %make_tables.1 = (bf16[512,256]{1,0:T(8,128)(2,1)S(1)}, bf16[256,512]{1,0:T(8,128)(2,1)S(1)}, bf16[512,512]{1,0:T(8,128)(2,1)S(1)}, bf16[512,512]{1,0:T(8,128)(2,1)S(1)}, f32[288,512]{1,0:T(8,128)S(1)}) custom-call(f32[32]{0:T(128)} %skip_ref, f32[512,256]{1,0:T(8,128)} %constant.6.clone.outer_ref, f32[512,256]{1,0:T(8,128)} %constant.7.clone.inner_ref, ...), custom_call_target="tpu_custom_call" | custom-call | tf_op jit(solution)/shard_map/make_tables/pallas_call | solution.py:191
  18.1 0.0 collective-permute-done.4.rest_5_
  18.1 0.0 collective-permute-done.5.rest_6_
  18.1 0.0 collective-permute-done.6.rest_7_
  18.1 0.0 collective-permute-done.7.rest_2_
  18.1 2.5 %convolve.1 = bf16[32,32,256]{2,1,0:T(8,128)(2,1)S(1)} custom-call(bf16[192,256]{1,0:T(8,128)(2,1)S(1)} %get-tuple-element.37.rest_0_, bf16[192,256]{1,0:T(8,128)(2,1)S(1)} %collective-permute-done.rest_1_, bf16[192,256]{1,0:T(8,128)(2,1)S(1)} %collective-permute-done.1.rest_2_, bf16[192,256]{1,0:T(8,128)(2,1)S(1)} %collective-permute-done.2.rest_3_, ...), custom_call_target="tpu_custom_call" | custom-call | flops 1048576000 | bytes 262144 | tf_op jit(solution)/shard_map/convolve/pallas_call | solution.py:278
  20.7 0.0 collective-permute-done.8.rest_1_
  20.7 18.5 %all_to_all.5.got_ref = bf16[32,32,256]{2,1,0:T(8,128)(2,1)S(1)} all-to-all(bf16[32,32,256]{2,1,0:T(8,128)(2,1)S(1)} %convolve.1), channel_id=1, replica_groups=mesh['ctx'=8,'ch'=4] {'ctx','ch'}, dimensions={0} | all-to-all | bytes 1048576 | tf_op jit(solution)/shard_map/all_to_all | solution.py:366
  39.2 1.0 %unpack.1 = bf16[128,2048]{1,0:T(8,128)(2,1)} custom-call(bf16[32,32,256]{2,1,0:T(8,128)(2,1)S(1)} %all_to_all.5.got_ref, bf16[32,2048]{1,0:T(8,128)(2,1)S(1)} %get-tuple-element.66.rest_0_, bf16[32,2048]{1,0:T(8,128)(2,1)S(1)} %collective-permute-done.8.rest_1_, bf16[32,2048]{1,0:T(8,128)(2,1)S(1)} %collective-permute-done.7.rest_2_), custom_call_target="tpu_custom_call" | custom-call | tf_op jit(solution)/shard_map/unpack/pallas_call | solution.py:333
Async XLA Ops:
  2.0 9.7 %collective-permute-start = (bf16[192,256]{1,0:T(8,128)(2,1)S(1)}, bf16[192,256]{1,0:T(8,128)(2,1)S(1)}, u32[]{:S(2)}, u32[]{:S(2)}) collective-permute-start(bf16[192,256]{1,0:T(8,128)(2,1)S(1)} %get-tuple-element.38), channel_id=1, source_target_pairs={{0,24},{4,28},{8,16},{12,20},{16,8},{20,12},{24,0},{28,4},{1,25},{... | collective-permute-start | bytes 294920 | tf_op jit(solution)/shard_map/ppermute | solution.py:156
  5.1 6.6 %collective-permute-start.1 = (bf16[192,256]{1,0:T(8,128)(2,1)S(1)}, bf16[192,256]{1,0:T(8,128)(2,1)S(1)}, u32[]{:S(2)}, u32[]{:S(2)}) collective-permute-start(bf16[192,256]{1,0:T(8,128)(2,1)S(1)} %get-tuple-element.39), channel_id=1, source_target_pairs={{0,8},{4,12},{8,0},{12,4},{16,24},{20,28},{24,16},{28,20},{1,9},{5... | collective-permute-start | bytes 294920 | tf_op jit(solution)/shard_map/ppermute | solution.py:156
  5.3 7.2 %collective-permute-start.2 = (bf16[192,256]{1,0:T(8,128)(2,1)S(1)}, bf16[192,256]{1,0:T(8,128)(2,1)S(1)}, u32[]{:S(2)}, u32[]{:S(2)}) collective-permute-start(bf16[192,256]{1,0:T(8,128)(2,1)S(1)} %get-tuple-element.40), channel_id=1, source_target_pairs={{0,16},{4,20},{8,24},{12,28},{16,0},{20,4},{24,8},{28,12},{1,17},{... | collective-permute-start | bytes 294920 | tf_op jit(solution)/shard_map/ppermute | solution.py:156
  5.5 12.7 %collective-permute-start.7 = (bf16[32,2048]{1,0:T(8,128)(2,1)S(1)}, bf16[32,2048]{1,0:T(8,128)(2,1)S(1)}, u32[]{:S(2)}, u32[]{:S(2)}) collective-permute-start(bf16[32,2048]{1,0:T(8,128)(2,1)S(1)} %get-tuple-element.45), channel_id=1, source_target_pairs={{0,2},{1,3},{2,0},{3,1},{4,6},{5,7},{6,4},{7,5},{8,10},{9,11},{10,... | collective-permute-start | bytes 393224 | tf_op jit(solution)/shard_map/ppermute | solution.py:156
  7.9 7.3 %collective-permute-start.3 = (bf16[192,256]{1,0:T(8,128)(2,1)S(1)}, bf16[192,256]{1,0:T(8,128)(2,1)S(1)}, u32[]{:S(2)}, u32[]{:S(2)}) collective-permute-start(bf16[192,256]{1,0:T(8,128)(2,1)S(1)} %get-tuple-element.41), channel_id=1, source_target_pairs={{0,28},{4,24},{8,20},{12,16},{16,12},{20,8},{24,4},{28,0},{1,29},{... | collective-permute-start | bytes 294920 | tf_op jit(solution)/shard_map/ppermute | solution.py:156
  11.7 6.4 %collective-permute-start.4 = (bf16[192,256]{1,0:T(8,128)(2,1)S(1)}, bf16[192,256]{1,0:T(8,128)(2,1)S(1)}, u32[]{:S(2)}, u32[]{:S(2)}) collective-permute-start(bf16[192,256]{1,0:T(8,128)(2,1)S(1)} %get-tuple-element.42), channel_id=1, source_target_pairs={{0,12},{4,8},{8,4},{12,0},{16,28},{20,24},{24,20},{28,16},{1,13},{... | collective-permute-start | bytes 294920 | tf_op jit(solution)/shard_map/ppermute | solution.py:156
  11.7 6.4 %collective-permute-start.5 = (bf16[192,256]{1,0:T(8,128)(2,1)S(1)}, bf16[192,256]{1,0:T(8,128)(2,1)S(1)}, u32[]{:S(2)}, u32[]{:S(2)}) collective-permute-start(bf16[192,256]{1,0:T(8,128)(2,1)S(1)} %get-tuple-element.43), channel_id=1, source_target_pairs={{0,20},{4,16},{8,28},{12,24},{16,4},{20,0},{24,12},{28,8},{1,21},{... | collective-permute-start | bytes 294920 | tf_op jit(solution)/shard_map/ppermute | solution.py:156
  12.5 5.6 %collective-permute-start.6 = (bf16[192,256]{1,0:T(8,128)(2,1)S(1)}, bf16[192,256]{1,0:T(8,128)(2,1)S(1)}, u32[]{:S(2)}, u32[]{:S(2)}) collective-permute-start(bf16[192,256]{1,0:T(8,128)(2,1)S(1)} %get-tuple-element.44), channel_id=1, source_target_pairs={{0,4},{4,0},{8,12},{12,8},{16,20},{20,16},{24,28},{28,24},{1,5},{5... | collective-permute-start | bytes 294920 | tf_op jit(solution)/shard_map/ppermute | solution.py:156
  15.2 5.5 %collective-permute-start.8 = (bf16[32,2048]{1,0:T(8,128)(2,1)S(1)}, bf16[32,2048]{1,0:T(8,128)(2,1)S(1)}, u32[]{:S(2)}, u32[]{:S(2)}) collective-permute-start(bf16[32,2048]{1,0:T(8,128)(2,1)S(1)} %get-tuple-element.63), channel_id=1, source_target_pairs={{0,1},{1,0},{2,3},{3,2},{4,5},{5,4},{6,7},{7,6},{8,9},{9,8},{10,11... | collective-permute-start | bytes 393224 | tf_op jit(solution)/shard_map/ppermute | solution.py:156

commit v22 on v21

--- a/solution.py
+++ b/solution.py
@@ -165,7 +165,7 @@
         pltpu.make_async_copy(turns_ref, turns_out.at[0:count, :], sems.at[2]),
         pltpu.make_async_copy(skip_ref, skip_s, sems.at[3]),
     ]
-    for copy in loads[::-1]:
+    for copy in loads[3:] + loads[:3]:
         copy.start()
     loads[3].wait()
     me = lax.axis_index("ctx")

time: 40.4 us -> 40.4 us (level)
  no operation moved by 1% of the time
where the time goes in v22:
time: 40.4 us; the launch traced here: 40.2 us
  blocking collectives  18.7 us (46%)
  starting transfers between devices  12.1 us (30%)
  Pallas kernels  6.96 us (17%)
  waiting for transfers between devices  2.36 us (6%)
    all_to_all x1, blocking collectives, body(): lax.all_to_all(mixed, ('ctx', 'ch'), split_axis=0, concat_axis=0, tiled=T...  18.7 us
    ppermute x9, starting transfers between devices, swap(): return lax.ppermute(piece, axis, [(i, i ^ d) for i in range(count)])  12.1 us
    pallas_call x1, Pallas kernels, convolve(): pl.pallas_call(functools.partial(conv_kernel, own, near, ch_count, parts)...  2.54 us
    ppermute x9, waiting for transfers between devices, swap(): return lax.ppermute(piece, axis, [(i, i ^ d) for i in range(count)])  2.36 us
    pallas_call x1, Pallas kernels, pack(): pl.pallas_call(functools.partial(pack_kernel, own, blocks, group, ch_coun...  2.02 us
    pallas_call x1, Pallas kernels, make_tables(): pl.pallas_call(functools.partial(tables_kernel, own), out_shape=[jax.Shap...  1.39 us
    pallas_call x1, Pallas kernels, unpack(): pl.pallas_call(functools.partial(unpack_kernel, own), out_shape=jax.Shape...  1.01 us
  transfers between devices with their start and end apart: 9, of which 1 were waited for; matrix products, arithmetic and copies ran while one was open for 0% of the time, Pallas kernels for 10%

profile of v22, /device:TPU:1, one launch (start us, length us, event | category | flops | bytes accessed | tf_op | source)
XLA Modules:
  0.0 40.2 jit_solution(2013882602246878915)
XLA Ops:
  0.0 2.0 %pack.1 = (bf16[192,256]{1,0:T(8,128)(2,1)S(1)}, bf16[192,256]{1,0:T(8,128)(2,1)S(1)}, bf16[192,256]{1,0:T(8,128)(2,1)S(1)}, bf16[192,256]{1,0:T(8,128)(2,1)S(1)...) custom-call(bf16[32,8192]{1,0:T(8,128)(2,1)} %pre_ref.1, ...), custom_call_target="tpu_custom_call" | custom-call | tf_op jit(solution)/shard_map/pack/pallas_call | solution.py:125
  2.0 3.1 %collective-permute-start = (bf16[192,256]{1,0:T(8,128)(2,1)S(1)}, bf16[192,256]{1,0:T(8,128)(2,1)S(1)}, u32[]{:S(2)}, u32[]{:S(2)}) collective-permute-start(bf16[192,256]{1,0:T(8,128)(2,1)S(1)} %get-tuple-element.38), channel_id=1, source_target_pairs={{0,24},{4,28},{8,16},{12,20},{16,8},{20,12},{24,0},{28,4},{1,25},{... | collective-permute-start | bytes 294920 | tf_op jit(solution)/shard_map/ppermute | solution.py:156
  5.1 0.3 collective-permute-start.1
  5.3 0.1 collective-permute-start.2
  5.5 2.4 %collective-permute-start.7 = (bf16[32,2048]{1,0:T(8,128)(2,1)S(1)}, bf16[32,2048]{1,0:T(8,128)(2,1)S(1)}, u32[]{:S(2)}, u32[]{:S(2)}) collective-permute-start(bf16[32,2048]{1,0:T(8,128)(2,1)S(1)} %get-tuple-element.45), channel_id=1, source_target_pairs={{0,2},{1,3},{2,0},{3,1},{4,6},{5,7},{6,4},{7,5},{8,10},{9,11},{10,... | collective-permute-start | bytes 393224 | tf_op jit(solution)/shard_map/ppermute | solution.py:156
  7.9 3.8 %collective-permute-start.3 = (bf16[192,256]{1,0:T(8,128)(2,1)S(1)}, bf16[192,256]{1,0:T(8,128)(2,1)S(1)}, u32[]{:S(2)}, u32[]{:S(2)}) collective-permute-start(bf16[192,256]{1,0:T(8,128)(2,1)S(1)} %get-tuple-element.41), channel_id=1, source_target_pairs={{0,28},{4,24},{8,20},{12,16},{16,12},{20,8},{24,4},{28,0},{1,29},{... | collective-permute-start | bytes 294920 | tf_op jit(solution)/shard_map/ppermute | solution.py:156
  11.7 0.0 collective-permute-done.rest_1_
  11.7 0.0 collective-permute-start.4
  11.7 0.0 collective-permute-done.1.rest_2_
  11.7 0.8 %collective-permute-start.5 = (bf16[192,256]{1,0:T(8,128)(2,1)S(1)}, bf16[192,256]{1,0:T(8,128)(2,1)S(1)}, u32[]{:S(2)}, u32[]{:S(2)}) collective-permute-start(bf16[192,256]{1,0:T(8,128)(2,1)S(1)} %get-tuple-element.43), channel_id=1, source_target_pairs={{0,20},{4,16},{8,28},{12,24},{16,4},{20,0},{24,12},{28,8},{1,21},{... | collective-permute-start | bytes 294920 | tf_op jit(solution)/shard_map/ppermute | solution.py:156
  12.5 0.0 collective-permute-done.2.rest_3_
  12.5 0.3 collective-permute-start.6
  12.8 2.3 %collective-permute-done.3.rest_4_ = bf16[192,256]{1,0:T(8,128)(2,1)S(1)} collective-permute-done((bf16[192,256]{1,0:T(8,128)(2,1)S(1)}, bf16[192,256]{1,0:T(8,128)(2,1)S(1)}, u32[]{:S(2)}, u32[]{:S(2)}) %collective-permute-start.3) | collective-permute-done | bytes 98336 | tf_op jit(solution)/shard_map/ppermute | solution.py:156
  15.2 1.3 %collective-permute-start.8 = (bf16[32,2048]{1,0:T(8,128)(2,1)S(1)}, bf16[32,2048]{1,0:T(8,128)(2,1)S(1)}, u32[]{:S(2)}, u32[]{:S(2)}) collective-permute-start(bf16[32,2048]{1,0:T(8,128)(2,1)S(1)} %get-tuple-element.63), channel_id=1, source_target_pairs={{0,1},{1,0},{2,3},{3,2},{4,5},{5,4},{6,7},{7,6},{8,9},{9,8},{10,11... | collective-permute-start | bytes 393224 | tf_op jit(solution)/shard_map/ppermute | solution.py:156
  16.5 1.4 %make_tables.1 = (bf16[512,256]{1,0:T(8,128)(2,1)S(1)}, bf16[256,512]{1,0:T(8,128)(2,1)S(1)}, bf16[512,512]{1,0:T(8,128)(2,1)S(1)}, bf16[512,512]{1,0:T(8,128)(2,1)S(1)}, f32[288,512]{1,0:T(8,128)S(1)}) custom-call(f32[32]{0:T(128)} %skip_ref, f32[512,256]{1,0:T(8,128)} %constant.6.clone.outer_ref, f32[512,256]{1,0:T(8,128)} %constant.7.clone.inner_ref, ...), custom_call_target="tpu_custom_call" | custom-call | tf_op jit(solution)/shard_map/make_tables/pallas_call | solution.py:191
  17.9 0.0 collective-permute-done.4.rest_5_
  17.9 0.0 collective-permute-done.5.rest_6_
  17.9 0.0 collective-permute-done.6.rest_7_
  17.9 0.0 collective-permute-done.7.rest_2_
  17.9 2.5 %convolve.1 = bf16[32,32,256]{2,1,0:T(8,128)(2,1)S(1)} custom-call(bf16[192,256]{1,0:T(8,128)(2,1)S(1)} %get-tuple-element.37.rest_0_, bf16[192,256]{1,0:T(8,128)(2,1)S(1)} %collective-permute-done.rest_1_, bf16[192,256]{1,0:T(8,128)(2,1)S(1)} %collective-permute-done.1.rest_2_, bf16[192,256]{1,0:T(8,128)(2,1)S(1)} %collective-permute-done.2.rest_3_, ...), custom_call_target="tpu_custom_call" | custom-call | flops 1048576000 | bytes 262144 | tf_op jit(solution)/shard_map/convolve/pallas_call | solution.py:278
  20.5 0.0 collective-permute-done.8.rest_1_
  20.5 18.7 %all_to_all.5.got_ref = bf16[32,32,256]{2,1,0:T(8,128)(2,1)S(1)} all-to-all(bf16[32,32,256]{2,1,0:T(8,128)(2,1)S(1)} %convolve.1), channel_id=1, replica_groups=mesh['ctx'=8,'ch'=4] {'ctx','ch'}, dimensions={0} | all-to-all | bytes 1048576 | tf_op jit(solution)/shard_map/all_to_all | solution.py:366
  39.2 1.0 %unpack.1 = bf16[128,2048]{1,0:T(8,128)(2,1)} custom-call(bf16[32,32,256]{2,1,0:T(8,128)(2,1)S(1)} %all_to_all.5.got_ref, bf16[32,2048]{1,0:T(8,128)(2,1)S(1)} %get-tuple-element.66.rest_0_, bf16[32,2048]{1,0:T(8,128)(2,1)S(1)} %collective-permute-done.8.rest_1_, bf16[32,2048]{1,0:T(8,128)(2,1)S(1)} %collective-permute-done.7.rest_2_), custom_call_target="tpu_custom_call" | custom-call | tf_op jit(solution)/shard_map/unpack/pallas_call | solution.py:333
Async XLA Ops:
  2.0 9.7 %collective-permute-start = (bf16[192,256]{1,0:T(8,128)(2,1)S(1)}, bf16[192,256]{1,0:T(8,128)(2,1)S(1)}, u32[]{:S(2)}, u32[]{:S(2)}) collective-permute-start(bf16[192,256]{1,0:T(8,128)(2,1)S(1)} %get-tuple-element.38), channel_id=1, source_target_pairs={{0,24},{4,28},{8,16},{12,20},{16,8},{20,12},{24,0},{28,4},{1,25},{... | collective-permute-start | bytes 294920 | tf_op jit(solution)/shard_map/ppermute | solution.py:156
  5.1 6.6 %collective-permute-start.1 = (bf16[192,256]{1,0:T(8,128)(2,1)S(1)}, bf16[192,256]{1,0:T(8,128)(2,1)S(1)}, u32[]{:S(2)}, u32[]{:S(2)}) collective-permute-start(bf16[192,256]{1,0:T(8,128)(2,1)S(1)} %get-tuple-element.39), channel_id=1, source_target_pairs={{0,8},{4,12},{8,0},{12,4},{16,24},{20,28},{24,16},{28,20},{1,9},{5... | collective-permute-start | bytes 294920 | tf_op jit(solution)/shard_map/ppermute | solution.py:156
  5.3 7.2 %collective-permute-start.2 = (bf16[192,256]{1,0:T(8,128)(2,1)S(1)}, bf16[192,256]{1,0:T(8,128)(2,1)S(1)}, u32[]{:S(2)}, u32[]{:S(2)}) collective-permute-start(bf16[192,256]{1,0:T(8,128)(2,1)S(1)} %get-tuple-element.40), channel_id=1, source_target_pairs={{0,16},{4,20},{8,24},{12,28},{16,0},{20,4},{24,8},{28,12},{1,17},{... | collective-permute-start | bytes 294920 | tf_op jit(solution)/shard_map/ppermute | solution.py:156
  5.5 12.4 %collective-permute-start.7 = (bf16[32,2048]{1,0:T(8,128)(2,1)S(1)}, bf16[32,2048]{1,0:T(8,128)(2,1)S(1)}, u32[]{:S(2)}, u32[]{:S(2)}) collective-permute-start(bf16[32,2048]{1,0:T(8,128)(2,1)S(1)} %get-tuple-element.45), channel_id=1, source_target_pairs={{0,2},{1,3},{2,0},{3,1},{4,6},{5,7},{6,4},{7,5},{8,10},{9,11},{10,... | collective-permute-start | bytes 393224 | tf_op jit(solution)/shard_map/ppermute | solution.py:156
  7.9 7.3 %collective-permute-start.3 = (bf16[192,256]{1,0:T(8,128)(2,1)S(1)}, bf16[192,256]{1,0:T(8,128)(2,1)S(1)}, u32[]{:S(2)}, u32[]{:S(2)}) collective-permute-start(bf16[192,256]{1,0:T(8,128)(2,1)S(1)} %get-tuple-element.41), channel_id=1, source_target_pairs={{0,28},{4,24},{8,20},{12,16},{16,12},{20,8},{24,4},{28,0},{1,29},{... | collective-permute-start | bytes 294920 | tf_op jit(solution)/shard_map/ppermute | solution.py:156
  11.7 6.1 %collective-permute-start.4 = (bf16[192,256]{1,0:T(8,128)(2,1)S(1)}, bf16[192,256]{1,0:T(8,128)(2,1)S(1)}, u32[]{:S(2)}, u32[]{:S(2)}) collective-permute-start(bf16[192,256]{1,0:T(8,128)(2,1)S(1)} %get-tuple-element.42), channel_id=1, source_target_pairs={{0,12},{4,8},{8,4},{12,0},{16,28},{20,24},{24,20},{28,16},{1,13},{... | collective-permute-start | bytes 294920 | tf_op jit(solution)/shard_map/ppermute | solution.py:156
  11.7 6.1 %collective-permute-start.5 = (bf16[192,256]{1,0:T(8,128)(2,1)S(1)}, bf16[192,256]{1,0:T(8,128)(2,1)S(1)}, u32[]{:S(2)}, u32[]{:S(2)}) collective-permute-start(bf16[192,256]{1,0:T(8,128)(2,1)S(1)} %get-tuple-element.43), channel_id=1, source_target_pairs={{0,20},{4,16},{8,28},{12,24},{16,4},{20,0},{24,12},{28,8},{1,21},{... | collective-permute-start | bytes 294920 | tf_op jit(solution)/shard_map/ppermute | solution.py:156
  12.5 5.4 %collective-permute-start.6 = (bf16[192,256]{1,0:T(8,128)(2,1)S(1)}, bf16[192,256]{1,0:T(8,128)(2,1)S(1)}, u32[]{:S(2)}, u32[]{:S(2)}) collective-permute-start(bf16[192,256]{1,0:T(8,128)(2,1)S(1)} %get-tuple-element.44), channel_id=1, source_target_pairs={{0,4},{4,0},{8,12},{12,8},{16,20},{20,16},{24,28},{28,24},{1,5},{5... | collective-permute-start | bytes 294920 | tf_op jit(solution)/shard_map/ppermute | solution.py:156
  15.2 5.3 %collective-permute-start.8 = (bf16[32,2048]{1,0:T(8,128)(2,1)S(1)}, bf16[32,2048]{1,0:T(8,128)(2,1)S(1)}, u32[]{:S(2)}, u32[]{:S(2)}) collective-permute-start(bf16[32,2048]{1,0:T(8,128)(2,1)S(1)} %get-tuple-element.63), channel_id=1, source_target_pairs={{0,1},{1,0},{2,3},{3,2},{4,5},{5,4},{6,7},{7,6},{8,9},{9,8},{10,11... | collective-permute-start | bytes 393224 | tf_op jit(solution)/shard_map/ppermute | solution.py:156

commit v23 on v22

--- a/solution.py
+++ b/solution.py
@@ -286,7 +286,7 @@
             pltpu.VMEM((own, blocks, W), jnp.float32),
         ],
         compiler_params=pltpu.CompilerParams(vmem_limit_bytes=32 * 2**20),
-        cost_estimate=pl.CostEstimate(flops=16000 * blocks * W, bytes_accessed=4 * blocks * W, transcendentals=0),
+        cost_estimate=pl.CostEstimate(flops=7000 * blocks * W, bytes_accessed=4 * blocks * W, transcendentals=0),
         name="convolve",
     )(*got, *tables)
 

time: 40.4 us -> 41.4 us (1.025)
  blocking collectives: 18.7 us -> 19.8 us
  waiting for transfers between devices: 2.36 us -> 1.62 us
  starting transfers between devices: 12.1 us -> 12.7 us
    all_to_all x1, blocking collectives: 18.7 us -> 19.8 us  [body(): lax.all_to_all(mixed, ('ctx', 'ch'), split_axis=0, concat_axis=0, tiled=T...]
    ppermute x9, waiting for transfers between devices: 2.36 us -> 1.62 us  [swap(): return lax.ppermute(piece, axis, [(i, i ^ d) for i in range(count)])]
    ppermute x9, starting transfers between devices: 12.1 us -> 12.7 us  [swap(): return lax.ppermute(piece, axis, [(i, i ^ d) for i in range(count)])]
  transfers between devices with their start and end apart: 9 -> 9, of which waited for: 1 -> 3; matrix products, arithmetic and copies ran while one was open for 0% -> 0% of each run, Pallas kernels for 10% -> 10%
where the time goes in v23:
time: 41.4 us; the launch traced here: 41.2 us
  blocking collectives  19.8 us (48%)
  starting transfers between devices  12.7 us (31%)
  Pallas kernels  6.95 us (17%)
  waiting for transfers between devices  1.62 us (4%)
    all_to_all x1, blocking collectives, body(): lax.all_to_all(mixed, ('ctx', 'ch'), split_axis=0, concat_axis=0, tiled=T...  19.8 us
    ppermute x9, starting transfers between devices, swap(): return lax.ppermute(piece, axis, [(i, i ^ d) for i in range(count)])  12.7 us
    pallas_call x1, Pallas kernels, convolve(): pl.pallas_call(functools.partial(conv_kernel, own, near, ch_count, parts)...  2.53 us
    pallas_call x1, Pallas kernels, pack(): pl.pallas_call(functools.partial(pack_kernel, own, blocks, group, ch_coun...  2.02 us
    ppermute x9, waiting for transfers between devices, swap(): return lax.ppermute(piece, axis, [(i, i ^ d) for i in range(count)])  1.62 us
    pallas_call x1, Pallas kernels, make_tables(): pl.pallas_call(functools.partial(tables_kernel, own), out_shape=[jax.Shap...  1.39 us
    pallas_call x1, Pallas kernels, unpack(): pl.pallas_call(functools.partial(unpack_kernel, own), out_shape=jax.Shape...  1.01 us
  transfers between devices with their start and end apart: 9, of which 3 were waited for; matrix products, arithmetic and copies ran while one was open for 0% of the time, Pallas kernels for 10%

profile of v23, /device:TPU:1, one launch (start us, length us, event | category | flops | bytes accessed | tf_op | source)
XLA Modules:
  0.0 41.2 jit_solution(18275887237956826327)
XLA Ops:
  0.0 2.0 %pack.1 = (bf16[192,256]{1,0:T(8,128)(2,1)S(1)}, bf16[192,256]{1,0:T(8,128)(2,1)S(1)}, bf16[192,256]{1,0:T(8,128)(2,1)S(1)}, bf16[192,256]{1,0:T(8,128)(2,1)S(1)...) custom-call(bf16[32,8192]{1,0:T(8,128)(2,1)} %pre_ref.1, ...), custom_call_target="tpu_custom_call" | custom-call | tf_op jit(solution)/shard_map/pack/pallas_call | solution.py:125
  2.0 3.1 %collective-permute-start = (bf16[192,256]{1,0:T(8,128)(2,1)S(1)}, bf16[192,256]{1,0:T(8,128)(2,1)S(1)}, u32[]{:S(2)}, u32[]{:S(2)}) collective-permute-start(bf16[192,256]{1,0:T(8,128)(2,1)S(1)} %get-tuple-element.38), channel_id=1, source_target_pairs={{0,24},{4,28},{8,16},{12,20},{16,8},{20,12},{24,0},{28,4},{1,25},{... | collective-permute-start | bytes 294920 | tf_op jit(solution)/shard_map/ppermute | solution.py:156
  5.1 0.3 collective-permute-start.1
  5.3 0.1 collective-permute-start.2
  5.5 3.7 %collective-permute-start.3 = (bf16[192,256]{1,0:T(8,128)(2,1)S(1)}, bf16[192,256]{1,0:T(8,128)(2,1)S(1)}, u32[]{:S(2)}, u32[]{:S(2)}) collective-permute-start(bf16[192,256]{1,0:T(8,128)(2,1)S(1)} %get-tuple-element.41), channel_id=1, source_target_pairs={{0,28},{4,24},{8,20},{12,16},{16,12},{20,8},{24,4},{28,0},{1,29},{... | collective-permute-start | bytes 294920 | tf_op jit(solution)/shard_map/ppermute | solution.py:156
  9.1 2.3 %collective-permute-start.7 = (bf16[32,2048]{1,0:T(8,128)(2,1)S(1)}, bf16[32,2048]{1,0:T(8,128)(2,1)S(1)}, u32[]{:S(2)}, u32[]{:S(2)}) collective-permute-start(bf16[32,2048]{1,0:T(8,128)(2,1)S(1)} %get-tuple-element.45), channel_id=1, source_target_pairs={{0,2},{1,3},{2,0},{3,1},{4,6},{5,7},{6,4},{7,5},{8,10},{9,11},{10,... | collective-permute-start | bytes 393224 | tf_op jit(solution)/shard_map/ppermute | solution.py:156
  11.4 0.0 collective-permute-done.rest_1_
  11.5 0.0 collective-permute-start.4
  11.5 0.0 collective-permute-done.1.rest_2_
  11.5 0.8 %collective-permute-start.5 = (bf16[192,256]{1,0:T(8,128)(2,1)S(1)}, bf16[192,256]{1,0:T(8,128)(2,1)S(1)}, u32[]{:S(2)}, u32[]{:S(2)}) collective-permute-start(bf16[192,256]{1,0:T(8,128)(2,1)S(1)} %get-tuple-element.43), channel_id=1, source_target_pairs={{0,20},{4,16},{8,28},{12,24},{16,4},{20,0},{24,12},{28,8},{1,21},{... | collective-permute-start | bytes 294920 | tf_op jit(solution)/shard_map/ppermute | solution.py:156
  12.2 0.0 collective-permute-done.2.rest_3_
  12.2 1.1 %collective-permute-start.6 = (bf16[192,256]{1,0:T(8,128)(2,1)S(1)}, bf16[192,256]{1,0:T(8,128)(2,1)S(1)}, u32[]{:S(2)}, u32[]{:S(2)}) collective-permute-start(bf16[192,256]{1,0:T(8,128)(2,1)S(1)} %get-tuple-element.44), channel_id=1, source_target_pairs={{0,4},{4,0},{8,12},{12,8},{16,20},{20,16},{24,28},{28,24},{1,5},{5... | collective-permute-start | bytes 294920 | tf_op jit(solution)/shard_map/ppermute | solution.py:156
  13.3 0.0 collective-permute-done.3.rest_4_
  13.3 1.5 %collective-permute-start.8 = (bf16[32,2048]{1,0:T(8,128)(2,1)S(1)}, bf16[32,2048]{1,0:T(8,128)(2,1)S(1)}, u32[]{:S(2)}, u32[]{:S(2)}) collective-permute-start(bf16[32,2048]{1,0:T(8,128)(2,1)S(1)} %get-tuple-element.63), channel_id=1, source_target_pairs={{0,1},{1,0},{2,3},{3,2},{4,5},{5,4},{6,7},{7,6},{8,9},{9,8},{10,11... | collective-permute-start | bytes 393224 | tf_op jit(solution)/shard_map/ppermute | solution.py:156
  14.8 1.4 %make_tables.1 = (bf16[512,256]{1,0:T(8,128)(2,1)S(1)}, bf16[256,512]{1,0:T(8,128)(2,1)S(1)}, bf16[512,512]{1,0:T(8,128)(2,1)S(1)}, bf16[512,512]{1,0:T(8,128)(2,1)S(1)}, f32[288,512]{1,0:T(8,128)S(1)}) custom-call(f32[32]{0:T(128)} %skip_ref, f32[512,256]{1,0:T(8,128)} %constant.6.clone.outer_ref, f32[512,256]{1,0:T(8,128)} %constant.7.clone.inner_ref, ...), custom_call_target="tpu_custom_call" | custom-call | tf_op jit(solution)/shard_map/make_tables/pallas_call | solution.py:191
  16.2 0.0 collective-permute-done.4.rest_5_
  16.2 0.6 %collective-permute-done.5.rest_6_ = bf16[192,256]{1,0:T(8,128)(2,1)S(1)} collective-permute-done((bf16[192,256]{1,0:T(8,128)(2,1)S(1)}, bf16[192,256]{1,0:T(8,128)(2,1)S(1)}, u32[]{:S(2)}, u32[]{:S(2)}) %collective-permute-start.5) | collective-permute-done | bytes 98336 | tf_op jit(solution)/shard_map/ppermute | solution.py:156
  16.8 0.0 collective-permute-done.6.rest_7_
  16.8 0.8 %collective-permute-done.7.rest_2_ = bf16[32,2048]{1,0:T(8,128)(2,1)S(1)} collective-permute-done((bf16[32,2048]{1,0:T(8,128)(2,1)S(1)}, bf16[32,2048]{1,0:T(8,128)(2,1)S(1)}, u32[]{:S(2)}, u32[]{:S(2)}) %collective-permute-start.7) | collective-permute-done | bytes 131104 | tf_op jit(solution)/shard_map/ppermute | solution.py:156
  17.6 2.5 %convolve.1 = bf16[32,32,256]{2,1,0:T(8,128)(2,1)S(1)} custom-call(bf16[192,256]{1,0:T(8,128)(2,1)S(1)} %get-tuple-element.37.rest_0_, bf16[192,256]{1,0:T(8,128)(2,1)S(1)} %collective-permute-done.rest_1_, bf16[192,256]{1,0:T(8,128)(2,1)S(1)} %collective-permute-done.1.rest_2_, bf16[192,256]{1,0:T(8,128)(2,1)S(1)} %collective-permute-done.2.rest_3_, ...), custom_call_target="tpu_custom_call" | custom-call | flops 458752000 | bytes 262144 | tf_op jit(solution)/shard_map/convolve/pallas_call | solution.py:278
  20.2 0.2 collective-permute-done.8.rest_1_
  20.3 19.8 %all_to_all.5.got_ref = bf16[32,32,256]{2,1,0:T(8,128)(2,1)S(1)} all-to-all(bf16[32,32,256]{2,1,0:T(8,128)(2,1)S(1)} %convolve.1), channel_id=1, replica_groups=mesh['ctx'=8,'ch'=4] {'ctx','ch'}, dimensions={0} | all-to-all | bytes 1048576 | tf_op jit(solution)/shard_map/all_to_all | solution.py:366
  40.2 1.0 %unpack.1 = bf16[128,2048]{1,0:T(8,128)(2,1)} custom-call(bf16[32,32,256]{2,1,0:T(8,128)(2,1)S(1)} %all_to_all.5.got_ref, bf16[32,2048]{1,0:T(8,128)(2,1)S(1)} %get-tuple-element.66.rest_0_, bf16[32,2048]{1,0:T(8,128)(2,1)S(1)} %collective-permute-done.8.rest_1_, bf16[32,2048]{1,0:T(8,128)(2,1)S(1)} %collective-permute-done.7.rest_2_), custom_call_target="tpu_custom_call" | custom-call | tf_op jit(solution)/shard_map/unpack/pallas_call | solution.py:333
Async XLA Ops:
  2.0 9.4 %collective-permute-start = (bf16[192,256]{1,0:T(8,128)(2,1)S(1)}, bf16[192,256]{1,0:T(8,128)(2,1)S(1)}, u32[]{:S(2)}, u32[]{:S(2)}) collective-permute-start(bf16[192,256]{1,0:T(8,128)(2,1)S(1)} %get-tuple-element.38), channel_id=1, source_target_pairs={{0,24},{4,28},{8,16},{12,20},{16,8},{20,12},{24,0},{28,4},{1,25},{... | collective-permute-start | bytes 294920 | tf_op jit(solution)/shard_map/ppermute | solution.py:156
  5.1 6.4 %collective-permute-start.1 = (bf16[192,256]{1,0:T(8,128)(2,1)S(1)}, bf16[192,256]{1,0:T(8,128)(2,1)S(1)}, u32[]{:S(2)}, u32[]{:S(2)}) collective-permute-start(bf16[192,256]{1,0:T(8,128)(2,1)S(1)} %get-tuple-element.39), channel_id=1, source_target_pairs={{0,8},{4,12},{8,0},{12,4},{16,24},{20,28},{24,16},{28,20},{1,9},{5... | collective-permute-start | bytes 294920 | tf_op jit(solution)/shard_map/ppermute | solution.py:156
  5.3 6.9 %collective-permute-start.2 = (bf16[192,256]{1,0:T(8,128)(2,1)S(1)}, bf16[192,256]{1,0:T(8,128)(2,1)S(1)}, u32[]{:S(2)}, u32[]{:S(2)}) collective-permute-start(bf16[192,256]{1,0:T(8,128)(2,1)S(1)} %get-tuple-element.40), channel_id=1, source_target_pairs={{0,16},{4,20},{8,24},{12,28},{16,0},{20,4},{24,8},{28,12},{1,17},{... | collective-permute-start | bytes 294920 | tf_op jit(solution)/shard_map/ppermute | solution.py:156
  5.5 7.9 %collective-permute-start.3 = (bf16[192,256]{1,0:T(8,128)(2,1)S(1)}, bf16[192,256]{1,0:T(8,128)(2,1)S(1)}, u32[]{:S(2)}, u32[]{:S(2)}) collective-permute-start(bf16[192,256]{1,0:T(8,128)(2,1)S(1)} %get-tuple-element.41), channel_id=1, source_target_pairs={{0,28},{4,24},{8,20},{12,16},{16,12},{20,8},{24,4},{28,0},{1,29},{... | collective-permute-start | bytes 294920 | tf_op jit(solution)/shard_map/ppermute | solution.py:156
  9.1 8.5 %collective-permute-start.7 = (bf16[32,2048]{1,0:T(8,128)(2,1)S(1)}, bf16[32,2048]{1,0:T(8,128)(2,1)S(1)}, u32[]{:S(2)}, u32[]{:S(2)}) collective-permute-start(bf16[32,2048]{1,0:T(8,128)(2,1)S(1)} %get-tuple-element.45), channel_id=1, source_target_pairs={{0,2},{1,3},{2,0},{3,1},{4,6},{5,7},{6,4},{7,5},{8,10},{9,11},{10,... | collective-permute-start | bytes 393224 | tf_op jit(solution)/shard_map/ppermute | solution.py:156
  11.5 4.7 %collective-permute-start.4 = (bf16[192,256]{1,0:T(8,128)(2,1)S(1)}, bf16[192,256]{1,0:T(8,128)(2,1)S(1)}, u32[]{:S(2)}, u32[]{:S(2)}) collective-permute-start(bf16[192,256]{1,0:T(8,128)(2,1)S(1)} %get-tuple-element.42), channel_id=1, source_target_pairs={{0,12},{4,8},{8,4},{12,0},{16,28},{20,24},{24,20},{28,16},{1,13},{... | collective-permute-start | bytes 294920 | tf_op jit(solution)/shard_map/ppermute | solution.py:156
  11.5 5.3 %collective-permute-start.5 = (bf16[192,256]{1,0:T(8,128)(2,1)S(1)}, bf16[192,256]{1,0:T(8,128)(2,1)S(1)}, u32[]{:S(2)}, u32[]{:S(2)}) collective-permute-start(bf16[192,256]{1,0:T(8,128)(2,1)S(1)} %get-tuple-element.43), channel_id=1, source_target_pairs={{0,20},{4,16},{8,28},{12,24},{16,4},{20,0},{24,12},{28,8},{1,21},{... | collective-permute-start | bytes 294920 | tf_op jit(solution)/shard_map/ppermute | solution.py:156
  12.2 4.6 %collective-permute-start.6 = (bf16[192,256]{1,0:T(8,128)(2,1)S(1)}, bf16[192,256]{1,0:T(8,128)(2,1)S(1)}, u32[]{:S(2)}, u32[]{:S(2)}) collective-permute-start(bf16[192,256]{1,0:T(8,128)(2,1)S(1)} %get-tuple-element.44), channel_id=1, source_target_pairs={{0,4},{4,0},{8,12},{12,8},{16,20},{20,16},{24,28},{28,24},{1,5},{5... | collective-permute-start | bytes 294920 | tf_op jit(solution)/shard_map/ppermute | solution.py:156
  13.3 7.0 %collective-permute-start.8 = (bf16[32,2048]{1,0:T(8,128)(2,1)S(1)}, bf16[32,2048]{1,0:T(8,128)(2,1)S(1)}, u32[]{:S(2)}, u32[]{:S(2)}) collective-permute-start(bf16[32,2048]{1,0:T(8,128)(2,1)S(1)} %get-tuple-element.63), channel_id=1, source_target_pairs={{0,1},{1,0},{2,3},{3,2},{4,5},{5,4},{6,7},{7,6},{8,9},{9,8},{10,11... | collective-permute-start | bytes 393224 | tf_op jit(solution)/shard_map/ppermute | solution.py:156
